TPU v7x, 32 devices: a whole 2x2x4 slice. The times are simulated.
32 devices in a mesh: docs: 4 (over y, x), wide: 8 (over z, core).
Axes of the slice: x: 2, y: 2, z: 4, core: 2. Of those that a mesh axis runs over, the one named last changes fastest.
Arguments:
- rows: bfloat16 [16384, 768], P(('docs', 'wide')), may hold values from -6 to 6
- cot_stream: float32 [16384, 768], P(('docs', 'wide')), may hold values from -6 to 6
- cot_joined: float32 [8192, 768], P(('docs', 'wide')), may hold values from -6 to 6
- page: int32 [16384], P(('docs', 'wide')), may hold values from -1 to 447, as said below
- key_mask: int32 [16384], P(('docs', 'wide')), may hold values 0 or 1
- w_qkv: float32 [2, 768, 2304], P(None, 'wide', 'docs'), may hold values from -0.21875 to 0.21875
- m_qkv: float32 [2, 768, 2304], P(None, 'wide', 'docs')
- v_qkv: float32 [2, 768, 2304], P(None, 'wide', 'docs'), as said below
- w_out: float32 [2, 768, 768], P(None, 'wide', 'docs'), may hold values from -0.875 to 0.875
- m_out: float32 [2, 768, 768], P(None, 'wide', 'docs')
- v_out: float32 [2, 768, 768], P(None, 'wide', 'docs'), as said below
- w_up: float32 [2, 768, 3072], P(None, 'wide', 'docs'), may hold values from -0.21875 to 0.21875
- m_up: float32 [2, 768, 3072], P(None, 'wide', 'docs')
- v_up: float32 [2, 768, 3072], P(None, 'wide', 'docs'), as said below
- w_down: float32 [2, 3072, 768], P(None, 'wide', 'docs'), may hold values from -0.109375 to 0.109375
- m_down: float32 [2, 3072, 768], P(None, 'wide', 'docs')
- v_down: float32 [2, 3072, 768], P(None, 'wide', 'docs'), as said below
- gains: float32 [5, 768], replicated
- m_gains: float32 [5, 768], replicated
- v_gains: float32 [5, 768], replicated, as said below
Outputs:
- stream_out: float32 [16384, 768], P(('docs', 'wide'))
- joined: float32 [8192, 768], P(('docs', 'wide'))
- grad_rows: float32 [16384, 768], P(('docs', 'wide'))
- new_w_qkv: float32 [2, 768, 2304], P(None, 'wide', 'docs')
- new_m_qkv: float32 [2, 768, 2304], P(None, 'wide', 'docs')
- new_v_qkv: float32 [2, 768, 2304], P(None, 'wide', 'docs')
- new_w_out: float32 [2, 768, 768], P(None, 'wide', 'docs')
- new_m_out: float32 [2, 768, 768], P(None, 'wide', 'docs')
- new_v_out: float32 [2, 768, 768], P(None, 'wide', 'docs')
- new_w_up: float32 [2, 768, 3072], P(None, 'wide', 'docs')
- new_m_up: float32 [2, 768, 3072], P(None, 'wide', 'docs')
- new_v_up: float32 [2, 768, 3072], P(None, 'wide', 'docs')
- new_w_down: float32 [2, 3072, 768], P(None, 'wide', 'docs')
- new_m_down: float32 [2, 3072, 768], P(None, 'wide', 'docs')
- new_v_down: float32 [2, 3072, 768], P(None, 'wide', 'docs')
- new_gains: float32 [5, 768], replicated
- new_m_gains: float32 [5, 768], replicated
- new_v_gains: float32 [5, 768], replicated
Inputs may be any that keep to these rules, and one draw needn't show every extreme that they name: Within each packed row pages are numbered from 0 in order, each at most 64 blocks, the first exactly 64; padding (-1) closes every packed row; the text and image rows of a block carry the same number; the largest page number is reached in every draw. `v_qkv`: second moments are positive. `v_out`: second moments are positive. `v_up`: second moments are positive. `v_down`: second moments are positive. `v_gains`: second moments are positive.
All inputs are finite; a program needn't handle non-finite values. No bound on the sum of `key_mask` on one device may be relied on, other than what follows from the above.
Results may differ from a plain program's by a relative error of at most 0.015.
The roundings to bfloat16 on the way count: a program that leaves them out, or rounds other values in their place, can miss the bound.
Values may be sent and summed in bfloat16 or wider, within the bound.
No kernel may reach another device: no remote copies, remote signals or barrier semaphores. Data moves between devices by JAX's collectives and lax.ppermute only.
A program may use at most 192 MiB of HBM per device.

v0:
```python
import jax
import jax.numpy as jnp
from jax import lax
from jax.sharding import PartitionSpec as P

HEADS = 12
STEP = 10


def from_behind(x, axis, by):
    count = lax.axis_size(axis)
    return lax.ppermute(x, axis, [(i, (i + by) % count) for i in range(count)])


def layer_norm(values, gain):
    centred = values - jnp.mean(values, axis=-1, keepdims=True)
    spread = jnp.mean(centred * centred, axis=-1, keepdims=True)
    return centred * lax.rsqrt(spread + 1e-05) * gain


def gelu_tanh(values):
    return jax.nn.gelu(values, approximate=True)


def adam_update(weight, first, second, grad, rate, decay):
    first_new = 0.9 * first + 0.1 * grad
    second_new = 0.999 * second + 0.001 * grad * grad
    first_hat = first_new / (1.0 - 0.9**STEP)
    second_hat = second_new / (1.0 - 0.999**STEP)
    weight_new = weight - rate * (first_hat / (jnp.sqrt(second_hat) + 1e-08) + decay * weight)
    return (weight_new, first_new, second_new)


def own_stream(piece, stream):
    return lax.dynamic_index_in_dim(piece, stream, 0, keepdims=False)


def placed_stream(piece, is_text):
    blank = jnp.zeros_like(piece)
    return jnp.where(is_text, jnp.stack((piece, blank)), jnp.stack((blank, piece)))


def fetch(w_qkv, w_out, w_up, w_down, stream):
    inner = (
        lax.all_gather(w_qkv.astype(jnp.bfloat16), "docs", axis=2, tiled=True),
        lax.all_gather(w_out.astype(jnp.bfloat16), "docs", axis=2, tiled=True),
        lax.all_gather(w_up.astype(jnp.bfloat16), "docs", axis=2, tiled=True),
        lax.all_gather(w_down.astype(jnp.bfloat16), "docs", axis=2, tiled=True),
    )
    whole = (
        lax.all_gather(inner[0], "wide", axis=1, tiled=True),
        lax.all_gather(inner[1], "wide", axis=1, tiled=True),
        lax.all_gather(inner[2], "wide", axis=1, tiled=True),
        lax.all_gather(inner[3], "wide", axis=1, tiled=True),
    )
    result = tuple((own_stream(piece, stream) for piece in whole))
    return result


def masked_scores(queries, key_rows, allowed, head_count, factor):
    count = queries.shape[0]
    raw = (
        jnp.einsum(
            "qhd,khd->hqk",
            queries.reshape(count, head_count, -1),
            key_rows.reshape(count, head_count, -1),
            preferred_element_type=jnp.float32,
        )
        * factor
    )
    return jnp.where(allowed[None], raw, -1000000000.0)


def shards(
    rows,
    cot_stream,
    cot_joined,
    page,
    key_mask,
    w_qkv,
    m_qkv,
    v_qkv,
    w_out,
    m_out,
    v_out,
    w_up,
    m_up,
    v_up,
    w_down,
    m_down,
    v_down,
    gains,
    m_gains,
    v_gains,
):
    half_size = lax.axis_size("wide") // 2
    stream = lax.axis_index("wide") // half_size
    is_text = stream == 0
    head_count = HEADS
    length = rows.shape[0]
    model_width = rows.shape[1]
    factor = float(model_width // head_count) ** (-0.5)
    qkv_low, out_low, up_low, down_low = fetch(w_qkv, w_out, w_up, w_down, stream)
    inputs = rows.astype(jnp.float32)
    valid_rows = (page >= 0).astype(jnp.float32)[:, None]
    gain_one = lax.dynamic_index_in_dim(gains, stream, 0, keepdims=False)
    gain_two = lax.dynamic_index_in_dim(gains, 2 + stream, 0, keepdims=False)
    gate_logit = gains[4]
    normed_one = layer_norm(inputs, gain_one).astype(jnp.bfloat16)
    projected = jnp.dot(normed_one, qkv_low, preferred_element_type=jnp.float32).astype(
        jnp.bfloat16
    )
    queries = projected[:, :model_width]
    own_kv = jnp.stack(
        (projected[:, model_width : 2 * model_width], projected[:, 2 * model_width :])
    )
    partner_kv = from_behind(own_kv, "wide", half_size)
    key_rows = partner_kv[0]
    value_heads = partner_kv[1].reshape(length, head_count, -1)
    position = lax.iota(jnp.int32, length)
    allowed = (page[:, None] == page[None, :]) & (
        (key_mask[None, :] == 1) | (position[:, None] == position[None, :])
    )
    scores = masked_scores(queries, key_rows, allowed, head_count, factor)
    row_top = jnp.max(scores, axis=-1, keepdims=True)
    log_total = row_top + jnp.log(jnp.sum(jnp.exp(scores - row_top), axis=-1, keepdims=True))
    probs_low = jnp.exp(scores - log_total).astype(jnp.bfloat16)
    attended = (
        jnp.einsum("hqk,khd->qhd", probs_low, value_heads, preferred_element_type=jnp.float32)
        .reshape(length, model_width)
        .astype(jnp.bfloat16)
    )
    branch = jnp.dot(attended, out_low, preferred_element_type=jnp.float32)
    middle = inputs + valid_rows * branch
    normed_two = layer_norm(middle, gain_two).astype(jnp.bfloat16)
    pre_act = jnp.dot(normed_two, up_low, preferred_element_type=jnp.float32)
    activated, gelu_back = jax.vjp(gelu_tanh, pre_act)
    acts_low = activated.astype(jnp.bfloat16)
    stream_out = middle + valid_rows * jnp.dot(
        acts_low, down_low, preferred_element_type=jnp.float32
    )
    half_rows = length // 2
    own_rows = lax.dynamic_slice_in_dim(stream_out, stream * half_rows, half_rows, 0)
    outgoing = lax.dynamic_slice_in_dim(stream_out, (1 - stream) * half_rows, half_rows, 0)
    partner_rows = from_behind(outgoing.astype(jnp.bfloat16), "wide", half_size).astype(
        outgoing.dtype
    )
    text_rows = jnp.where(is_text, own_rows, partner_rows)
    image_rows = jnp.where(is_text, partner_rows, own_rows)
    gate_mix = jax.nn.sigmoid(gate_logit)
    joined_rows = gate_mix * text_rows + (1.0 - gate_mix) * image_rows
    qkv_low, out_low, up_low, down_low = fetch(w_qkv, w_out, w_up, w_down, stream)
    gate_grad = jnp.sum(cot_joined * (text_rows - image_rows), axis=0) * gate_mix * (1.0 - gate_mix)
    text_grad = cot_joined * gate_mix
    image_grad = cot_joined * (1.0 - gate_mix)
    own_grad = jnp.where(is_text, text_grad, image_grad)
    other_grad = jnp.where(is_text, image_grad, text_grad)
    returned = from_behind(other_grad, "wide", half_size)
    upper_grad = jnp.where(is_text, own_grad, returned)
    lower_grad = jnp.where(is_text, returned, own_grad)
    out_grad = cot_stream + jnp.concatenate((upper_grad, lower_grad), axis=0)
    ffn_grad = (out_grad * valid_rows).astype(jnp.bfloat16)
    down_grad = jnp.dot(acts_low.T, ffn_grad, preferred_element_type=jnp.float32)
    acts_grad = jnp.dot(ffn_grad, down_low.T, preferred_element_type=jnp.float32)
    pre_grad = gelu_back(acts_grad)[0].astype(jnp.bfloat16)
    up_grad = jnp.dot(normed_two.T, pre_grad, preferred_element_type=jnp.float32)
    normed_two_grad = jnp.dot(pre_grad, up_low.T, preferred_element_type=jnp.float32)
    unused_two, norm_two_back = jax.vjp(layer_norm, middle, gain_two)
    middle_part, gain_two_grad = norm_two_back(normed_two_grad)
    middle_grad = out_grad + middle_part
    branch_grad = (middle_grad * valid_rows).astype(jnp.bfloat16)
    out_proj_grad = jnp.dot(attended.T, branch_grad, preferred_element_type=jnp.float32)
    attended_grad = jnp.dot(branch_grad, out_low.T, preferred_element_type=jnp.float32).astype(
        jnp.bfloat16
    )
    attended_grad = attended_grad.reshape(length, head_count, -1)
    probability = jnp.exp(masked_scores(queries, key_rows, allowed, head_count, factor) - log_total)
    probs_again = probability.astype(jnp.bfloat16)
    prob_grad = jnp.einsum(
        "qhd,khd->hqk", attended_grad, value_heads, preferred_element_type=jnp.float32
    )
    value_grad = jnp.einsum(
        "hqk,qhd->khd", probs_again, attended_grad, preferred_element_type=jnp.float32
    ).reshape(length, model_width)
    score_grad = (
        probability * (prob_grad - jnp.sum(prob_grad * probability, axis=-1, keepdims=True))
    ).astype(jnp.bfloat16)
    query_grad = (
        jnp.einsum(
            "hqk,khd->qhd",
            score_grad,
            key_rows.reshape(length, head_count, -1),
            preferred_element_type=jnp.float32,
        )
        * factor
    ).reshape(length, model_width)
    key_grad = (
        jnp.einsum(
            "hqk,qhd->khd",
            score_grad,
            queries.reshape(length, head_count, -1),
            preferred_element_type=jnp.float32,
        )
        * factor
    ).reshape(length, model_width)
    kv_grad = jnp.stack((key_grad, value_grad)).astype(jnp.bfloat16)
    own_kv_grad = from_behind(kv_grad, "wide", half_size)
    proj_grad = jnp.concatenate(
        (query_grad.astype(jnp.bfloat16), own_kv_grad[0], own_kv_grad[1]), axis=1
    )
    qkv_grad = jnp.dot(normed_one.T, proj_grad, preferred_element_type=jnp.float32)
    normed_one_grad = jnp.dot(proj_grad, qkv_low.T, preferred_element_type=jnp.float32)
    unused_one, norm_one_back = jax.vjp(layer_norm, inputs, gain_one)
    input_part, gain_one_grad = norm_one_back(normed_one_grad)
    grad_rows = middle_grad + input_part
    placed = tuple(
        (placed_stream(piece, is_text) for piece in (qkv_grad, out_proj_grad, up_grad, down_grad))
    )
    halves = (
        lax.psum_scatter(placed[0], "wide", scatter_dimension=1, tiled=True),
        lax.psum_scatter(placed[1], "wide", scatter_dimension=1, tiled=True),
        lax.psum_scatter(placed[2], "wide", scatter_dimension=1, tiled=True),
        lax.psum_scatter(placed[3], "wide", scatter_dimension=1, tiled=True),
    )
    reduced = (
        lax.psum_scatter(halves[0], "docs", scatter_dimension=2, tiled=True),
        lax.psum_scatter(halves[1], "docs", scatter_dimension=2, tiled=True),
        lax.psum_scatter(halves[2], "docs", scatter_dimension=2, tiled=True),
        lax.psum_scatter(halves[3], "docs", scatter_dimension=2, tiled=True),
    )
    slot_index = lax.iota(jnp.int32, 5)[:, None]
    small_terms = (
        jnp.where(slot_index == stream, gain_one_grad[None, :], 0.0)
        + jnp.where(slot_index == 2 + stream, gain_two_grad[None, :], 0.0)
        + jnp.where(slot_index == 4, gate_grad[None, :], 0.0)
    )
    gains_grad = lax.psum(small_terms, ("docs", "wide"))
    qkv_new = adam_update(w_qkv, m_qkv, v_qkv, reduced[0], 0.12, 0.01)
    out_new = adam_update(w_out, m_out, v_out, reduced[1], 0.5, 0.01)
    up_new = adam_update(w_up, m_up, v_up, reduced[2], 0.12, 0.01)
    down_new = adam_update(w_down, m_down, v_down, reduced[3], 0.06, 0.01)
    gains_new = adam_update(gains, m_gains, v_gains, gains_grad, 0.8, 0.0)
    return (
        stream_out,
        joined_rows,
        grad_rows,
        qkv_new[0],
        qkv_new[1],
        qkv_new[2],
        out_new[0],
        out_new[1],
        out_new[2],
        up_new[0],
        up_new[1],
        up_new[2],
        down_new[0],
        down_new[1],
        down_new[2],
        gains_new[0],
        gains_new[1],
        gains_new[2],
    )


def solution(mesh):
    return jax.shard_map(
        shards,
        mesh=mesh,
        in_specs=(
            P(("docs", "wide"), None),
            P(("docs", "wide"), None),
            P(("docs", "wide"), None),
            P(("docs", "wide")),
            P(("docs", "wide")),
            P(None, "wide", "docs"),
            P(None, "wide", "docs"),
            P(None, "wide", "docs"),
            P(None, "wide", "docs"),
            P(None, "wide", "docs"),
            P(None, "wide", "docs"),
            P(None, "wide", "docs"),
            P(None, "wide", "docs"),
            P(None, "wide", "docs"),
            P(None, "wide", "docs"),
            P(None, "wide", "docs"),
            P(None, "wide", "docs"),
            P(),
            P(),
            P(),
        ),
        out_specs=(
            P(("docs", "wide"), None),
            P(("docs", "wide"), None),
            P(("docs", "wide"), None),
            P(None, "wide", "docs"),
            P(None, "wide", "docs"),
            P(None, "wide", "docs"),
            P(None, "wide", "docs"),
            P(None, "wide", "docs"),
            P(None, "wide", "docs"),
            P(None, "wide", "docs"),
            P(None, "wide", "docs"),
            P(None, "wide", "docs"),
            P(None, "wide", "docs"),
            P(None, "wide", "docs"),
            P(None, "wide", "docs"),
            P(),
            P(),
            P(),
        ),
        check_vma=False,
    )
```

profile of v0, /device:TPU:0, one launch (start us, length us, event | category | flops | bytes accessed | tf_op | source)
XLA Modules:
  0.0 1354.8 jit_solution(5114454889149823214)
XLA Ops:
  12.3 19.2 %all_gather.32 = bf16[2,96,2304]{1,0,2:T(2,128)(2,1)S(1)} all-gather(bf16[2,96,576]{1,0,2:T(2,128)(2,1)S(1)} %copy.110), channel_id=1, replica_groups=mesh['docs'=4,'wide'=8] {'docs'}, dimensions={2}, use_global_device_ids=true | all-gather | bytes 1105920 | tf_op jit(solution)/shard_map/all_gather | solution.py:45
  31.5 2.4 copy.111
  34.1 12.6 all_gather.34
  48.5 29.0 %all-gather.15.cloned.1.call-done = bf16[2,384,768]{1,2,0:T(8,128)(2,1)} async-done(((bf16[2,384,192]{1,2,0:T(8,128)(2,1)}), bf16[2,384,768]{1,2,0:T(8,128)(2,1)}) %all-gather.15.cloned.1.call-update) | async-done | bytes 1179664 | tf_op jit(solution)/shard_map/all_gather | solution.py:48
  79.0 71.9 %all-gather.7.cloned.1.call-done = bf16[2,768,2304]{2,1,0:T(8,128)(2,1)} async-done(((bf16[2,96,2304]{2,1,0:T(8,128)(2,1)}), bf16[2,768,2304]{2,1,0:T(8,128)(2,1)}) %all-gather.7.cloned.1.call-update) | async-done | bytes 7077904 | tf_op jit(solution)/shard_map/all_gather | solution.py:51
  150.9 4.1 convolution_convert_fusion
  158.1 110.5 %collective-permute-done = bf16[2,512,768]{2,1,0:T(8,128)(2,1)} collective-permute-done((bf16[2,512,768]{2,1,0:T(8,128)(2,1)}, bf16[2,512,768]{2,1,0:T(8,128)(2,1)}, u32[]{:S(2)}, u32[]{:S(2)}) %collective-permute-start) | collective-permute-done | bytes 1572896 | tf_op jit(solution)/shard_map/ppermute | solution.py:12
  268.6 2.4 fusion.81
  273.0 2.1 fusion
  275.1 2.6 exponential_reduce_fusion
  279.6 3.7 convolution_convert_fusion.3
  283.3 2.5 fusion.82
  286.1 37.1 %all-gather.13.cloned.1.call-done = bf16[2,768,3072]{2,1,0:T(8,128)(2,1)} async-done(((bf16[2,96,3072]{2,1,0:T(8,128)(2,1)}), bf16[2,768,3072]{2,1,0:T(8,128)(2,1)}) %all-gather.13.cloned.1.call-update) | async-done | bytes 9437200 | tf_op jit(solution)/shard_map/all_gather | solution.py:53
  323.2 7.0 fusion.15
  330.2 85.2 %all-gather.17.cloned.1.call-done = bf16[2,3072,768]{1,2,0:T(8,128)(2,1)} async-done(((bf16[2,384,768]{1,2,0:T(8,128)(2,1)}), bf16[2,3072,768]{1,2,0:T(8,128)(2,1)}) %all-gather.17.cloned.1.call-update) | async-done | bytes 9437200 | tf_op jit(solution)/shard_map/all_gather | solution.py:54
  415.4 7.4 multiply_add_fusion
  425.0 18.2 %collective-permute-done.1 = bf16[256,768]{1,0:T(8,128)(2,1)S(1)} collective-permute-done((bf16[256,768]{1,0:T(8,128)(2,1)S(1)}, bf16[256,768]{1,0:T(8,128)(2,1)S(1)}, u32[]{:S(2)}, u32[]{:S(2)}) %collective-permute-start.1) | collective-permute-done | bytes 393248 | tf_op jit(solution)/shard_map/ppermute | solution.py:12
  444.7 36.0 %collective-permute-done.2 = f32[256,768]{1,0:T(8,128)S(1)} collective-permute-done((f32[256,768]{1,0:T(8,128)S(1)}, f32[256,768]{1,0:T(8,128)S(1)}, u32[]{:S(2)}, u32[]{:S(2)}) %collective-permute-start.2) | collective-permute-done | bytes 786464 | tf_op jit(solution)/shard_map/ppermute | solution.py:12
  484.1 7.8 fusion.8
  491.9 2.9 multiply_reduce_fusion.1
  497.5 2.5 pad_select_fusion.3
  500.1 3.0 convolution_convert_fusion.1
  503.1 2.3 copy.118
  505.4 13.9 %multiply_reduce_fusion = (f32[12,512]{1,0:T(8,128)S(1)}, f32[12,512,512]{1,2,0:T(8,128)}) fusion(f32[12,512,512]{1,2,0:T(8,128)} %copy-done, f32[12,512]{1,0:T(8,128)S(1)} %log_add_fusion, pred[512,512]{0,1:T(8,128)(4,1)S(1)} %fusion.41, bf16[512,12,64]{0,2,1:T(8,128)(2,1)} %bitcast.92, bf16[512,12,64]{0,2,1:T(8,128)(2,1)} %bitcast.91), kind=kOutput, calls=%fused_computation.4 | convolution fusion | flops 418375680 | bytes 27049984 | tf_op jit(solution)/shard_map/qhd,khd->hqk/dot_general | solution.py:179
  519.4 7.3 multiply_convert_fusion
  526.7 2.0 multiply_convert_fusion.2
  528.7 3.8 convolution_convert_fusion.2
  535.1 86.1 %collective-permute-done.3 = bf16[2,512,768]{1,2,0:T(8,128)(2,1)S(1)} collective-permute-done((bf16[2,512,768]{1,2,0:T(8,128)(2,1)S(1)}, bf16[2,512,768]{1,2,0:T(8,128)(2,1)S(1)}, u32[]{:S(2)}, u32[]{:S(2)}) %collective-permute-start.3) | collective-permute-done | bytes 1572896 | tf_op jit(solution)/shard_map/ppermute | solution.py:12
  622.5 5.2 convolution_bitcast_fusion
  627.6 10.9 pad_select_fusion.2
  638.6 5.6 convolution_bitcast_fusion.1
  644.2 6.6 pad_select_fusion
  651.1 4.7 convolution_bitcast_fusion.2
  655.8 7.2 pad_select_fusion.1
  666.0 115.4 %reduce-scatter.12.cloned.1.call-done = f32[2,96,2304]{2,1,0:T(8,128)} async-done(((f32[2,768,2304]{2,1,0:T(8,128)}), f32[2,96,2304]{2,1,0:T(8,128)}) %reduce-scatter.12.cloned.1.call-update) | async-done | bytes 1769488 | tf_op jit(solution)/shard_map/reduce_scatter | solution.py:220
  781.4 4.1 copy.130
  785.5 3.9 reshape.191
  789.5 180.5 %reduce-scatter.20.cloned.1.call-done = f32[2,384,768]{2,1,0:T(8,128)} async-done(((f32[2,3072,768]{2,1,0:T(8,128)}), f32[2,384,768]{2,1,0:T(8,128)}) %reduce-scatter.20.cloned.1.call-update) | async-done | bytes 2359312 | tf_op jit(solution)/shard_map/reduce_scatter | solution.py:223
  970.1 5.3 copy.122
  975.5 183.1 %reduce-scatter.16.cloned.1.call-done = f32[2,96,3072]{2,1,0:T(8,128)} async-done(((f32[2,768,3072]{2,1,0:T(8,128)}), f32[2,96,3072]{2,1,0:T(8,128)}) %reduce-scatter.16.cloned.1.call-update) | async-done | bytes 2359312 | tf_op jit(solution)/shard_map/reduce_scatter | solution.py:222
  1160.0 4.8 fusion.35
  1166.8 38.5 %psum.7 = f32[5,768]{1,0:T(8,128)S(1)} all-reduce(f32[5,768]{1,0:T(8,128)S(1)} %select_add_fusion), channel_id=1, replica_groups=mesh['docs'=4,'wide'=8] {'docs','wide'}, use_global_device_ids=true, to_apply=%region_22.23 | all-reduce | flops 3840 | bytes 30720 | tf_op jit(solution)/shard_map/psum | solution.py:237
  1206.0 3.2 add_add_fusion.2
  1211.4 15.9 %reduce-scatter.22.cloned.1.call-done = f32[576,192]{1,0:T(8,128)} async-done(((f32[2304,192]{1,0:T(8,128)}), f32[576,192]{1,0:T(8,128)}) %reduce-scatter.22.cloned.1.call-update) | async-done | bytes 442384
  1229.0 2.6 multiply_subtract_fusion.2
  1231.6 72.8 %all-reduce.11.cloned.1.call-done = f32[2,384,768]{1,0,2:T(2,128)} async-done(((f32[2,384,768]{1,0,2:T(2,128)}), f32[2,384,768]{1,0,2:T(2,128)}) %all-reduce.11.cloned.1.call-update) | async-done | bytes 2359312
  1307.2 37.8 %reduce-scatter.18.cloned.1.call-done = f32[2,96,768]{2,1,0:T(8,128)} async-done(((f32[2,96,3072]{2,1,0:T(8,128)}), f32[2,96,768]{2,1,0:T(8,128)}) %reduce-scatter.18.cloned.1.call-update) | async-done | bytes 589840 | tf_op jit(solution)/shard_map/reduce_scatter | solution.py:228
  1345.1 2.7 multiply_subtract_fusion.1
  (189 shorter events, 42.6 us)
Async XLA Ops:
  7.2 40.7 %all-gather.11.cloned.1.call-start = ((), (), s32[]{:S(2)}) async-start(), calls=%async_computation.9 | async-start | bytes 1474560 | tf_op jit(solution)/shard_map/all_gather | solution.py:47
  9.1 68.3 %all-gather.15.cloned.1.call-start = ((), (), s32[]{:S(2)}) async-start(), calls=%async_computation.11 | async-start | bytes 1474560 | tf_op jit(solution)/shard_map/all_gather | solution.py:48
  10.9 23.1 %copy-start.24 = (f32[2,96,192]{2,1,0:T(8,128)S(1)}, f32[2,96,192]{2,1,0:T(8,128)}, u32[]{:S(2)}) copy-start(f32[2,96,192]{2,1,0:T(8,128)} %param.28) | copy-start | bytes 442372
  11.0 139.9 %all-gather.7.cloned.1.call-start = ((), (), s32[]{:S(2)}) async-start(), calls=%async_computation.7 | async-start | bytes 7962624 | tf_op jit(solution)/shard_map/all_gather | solution.py:51
  31.5 46.0 %copy-start.1 = (bf16[512,768]{1,0:T(8,128)(2,1)S(1)}, bf16[512,768]{1,0:T(8,128)(2,1)}, u32[]{:S(2)}) copy-start(bf16[512,768]{1,0:T(8,128)(2,1)} %param.20) | copy-start | bytes 2359300
  33.9 249.4 %all-gather.9.cloned.1.call-start = ((), (), s32[]{:S(2)}) async-start(), calls=%async_computation.8 | async-start | bytes 2654208 | tf_op jit(solution)/shard_map/all_gather | solution.py:52
  47.8 275.4 %all-gather.13.cloned.1.call-start = ((), (), s32[]{:S(2)}) async-start(), calls=%async_computation.10 | async-start | bytes 10616832 | tf_op jit(solution)/shard_map/all_gather | solution.py:53
  48.4 367.0 %all-gather.17.cloned.1.call-start = ((), (), s32[]{:S(2)}) async-start(), calls=%async_computation.12 | async-start | bytes 10616832 | tf_op jit(solution)/shard_map/all_gather | solution.py:54
  77.4 585.7 %reduce-scatter.14.cloned.1.call-start = ((), (), s32[]{:S(2)}) async-start(), calls=%async_computation.14 | async-start | bytes 5308416 | tf_op jit(solution)/shard_map/reduce_scatter | solution.py:221
  78.1 76.9 %copy-start.37 = (f32[512]{0:T(512)}, f32[512]{0:T(512)S(1)}, u32[]{:S(2)}) copy-start(f32[512]{0:T(512)S(1)} %fusion.34) | copy-start | bytes 6148
  156.5 112.2 %collective-permute-start = (bf16[2,512,768]{2,1,0:T(8,128)(2,1)}, bf16[2,512,768]{2,1,0:T(8,128)(2,1)}, u32[]{:S(2)}, u32[]{:S(2)}) collective-permute-start(bf16[2,512,768]{2,1,0:T(8,128)(2,1)} %pad_maximum_fusion.1), channel_id=1, source_target_pairs={{0,4},{1,5},{2,6},{3,7},{4,0},{5,1},{6,2},{7,3},{8,12},{9,13},{10,... | collective-permute-start | bytes 4718600 | tf_op jit(solution)/shard_map/ppermute | solution.py:12
  158.1 114.9 %copy-start.6 = (bf16[512,768]{0,1:T(8,128)(2,1)}, bf16[512,768]{0,1:T(8,128)(2,1)S(1)}, u32[]{:S(2)}) copy-start(bf16[512,768]{0,1:T(8,128)(2,1)S(1)} %copy.113) | copy-start | bytes 2359300
  271.2 6.4 copy-start.11
  330.2 113.0 %copy-start.8 = (f32[256,768]{1,0:T(8,128)S(1)}, f32[256,768]{1,0:T(8,128)}, u32[]{:S(2)}) copy-start(f32[256,768]{1,0:T(8,128)} %param.22) | copy-start | bytes 2359300
  424.0 19.2 %collective-permute-start.1 = (bf16[256,768]{1,0:T(8,128)(2,1)S(1)}, bf16[256,768]{1,0:T(8,128)(2,1)S(1)}, u32[]{:S(2)}, u32[]{:S(2)}) collective-permute-start(bf16[256,768]{1,0:T(8,128)(2,1)S(1)} %dynamic-slice_convert_fusion), channel_id=1, source_target_pairs={{0,4},{1,5},{2,6},{3,7},{4,0},{5,1},{6,2},{7,3},{8,12},{9,13},{10,... | collective-permute-start | bytes 1179656 | tf_op jit(solution)/shard_map/ppermute | solution.py:12
  425.0 55.7 %copy-start.17 = (f32[512,768]{1,0:T(8,128)S(1)}, f32[512,768]{1,0:T(8,128)}, u32[]{:S(2)}) copy-start(f32[512,768]{1,0:T(8,128)} %copy-done.16) | copy-start | bytes 4718596
  444.5 37.4 %copy-start.9 = (f32[512,768]{1,0:T(8,128)S(1)}, f32[512,768]{1,0:T(8,128)}, u32[]{:S(2)}) copy-start(f32[512,768]{1,0:T(8,128)} %param.21) | copy-start | bytes 4718596
  444.6 36.0 %collective-permute-start.2 = (f32[256,768]{1,0:T(8,128)S(1)}, f32[256,768]{1,0:T(8,128)S(1)}, u32[]{:S(2)}, u32[]{:S(2)}) collective-permute-start(f32[256,768]{1,0:T(8,128)S(1)} %multiply_select_fusion.1), channel_id=1, source_target_pairs={{0,4},{1,5},{2,6},{3,7},{4,0},{5,1},{6,2},{7,3},{8,12},{9,13},{10,... | collective-permute-start | bytes 2359304 | tf_op jit(solution)/shard_map/ppermute | solution.py:12
  482.0 9.9 slice-start.3
  484.1 7.8 slice-start.4
  484.1 7.8 slice-start.5
  500.0 281.4 %reduce-scatter.12.cloned.1.call-start = ((), (), s32[]{:S(2)}) async-start(), calls=%async_computation.13 | async-start | bytes 15925248 | tf_op jit(solution)/shard_map/reduce_scatter | solution.py:220
  505.4 14.0 %slice-start = ((s8[12582912]{0:T(1024)(128)(4,1)}), s8[4194304]{0:T(1024)(128)(4,1)S(1)}, s32[]{:S(2)}) async-start(s8[12582912]{0:T(1024)(128)(4,1)} %bitcast.83), calls=%async_computation.21 | async-start | bytes 8388608
  505.4 14.0 %slice-start.1 = ((s8[12582912]{0:T(1024)(128)(4,1)}), s8[4194304]{0:T(1024)(128)(4,1)S(1)}, s32[]{:S(2)}) async-start(s8[12582912]{0:T(1024)(128)(4,1)} %bitcast.83), calls=%async_computation.22 | async-start | bytes 8388608
  505.4 14.0 %slice-start.2 = ((s8[12582912]{0:T(1024)(128)(4,1)}), s8[4194304]{0:T(1024)(128)(4,1)S(1)}, s32[]{:S(2)}) async-start(s8[12582912]{0:T(1024)(128)(4,1)} %bitcast.83), calls=%async_computation.23 | async-start | bytes 8388608
  519.3 7.3 copy-start.7
  533.8 87.4 %collective-permute-start.3 = (bf16[2,512,768]{1,2,0:T(8,128)(2,1)S(1)}, bf16[2,512,768]{1,2,0:T(8,128)(2,1)S(1)}, u32[]{:S(2)}, u32[]{:S(2)}) collective-permute-start(bf16[2,512,768]{1,2,0:T(8,128)(2,1)S(1)} %pad_maximum_fusion.2), channel_id=1, source_target_pairs={{0,4},{1,5},{2,6},{3,7},{4,0},{5,1},{6,2},{7,3},{8,12},{9,13},{10,... | collective-permute-start | bytes 4718600 | tf_op jit(solution)/shard_map/ppermute | solution.py:12
  535.1 86.3 %copy-start.14 = (bf16[12,64,512]{2,1,0:T(8,128)(2,1)}, bf16[12,64,512]{2,1,0:T(8,128)(2,1)S(1)}, u32[]{:S(2)}) copy-start(bf16[12,64,512]{2,1,0:T(8,128)(2,1)S(1)} %multiply_convert_fusion.3) | copy-start | bytes 2359300
  535.1 87.4 %copy-start.2 = (bf16[512,768]{1,0:T(8,128)(2,1)S(1)}, bf16[512,768]{1,0:T(8,128)(2,1)}, u32[]{:S(2)}) copy-start(bf16[512,768]{1,0:T(8,128)(2,1)} %param.20) | copy-start | bytes 2359300
  638.5 331.5 %reduce-scatter.20.cloned.1.call-start = ((), (), s32[]{:S(2)}) async-start(), calls=%async_computation.17 | async-start | bytes 21233664 | tf_op jit(solution)/shard_map/reduce_scatter | solution.py:223
  650.8 507.8 %reduce-scatter.16.cloned.1.call-start = ((), (), s32[]{:S(2)}) async-start(), calls=%async_computation.15 | async-start | bytes 21233664 | tf_op jit(solution)/shard_map/reduce_scatter | solution.py:222
  663.1 546.1 %reduce-scatter.24.cloned.1.call-start = ((), (), s32[]{:S(2)}) async-start(), calls=%async_computation.19 | async-start | bytes 983040
  665.9 561.3 %reduce-scatter.22.cloned.1.call-start = ((), (), s32[]{:S(2)}) async-start(), calls=%async_computation.18 | async-start | bytes 2949120
  789.5 515.0 %all-reduce.11.cloned.1.call-start = ((), (), s32[]{:S(2)}) async-start(), calls=%async_computation.20 | async-start | bytes 4718592
  975.4 183.2 %copy-start.40 = (u32[32]{0:T(128)S(1)}, u32[32]{0:T(128)}, u32[]{:S(2)}) copy-start(u32[32]{0:T(128)} %constant.188) | copy-start | bytes 388
  975.4 184.5 %copy-start.3 = (bf16[512,768]{1,0:T(8,128)(2,1)S(1)}, bf16[512,768]{1,0:T(8,128)(2,1)}, u32[]{:S(2)}) copy-start(bf16[512,768]{1,0:T(8,128)(2,1)} %param.20) | copy-start | bytes 2359300
  975.4 184.5 %copy-start.15 = (bf16[12,64,512]{2,1,0:T(8,128)(2,1)S(1)}, bf16[12,64,512]{2,1,0:T(8,128)(2,1)}, u32[]{:S(2)}) copy-start(bf16[12,64,512]{2,1,0:T(8,128)(2,1)} %copy-done.14) | copy-start | bytes 2359300
  975.5 369.6 %reduce-scatter.18.cloned.1.call-start = ((), (), s32[]{:S(2)}) async-start(), calls=%async_computation.16 | async-start | bytes 2949120 | tf_op jit(solution)/shard_map/reduce_scatter | solution.py:228
  1160.0 4.8 copy-start.38
  1160.0 45.3 %copy-start.33 = (f32[5,768]{1,0:T(8,128)S(1)}, f32[5,768]{1,0:T(8,128)}, u32[]{:S(2)}) copy-start(f32[5,768]{1,0:T(8,128)} %param.37) | copy-start | bytes 46084
  1160.0 45.3 %copy-start.34 = (f32[5,768]{1,0:T(8,128)S(1)}, f32[5,768]{1,0:T(8,128)}, u32[]{:S(2)}) copy-start(f32[5,768]{1,0:T(8,128)} %param.38) | copy-start | bytes 46084
  1160.0 45.3 %copy-start.35 = (f32[5,768]{1,0:T(8,128)S(1)}, f32[5,768]{1,0:T(8,128)}, u32[]{:S(2)}) copy-start(f32[5,768]{1,0:T(8,128)} %param.39) | copy-start | bytes 46084
  1209.1 19.9 %copy-start.20 = (f32[2,96,576]{2,1,0:T(8,128)S(1)}, f32[2,96,576]{2,1,0:T(8,128)}, u32[]{:S(2)}) copy-start(f32[2,96,576]{2,1,0:T(8,128)} %param.25) | copy-start | bytes 1327108
  1228.7 77.0 %copy-start.18 = (f32[2,384,192]{1,2,0:T(8,128)S(1)}, f32[2,384,192]{1,2,0:T(8,128)}, u32[]{:S(2)}) copy-start(f32[2,384,192]{1,2,0:T(8,128)} %param.34) | copy-start | bytes 1769476
  1228.7 77.0 %copy-start.28 = (f32[2,384,192]{1,2,0:T(8,128)S(1)}, f32[2,384,192]{1,2,0:T(8,128)}, u32[]{:S(2)}) copy-start(f32[2,384,192]{1,2,0:T(8,128)} %param.35) | copy-start | bytes 1769476
  1228.7 77.0 %copy-start.29 = (f32[2,384,192]{1,2,0:T(8,128)S(1)}, f32[2,384,192]{1,2,0:T(8,128)}, u32[]{:S(2)}) copy-start(f32[2,384,192]{1,2,0:T(8,128)} %param.36) | copy-start | bytes 1769476
  1231.6 113.4 %copy-start.19 = (f32[2,96,768]{2,1,0:T(8,128)S(1)}, f32[2,96,768]{2,1,0:T(8,128)}, u32[]{:S(2)}) copy-start(f32[2,96,768]{2,1,0:T(8,128)} %param.31) | copy-start | bytes 1769476
  1231.6 113.4 %copy-start.30 = (f32[2,96,768]{2,1,0:T(8,128)S(1)}, f32[2,96,768]{2,1,0:T(8,128)}, u32[]{:S(2)}) copy-start(f32[2,96,768]{2,1,0:T(8,128)} %param.32) | copy-start | bytes 1769476
  (18 other events, 44.1 us)
Sparse Core Ops, SparseCore 0:
  10.4 36.4 all-gather.10
  49.3 28.0 all-gather.14
  79.6 71.2 all-gather.6
  152.9 69.7 all-gather.8
  224.1 99.0 all-gather.12
  324.7 90.7 all-gather.16
  500.1 71.3 reduce-scatter.13
  638.7 142.6 reduce-scatter.11
  783.7 186.2 reduce-scatter.19
  972.3 186.3 reduce-scatter.15
  1161.6 24.7 reduce-scatter.23
  1189.2 37.9 reduce-scatter.21
  1230.4 74.0 all-reduce.10
  1307.6 37.3 reduce-scatter.17
where the time goes:
time: 1360 us; the launch traced here: 1350 us
  waiting for transfers between devices  1080 us (79%)
  matrix products  82.4 us (6%)
  blocking collectives  70.3 us (5%)
  other arithmetic  62.8 us (5%)
  local copies, waits for them, and re-layouts  40.1 us (3%)
  between operations  15.9 us (1%)
    ppermute x4, waiting for transfers between devices, from_behind(): return lax.ppermute(x, axis, [(i, (i + by) % count) for i in range(count)])  251 us
    reduce_scatter x1, waiting for transfers between devices, shards(): lax.psum_scatter(placed[2], 'wide', scatter_dimension=1, tiled=True)  183 us
    reduce_scatter x1, waiting for transfers between devices, shards(): lax.psum_scatter(placed[3], 'wide', scatter_dimension=1, tiled=True)  181 us
    reduce_scatter x1, waiting for transfers between devices, shards(): lax.psum_scatter(placed[0], 'wide', scatter_dimension=1, tiled=True)  115 us
    unnamed x17, waiting for transfers between devices  89.4 us
    all_gather x1, waiting for transfers between devices, fetch(): lax.all_gather(inner[3], 'wide', axis=1, tiled=True)  85.2 us
    all_gather x1, waiting for transfers between devices, fetch(): lax.all_gather(inner[0], 'wide', axis=1, tiled=True)  71.9 us
    psum x1, blocking collectives, shards(): gains_grad = lax.psum(small_terms, ('docs', 'wide'))  38.5 us
  transfers between devices with their start and end apart: 18, of which 14 were waited for; matrix products, arithmetic and copies ran while one was open for 11% of the time, Pallas kernels for 0%

commit v1 on v0

v1 whole, which is shorter than its diff:
```python
import functools

import jax
import jax.numpy as jnp
from jax import lax
from jax.experimental import pallas as pl
from jax.experimental.pallas import tpu as pltpu
from jax.sharding import PartitionSpec as P

HEADS = 12
STEP = 10
LANES = 128
CHUNK = 128
NEG = -1000000000.0
LOW = jnp.bfloat16
FULL = jnp.float32


def flip(value, axis, mask):
    count = lax.axis_size(axis)
    return lax.ppermute(value, axis, [(i, i ^ mask) for i in range(count)])


def flipped(codes, axis, mask):
    d_mask = mask if axis == "docs" else 0
    w_mask = mask if axis == "wide" else 0
    return [(d ^ d_mask, w ^ w_mask) for d, w in codes]


def gather(unit, order):
    arrays, codes = [unit[None]], [[(0, 0)]]
    for axis, mask in order:
        held = arrays[0] if len(arrays) == 1 else jnp.concatenate(arrays, axis=0)
        known = [code for group in codes for code in group]
        arrays.append(flip(held, axis, mask))
        codes.append(flipped(known, axis, mask))
    return arrays, codes


def sum_codes(order):
    codes = [(0, 0)]
    for axis, mask in reversed(order):
        codes = codes + flipped(codes, axis, mask)
    return codes


def reduce_pieces(keep, send, order):
    parts = [keep]
    outgoing = send
    for step, (axis, mask) in enumerate(order):
        parts.append(flip(outgoing, axis, mask))
        if step + 1 < len(order):
            half = parts[0].shape[0] // 2
            outgoing = sum(part[half:].astype(FULL) for part in parts).astype(LOW)
            parts = [part[:half] for part in parts]
    return sum(part[0].astype(FULL) for part in parts)


def small_sum(value, steps):
    for axis, mask in steps:
        value = value + flip(value, axis, mask)
    return value


class Blocks:
    def __init__(self, count, size):
        self.count, self.size = count, size
        shifts = [(i * size) % LANES for i in range(count)]
        self.shifts = sorted(set(shifts))
        self.wide = -(-(size + max(shifts)) // LANES) * LANES
        self.aligned = max(shifts) == 0 and size % LANES == 0
        self.total = count * size
        self.room = max(self.start(i) + self.wide for i in range(count))

    def start(self, index):
        return index * self.size // LANES * LANES

    def start_dynamic(self, index):
        return pl.multiple_of(index * self.size // LANES * LANES, LANES)

    def pad(self, value, index):
        result = None
        for shift in self.shifts:
            low = [(0, 0)] * (value.ndim - 1) + [(shift, self.wide - self.size - shift)]
            placed = jnp.pad(value, low)
            here = (index * self.size) % LANES == shift
            result = placed if result is None else jnp.where(here, placed, result)
        return result

    def cut(self, value, index):
        result = None
        for shift in self.shifts:
            piece = value[..., shift : shift + self.size]
            here = (index * self.size) % LANES == shift
            result = piece if result is None else jnp.where(here, piece, result)
        return result

    def tile_owners(self, tile):
        low, high = tile * LANES, (tile + 1) * LANES
        return [
            (i, low - self.start(i))
            for i in range(self.count)
            if i * self.size < high and (i + 1) * self.size > low
        ]


def matmul(left, right):
    return lax.dot_general(left, right, (((1,), (0,)), ((), ())), preferred_element_type=FULL)


def matmul_nt(left, right):
    return lax.dot_general(left, right, (((1,), (1,)), ((), ())), preferred_element_type=FULL)


def matmul_tn(left, right):
    return lax.dot_general(left, right, (((0,), (0,)), ((), ())), preferred_element_type=FULL)


def normed(values):
    centred = values - jnp.mean(values, axis=-1, keepdims=True)
    spread = jnp.mean(centred * centred, axis=-1, keepdims=True)
    scale = lax.rsqrt(spread + 1e-05)
    return centred * scale, scale


def norm_back(grad, unit, scale, gain):
    inner = grad * gain
    mean_inner = jnp.mean(inner, axis=-1, keepdims=True)
    mean_both = jnp.mean(inner * unit, axis=-1, keepdims=True)
    return scale * (inner - mean_inner - unit * mean_both)


def rows_at(index, size=CHUNK):
    return pl.ds(pl.multiple_of(index * size, size), size)


def places(pos, codes, half):
    for index, (d_mask, w_mask) in enumerate(codes):
        doc = pos[0] ^ d_mask
        inner = pos[1] ^ w_mask
        for slot in (0, 1):
            owner = pos[2] if slot == 0 else 1 - pos[2]
            yield index, slot, doc, owner * half + inner


def load_pieces(pos, refs, codes, half, lanes, target, sem):
    for ref, group in zip(refs, codes):
        for index, slot, doc, inner in places(pos, group, half):
            pltpu.make_async_copy(
                ref.at[index, slot, :, pl.ds(lanes[0], lanes[1])], target(doc, inner), sem
            ).start()


def wait_whole(ref, sem):
    pltpu.make_async_copy(ref, ref, sem).wait()


def row_target(ref, blocks, rows):
    if blocks.aligned:
        return lambda doc, inner: ref.at[
            pl.ds(pl.multiple_of(inner * rows, rows), rows),
            pl.ds(blocks.start_dynamic(doc), blocks.wide),
        ]
    return lambda doc, inner: ref.at[doc, pl.ds(pl.multiple_of(inner * rows, rows), rows), :]


def column_target(ref, blocks, rows):
    if blocks.aligned:
        return lambda doc, inner: ref.at[
            pl.ds(pl.multiple_of(doc * rows, rows), rows),
            pl.ds(blocks.start_dynamic(inner), blocks.wide),
        ]
    return lambda doc, inner: ref.at[inner, pl.ds(pl.multiple_of(doc * rows, rows), rows), :]


def held_shape(blocks, height):
    return (height, blocks.total) if blocks.aligned else (blocks.count, height, blocks.wide)


def merge_tiles(held, whole, blocks):
    for tile in range(blocks.total // LANES):
        value = None
        for index, offset in blocks.tile_owners(tile):
            piece = held[index, :, offset : offset + LANES]
            value = piece if value is None else value + piece
        whole[:, tile * LANES : (tile + 1) * LANES] = value


def project_kernel(
    shape, pos, own, other, gains, page_col, page_row, mask_row, *refs
):
    codes, half, rows, blocks, length, width, factor = shape
    pieces = refs[: len(codes)]
    (q_out, k_out, v_out, att_out, lse_out, weight) = refs[len(codes) : len(codes) + 6]
    (held, h_own, h_oth, allowed, sem) = refs[len(codes) + 6 :]
    load_pieces(pos, pieces, codes, half, (0, blocks.wide), row_target(held, blocks, rows), sem)
    for i in range(length // CHUNK):
        part = pl.ds(i * CHUNK, CHUNK)
        unit, _ = normed(own[part, :].astype(FULL))
        h_own[part, :] = (unit * gains[0:1, :]).astype(LOW)
        unit, _ = normed(other[part, :].astype(FULL))
        h_oth[part, :] = (unit * gains[1:2, :]).astype(LOW)
        row = lax.broadcasted_iota(jnp.int32, (CHUNK, length), 0) + i * CHUNK
        col = lax.broadcasted_iota(jnp.int32, (CHUNK, length), 1)
        ok = (page_col[part, :] == page_row[...]) & ((mask_row[...] == 1) | (row == col))
        allowed[part, :] = jnp.where(ok, 1.0, 0.0)
    wait_whole(held, sem)
    merge_tiles(held, weight, blocks)
    lse_out[...] = jnp.zeros_like(lse_out)

    q_out[...] = (matmul(h_own[...], weight[:, :width]).astype(LOW) * factor).astype(LOW)
    k_out[...] = matmul(h_oth[...], weight[:, width : 2 * width]).astype(LOW)
    v_out[...] = matmul(h_oth[...], weight[:, 2 * width :]).astype(LOW)
    size = width // HEADS
    per = LANES // size

    @pl.loop(0, width // LANES)
    def _(pair):
        cols = pl.ds(pl.multiple_of(pair * LANES, LANES), LANES)
        keys = k_out[:, cols]
        values = v_out[:, cols]
        for i in range(length // CHUNK):
            part = pl.ds(i * CHUNK, CHUNK)
            queries = q_out[part, cols]
            lane = lax.broadcasted_iota(jnp.int32, queries.shape, 1)
            result = None
            sums = lse_out[part, :]
            for sub in range(per):
                inside = lane // size == sub
                scores = matmul_nt(jnp.where(inside, queries, jnp.zeros_like(queries)), keys)
                scores = jnp.where(allowed[part, :] > 0.5, scores, NEG)
                top = jnp.max(scores, axis=-1, keepdims=True)
                exps = jnp.exp(scores - top)
                total = jnp.sum(exps, axis=-1, keepdims=True)
                probs = (exps * (1.0 / total)).astype(LOW)
                out = matmul(probs, values)
                result = out if result is None else jnp.where(inside, out, result)
                sums = jnp.where(lane == pair * per + sub, top + jnp.log(total), sums)
            lse_out[part, :] = sums
            att_out[part, cols] = result.astype(LOW)


def feed_kernel(
    shape, pos, att, own, cot, cotj_own, cotj_oth, coef, gain, page_col, *refs
):
    (up_codes, down_codes, up_sums, down_sums, half, rows, down_rows, ups, outs, downs, length, width, hidden, block) = shape
    n_up, n_down = len(up_codes), len(down_codes)
    up_pieces, down_pieces = refs[:n_up], refs[n_up : n_up + n_down]
    refs = refs[n_up + n_down :]
    (out_ref, away_ref, dmid_ref, datt_ref, dgain_ref, up_keep, up_send, down_keep, down_send) = refs[:9]
    (w_up, o_held, w_out, d_held, w_down, g_up, g_out, g_down, mid, unit_ref, scale_ref, dz, h2, h2_t, dffn, dffn_t, att_t, acts, dpre, acc, dacc, dbranch, sem_up, sem_out, sem_down, sem_keep, sem_send, sem_dkeep, sem_dsend) = refs[9:]
    load_pieces(pos, up_pieces, up_codes, half, (ups.wide, outs.wide), row_target(o_held, outs, rows), sem_out)
    load_pieces(pos, up_pieces, up_codes, half, (0, ups.wide), row_target(w_up, ups, rows), sem_up)
    load_pieces(pos, down_pieces, down_codes, half, (0, downs.wide), column_target(d_held, downs, down_rows), sem_down)
    half_rows = length // 2
    parts = length // CHUNK
    for which, ref in ((pos[2], cotj_own), (1 - pos[2], cotj_oth)):
        for i in range(half_rows // CHUNK):
            part = pl.ds(pl.multiple_of(which * half_rows + i * CHUNK, CHUNK), CHUNK)
            grad = cot[part, :] + coef[...] * ref[pl.ds(i * CHUNK, CHUNK), :].astype(FULL)
            valid = jnp.where(page_col[part, :] >= 0, 1.0, 0.0)
            dz[part, :] = grad
            dffn[part, :] = (grad * valid).astype(LOW)
    dffn_t[...] = dffn[...].T
    att_t[...] = att[...].T
    wait_whole(o_held, sem_out)
    merge_tiles(o_held, w_out, outs)

    @pl.loop(0, parts)
    def _(i):
        part = rows_at(i)
        valid = jnp.where(page_col[part, :] >= 0, 1.0, 0.0)
        middle = own[part, :].astype(FULL) + valid * matmul(att[part, :], w_out[...])
        unit, scale = normed(middle)
        mid[part, :] = middle
        unit_ref[part, :] = unit
        scale_ref[part, :] = jnp.broadcast_to(scale, (CHUNK, LANES))
        h2[part, :] = (unit * gain[...]).astype(LOW)

    h2_t[...] = h2[...].T
    acc[...] = jnp.zeros_like(acc)
    dacc[...] = jnp.zeros_like(dacc)
    wait_whole(w_up, sem_up)
    wait_whole(d_held, sem_down)
    if not downs.aligned:
        merge_tiles(d_held, w_down, downs)
    down = d_held if downs.aligned else w_down
    c0, c1 = 0.7978845608028654, 0.044715

    @pl.loop(0, hidden // block)
    def _(f):
        cols = pl.ds(pl.multiple_of(f * block, LANES), block)

        @pl.loop(0, parts)
        def _(i):
            part = rows_at(i)
            pre = matmul(h2[part, :], w_up[:, cols])
            dact = matmul(dffn[part, :], down[:, cols])
            square = pre * pre
            flat = jnp.tanh(c0 * (pre + c1 * square * pre))
            cdf = 0.5 * (1.0 + flat)
            slope = cdf + pre * (0.5 * (1.0 - flat * flat)) * (c0 * (1.0 + 3.0 * c1 * square))
            act = (pre * cdf).astype(LOW)
            dp = (slope * dact).astype(LOW)
            acts[part, :] = act
            dpre[part, :] = dp
            acc[part, :] += matmul_nt(act, down[:, cols])
            dacc[part, :] += matmul_nt(dp, w_up[:, cols])

        g_down[:, cols] = matmul(dffn_t[...], acts[...]).astype(LOW)
        g_up[:, cols] = matmul(h2_t[...], dpre[...]).astype(LOW)

    if downs.room > downs.total:
        g_down[:, downs.total :] = jnp.zeros((width, downs.room - downs.total), LOW)
    if outs.room > outs.total:
        g_out[:, outs.total :] = jnp.zeros((width, outs.room - outs.total), LOW)
    for codes, keep, send, s_keep, s_send in ((down_sums, down_keep, down_send, sem_dkeep, sem_dsend),):
        count = len(codes) // 2
        for index, slot, doc, inner in places(pos, codes, half):
            target, sem = (keep, s_keep) if index < count else (send, s_send)
            pltpu.make_async_copy(
                g_down.at[
                    pl.ds(pl.multiple_of(doc * down_rows, down_rows), down_rows),
                    pl.ds(downs.start_dynamic(inner), downs.wide),
                ],
                target.at[index % count, slot],
                sem,
            ).start()
    count = len(up_sums) // 2
    for index, slot, doc, inner in places(pos, up_sums, half):
        target, sem = (up_keep, sem_keep) if index < count else (up_send, sem_send)
        height = pl.ds(pl.multiple_of(inner * rows, rows), rows)
        pltpu.make_async_copy(
            g_up.at[height, pl.ds(ups.start_dynamic(doc), ups.wide)],
            target.at[index % count, slot, :, pl.ds(0, ups.wide)],
            sem,
        ).start()

    dgain_ref[...] = jnp.zeros_like(dgain_ref)

    @pl.loop(0, parts)
    def _(i):
        part = rows_at(i)
        valid = jnp.where(page_col[part, :] >= 0, 1.0, 0.0)
        out_ref[part, :] = mid[part, :] + valid * acc[part, :]
        grad, unit = dacc[part, :], unit_ref[part, :]
        dgain_ref[0:1, :] += jnp.sum(grad * unit, axis=0, keepdims=True)
        dmid = dz[part, :] + norm_back(grad, unit, scale_ref[part, 0:1], gain[...])
        dmid_ref[part, :] = dmid
        low = (dmid * valid).astype(LOW)
        dbranch[part, :] = low
        datt_ref[part, :] = matmul_nt(low, w_out[...]).astype(LOW)

    for i in range(half_rows // CHUNK):
        part = pl.ds(pl.multiple_of((1 - pos[2]) * half_rows + i * CHUNK, CHUNK), CHUNK)
        away_ref[pl.ds(i * CHUNK, CHUNK), :] = out_ref[part, :].astype(LOW)
    g_out[:, : outs.total] = matmul(att_t[...], dbranch[...]).astype(LOW)
    for index, slot, doc, inner in places(pos, up_sums, half):
        target, sem = (up_keep, sem_keep) if index < count else (up_send, sem_send)
        height = pl.ds(pl.multiple_of(inner * rows, rows), rows)
        pltpu.make_async_copy(
            g_out.at[height, pl.ds(outs.start_dynamic(doc), outs.wide)],
            target.at[index % count, slot, :, pl.ds(ups.wide, outs.wide)],
            sem,
        ).start()
    wait_whole(down_keep, sem_dkeep)
    wait_whole(down_send, sem_dsend)
    wait_whole(up_keep, sem_keep)
    wait_whole(up_send, sem_send)


def back_kernel(
    shape, pos, own, other, gains, page_col, page_row, mask_col, q_ref, k_ref, v_ref, att, datt, lse, weight, *refs
):
    (codes, half, rows, blocks, length, width, factor) = shape
    (own_ref, oth_ref, dgain_ref, keep, send) = refs[:5]
    (dq, dk, dv, h_t, allowed, flat, lse_t, dots_t, dscore, grad, sem_keep, sem_send) = refs[5:]
    size = width // HEADS
    per = LANES // size
    parts = length // CHUNK
    for i in range(parts):
        part = pl.ds(i * CHUNK, CHUNK)
        row = lax.broadcasted_iota(jnp.int32, (CHUNK, length), 0) + i * CHUNK
        col = lax.broadcasted_iota(jnp.int32, (CHUNK, length), 1)
        ok = (page_col[part, :] == page_row[...]) & ((mask_col[part, :] == 1) | (row == col))
        allowed[part, :] = jnp.where(ok, 1.0, 0.0)
    head = lax.broadcasted_iota(jnp.int32, (LANES, width), 0)
    lane = lax.broadcasted_iota(jnp.int32, (LANES, width), 1)
    chosen = jnp.where(lane // size == head, 1.0, 0.0)
    flat[...] = att[...].astype(FULL) * datt[...].astype(FULL)
    dots_t[...] = lax.dot_general(
        chosen, flat[...], (((1,), (1,)), ((), ())), preferred_element_type=FULL,
        precision=lax.Precision.HIGHEST,
    )
    lse_t[...] = lse[...].T

    @pl.loop(0, width // LANES)
    def _(pair):
        cols = pl.ds(pl.multiple_of(pair * LANES, LANES), LANES)
        queries, grads, keys_all = q_ref[:, cols], datt[:, cols], k_ref[:, cols]
        lane = lax.broadcasted_iota(jnp.int32, (length, LANES), 1)
        lane_part = lax.broadcasted_iota(jnp.int32, (CHUNK, LANES), 1)
        zero = jnp.zeros_like(queries)
        dq_pair = None
        for sub in range(per):
            inside = lane // size == sub
            inside_part = lane_part // size == sub
            q_head = jnp.where(inside, queries, zero)
            g_head = jnp.where(inside, grads, zero)
            lse_row = lse_t[pl.ds(pair * per + sub, 1), :]
            dot_row = dots_t[pl.ds(pair * per + sub, 1), :]
            for i in range(parts):
                part = pl.ds(i * CHUNK, CHUNK)
                scores = matmul_nt(k_ref[part, cols], q_head)
                scores = jnp.where(allowed[part, :] > 0.5, scores, NEG)
                probs = jnp.exp(scores - lse_row)
                dprob = matmul_nt(v_ref[part, cols], g_head)
                low = (probs * (dprob - dot_row)).astype(LOW)
                dscore[part, :] = low
                dv_part = matmul(probs.astype(LOW), grads).astype(LOW)
                dk_part = matmul(low, queries).astype(LOW)
                if sub > 0:
                    dv_part = jnp.where(inside_part, dv_part, dv[part, cols])
                    dk_part = jnp.where(inside_part, dk_part, dk[part, cols])
                dv[part, cols] = dv_part
                dk[part, cols] = dk_part
            dq_head = matmul_tn(dscore[...], keys_all)
            dq_pair = dq_head if dq_pair is None else jnp.where(inside, dq_head, dq_pair)
        dq[:, cols] = (dq_pair * factor).astype(LOW)

    for which, source in ((0, own), (1, other)):
        for i in range(parts):
            part = pl.ds(i * CHUNK, CHUNK)
            unit, _ = normed(source[part, :].astype(FULL))
            flat[part, :] = unit * gains[which : which + 1, :]
        h_t[which] = flat[...].astype(LOW).T
    grad[:, :width] = matmul(h_t[0], dq[...]).astype(LOW)
    grad[:, width : 2 * width] = matmul(h_t[1], dk[...]).astype(LOW)
    grad[:, 2 * width : 3 * width] = matmul(h_t[1], dv[...]).astype(LOW)
    if blocks.room > blocks.total:
        grad[:, blocks.total :] = jnp.zeros((width, blocks.room - blocks.total), LOW)
    count = len(codes) // 2
    for index, slot, doc, inner in places(pos, codes, half):
        target, sem = (keep, sem_keep) if index < count else (send, sem_send)
        pltpu.make_async_copy(
            grad.at[
                pl.ds(pl.multiple_of(inner * rows, rows), rows),
                pl.ds(blocks.start_dynamic(doc), blocks.wide),
            ],
            target.at[index % count, slot],
            sem,
        ).start()
    dgain_ref[...] = jnp.zeros_like(dgain_ref)
    for i in range(parts):
        part = pl.ds(i * CHUNK, CHUNK)
        unit, _ = normed(own[part, :].astype(FULL))
        value = matmul_nt(dq[part, :], weight[:, :width])
        own_ref[part, :] = value
        dgain_ref[0:1, :] += jnp.sum(value * unit, axis=0, keepdims=True)
        unit, _ = normed(other[part, :].astype(FULL))
        value = matmul_nt(dk[part, :], weight[:, width : 2 * width])
        value = value + matmul_nt(dv[part, :], weight[:, 2 * width :])
        oth_ref[part, :] = value.astype(LOW)
        dgain_ref[1:2, :] += jnp.sum(value * unit, axis=0, keepdims=True)
    wait_whole(keep, sem_keep)
    wait_whole(send, sem_send)


def tail_kernel(length, own, gain, mine, theirs, dmid, out_ref):
    for i in range(length // CHUNK):
        part = pl.ds(i * CHUNK, CHUNK)
        unit, scale = normed(own[part, :].astype(FULL))
        grad = mine[part, :] + theirs[part, :].astype(FULL)
        out_ref[part, :] = dmid[part, :] + norm_back(grad, unit, scale, gain[...])


VMEM = pl.BlockSpec(memory_space=pltpu.VMEM)
ANY = pl.BlockSpec(memory_space=pl.ANY)
SMEM = pl.BlockSpec(memory_space=pltpu.SMEM)


def params(mebibytes):
    return pltpu.CompilerParams(vmem_limit_bytes=mebibytes * 1024 * 1024)


def adam_update(weight, first, second, grad, rate, decay):
    first_new = 0.9 * first + 0.1 * grad
    second_new = 0.999 * second + 0.001 * grad * grad
    first_hat = first_new / (1.0 - 0.9**STEP)
    second_hat = second_new / (1.0 - 0.999**STEP)
    weight_new = weight - rate * (first_hat / (jnp.sqrt(second_hat) + 1e-08) + decay * weight)
    return (weight_new, first_new, second_new)


def shards(
    rows, cot_stream, cot_joined, page, key_mask,
    w_qkv, m_qkv, v_qkv, w_out, m_out, v_out, w_up, m_up, v_up, w_down, m_down, v_down,
    gains, m_gains, v_gains,
):
    docs, wide = lax.axis_size("docs"), lax.axis_size("wide")
    half = wide // 2
    doc, place = lax.axis_index("docs"), lax.axis_index("wide")
    stream = place // half
    is_text = stream == 0
    pos = jnp.stack((doc, place % half, stream)).astype(jnp.int32)
    length, width = rows.shape
    half_rows = length // 2
    factor = float(width // HEADS) ** (-0.5)
    piece_rows = w_qkv.shape[1]
    hidden = w_up.shape[2] * docs
    qkvs, outs, ups = Blocks(docs, w_qkv.shape[2]), Blocks(docs, w_out.shape[2]), Blocks(docs, w_up.shape[2])
    downs = Blocks(wide, w_down.shape[1])
    down_rows = w_down.shape[2]

    core = [("wide", 1)]
    along_x = [("docs", 1)]
    along_y = [("docs", 1 << b) for b in range(1, docs.bit_length() - 1)]
    along_z = [("wide", 1 << b) for b in range(1, half.bit_length() - 1)]
    across = ("wide", half)

    def swap(value):
        return flip(value, *across)

    other_rows = swap(rows)
    column = doc * w_qkv.shape[2] + lax.iota(jnp.int32, w_qkv.shape[2])
    is_query = (column < width)[None, None, :]
    pair_qkv = jnp.where(is_query, w_qkv, w_qkv[::-1]).astype(LOW)

    def own_first(pair):
        return jnp.where(is_text, pair, pair[::-1])

    unit_a = qkvs.pad(own_first(pair_qkv), doc)
    unit_b = jnp.concatenate(
        (ups.pad(own_first(w_up.astype(LOW)), doc), outs.pad(own_first(w_out.astype(LOW)), doc)), axis=-1
    )
    unit_c = downs.pad(jnp.swapaxes(own_first(w_down.astype(LOW)), 1, 2), place)
    unit_a = jnp.stack((unit_a[0], swap(unit_a[1])))
    unit_b = jnp.stack((unit_b[0], swap(unit_b[1])))
    if downs.aligned:
        unit_c = jnp.stack((unit_c[0], swap(unit_c[1])))
    else:
        raw = jnp.swapaxes(own_first(w_down.astype(LOW)), 1, 2)
        unit_c = jnp.stack((unit_c[0], downs.pad(swap(raw[1]), (place + half) % wide)))
    pieces_a, codes_a = gather(unit_a, along_z + along_x + along_y + core)
    pieces_b, codes_b = gather(unit_b, along_z + along_y + along_x + core)
    pieces_c, codes_c = gather(unit_c, along_x + along_z + along_y + core)
    other_joined = swap(cot_joined.astype(LOW))

    page_col, page_row = page[:, None], page[None, :]
    mask_col, mask_row = key_mask[:, None], key_mask[None, :]
    gain_own = lax.dynamic_index_in_dim(gains, stream, 0, keepdims=True)
    gain_oth = lax.dynamic_index_in_dim(gains, 1 - stream, 0, keepdims=True)
    gain_one = jnp.concatenate((gain_own, gain_oth), axis=0)
    gain_two = lax.dynamic_index_in_dim(gains, 2 + stream, 0, keepdims=True)
    mix = jax.nn.sigmoid(gains[4])[None, :]
    coef = jnp.where(is_text, mix, 1.0 - mix)

    low_rows = jax.ShapeDtypeStruct((length, width), LOW)
    full_rows = jax.ShapeDtypeStruct((length, width), FULL)

    shape = (codes_a, half, piece_rows, qkvs, length, width, factor)
    queries, keys, values, attended, lse, weight_qkv = pl.pallas_call(
        functools.partial(project_kernel, shape),
        out_shape=(low_rows, low_rows, low_rows, low_rows,
                   jax.ShapeDtypeStruct((length, LANES), FULL),
                   jax.ShapeDtypeStruct((width, 3 * width), LOW)),
        in_specs=[SMEM] + [VMEM] * 6 + [ANY] * len(pieces_a),
        out_specs=(VMEM,) * 6,
        scratch_shapes=[
            pltpu.VMEM((docs, width, qkvs.wide), LOW),
            pltpu.VMEM((length, width), LOW),
            pltpu.VMEM((length, width), LOW),
            pltpu.VMEM((length, length), FULL),
            pltpu.SemaphoreType.DMA,
        ],
        compiler_params=params(48),
        cost_estimate=pl.CostEstimate(flops=5_000_000_000, bytes_accessed=20_000_000, transcendentals=3_000_000),
        name="project_attend",
    )(pos, rows, other_rows, gain_one, page_col, page_row, mask_row, *pieces_a)

    order_b = core + along_x + along_y + along_z
    order_c = core + along_y + along_x + along_z
    order_a = core + along_x + along_y + along_z
    sums_a, sums_b, sums_c = sum_codes(order_a), sum_codes(order_b), sum_codes(order_c)
    sent = len(sums_a) // 2
    block = 3 * LANES
    shape = (codes_b, codes_c, sums_b, sums_c, half, piece_rows, down_rows, ups, outs, downs, length, width, hidden, block)
    shape_b = jax.ShapeDtypeStruct((sent, 2, piece_rows, ups.wide + outs.wide), LOW)
    shape_c = jax.ShapeDtypeStruct((sent, 2, down_rows, downs.wide), LOW)
    (stream_out, away, middle_grad, attended_grad, dgain_two, keep_b, send_b, keep_c, send_c) = pl.pallas_call(
        functools.partial(feed_kernel, shape),
        out_shape=(full_rows, jax.ShapeDtypeStruct((half_rows, width), LOW), full_rows, low_rows,
                   jax.ShapeDtypeStruct((8, width), FULL), shape_b, shape_b, shape_c, shape_c),
        in_specs=[SMEM] + [VMEM] * 8 + [ANY] * (len(pieces_b) + len(pieces_c)),
        out_specs=(VMEM,) * 5 + (ANY,) * 4,
        scratch_shapes=[
            pltpu.VMEM((width, hidden), LOW),
            pltpu.VMEM(held_shape(outs, width), LOW),
            pltpu.VMEM((width, width), LOW),
            pltpu.VMEM(held_shape(downs, width), LOW),
            pltpu.VMEM((8, LANES) if downs.aligned else (width, hidden), LOW),
            pltpu.VMEM((width, hidden), LOW),
            pltpu.VMEM((width, outs.room), LOW),
            pltpu.VMEM((width, downs.room), LOW),
            pltpu.VMEM((length, width), FULL),
            pltpu.VMEM((length, width), FULL),
            pltpu.VMEM((length, LANES), FULL),
            pltpu.VMEM((length, width), FULL),
            pltpu.VMEM((length, width), LOW),
            pltpu.VMEM((width, length), LOW),
            pltpu.VMEM((length, width), LOW),
            pltpu.VMEM((width, length), LOW),
            pltpu.VMEM((width, length), LOW),
            pltpu.VMEM((length, block), LOW),
            pltpu.VMEM((length, block), LOW),
            pltpu.VMEM((length, width), FULL),
            pltpu.VMEM((length, width), FULL),
            pltpu.VMEM((length, width), LOW),
        ] + [pltpu.SemaphoreType.DMA] * 7,
        compiler_params=params(60),
        cost_estimate=pl.CostEstimate(flops=17_000_000_000, bytes_accessed=45_000_000, transcendentals=1_600_000),
        name="feed_forward_back",
    )(pos, attended, rows, cot_stream, cot_joined, other_joined, coef, gain_two, page_col, *pieces_b, *pieces_c)

    partner_rows = swap(away)

    shape = (sums_a, half, piece_rows, qkvs, length, width, factor)
    shape_a = jax.ShapeDtypeStruct((sent, 2, piece_rows, qkvs.wide), LOW)
    own_part, away_part, dgain_one, keep_a, send_a = pl.pallas_call(
        functools.partial(back_kernel, shape),
        out_shape=(full_rows, low_rows, jax.ShapeDtypeStruct((8, width), FULL), shape_a, shape_a),
        in_specs=[SMEM] + [VMEM] * 13,
        out_specs=(VMEM,) * 3 + (ANY,) * 2,
        scratch_shapes=[
            pltpu.VMEM((length, width), LOW),
            pltpu.VMEM((length, width), LOW),
            pltpu.VMEM((length, width), LOW),
            pltpu.VMEM((2, width, length), LOW),
            pltpu.VMEM((length, length), FULL),
            pltpu.VMEM((length, width), FULL),
            pltpu.VMEM((LANES, length), FULL),
            pltpu.VMEM((LANES, length), FULL),
            pltpu.VMEM((length, length), LOW),
            pltpu.VMEM((width, qkvs.room), LOW),
        ] + [pltpu.SemaphoreType.DMA] * 2,
        compiler_params=params(56),
        cost_estimate=pl.CostEstimate(flops=9_000_000_000, bytes_accessed=20_000_000, transcendentals=3_000_000),
        name="attend_back",
    )(pos, rows, other_rows, gain_one, page_col, page_row, mask_col, queries, keys, values, attended, attended_grad, lse, weight_qkv)

    back_part = swap(away_part)
    grad_rows = pl.pallas_call(
        functools.partial(tail_kernel, length),
        out_shape=full_rows,
        in_specs=[VMEM] * 5,
        out_specs=VMEM,
        compiler_params=params(32),
        name="norm_tail",
    )(rows, gain_own, own_part, back_part, middle_grad)

    own_rows = lax.dynamic_slice_in_dim(stream_out, stream * half_rows, half_rows, 0)
    partner_rows = partner_rows.astype(FULL)
    text_rows = jnp.where(is_text, own_rows, partner_rows)
    image_rows = jnp.where(is_text, partner_rows, own_rows)
    joined_rows = mix * text_rows + (1.0 - mix) * image_rows
    gate_grad = jnp.sum(cot_joined * (text_rows - image_rows), axis=0, keepdims=True) * mix * (1.0 - mix)

    total_b = reduce_pieces(keep_b, send_b, order_b)
    total_c = reduce_pieces(keep_c, send_c, order_c)
    total_a = reduce_pieces(keep_a, send_a, order_a)

    def both(total):
        mine = total[0]
        theirs = swap(total[1].astype(LOW)).astype(FULL)
        return mine, theirs

    def placed(mine, theirs):
        return jnp.where(is_text, jnp.stack((mine, theirs)), jnp.stack((theirs, mine)))

    mine_b, theirs_b = both(total_b)
    grad_b = placed(mine_b, theirs_b)
    grad_up = ups.cut(grad_b[..., : ups.wide], doc)
    grad_out = outs.cut(grad_b[..., ups.wide :], doc)
    if downs.aligned:
        mine_c, theirs_c = both(total_c)
    else:
        mine_c = downs.cut(total_c[0], place)
        theirs_c = swap(downs.cut(total_c[1], (place + half) % wide).astype(LOW)).astype(FULL)
    grad_down = jnp.swapaxes(placed(mine_c, theirs_c), 1, 2)
    mine_a, theirs_a = both(total_a)
    mine_a, theirs_a = qkvs.cut(mine_a, doc), qkvs.cut(theirs_a, doc)
    query_here = is_query[0]
    grad_qkv = placed(
        jnp.where(query_here, mine_a, theirs_a), jnp.where(query_here, theirs_a, mine_a)
    )

    slot_index = lax.iota(jnp.int32, 5)[:, None]
    small_terms = (
        jnp.where(slot_index == stream, dgain_one[0:1], 0.0)
        + jnp.where(slot_index == 1 - stream, dgain_one[1:2], 0.0)
        + jnp.where(slot_index == 2 + stream, dgain_two[0:1], 0.0)
        + jnp.where(slot_index == 4, gate_grad, 0.0)
    )
    gains_grad = small_sum(small_terms, core + along_x + along_y + along_z + [across])

    qkv_new = adam_update(w_qkv, m_qkv, v_qkv, grad_qkv, 0.12, 0.01)
    out_new = adam_update(w_out, m_out, v_out, grad_out, 0.5, 0.01)
    up_new = adam_update(w_up, m_up, v_up, grad_up, 0.12, 0.01)
    down_new = adam_update(w_down, m_down, v_down, grad_down, 0.06, 0.01)
    gains_new = adam_update(gains, m_gains, v_gains, gains_grad, 0.8, 0.0)
    return (stream_out, joined_rows, grad_rows, *qkv_new, *out_new, *up_new, *down_new, *gains_new)


def solution(mesh):
    by_rows = P(("docs", "wide"), None)
    by_row = P(("docs", "wide"))
    weight = P(None, "wide", "docs")
    return jax.shard_map(
        shards,
        mesh=mesh,
        in_specs=(by_rows,) * 3 + (by_row,) * 2 + (weight,) * 12 + (P(),) * 3,
        out_specs=(by_rows,) * 3 + (weight,) * 12 + (P(),) * 3,
        check_vma=False,
    )
```

time: 1360 us -> 463 us (0.34)
  waiting for transfers between devices: 1080 us -> 272 us
  Pallas kernels: 0 us -> 104 us
  matrix products: 82.4 us -> 0 us
  blocking collectives: 70.3 us -> 0 us
  starting transfers between devices: 3 us -> 43.9 us
  local copies, waits for them, and re-layouts: 40.1 us -> 7.46 us
  other arithmetic: 62.8 us -> 34.1 us
  between operations: 15.9 us -> 1.56 us
    reduce_scatter x5 -> x0, waiting for transfers between devices: 517 us -> none  [the longest x1 183 us: shards(): lax.psum_scatter(placed[2], 'wide', scatter_dimension=1, tiled=True)]
    all_gather x6 -> x0, waiting for transfers between devices: 223 us -> none  [the longest x1 85.2 us: fetch(): lax.all_gather(inner[3], 'wide', axis=1, tiled=True)]
    pallas_call x0 -> x4, Pallas kernels: none -> 104 us  [the longest x1 49 us: shards(): pl.pallas_call(functools.partial(feed_kernel, shape), out_shape=(full_row...]
    unnamed x17 -> x0, waiting for transfers between devices: 89.4 us -> none
    dot_general x18 -> x0, matrix products: 82.4 us -> none  [the longest x1 13.9 us: shards(): jnp.einsum('qhd,khd->hqk', attended_grad, value_heads, preferred_element_...]
    ppermute x4 -> x39, starting transfers between devices: 2.17 us -> 43.9 us  [flip(): return lax.ppermute(value, axis, [(i, i ^ mask) for i in range(count)])]
    psum x1 -> x0, blocking collectives: 38.5 us -> none  [shards(): gains_grad = lax.psum(small_terms, ('docs', 'wide'))]
    all_gather x2 -> x0, blocking collectives: 31.8 us -> none  [the longest x1 19.2 us: fetch(): lax.all_gather(w_qkv.astype(jnp.bfloat16), 'docs', axis=2, tiled=True)]
  transfers between devices with their start and end apart: 18 -> 39, of which waited for: 14 -> 21; matrix products, arithmetic and copies ran while one was open for 11% -> 7% of each run, Pallas kernels for 0% -> 6%
where the time goes in v1:
time: 463 us
  waiting for transfers between devices  272 us (59%)
  Pallas kernels  104 us (22%)
  starting transfers between devices  43.9 us (9%)
  other arithmetic  34.1 us (7%)
  local copies, waits for them, and re-layouts  7.46 us (2%)
    ppermute x39, waiting for transfers between devices, flip(): return lax.ppermute(value, axis, [(i, i ^ mask) for i in range(count)])  272 us
    pallas_call x1, Pallas kernels, shards(): pl.pallas_call(functools.partial(feed_kernel, shape), out_shape=(full_row...  49 us
    ppermute x39, starting transfers between devices, flip(): return lax.ppermute(value, axis, [(i, i ^ mask) for i in range(count)])  43.9 us
    pallas_call x1, Pallas kernels, shards(): pl.pallas_call(functools.partial(back_kernel, shape), out_shape=(full_row...  27 us
    pallas_call x1, Pallas kernels, shards(): pl.pallas_call(functools.partial(project_kernel, shape), out_shape=(low_r...  25.7 us
    convert_element_type x9, other arithmetic, reduce_pieces(): outgoing = sum((part[half:].astype(FULL) for part in parts)).astype(LOW)  12.7 us
  transfers between devices with their start and end apart: 39, of which 21 were waited for; matrix products, arithmetic and copies ran while one was open for 7% of the time, Pallas kernels for 6%

profile of v1, /device:TPU:0, one launch (start us, length us, event | category | flops | bytes accessed | tf_op | source)
XLA Modules:
  0.0 462.5 jit_solution(8566696518171023513)
XLA Ops:
  3.0 4.1 collective-permute-start.7
  7.2 9.1 %collective-permute-done.7 = bf16[96,1024]{1,0:T(8,128)(2,1)S(1)} collective-permute-done((bf16[96,1024]{1,0:T(8,128)(2,1)S(1)}, bf16[96,1024]{1,0:T(8,128)(2,1)S(1)}, u32[]{:S(2)}, u32[]{:S(2)}) %collective-permute-start.7) | collective-permute-done | bytes 196640 | tf_op jit(solution)/shard_map/ppermute | solution.py:21
  17.2 3.4 collective-permute-start.12
  20.6 9.2 %collective-permute-done.8.refs_1_ = bf16[1,2,96,1024]{3,2,1,0:T(8,128)(2,1)S(1)} collective-permute-done((bf16[1,2,96,1024]{3,2,1,0:T(8,128)(2,1)S(1)}, bf16[1,2,96,1024]{3,2,1,0:T(8,128)(2,1)S(1)}, u32[]{:S(2)}, u32[]{:S(2)}) %collective-permute-start.8) | collective-permute-done | bytes 393248 | tf_op jit(solution)/shard_map/ppermute | solution.py:21
  31.6 1.6 collective-permute-start.13
  33.1 14.7 %collective-permute-done.9.refs_2_ = bf16[2,2,96,1024]{3,2,1,0:T(8,128)(2,1)S(1)} collective-permute-done((bf16[2,2,96,1024]{3,2,1,0:T(8,128)(2,1)S(1)}, bf16[2,2,96,1024]{3,2,1,0:T(8,128)(2,1)S(1)}, u32[]{:S(2)}, u32[]{:S(2)}) %collective-permute-start.9) | collective-permute-done | bytes 786464 | tf_op jit(solution)/shard_map/ppermute | solution.py:21
  49.0 3.8 collective-permute-start.1
  52.8 3.4 collective-permute-done.1
  56.2 2.0 collective-permute-start.2
  58.4 6.7 %collective-permute-done.2.refs_1_ = bf16[1,2,96,640]{3,2,1,0:T(8,128)(2,1)S(1)} collective-permute-done((bf16[1,2,96,640]{3,2,1,0:T(8,128)(2,1)S(1)}, bf16[1,2,96,640]{3,2,1,0:T(8,128)(2,1)S(1)}, u32[]{:S(2)}, u32[]{:S(2)}) %collective-permute-start.2) | collective-permute-done | bytes 245792 | tf_op jit(solution)/shard_map/ppermute | solution.py:21
  65.8 8.3 %collective-permute-done.14.refs_7_ = bf16[2,2,192,384]{3,2,1,0:T(8,128)(2,1)S(1)} collective-permute-done((bf16[2,2,192,384]{3,2,1,0:T(8,128)(2,1)S(1)}, bf16[2,2,192,384]{3,2,1,0:T(8,128)(2,1)S(1)}, u32[]{:S(2)}, u32[]{:S(2)}) %collective-permute-start.14) | collective-permute-done | bytes 589856 | tf_op jit(solution)/shard_map/ppermute | solution.py:21
  74.3 1.6 collective-permute-start.15
  75.9 16.4 %collective-permute-done.3.refs_2_ = bf16[2,2,96,640]{3,2,1,0:T(8,128)(2,1)S(1)} collective-permute-done((bf16[2,2,96,640]{3,2,1,0:T(8,128)(2,1)S(1)}, bf16[2,2,96,640]{3,2,1,0:T(8,128)(2,1)S(1)}, u32[]{:S(2)}, u32[]{:S(2)}) %collective-permute-start.3) | collective-permute-done | bytes 491552 | tf_op jit(solution)/shard_map/ppermute | solution.py:21
  93.2 2.2 pad_maximum_fusion
  95.4 24.3 %collective-permute-done.4.refs_3_ = bf16[4,2,96,640]{3,2,1,0:T(8,128)(2,1)S(1)} collective-permute-done((bf16[4,2,96,640]{3,2,1,0:T(8,128)(2,1)S(1)}, bf16[4,2,96,640]{3,2,1,0:T(8,128)(2,1)S(1)}, u32[]{:S(2)}, u32[]{:S(2)}) %collective-permute-start.4) | collective-permute-done | bytes 983072 | tf_op jit(solution)/shard_map/ppermute | solution.py:21
  119.7 1.6 pad_maximum_fusion.2
  121.5 1.8 pad_maximum_fusion.1
  123.9 2.6 collective-permute-start
  128.7 41.9 %collective-permute-done.other = bf16[512,768]{1,0:T(8,128)(2,1)} collective-permute-done((bf16[512,768]{1,0:T(8,128)(2,1)S(1)}, bf16[512,768]{1,0:T(8,128)(2,1)}, u32[]{:S(2)}, u32[]{:S(2)}) %collective-permute-start) | collective-permute-done | bytes 786464 | tf_op jit(solution)/shard_map/ppermute | solution.py:21
  170.6 25.7 %project_attend.1 = (bf16[512,768]{1,0:T(8,128)(2,1)S(1)}, bf16[512,768]{1,0:T(8,128)(2,1)S(1)}, bf16[512,768]{1,0:T(8,128)(2,1)S(1)}, bf16[512,768]{1,0:T(8,128...) custom-call(s32[3]{0:T(128)S(1)} %pad_add_fusion.pos, bf16[512,768]{1,0:T(8,128)(2,1)S(1)} %copy-done.2, ...), custom_call_target="tpu_custom_call" | custom-call | flops 5000000000 | bytes 20000000 | tf_op jit(solution)/shard_map/project_attend/pallas_call | solution.py:562
  200.6 49.0 %feed_forward_back.1 = (f32[512,768]{1,0:T(8,128)}, bf16[256,768]{1,0:T(8,128)(2,1)}, f32[512,768]{1,0:T(8,128)}, bf16[512,768]{1,0:T(8,128)(2,1)}, f32[8,768]{1...) custom-call(s32[3]{0:T(128)} %copy-done.8, ...), custom_call_target="tpu_custom_call" | custom-call | flops 16999999488 | bytes 45000000 | tf_op jit(solution)/shard_map/feed_forward_back/pallas_call | solution.py:590
  249.7 27.0 %attend_back.1 = (f32[512,768]{1,0:T(8,128)}, bf16[512,768]{1,0:T(8,128)(2,1)}, f32[8,768]{1,0:T(8,128)}, bf16[8,2,96,640]{3,2,1,0:T(8,128)(2,1)}, bf16[8,2,96,640]{3,2,1,0:T(8,128)(2,1)}) custom-call(s32[3]{0:T(128)} %copy-done.8, bf16[512,768]{1,0:T(8,128)(2,1)} %own.7, bf16[512,768]{1,0:T(8,128)(2,1)} %collective-permute-done.other, f32[2,768]{1,0:T(2,128)} %copy-done.5, ...), custom_call_target="tpu_custom_call" | custom-call | flops 8999999488 | bytes 20000000 | tf_op jit(solution)/shard_map/attend_back/pallas_call | solution.py:629
  279.1 19.0 %collective-permute-done.17 = bf16[256,768]{1,0:T(8,128)(2,1)S(1)} collective-permute-done((bf16[256,768]{1,0:T(8,128)(2,1)S(1)}, bf16[256,768]{1,0:T(8,128)(2,1)S(1)}, u32[]{:S(2)}, u32[]{:S(2)}) %collective-permute-start.17) | collective-permute-done | bytes 393248 | tf_op jit(solution)/shard_map/ppermute | solution.py:21
  298.5 1.6 add_convert_fusion.2
  300.8 1.6 collective-permute-start.35
  302.4 22.6 %collective-permute-done.35 = f32[5,768]{1,0:T(8,128)S(1)} collective-permute-done((f32[5,768]{1,0:T(8,128)S(1)}, f32[5,768]{1,0:T(8,128)S(1)}, u32[]{:S(2)}, u32[]{:S(2)}) %collective-permute-start.35) | collective-permute-done | bytes 15392 | tf_op jit(solution)/shard_map/ppermute | solution.py:21
  325.0 1.7 collective-permute-start.36
  326.7 2.2 collective-permute-done.36
  328.9 1.6 add_convert_fusion.1
  330.5 1.7 collective-permute-start.30
  333.3 10.8 %collective-permute-done.37 = f32[5,768]{1,0:T(8,128)S(1)} collective-permute-done((f32[5,768]{1,0:T(8,128)S(1)}, f32[5,768]{1,0:T(8,128)S(1)}, u32[]{:S(2)}, u32[]{:S(2)}) %collective-permute-start.37) | collective-permute-done | bytes 15392 | tf_op jit(solution)/shard_map/ppermute | solution.py:21
  344.1 2.2 collective-permute-start.38
  348.1 15.0 %collective-permute-done.38 = f32[5,768]{1,0:T(8,128)S(1)} collective-permute-done((f32[5,768]{1,0:T(8,128)S(1)}, f32[5,768]{1,0:T(8,128)S(1)}, u32[]{:S(2)}, u32[]{:S(2)}) %collective-permute-start.38) | collective-permute-done | bytes 15392 | tf_op jit(solution)/shard_map/ppermute | solution.py:21
  363.7 2.2 norm_tail.1
  365.9 2.1 add_convert_fusion
  372.7 4.7 %collective-permute-done.22 = bf16[1,2,96,640]{3,2,1,0:T(8,128)(2,1)S(1)} collective-permute-done((bf16[1,2,96,640]{3,2,1,0:T(8,128)(2,1)S(1)}, bf16[1,2,96,640]{3,2,1,0:T(8,128)(2,1)S(1)}, u32[]{:S(2)}, u32[]{:S(2)}) %collective-permute-start.22) | collective-permute-done | bytes 245792 | tf_op jit(solution)/shard_map/ppermute | solution.py:21
  379.9 6.1 %collective-permute-done.23 = bf16[96,640]{1,0:T(8,128)(2,1)S(1)} collective-permute-done((bf16[96,640]{1,0:T(8,128)(2,1)S(1)}, bf16[96,640]{1,0:T(8,128)(2,1)S(1)}, u32[]{:S(2)}, u32[]{:S(2)}) %collective-permute-start.23) | collective-permute-done | bytes 122912 | tf_op jit(solution)/shard_map/ppermute | solution.py:21
  386.3 30.7 %collective-permute-done.31 = bf16[2,2,192,384]{3,2,1,0:T(8,128)(2,1)S(1)} collective-permute-done((bf16[2,2,192,384]{3,2,1,0:T(8,128)(2,1)S(1)}, bf16[2,2,192,384]{3,2,1,0:T(8,128)(2,1)S(1)}, u32[]{:S(2)}, u32[]{:S(2)}) %collective-permute-start.31) | collective-permute-done | bytes 589856 | tf_op jit(solution)/shard_map/ppermute | solution.py:21
  418.3 1.6 add_convert_fusion.3
  420.4 1.6 multiply_subtract_fusion.2
  422.0 4.3 collective-permute-done.32
  427.5 1.5 collective-permute-start.33
  429.1 9.4 %collective-permute-done.26 = bf16[2,2,96,1024]{3,2,1,0:T(8,128)(2,1)S(1)} collective-permute-done((bf16[2,2,96,1024]{3,2,1,0:T(8,128)(2,1)S(1)}, bf16[2,2,96,1024]{3,2,1,0:T(8,128)(2,1)S(1)}, u32[]{:S(2)}, u32[]{:S(2)}) %collective-permute-start.26) | collective-permute-done | bytes 786464 | tf_op jit(solution)/shard_map/ppermute | solution.py:21
  439.8 1.8 collective-permute-start.27
  441.6 1.6 multiply_subtract_fusion
  443.2 5.9 %collective-permute-done.27 = bf16[1,2,96,1024]{3,2,1,0:T(8,128)(2,1)S(1)} collective-permute-done((bf16[1,2,96,1024]{3,2,1,0:T(8,128)(2,1)S(1)}, bf16[1,2,96,1024]{3,2,1,0:T(8,128)(2,1)S(1)}, u32[]{:S(2)}, u32[]{:S(2)}) %collective-permute-start.27) | collective-permute-done | bytes 393248 | tf_op jit(solution)/shard_map/ppermute | solution.py:21
  450.5 2.7 collective-permute-start.28
  453.2 6.6 %collective-permute-done.28 = bf16[96,1024]{1,0:T(8,128)(2,1)S(1)} collective-permute-done((bf16[96,1024]{1,0:T(8,128)(2,1)S(1)}, bf16[96,1024]{1,0:T(8,128)(2,1)S(1)}, u32[]{:S(2)}, u32[]{:S(2)}) %collective-permute-start.28) | collective-permute-done | bytes 196640 | tf_op jit(solution)/shard_map/ppermute | solution.py:21
  (206 shorter events, 37.9 us)
Async XLA Ops:
  3.0 13.2 %collective-permute-start.7 = (bf16[96,1024]{1,0:T(8,128)(2,1)S(1)}, bf16[96,1024]{1,0:T(8,128)(2,1)S(1)}, u32[]{:S(2)}, u32[]{:S(2)}) collective-permute-start(bf16[96,1024]{1,0:T(8,128)(2,1)S(1)} %get-tuple-element.83), channel_id=1, source_target_pairs={{0,4},{1,5},{2,6},{3,7},{4,0},{5,1},{6,2},{7,3},{8,12},{9,13},{10,... | collective-permute-start | bytes 589832 | tf_op jit(solution)/shard_map/ppermute | solution.py:21
  16.3 76.9 %copy-start.14 = (bf16[1,2,96,1024]{3,2,1,0:T(8,128)(2,1)}, bf16[1,2,96,1024]{3,2,1,0:T(8,128)(2,1)S(1)}, u32[]{:S(2)}) copy-start(bf16[1,2,96,1024]{3,2,1,0:T(8,128)(2,1)S(1)} %maximum_bitcast_fusion.refs_0_) | copy-start | bytes 1179652
  16.3 13.5 %collective-permute-start.8 = (bf16[1,2,96,1024]{3,2,1,0:T(8,128)(2,1)S(1)}, bf16[1,2,96,1024]{3,2,1,0:T(8,128)(2,1)S(1)}, u32[]{:S(2)}, u32[]{:S(2)}) collective-permute-start(bf16[1,2,96,1024]{3,2,1,0:T(8,128)(2,1)S(1)} %maximum_bitcast_fusion.refs_0_), channel_id=1, source_target_pairs={{0,2},{1,3},{2,0},{3,1},{4,6},{5,7},{6,4},{7,5},{8,10},{9,11},{10,... | collective-permute-start | bytes 1179656 | tf_op jit(solution)/shard_map/ppermute | solution.py:21
  17.2 14.3 %collective-permute-start.12 = (bf16[192,384]{1,0:T(8,128)(2,1)S(1)}, bf16[192,384]{1,0:T(8,128)(2,1)S(1)}, u32[]{:S(2)}, u32[]{:S(2)}) collective-permute-start(bf16[192,384]{1,0:T(8,128)(2,1)S(1)} %get-tuple-element.85), channel_id=1, source_target_pairs={{0,4},{1,5},{2,6},{3,7},{4,0},{5,1},{6,2},{7,3},{8,12},{9,13},{10,... | collective-permute-start | bytes 442376 | tf_op jit(solution)/shard_map/ppermute | solution.py:21
  29.8 63.3 %copy-start.16 = (bf16[1,2,96,1024]{3,2,1,0:T(8,128)(2,1)}, bf16[1,2,96,1024]{3,2,1,0:T(8,128)(2,1)S(1)}, u32[]{:S(2)}) copy-start(bf16[1,2,96,1024]{3,2,1,0:T(8,128)(2,1)S(1)} %collective-permute-done.8.refs_1_) | copy-start | bytes 1179652
  29.9 17.9 %collective-permute-start.9 = (bf16[2,2,96,1024]{3,2,1,0:T(8,128)(2,1)S(1)}, bf16[2,2,96,1024]{3,2,1,0:T(8,128)(2,1)S(1)}, u32[]{:S(2)}, u32[]{:S(2)}) collective-permute-start(bf16[2,2,96,1024]{3,2,1,0:T(8,128)(2,1)S(1)} %pad_maximum_fusion.6), channel_id=1, source_target_pairs={{0,16},{8,24},{16,0},{24,8},{1,17},{9,25},{17,1},{25,9},{2,18},{10... | collective-permute-start | bytes 2359304 | tf_op jit(solution)/shard_map/ppermute | solution.py:21
  31.6 89.9 %copy-start.15 = (bf16[1,2,192,384]{3,2,1,0:T(8,128)(2,1)}, bf16[1,2,192,384]{3,2,1,0:T(8,128)(2,1)S(1)}, u32[]{:S(2)}) copy-start(bf16[1,2,192,384]{3,2,1,0:T(8,128)(2,1)S(1)} %maximum_bitcast_fusion.1.refs_5_) | copy-start | bytes 884740
  31.6 26.6 %collective-permute-start.13 = (bf16[1,2,192,384]{3,2,1,0:T(8,128)(2,1)S(1)}, bf16[1,2,192,384]{3,2,1,0:T(8,128)(2,1)S(1)}, u32[]{:S(2)}, u32[]{:S(2)}) collective-permute-start(bf16[1,2,192,384]{3,2,1,0:T(8,128)(2,1)S(1)} %maximum_bitcast_fusion.1.refs_5_), channel_id=1, source_target_pairs={{0,8},{8,0},{16,24},{24,16},{1,9},{9,1},{17,25},{25,17},{2,10},{10... | collective-permute-start | bytes 884744 | tf_op jit(solution)/shard_map/ppermute | solution.py:21
  48.0 45.2 %collective-permute-start.10 = (bf16[4,2,96,1024]{3,2,1,0:T(8,128)(2,1)S(1)}, bf16[4,2,96,1024]{3,2,1,0:T(8,128)(2,1)S(1)}, u32[]{:S(2)}, u32[]{:S(2)}) collective-permute-start(bf16[4,2,96,1024]{3,2,1,0:T(8,128)(2,1)S(1)} %pad_maximum_fusion.3), channel_id=1, source_target_pairs={{0,8},{8,0},{16,24},{24,16},{1,9},{9,1},{17,25},{25,17},{2,10},{10... | collective-permute-start | bytes 4718600 | tf_op jit(solution)/shard_map/ppermute | solution.py:21
  49.0 7.1 %collective-permute-start.1 = (bf16[96,640]{1,0:T(8,128)(2,1)S(1)}, bf16[96,640]{1,0:T(8,128)(2,1)S(1)}, u32[]{:S(2)}, u32[]{:S(2)}) collective-permute-start(bf16[96,640]{1,0:T(8,128)(2,1)S(1)} %get-tuple-element.87), channel_id=1, source_target_pairs={{0,4},{1,5},{2,6},{3,7},{4,0},{5,1},{6,2},{7,3},{8,12},{9,13},{10,... | collective-permute-start | bytes 368648 | tf_op jit(solution)/shard_map/ppermute | solution.py:21
  56.2 9.0 %collective-permute-start.2 = (bf16[1,2,96,640]{3,2,1,0:T(8,128)(2,1)S(1)}, bf16[1,2,96,640]{3,2,1,0:T(8,128)(2,1)S(1)}, u32[]{:S(2)}, u32[]{:S(2)}) collective-permute-start(bf16[1,2,96,640]{3,2,1,0:T(8,128)(2,1)S(1)} %maximum_bitcast_fusion.2.refs_0_), channel_id=1, source_target_pairs={{0,2},{1,3},{2,0},{3,1},{4,6},{5,7},{6,4},{7,5},{8,10},{9,11},{10,... | collective-permute-start | bytes 737288 | tf_op jit(solution)/shard_map/ppermute | solution.py:21
  58.2 63.3 %copy-start.21 = (bf16[1,2,192,384]{3,2,1,0:T(8,128)(2,1)}, bf16[1,2,192,384]{3,2,1,0:T(8,128)(2,1)S(1)}, u32[]{:S(2)}) copy-start(bf16[1,2,192,384]{3,2,1,0:T(8,128)(2,1)S(1)} %collective-permute-done.13.refs_6_) | copy-start | bytes 884740
  58.3 15.8 %collective-permute-start.14 = (bf16[2,2,192,384]{3,2,1,0:T(8,128)(2,1)S(1)}, bf16[2,2,192,384]{3,2,1,0:T(8,128)(2,1)S(1)}, u32[]{:S(2)}, u32[]{:S(2)}) collective-permute-start(bf16[2,2,192,384]{3,2,1,0:T(8,128)(2,1)S(1)} %pad_maximum_fusion.7), channel_id=1, source_target_pairs={{0,2},{1,3},{2,0},{3,1},{4,6},{5,7},{6,4},{7,5},{8,10},{9,11},{10,... | collective-permute-start | bytes 1769480 | tf_op jit(solution)/shard_map/ppermute | solution.py:21
  65.2 27.1 %collective-permute-start.3 = (bf16[2,2,96,640]{3,2,1,0:T(8,128)(2,1)S(1)}, bf16[2,2,96,640]{3,2,1,0:T(8,128)(2,1)S(1)}, u32[]{:S(2)}, u32[]{:S(2)}) collective-permute-start(bf16[2,2,96,640]{3,2,1,0:T(8,128)(2,1)S(1)} %pad_maximum_fusion.8), channel_id=1, source_target_pairs={{0,8},{8,0},{16,24},{24,16},{1,9},{9,1},{17,25},{25,17},{2,10},{10... | collective-permute-start | bytes 1474568 | tf_op jit(solution)/shard_map/ppermute | solution.py:21
  74.3 47.2 %collective-permute-start.15 = (bf16[4,2,192,384]{3,2,1,0:T(8,128)(2,1)S(1)}, bf16[4,2,192,384]{3,2,1,0:T(8,128)(2,1)S(1)}, u32[]{:S(2)}, u32[]{:S(2)}) collective-permute-start(bf16[4,2,192,384]{3,2,1,0:T(8,128)(2,1)S(1)} %pad_maximum_fusion.4), channel_id=1, source_target_pairs={{0,16},{8,24},{16,0},{24,8},{1,17},{9,25},{17,1},{25,9},{2,18},{10... | collective-permute-start | bytes 3538952 | tf_op jit(solution)/shard_map/ppermute | solution.py:21
  92.4 27.3 %collective-permute-start.4 = (bf16[4,2,96,640]{3,2,1,0:T(8,128)(2,1)S(1)}, bf16[4,2,96,640]{3,2,1,0:T(8,128)(2,1)S(1)}, u32[]{:S(2)}, u32[]{:S(2)}) collective-permute-start(bf16[4,2,96,640]{3,2,1,0:T(8,128)(2,1)S(1)} %pad_maximum_fusion.5), channel_id=1, source_target_pairs={{0,16},{8,24},{16,0},{24,8},{1,17},{9,25},{17,1},{25,9},{2,18},{10... | collective-permute-start | bytes 2949128 | tf_op jit(solution)/shard_map/ppermute | solution.py:21
  95.4 104.5 %collective-permute-start.11 = (bf16[8,2,96,1024]{3,2,1,0:T(8,128)(2,1)}, bf16[8,2,96,1024]{3,2,1,0:T(8,128)(2,1)}, u32[]{:S(2)}, u32[]{:S(2)}) collective-permute-start(bf16[8,2,96,1024]{3,2,1,0:T(8,128)(2,1)} %pad_maximum_fusion), channel_id=1, source_target_pairs={{0,1},{1,0},{2,3},{3,2},{4,5},{5,4},{6,7},{7,6},{8,9},{9,8},{10,11... | collective-permute-start | bytes 9437192 | tf_op jit(solution)/shard_map/ppermute | solution.py:21
  121.4 49.2 %collective-permute-start.5 = (bf16[8,2,96,640]{3,2,1,0:T(8,128)(2,1)}, bf16[8,2,96,640]{3,2,1,0:T(8,128)(2,1)}, u32[]{:S(2)}, u32[]{:S(2)}) collective-permute-start(bf16[8,2,96,640]{3,2,1,0:T(8,128)(2,1)} %pad_maximum_fusion.2), channel_id=1, source_target_pairs={{0,1},{1,0},{2,3},{3,2},{4,5},{5,4},{6,7},{7,6},{8,9},{9,8},{10,11... | collective-permute-start | bytes 5898248 | tf_op jit(solution)/shard_map/ppermute | solution.py:21
  123.3 76.5 %collective-permute-start.16 = (bf16[8,2,192,384]{3,2,1,0:T(8,128)(2,1)}, bf16[8,2,192,384]{3,2,1,0:T(8,128)(2,1)}, u32[]{:S(2)}, u32[]{:S(2)}) collective-permute-start(bf16[8,2,192,384]{3,2,1,0:T(8,128)(2,1)} %pad_maximum_fusion.1), channel_id=1, source_target_pairs={{0,1},{1,0},{2,3},{3,2},{4,5},{5,4},{6,7},{7,6},{8,9},{9,8},{10,11... | collective-permute-start | bytes 7077896 | tf_op jit(solution)/shard_map/ppermute | solution.py:21
  123.9 46.7 %collective-permute-start = (bf16[512,768]{1,0:T(8,128)(2,1)S(1)}, bf16[512,768]{1,0:T(8,128)(2,1)}, u32[]{:S(2)}, u32[]{:S(2)}) collective-permute-start(bf16[512,768]{1,0:T(8,128)(2,1)S(1)} %copy-done.2), channel_id=1, source_target_pairs={{0,4},{1,5},{2,6},{3,7},{4,0},{5,1},{6,2},{7,3},{8,12},{9,13},{10,... | collective-permute-start | bytes 2359304 | tf_op jit(solution)/shard_map/ppermute | solution.py:21
  126.5 73.4 %collective-permute-start.6 = (bf16[256,768]{1,0:T(8,128)(2,1)S(1)}, bf16[256,768]{1,0:T(8,128)(2,1)S(1)}, u32[]{:S(2)}, u32[]{:S(2)}) collective-permute-start(bf16[256,768]{1,0:T(8,128)(2,1)S(1)} %convert_element_type.218), channel_id=1, source_target_pairs={{0,4},{1,5},{2,6},{3,7},{4,0},{5,1},{6,2},{7,3},{8,12},{9,13},{10,... | collective-permute-start | bytes 1179656 | tf_op jit(solution)/shard_map/ppermute | solution.py:21
  127.1 69.2 %copy-start.4 = (s32[512,1]{1,0:T(8,128)}, s32[512,1]{1,0:T(8,128)S(1)}, u32[]{:S(2)}) copy-start(s32[512,1]{1,0:T(8,128)S(1)} %copy.38.page_col) | copy-start | bytes 6148
  128.0 68.3 %copy-start.8 = (s32[3]{0:T(128)}, s32[3]{0:T(128)S(1)}, u32[]{:S(2)}) copy-start(s32[3]{0:T(128)S(1)} %pad_add_fusion.pos) | copy-start | bytes 40
  128.7 67.7 %copy-start.5 = (f32[2,768]{1,0:T(2,128)}, f32[2,768]{1,0:T(2,128)S(1)}, u32[]{:S(2)}) copy-start(f32[2,768]{1,0:T(2,128)S(1)} %pad_maximum_fusion.10.gains) | copy-start | bytes 18436
  199.8 49.8 %copy-start.13 = (f32[512,128]{1,0:T(8,128)}, f32[512,128]{1,0:T(8,128)S(1)}, u32[]{:S(2)}) copy-start(f32[512,128]{1,0:T(8,128)S(1)} %get-tuple-element.45.lse) | copy-start | bytes 786436
  249.6 48.5 %copy-start.18 = (f32[256,768]{1,0:T(8,128)S(1)}, f32[256,768]{1,0:T(8,128)}, u32[]{:S(2)}) copy-start(f32[256,768]{1,0:T(8,128)} %cotj_own.1) | copy-start | bytes 2359300
  276.7 21.8 %collective-permute-start.19 = (bf16[8,2,96,640]{3,2,1,0:T(8,128)(2,1)}, bf16[8,2,96,640]{3,2,1,0:T(8,128)(2,1)}, u32[]{:S(2)}, u32[]{:S(2)}) collective-permute-start(bf16[8,2,96,640]{3,2,1,0:T(8,128)(2,1)} %get-tuple-element.51), channel_id=1, source_target_pairs={{0,1},{1,0},{2,3},{3,2},{4,5},{5,4},{6,7},{7,6},{8,9},{9,8},{10,11... | collective-permute-start | bytes 5898248 | tf_op jit(solution)/shard_map/ppermute | solution.py:21
  276.8 52.2 %collective-permute-start.29 = (bf16[8,2,192,384]{3,2,1,0:T(8,128)(2,1)}, bf16[8,2,192,384]{3,2,1,0:T(8,128)(2,1)}, u32[]{:S(2)}, u32[]{:S(2)}) collective-permute-start(bf16[8,2,192,384]{3,2,1,0:T(8,128)(2,1)} %get-tuple-element.55), channel_id=1, source_target_pairs={{0,1},{1,0},{2,3},{3,2},{4,5},{5,4},{6,7},{7,6},{8,9},{9,8},{10,11... | collective-permute-start | bytes 7077896 | tf_op jit(solution)/shard_map/ppermute | solution.py:21
  277.3 88.7 %collective-permute-start.24 = (bf16[8,2,96,1024]{3,2,1,0:T(8,128)(2,1)}, bf16[8,2,96,1024]{3,2,1,0:T(8,128)(2,1)}, u32[]{:S(2)}, u32[]{:S(2)}) collective-permute-start(bf16[8,2,96,1024]{3,2,1,0:T(8,128)(2,1)} %get-tuple-element.53), channel_id=1, source_target_pairs={{0,1},{1,0},{2,3},{3,2},{4,5},{5,4},{6,7},{7,6},{8,9},{9,8},{10,11... | collective-permute-start | bytes 9437192 | tf_op jit(solution)/shard_map/ppermute | solution.py:21
  277.3 20.8 %collective-permute-start.17 = (bf16[256,768]{1,0:T(8,128)(2,1)S(1)}, bf16[256,768]{1,0:T(8,128)(2,1)S(1)}, u32[]{:S(2)}, u32[]{:S(2)}) collective-permute-start(bf16[256,768]{1,0:T(8,128)(2,1)S(1)} %copy-done.49), channel_id=1, source_target_pairs={{0,4},{1,5},{2,6},{3,7},{4,0},{5,1},{6,2},{7,3},{8,12},{9,13},{10,... | collective-permute-start | bytes 1179656 | tf_op jit(solution)/shard_map/ppermute | solution.py:21
  298.5 2.3 collective-permute-start.34
  300.1 46.2 %collective-permute-start.20 = (bf16[4,2,96,640]{3,2,1,0:T(8,128)(2,1)S(1)}, bf16[4,2,96,640]{3,2,1,0:T(8,128)(2,1)S(1)}, u32[]{:S(2)}, u32[]{:S(2)}) collective-permute-start(bf16[4,2,96,640]{3,2,1,0:T(8,128)(2,1)S(1)} %add_convert_fusion.2), channel_id=1, source_target_pairs={{0,8},{8,0},{16,24},{24,16},{1,9},{9,1},{17,25},{25,17},{2,10},{10... | collective-permute-start | bytes 2949128 | tf_op jit(solution)/shard_map/ppermute | solution.py:21
  300.8 24.1 %collective-permute-start.35 = (f32[5,768]{1,0:T(8,128)S(1)}, f32[5,768]{1,0:T(8,128)S(1)}, u32[]{:S(2)}, u32[]{:S(2)}) collective-permute-start(f32[5,768]{1,0:T(8,128)S(1)} %fusion.13), channel_id=1, source_target_pairs={{0,8},{8,0},{16,24},{24,16},{1,9},{9,1},{17,25},{25,17},{2,10},{10... | collective-permute-start | bytes 46088 | tf_op jit(solution)/shard_map/ppermute | solution.py:21
  325.0 3.9 collective-permute-start.36
  326.7 37.0 %collective-permute-start.18 = (bf16[512,768]{1,0:T(8,128)(2,1)S(1)}, bf16[512,768]{1,0:T(8,128)(2,1)S(1)}, u32[]{:S(2)}, u32[]{:S(2)}) collective-permute-start(bf16[512,768]{1,0:T(8,128)(2,1)S(1)} %copy-done.47), channel_id=1, source_target_pairs={{0,4},{1,5},{2,6},{3,7},{4,0},{5,1},{6,2},{7,3},{8,12},{9,13},{10,... | collective-permute-start | bytes 2359304 | tf_op jit(solution)/shard_map/ppermute | solution.py:21
  328.9 15.2 %collective-permute-start.37 = (f32[5,768]{1,0:T(8,128)S(1)}, f32[5,768]{1,0:T(8,128)S(1)}, u32[]{:S(2)}, u32[]{:S(2)}) collective-permute-start(f32[5,768]{1,0:T(8,128)S(1)} %add.340), channel_id=1, source_target_pairs={{0,2},{1,3},{2,0},{3,1},{4,6},{5,7},{6,4},{7,5},{8,10},{9,11},{10,... | collective-permute-start | bytes 46088 | tf_op jit(solution)/shard_map/ppermute | solution.py:21
  330.5 40.0 %collective-permute-start.30 = (bf16[4,2,192,384]{3,2,1,0:T(8,128)(2,1)S(1)}, bf16[4,2,192,384]{3,2,1,0:T(8,128)(2,1)S(1)}, u32[]{:S(2)}, u32[]{:S(2)}) collective-permute-start(bf16[4,2,192,384]{3,2,1,0:T(8,128)(2,1)S(1)} %add_convert_fusion.1), channel_id=1, source_target_pairs={{0,16},{8,24},{16,0},{24,8},{1,17},{9,25},{17,1},{25,9},{2,18},{10... | collective-permute-start | bytes 3538952 | tf_op jit(solution)/shard_map/ppermute | solution.py:21
  344.1 19.0 %collective-permute-start.38 = (f32[5,768]{1,0:T(8,128)S(1)}, f32[5,768]{1,0:T(8,128)S(1)}, u32[]{:S(2)}, u32[]{:S(2)}) collective-permute-start(f32[5,768]{1,0:T(8,128)S(1)} %add.341), channel_id=1, source_target_pairs={{0,4},{1,5},{2,6},{3,7},{4,0},{5,1},{6,2},{7,3},{8,12},{9,13},{10,... | collective-permute-start | bytes 46088 | tf_op jit(solution)/shard_map/ppermute | solution.py:21
  347.5 21.1 %collective-permute-start.21 = (bf16[2,2,96,640]{3,2,1,0:T(8,128)(2,1)S(1)}, bf16[2,2,96,640]{3,2,1,0:T(8,128)(2,1)S(1)}, u32[]{:S(2)}, u32[]{:S(2)}) collective-permute-start(bf16[2,2,96,640]{3,2,1,0:T(8,128)(2,1)S(1)} %add_convert_fusion.5), channel_id=1, source_target_pairs={{0,16},{8,24},{16,0},{24,8},{1,17},{9,25},{17,1},{25,9},{2,18},{10... | collective-permute-start | bytes 1474568 | tf_op jit(solution)/shard_map/ppermute | solution.py:21
  368.0 50.2 %collective-permute-start.25 = (bf16[4,2,96,1024]{3,2,1,0:T(8,128)(2,1)S(1)}, bf16[4,2,96,1024]{3,2,1,0:T(8,128)(2,1)S(1)}, u32[]{:S(2)}, u32[]{:S(2)}) collective-permute-start(bf16[4,2,96,1024]{3,2,1,0:T(8,128)(2,1)S(1)} %add_convert_fusion), channel_id=1, source_target_pairs={{0,8},{8,0},{16,24},{24,16},{1,9},{9,1},{17,25},{25,17},{2,10},{10... | collective-permute-start | bytes 4718600 | tf_op jit(solution)/shard_map/ppermute | solution.py:21
  369.7 7.7 %collective-permute-start.22 = (bf16[1,2,96,640]{3,2,1,0:T(8,128)(2,1)S(1)}, bf16[1,2,96,640]{3,2,1,0:T(8,128)(2,1)S(1)}, u32[]{:S(2)}, u32[]{:S(2)}) collective-permute-start(bf16[1,2,96,640]{3,2,1,0:T(8,128)(2,1)S(1)} %add_convert_fusion.8), channel_id=1, source_target_pairs={{0,2},{1,3},{2,0},{3,1},{4,6},{5,7},{6,4},{7,5},{8,10},{9,11},{10,... | collective-permute-start | bytes 737288 | tf_op jit(solution)/shard_map/ppermute | solution.py:21
  371.8 45.3 %collective-permute-start.31 = (bf16[2,2,192,384]{3,2,1,0:T(8,128)(2,1)S(1)}, bf16[2,2,192,384]{3,2,1,0:T(8,128)(2,1)S(1)}, u32[]{:S(2)}, u32[]{:S(2)}) collective-permute-start(bf16[2,2,192,384]{3,2,1,0:T(8,128)(2,1)S(1)} %add_convert_fusion.4), channel_id=1, source_target_pairs={{0,8},{8,0},{16,24},{24,16},{1,9},{9,1},{17,25},{25,17},{2,10},{10... | collective-permute-start | bytes 1769480 | tf_op jit(solution)/shard_map/ppermute | solution.py:21
  378.5 7.6 %collective-permute-start.23 = (bf16[96,640]{1,0:T(8,128)(2,1)S(1)}, bf16[96,640]{1,0:T(8,128)(2,1)S(1)}, u32[]{:S(2)}, u32[]{:S(2)}) collective-permute-start(bf16[96,640]{1,0:T(8,128)(2,1)S(1)} %fusion.11), channel_id=1, source_target_pairs={{0,4},{1,5},{2,6},{3,7},{4,0},{5,1},{6,2},{7,3},{8,12},{9,13},{10,... | collective-permute-start | bytes 368648 | tf_op jit(solution)/shard_map/ppermute | solution.py:21
  418.2 8.2 %collective-permute-start.32 = (bf16[1,2,192,384]{3,2,1,0:T(8,128)(2,1)S(1)}, bf16[1,2,192,384]{3,2,1,0:T(8,128)(2,1)S(1)}, u32[]{:S(2)}, u32[]{:S(2)}) collective-permute-start(bf16[1,2,192,384]{3,2,1,0:T(8,128)(2,1)S(1)} %add_convert_fusion.7), channel_id=1, source_target_pairs={{0,2},{1,3},{2,0},{3,1},{4,6},{5,7},{6,4},{7,5},{8,10},{9,11},{10,... | collective-permute-start | bytes 884744 | tf_op jit(solution)/shard_map/ppermute | solution.py:21
  419.8 18.7 %collective-permute-start.26 = (bf16[2,2,96,1024]{3,2,1,0:T(8,128)(2,1)S(1)}, bf16[2,2,96,1024]{3,2,1,0:T(8,128)(2,1)S(1)}, u32[]{:S(2)}, u32[]{:S(2)}) collective-permute-start(bf16[2,2,96,1024]{3,2,1,0:T(8,128)(2,1)S(1)} %add_convert_fusion.3), channel_id=1, source_target_pairs={{0,16},{8,24},{16,0},{24,8},{1,17},{9,25},{17,1},{25,9},{2,18},{10... | collective-permute-start | bytes 2359304 | tf_op jit(solution)/shard_map/ppermute | solution.py:21
  427.5 14.0 %collective-permute-start.33 = (bf16[192,384]{1,0:T(8,128)(2,1)S(1)}, bf16[192,384]{1,0:T(8,128)(2,1)S(1)}, u32[]{:S(2)}, u32[]{:S(2)}) collective-permute-start(bf16[192,384]{1,0:T(8,128)(2,1)S(1)} %fusion.10), channel_id=1, source_target_pairs={{0,4},{1,5},{2,6},{3,7},{4,0},{5,1},{6,2},{7,3},{8,12},{9,13},{10,... | collective-permute-start | bytes 442376 | tf_op jit(solution)/shard_map/ppermute | solution.py:21
  439.8 9.3 %collective-permute-start.27 = (bf16[1,2,96,1024]{3,2,1,0:T(8,128)(2,1)S(1)}, bf16[1,2,96,1024]{3,2,1,0:T(8,128)(2,1)S(1)}, u32[]{:S(2)}, u32[]{:S(2)}) collective-permute-start(bf16[1,2,96,1024]{3,2,1,0:T(8,128)(2,1)S(1)} %add_convert_fusion.6), channel_id=1, source_target_pairs={{0,2},{1,3},{2,0},{3,1},{4,6},{5,7},{6,4},{7,5},{8,10},{9,11},{10,... | collective-permute-start | bytes 1179656 | tf_op jit(solution)/shard_map/ppermute | solution.py:21
  450.5 9.3 %collective-permute-start.28 = (bf16[96,1024]{1,0:T(8,128)(2,1)S(1)}, bf16[96,1024]{1,0:T(8,128)(2,1)S(1)}, u32[]{:S(2)}, u32[]{:S(2)}) collective-permute-start(bf16[96,1024]{1,0:T(8,128)(2,1)S(1)} %fusion.8), channel_id=1, source_target_pairs={{0,4},{1,5},{2,6},{3,7},{4,0},{5,1},{6,2},{7,3},{8,12},{9,13},{10,... | collective-permute-start | bytes 589832 | tf_op jit(solution)/shard_map/ppermute | solution.py:21
  (41 other events, 682.3 us)

commit v2 on v1

--- a/solution.py
+++ b/solution.py
@@ -11,6 +11,7 @@
 STEP = 10
 LANES = 128
 CHUNK = 128
+ROW_PARTS = (1, 2, 5)
 NEG = -1000000000.0
 LOW = jnp.bfloat16
 FULL = jnp.float32
@@ -27,13 +28,39 @@
     return [(d ^ d_mask, w ^ w_mask) for d, w in codes]
 
 
-def gather(unit, order):
-    arrays, codes = [unit[None]], [[(0, 0)]]
-    for axis, mask in order:
-        held = arrays[0] if len(arrays) == 1 else jnp.concatenate(arrays, axis=0)
-        known = [code for group in codes for code in group]
-        arrays.append(flip(held, axis, mask))
-        codes.append(flipped(known, axis, mask))
+def after(value, *others):
+    return lax.optimization_barrier((value, *others))[0]
+
+
+class Doubling:
+    def __init__(self, unit, slot, order, last):
+        self.slot, self.last = slot, last
+        self.arrays, self.codes = [unit[None]], [[(0, 0)]]
+        for axis, mask in order:
+            held, known = self.held()
+            self.arrays.append(flip(held, axis, mask))
+            self.codes.append(flipped(known, axis, mask))
+
+    def held(self):
+        held = self.arrays[0] if len(self.arrays) == 1 else jnp.concatenate(self.arrays, axis=0)
+        return held, [code for group in self.codes for code in group]
+
+    def finish(self, *others):
+        newest, newest_known = self.arrays.pop(), self.codes.pop()
+        held, known = self.held()
+        axis, mask = self.last
+        crossed = flip(after(newest, *others) if others else newest, axis, mask)
+        arrays = self.arrays + [newest, flip(held, axis, mask), crossed]
+        codes = self.codes + [newest_known, flipped(known, axis, mask), flipped(newest_known, axis, mask)]
+        return arrays, [(self.slot, group) for group in codes]
+
+
+def finish_both(pair, *others):
+    arrays, codes = [], []
+    for one in pair:
+        some, known = one.finish(*others)
+        arrays += some
+        codes += known
     return arrays, codes
 
 
@@ -44,22 +71,64 @@
     return codes
 
 
-def reduce_pieces(keep, send, order):
-    parts = [keep]
-    outgoing = send
-    for step, (axis, mask) in enumerate(order):
-        parts.append(flip(outgoing, axis, mask))
-        if step + 1 < len(order):
-            half = parts[0].shape[0] // 2
-            outgoing = sum(part[half:].astype(FULL) for part in parts).astype(LOW)
-            parts = [part[:half] for part in parts]
-    return sum(part[0].astype(FULL) for part in parts)
-
-
-def small_sum(value, steps):
-    for axis, mask in steps:
-        value = value + flip(value, axis, mask)
-    return value
+class Halving:
+    def __init__(self, kept, sent, first, orders, after_both):
+        self.parts, self.outgoing = [kept], sent
+        self.first, self.orders, self.joint = first, orders, after_both
+        self.step, self.last = 0, ()
+        self.count = 1 + len(orders[0]) + len(after_both)
+
+    def left(self):
+        return self.step < self.count
+
+    def hold(self, *others):
+        self.outgoing = jax.tree.map(lambda value: after(value, *others), self.outgoing)
+
+    def send(self):
+        own = len(self.orders[0])
+        if self.step == 0:
+            arrived = flip(self.outgoing, *self.first)
+            parts = self.parts + [arrived]
+            middle = arrived.shape[0] // 2
+            self.slots = [[part[:middle] for part in parts], [part[middle:] for part in parts]]
+            self.last = (arrived,)
+            self.outgoing = [None, None]
+            for slot in (0, 1):
+                self.outgoing[slot], self.slots[slot] = split_sums(self.slots[slot])
+        elif self.step < own:
+            arrived = [flip(self.outgoing[slot], *self.orders[slot][self.step - 1]) for slot in (0, 1)]
+            self.last = tuple(arrived)
+            for slot in (0, 1):
+                self.outgoing[slot], self.slots[slot] = split_sums(self.slots[slot] + [arrived[slot]])
+        elif self.step == own:
+            arrived = [flip(self.outgoing[slot], *self.orders[slot][self.step - 1]) for slot in (0, 1)]
+            self.last = tuple(arrived)
+            self.slots = [self.slots[slot] + [arrived[slot]] for slot in (0, 1)]
+            pairs = [split_sums(parts) if self.joint else (None, parts) for parts in self.slots]
+            if self.joint:
+                self.outgoing = jnp.concatenate([pair[0] for pair in pairs], axis=0)
+            self.slots = [pair[1] for pair in pairs]
+        else:
+            arrived = flip(self.outgoing, *self.joint[self.step - 1 - own])
+            middle = arrived.shape[0] // 2
+            self.last = (arrived,)
+            self.slots = [self.slots[0] + [arrived[:middle]], self.slots[1] + [arrived[middle:]]]
+            if self.step + 1 < self.count:
+                pairs = [split_sums(parts) for parts in self.slots]
+                self.outgoing = jnp.concatenate([pair[0] for pair in pairs], axis=0)
+                self.slots = [pair[1] for pair in pairs]
+        self.step += 1
+
+    def total(self):
+        while self.left():
+            self.send()
+        return tuple(sum(part[0].astype(FULL) for part in parts) for parts in self.slots)
+
+
+def split_sums(parts):
+    half = parts[0].shape[0] // 2
+    outgoing = sum(part[half:].astype(FULL) for part in parts).astype(LOW)
+    return outgoing, [part[:half] for part in parts]
 
 
 class Blocks:
@@ -134,20 +203,28 @@
     return pl.ds(pl.multiple_of(index * size, size), size)
 
 
-def places(pos, codes, half):
+def places(pos, slot, codes, half):
+    owner = pos[2] if slot == 0 else 1 - pos[2]
     for index, (d_mask, w_mask) in enumerate(codes):
-        doc = pos[0] ^ d_mask
-        inner = pos[1] ^ w_mask
-        for slot in (0, 1):
-            owner = pos[2] if slot == 0 else 1 - pos[2]
-            yield index, slot, doc, owner * half + inner
+        yield index, pos[0] ^ d_mask, owner * half + (pos[1] ^ w_mask)
 
 
 def load_pieces(pos, refs, codes, half, lanes, target, sem):
-    for ref, group in zip(refs, codes):
-        for index, slot, doc, inner in places(pos, group, half):
+    for ref, (slot, group) in zip(refs, codes):
+        for index, doc, inner in places(pos, slot, group, half):
             pltpu.make_async_copy(
-                ref.at[index, slot, :, pl.ds(lanes[0], lanes[1])], target(doc, inner), sem
+                ref.at[index, :, pl.ds(lanes[0], lanes[1])], target(doc, inner), sem
+            ).start()
+
+
+def store_pieces(pos, source, sums, half, targets, lanes, sem):
+    for slot, codes in enumerate(sums):
+        count = len(codes) // 2
+        for index, doc, inner in places(pos, slot, codes, half):
+            pltpu.make_async_copy(
+                source(doc, inner),
+                targets[index // count].at[slot * count + index % count, :, pl.ds(lanes[0], lanes[1])],
+                sem,
             ).start()
 
 
@@ -243,12 +320,13 @@
 def feed_kernel(
     shape, pos, att, own, cot, cotj_own, cotj_oth, coef, gain, page_col, *refs
 ):
-    (up_codes, down_codes, up_sums, down_sums, half, rows, down_rows, ups, outs, downs, length, width, hidden, block) = shape
+    (up_codes, down_codes, sums, half, rows, down_rows, ups, outs, downs, length, width, hidden, block) = shape
     n_up, n_down = len(up_codes), len(down_codes)
     up_pieces, down_pieces = refs[:n_up], refs[n_up : n_up + n_down]
     refs = refs[n_up + n_down :]
-    (out_ref, away_ref, dmid_ref, datt_ref, dgain_ref, up_keep, up_send, down_keep, down_send) = refs[:9]
-    (w_up, o_held, w_out, d_held, w_down, g_up, g_out, g_down, mid, unit_ref, scale_ref, dz, h2, h2_t, dffn, dffn_t, att_t, acts, dpre, acc, dacc, dbranch, sem_up, sem_out, sem_down, sem_keep, sem_send, sem_dkeep, sem_dsend) = refs[9:]
+    mid, unit_ref, scale_ref, dz, acc, dacc, w_out, g_up = refs[:8]
+    down_targets = refs[8:10]
+    (w_up, o_held, d_held, w_down, g_down, h2, h2_t, dffn, dffn_t, acts, dpre, sem_up, sem_out, sem_down, sem_gdown) = refs[10:]
     load_pieces(pos, up_pieces, up_codes, half, (ups.wide, outs.wide), row_target(o_held, outs, rows), sem_out)
     load_pieces(pos, up_pieces, up_codes, half, (0, ups.wide), row_target(w_up, ups, rows), sem_up)
     load_pieces(pos, down_pieces, down_codes, half, (0, downs.wide), column_target(d_held, downs, down_rows), sem_down)
@@ -262,7 +340,6 @@
             dz[part, :] = grad
             dffn[part, :] = (grad * valid).astype(LOW)
     dffn_t[...] = dffn[...].T
-    att_t[...] = att[...].T
     wait_whole(o_held, sem_out)
     merge_tiles(o_held, w_out, outs)
 
@@ -312,30 +389,34 @@
 
     if downs.room > downs.total:
         g_down[:, downs.total :] = jnp.zeros((width, downs.room - downs.total), LOW)
-    if outs.room > outs.total:
-        g_out[:, outs.total :] = jnp.zeros((width, outs.room - outs.total), LOW)
-    for codes, keep, send, s_keep, s_send in ((down_sums, down_keep, down_send, sem_dkeep, sem_dsend),):
-        count = len(codes) // 2
-        for index, slot, doc, inner in places(pos, codes, half):
-            target, sem = (keep, s_keep) if index < count else (send, s_send)
-            pltpu.make_async_copy(
-                g_down.at[
-                    pl.ds(pl.multiple_of(doc * down_rows, down_rows), down_rows),
-                    pl.ds(downs.start_dynamic(inner), downs.wide),
-                ],
-                target.at[index % count, slot],
-                sem,
-            ).start()
-    count = len(up_sums) // 2
-    for index, slot, doc, inner in places(pos, up_sums, half):
-        target, sem = (up_keep, sem_keep) if index < count else (up_send, sem_send)
-        height = pl.ds(pl.multiple_of(inner * rows, rows), rows)
-        pltpu.make_async_copy(
-            g_up.at[height, pl.ds(ups.start_dynamic(doc), ups.wide)],
-            target.at[index % count, slot, :, pl.ds(0, ups.wide)],
-            sem,
-        ).start()
-
+    store_pieces(
+        pos,
+        lambda doc, inner: g_down.at[
+            pl.ds(pl.multiple_of(doc * down_rows, down_rows), down_rows),
+            pl.ds(downs.start_dynamic(inner), downs.wide),
+        ],
+        sums, half, down_targets, (0, downs.wide), sem_gdown,
+    )
+    for target in down_targets:
+        wait_whole(target, sem_gdown)
+
+
+def branch_kernel(shape, pos, att, gain, page_col, mid, unit_ref, scale_ref, dz, acc, dacc, w_out, g_up, *refs):
+    sums, half, rows, ups, outs, length, width = shape
+    out_ref, away_ref, dmid_ref, datt_ref, dgain_ref = refs[:5]
+    up_targets = refs[5:7]
+    g_out, att_t, dbranch, sem_gup = refs[7:]
+    half_rows = length // 2
+    parts = length // CHUNK
+    store_pieces(
+        pos,
+        lambda doc, inner: g_up.at[
+            pl.ds(pl.multiple_of(inner * rows, rows), rows),
+            pl.ds(ups.start_dynamic(doc), ups.wide),
+        ],
+        sums, half, up_targets, (0, ups.wide), sem_gup,
+    )
+    att_t[...] = att[...].T
     dgain_ref[...] = jnp.zeros_like(dgain_ref)
 
     @pl.loop(0, parts)
@@ -355,26 +436,25 @@
         part = pl.ds(pl.multiple_of((1 - pos[2]) * half_rows + i * CHUNK, CHUNK), CHUNK)
         away_ref[pl.ds(i * CHUNK, CHUNK), :] = out_ref[part, :].astype(LOW)
     g_out[:, : outs.total] = matmul(att_t[...], dbranch[...]).astype(LOW)
-    for index, slot, doc, inner in places(pos, up_sums, half):
-        target, sem = (up_keep, sem_keep) if index < count else (up_send, sem_send)
-        height = pl.ds(pl.multiple_of(inner * rows, rows), rows)
-        pltpu.make_async_copy(
-            g_out.at[height, pl.ds(outs.start_dynamic(doc), outs.wide)],
-            target.at[index % count, slot, :, pl.ds(ups.wide, outs.wide)],
-            sem,
-        ).start()
-    wait_whole(down_keep, sem_dkeep)
-    wait_whole(down_send, sem_dsend)
-    wait_whole(up_keep, sem_keep)
-    wait_whole(up_send, sem_send)
-
-
-def back_kernel(
-    shape, pos, own, other, gains, page_col, page_row, mask_col, q_ref, k_ref, v_ref, att, datt, lse, weight, *refs
+    if outs.room > outs.total:
+        g_out[:, outs.total :] = jnp.zeros((width, outs.room - outs.total), LOW)
+    store_pieces(
+        pos,
+        lambda doc, inner: g_out.at[
+            pl.ds(pl.multiple_of(inner * rows, rows), rows),
+            pl.ds(outs.start_dynamic(doc), outs.wide),
+        ],
+        sums, half, up_targets, (ups.wide, outs.wide), sem_gup,
+    )
+    for target in up_targets:
+        wait_whole(target, sem_gup)
+
+
+def scores_back_kernel(
+    shape, pairs, page_col, page_row, mask_col, q_ref, k_ref, v_ref, att, datt, lse, dq, dk, dv,
+    allowed, flat, lse_t, dots_t, dscore,
 ):
-    (codes, half, rows, blocks, length, width, factor) = shape
-    (own_ref, oth_ref, dgain_ref, keep, send) = refs[:5]
-    (dq, dk, dv, h_t, allowed, flat, lse_t, dots_t, dscore, grad, sem_keep, sem_send) = refs[5:]
+    length, width, factor = shape
     size = width // HEADS
     per = LANES // size
     parts = length // CHUNK
@@ -394,9 +474,10 @@
     )
     lse_t[...] = lse[...].T
 
-    @pl.loop(0, width // LANES)
+    @pl.loop(pairs[0], pairs[1])
     def _(pair):
         cols = pl.ds(pl.multiple_of(pair * LANES, LANES), LANES)
+        here = pl.ds(pl.multiple_of((pair - pairs[0]) * LANES, LANES), LANES)
         queries, grads, keys_all = q_ref[:, cols], datt[:, cols], k_ref[:, cols]
         lane = lax.broadcasted_iota(jnp.int32, (length, LANES), 1)
         lane_part = lax.broadcasted_iota(jnp.int32, (CHUNK, LANES), 1)
@@ -420,50 +501,61 @@
                 dv_part = matmul(probs.astype(LOW), grads).astype(LOW)
                 dk_part = matmul(low, queries).astype(LOW)
                 if sub > 0:
-                    dv_part = jnp.where(inside_part, dv_part, dv[part, cols])
-                    dk_part = jnp.where(inside_part, dk_part, dk[part, cols])
-                dv[part, cols] = dv_part
-                dk[part, cols] = dk_part
+                    dv_part = jnp.where(inside_part, dv_part, dv[part, here])
+                    dk_part = jnp.where(inside_part, dk_part, dk[part, here])
+                dv[part, here] = dv_part
+                dk[part, here] = dk_part
             dq_head = matmul_tn(dscore[...], keys_all)
             dq_pair = dq_head if dq_pair is None else jnp.where(inside, dq_head, dq_pair)
-        dq[:, cols] = (dq_pair * factor).astype(LOW)
-
+        dq[:, here] = (dq_pair * factor).astype(LOW)
+
+
+def project_back_kernel(shape, pos, own, other, gains, weight, *refs):
+    (sums, half, rows, blocks, length, width, runs) = shape
+    grads = [refs[3 * i : 3 * i + 3] for i in range(len(runs))]
+    refs = refs[3 * len(runs) :]
+    own_ref, oth_ref, dgain_ref = refs[:3]
+    targets = refs[3:5]
+    h_t, flat, grad, sem = refs[5:]
+    parts = length // CHUNK
     for which, source in ((0, own), (1, other)):
         for i in range(parts):
             part = pl.ds(i * CHUNK, CHUNK)
             unit, _ = normed(source[part, :].astype(FULL))
             flat[part, :] = unit * gains[which : which + 1, :]
         h_t[which] = flat[...].astype(LOW).T
-    grad[:, :width] = matmul(h_t[0], dq[...]).astype(LOW)
-    grad[:, width : 2 * width] = matmul(h_t[1], dk[...]).astype(LOW)
-    grad[:, 2 * width : 3 * width] = matmul(h_t[1], dv[...]).astype(LOW)
+    for (low, high), trio in zip(runs, grads):
+        for block, (which, ref) in enumerate(zip((0, 1, 1), trio)):
+            grad[:, block * width + low : block * width + high] = matmul(h_t[which], ref[...]).astype(LOW)
     if blocks.room > blocks.total:
         grad[:, blocks.total :] = jnp.zeros((width, blocks.room - blocks.total), LOW)
-    count = len(codes) // 2
-    for index, slot, doc, inner in places(pos, codes, half):
-        target, sem = (keep, sem_keep) if index < count else (send, sem_send)
-        pltpu.make_async_copy(
-            grad.at[
-                pl.ds(pl.multiple_of(inner * rows, rows), rows),
-                pl.ds(blocks.start_dynamic(doc), blocks.wide),
-            ],
-            target.at[index % count, slot],
-            sem,
-        ).start()
+    store_pieces(
+        pos,
+        lambda doc, inner: grad.at[
+            pl.ds(pl.multiple_of(inner * rows, rows), rows),
+            pl.ds(blocks.start_dynamic(doc), blocks.wide),
+        ],
+        sums, half, targets, (0, blocks.wide), sem,
+    )
     dgain_ref[...] = jnp.zeros_like(dgain_ref)
     for i in range(parts):
         part = pl.ds(i * CHUNK, CHUNK)
         unit, _ = normed(own[part, :].astype(FULL))
-        value = matmul_nt(dq[part, :], weight[:, :width])
+        value = sum(
+            matmul_nt(trio[0][part, :], weight[:, low:high]) for (low, high), trio in zip(runs, grads)
+        )
         own_ref[part, :] = value
         dgain_ref[0:1, :] += jnp.sum(value * unit, axis=0, keepdims=True)
         unit, _ = normed(other[part, :].astype(FULL))
-        value = matmul_nt(dk[part, :], weight[:, width : 2 * width])
-        value = value + matmul_nt(dv[part, :], weight[:, 2 * width :])
+        value = sum(
+            matmul_nt(trio[block][part, :], weight[:, block * width + low : block * width + high])
+            for (low, high), trio in zip(runs, grads)
+            for block in (1, 2)
+        )
         oth_ref[part, :] = value.astype(LOW)
         dgain_ref[1:2, :] += jnp.sum(value * unit, axis=0, keepdims=True)
-    wait_whole(keep, sem_keep)
-    wait_whole(send, sem_send)
+    for target in targets:
+        wait_whole(target, sem)
 
 
 def tail_kernel(length, own, gain, mine, theirs, dmid, out_ref):
@@ -477,6 +569,9 @@
 VMEM = pl.BlockSpec(memory_space=pltpu.VMEM)
 ANY = pl.BlockSpec(memory_space=pl.ANY)
 SMEM = pl.BlockSpec(memory_space=pltpu.SMEM)
+
+
+LITTLE = pl.CostEstimate(flops=1_000, bytes_accessed=1_000, transcendentals=0)
 
 
 def params(mebibytes):
@@ -521,7 +616,6 @@
     def swap(value):
         return flip(value, *across)
 
-    other_rows = swap(rows)
     column = doc * w_qkv.shape[2] + lax.iota(jnp.int32, w_qkv.shape[2])
     is_query = (column < width)[None, None, :]
     pair_qkv = jnp.where(is_query, w_qkv, w_qkv[::-1]).astype(LOW)
@@ -534,17 +628,25 @@
         (ups.pad(own_first(w_up.astype(LOW)), doc), outs.pad(own_first(w_out.astype(LOW)), doc)), axis=-1
     )
     unit_c = downs.pad(jnp.swapaxes(own_first(w_down.astype(LOW)), 1, 2), place)
-    unit_a = jnp.stack((unit_a[0], swap(unit_a[1])))
-    unit_b = jnp.stack((unit_b[0], swap(unit_b[1])))
+    unit_a = (unit_a[0], swap(unit_a[1]))
+    unit_b = (unit_b[0], swap(unit_b[1]))
     if downs.aligned:
-        unit_c = jnp.stack((unit_c[0], swap(unit_c[1])))
+        unit_c = (unit_c[0], swap(unit_c[1]))
     else:
         raw = jnp.swapaxes(own_first(w_down.astype(LOW)), 1, 2)
-        unit_c = jnp.stack((unit_c[0], downs.pad(swap(raw[1]), (place + half) % wide)))
-    pieces_a, codes_a = gather(unit_a, along_z + along_x + along_y + core)
-    pieces_b, codes_b = gather(unit_b, along_z + along_y + along_x + core)
-    pieces_c, codes_c = gather(unit_c, along_x + along_z + along_y + core)
-    other_joined = swap(cot_joined.astype(LOW))
+        unit_c = (unit_c[0], downs.pad(swap(raw[1]), (place + half) % wide))
+    chunks, begin = [], 0
+    for size in [length * part // 8 for part in ROW_PARTS]:
+        some = rows[begin : begin + size]
+        chunks.append(swap(after(some, chunks[-1]) if chunks else some))
+        begin += size
+    other_rows = jnp.concatenate(chunks, axis=0)
+    zxy, zyx = along_z + along_x + along_y, along_z + along_y + along_x
+    both_a = [Doubling(unit_a[i], i, order, core[0]) for i, order in enumerate((zxy, zyx))]
+    both_b = [Doubling(unit_b[i], i, order, core[0]) for i, order in enumerate((zxy, zyx))]
+    both_c = [Doubling(unit_c[i], i, order, core[0]) for i, order in enumerate((zyx, zxy))]
+    pieces_a, codes_a = finish_both(both_a)
+    other_joined = swap(after(cot_joined.astype(LOW), chunks[-1]))
 
     page_col, page_row = page[:, None], page[None, :]
     mask_col, mask_row = key_mask[:, None], key_mask[None, :]
@@ -574,81 +676,148 @@
             pltpu.SemaphoreType.DMA,
         ],
         compiler_params=params(48),
-        cost_estimate=pl.CostEstimate(flops=5_000_000_000, bytes_accessed=20_000_000, transcendentals=3_000_000),
+        cost_estimate=LITTLE,
         name="project_attend",
     )(pos, rows, other_rows, gain_one, page_col, page_row, mask_row, *pieces_a)
 
-    order_b = core + along_x + along_y + along_z
-    order_c = core + along_y + along_x + along_z
-    order_a = core + along_x + along_y + along_z
-    sums_a, sums_b, sums_c = sum_codes(order_a), sum_codes(order_b), sum_codes(order_c)
-    sent = len(sums_a) // 2
+    pieces_b, codes_b = finish_both(both_b, lse)
+    pieces_c, codes_c = finish_both(both_c, lse)
+    orders = (core + along_x + along_y + along_z, core + along_y + along_x + along_z)
+    own_orders = tuple(order[1 : 1 + len(along_x + along_y)] for order in orders)
+    sums = tuple(sum_codes(order) for order in orders)
+    sent_count = len(sums[0])
     block = 3 * LANES
-    shape = (codes_b, codes_c, sums_b, sums_c, half, piece_rows, down_rows, ups, outs, downs, length, width, hidden, block)
-    shape_b = jax.ShapeDtypeStruct((sent, 2, piece_rows, ups.wide + outs.wide), LOW)
-    shape_c = jax.ShapeDtypeStruct((sent, 2, down_rows, downs.wide), LOW)
-    (stream_out, away, middle_grad, attended_grad, dgain_two, keep_b, send_b, keep_c, send_c) = pl.pallas_call(
+    shape = (codes_b, codes_c, sums, half, piece_rows, down_rows, ups, outs, downs, length, width, hidden, block)
+    shape_b = jax.ShapeDtypeStruct((sent_count, piece_rows, ups.wide + outs.wide), LOW)
+    shape_c = jax.ShapeDtypeStruct((sent_count, down_rows, downs.wide), LOW)
+    *carried, kept_c, sent_c = pl.pallas_call(
         functools.partial(feed_kernel, shape),
-        out_shape=(full_rows, jax.ShapeDtypeStruct((half_rows, width), LOW), full_rows, low_rows,
-                   jax.ShapeDtypeStruct((8, width), FULL), shape_b, shape_b, shape_c, shape_c),
+        out_shape=(full_rows, full_rows, jax.ShapeDtypeStruct((length, LANES), FULL), full_rows, full_rows, full_rows,
+                   jax.ShapeDtypeStruct((width, width), LOW), jax.ShapeDtypeStruct((width, hidden), LOW)) + (shape_c,) * 2,
         in_specs=[SMEM] + [VMEM] * 8 + [ANY] * (len(pieces_b) + len(pieces_c)),
-        out_specs=(VMEM,) * 5 + (ANY,) * 4,
+        out_specs=(VMEM,) * 8 + (ANY,) * 2,
         scratch_shapes=[
             pltpu.VMEM((width, hidden), LOW),
             pltpu.VMEM(held_shape(outs, width), LOW),
-            pltpu.VMEM((width, width), LOW),
             pltpu.VMEM(held_shape(downs, width), LOW),
             pltpu.VMEM((8, LANES) if downs.aligned else (width, hidden), LOW),
-            pltpu.VMEM((width, hidden), LOW),
-            pltpu.VMEM((width, outs.room), LOW),
             pltpu.VMEM((width, downs.room), LOW),
-            pltpu.VMEM((length, width), FULL),
-            pltpu.VMEM((length, width), FULL),
-            pltpu.VMEM((length, LANES), FULL),
-            pltpu.VMEM((length, width), FULL),
             pltpu.VMEM((length, width), LOW),
             pltpu.VMEM((width, length), LOW),
             pltpu.VMEM((length, width), LOW),
             pltpu.VMEM((width, length), LOW),
-            pltpu.VMEM((width, length), LOW),
             pltpu.VMEM((length, block), LOW),
             pltpu.VMEM((length, block), LOW),
-            pltpu.VMEM((length, width), FULL),
-            pltpu.VMEM((length, width), FULL),
-            pltpu.VMEM((length, width), LOW),
-        ] + [pltpu.SemaphoreType.DMA] * 7,
+        ] + [pltpu.SemaphoreType.DMA] * 4,
         compiler_params=params(60),
-        cost_estimate=pl.CostEstimate(flops=17_000_000_000, bytes_accessed=45_000_000, transcendentals=1_600_000),
+        cost_estimate=LITTLE,
         name="feed_forward_back",
     )(pos, attended, rows, cot_stream, cot_joined, other_joined, coef, gain_two, page_col, *pieces_b, *pieces_c)
 
-    partner_rows = swap(away)
-
-    shape = (sums_a, half, piece_rows, qkvs, length, width, factor)
-    shape_a = jax.ShapeDtypeStruct((sent, 2, piece_rows, qkvs.wide), LOW)
-    own_part, away_part, dgain_one, keep_a, send_a = pl.pallas_call(
-        functools.partial(back_kernel, shape),
-        out_shape=(full_rows, low_rows, jax.ShapeDtypeStruct((8, width), FULL), shape_a, shape_a),
-        in_specs=[SMEM] + [VMEM] * 13,
+    shape = (sums, half, piece_rows, ups, outs, length, width)
+    (stream_out, away, middle_grad, attended_grad, dgain_two, kept_b, sent_b) = pl.pallas_call(
+        functools.partial(branch_kernel, shape),
+        out_shape=(full_rows, jax.ShapeDtypeStruct((half_rows, width), LOW), full_rows, low_rows,
+                   jax.ShapeDtypeStruct((8, width), FULL)) + (shape_b,) * 2,
+        in_specs=[SMEM] + [VMEM] * 11,
+        out_specs=(VMEM,) * 5 + (ANY,) * 2,
+        scratch_shapes=[
+            pltpu.VMEM((width, outs.room), LOW),
+            pltpu.VMEM((width, length), LOW),
+            pltpu.VMEM((length, width), LOW),
+            pltpu.SemaphoreType.DMA,
+        ],
+        compiler_params=params(48),
+        cost_estimate=LITTLE,
+        name="branch_back",
+    )(pos, attended, gain_two, page_col, *carried)
+
+    def attend_back(pairs, *operands):
+        low_cols = jax.ShapeDtypeStruct((length, (pairs[1] - pairs[0]) * LANES), LOW)
+        return pl.pallas_call(
+            functools.partial(scores_back_kernel, (length, width, factor), pairs),
+            out_shape=(low_cols,) * 3,
+            in_specs=[VMEM] * 9,
+            out_specs=(VMEM,) * 3,
+            scratch_shapes=[
+                pltpu.VMEM((length, length), FULL),
+                pltpu.VMEM((length, width), FULL),
+                pltpu.VMEM((LANES, length), FULL),
+                pltpu.VMEM((LANES, length), FULL),
+                pltpu.VMEM((length, length), LOW),
+            ],
+            compiler_params=params(40),
+            cost_estimate=LITTLE,
+            name="attend_back",
+        )(page_col, page_row, mask_col, *operands)
+
+    def halving(kept, sent):
+        return Halving(kept, sent, core[0], own_orders, along_z)
+
+    sums_c, sums_b = halving(kept_c, sent_c), halving(kept_b, sent_b)
+    sums_c.send()
+    first = after(queries, *sums_c.last)
+    sums_c.send()
+    sums_b.send()
+    partner_rows = swap(after(away, first))
+    pair_count = width // LANES
+    cuts = (0, pair_count // 2, pair_count)
+    grads_one = attend_back(cuts[:2], first, keys, values, attended, attended_grad, lse)
+    second = after(queries, *grads_one, *sums_c.last, *sums_b.last)
+    sums_b.hold(grads_one[0], *sums_c.last)
+    sums_c.hold(grads_one[0], *sums_b.last)
+    sums_b.send()
+    sums_c.send()
+    grads_two = attend_back(cuts[1:], second, keys, values, attended, attended_grad, lse)
+
+    runs = tuple((low * LANES, high * LANES) for low, high in zip(cuts[:-1], cuts[1:]))
+    shape = (sums, half, piece_rows, qkvs, length, width, runs)
+    shape_a = jax.ShapeDtypeStruct((sent_count, piece_rows, qkvs.wide), LOW)
+    own_part, away_part, dgain_one, kept_a, sent_a = pl.pallas_call(
+        functools.partial(project_back_kernel, shape),
+        out_shape=(full_rows, low_rows, jax.ShapeDtypeStruct((8, width), FULL)) + (shape_a,) * 2,
+        in_specs=[SMEM] + [VMEM] * (4 + 3 * len(runs)),
         out_specs=(VMEM,) * 3 + (ANY,) * 2,
         scratch_shapes=[
-            pltpu.VMEM((length, width), LOW),
-            pltpu.VMEM((length, width), LOW),
-            pltpu.VMEM((length, width), LOW),
             pltpu.VMEM((2, width, length), LOW),
-            pltpu.VMEM((length, length), FULL),
             pltpu.VMEM((length, width), FULL),
-            pltpu.VMEM((LANES, length), FULL),
-            pltpu.VMEM((LANES, length), FULL),
-            pltpu.VMEM((length, length), LOW),
             pltpu.VMEM((width, qkvs.room), LOW),
-        ] + [pltpu.SemaphoreType.DMA] * 2,
-        compiler_params=params(56),
-        cost_estimate=pl.CostEstimate(flops=9_000_000_000, bytes_accessed=20_000_000, transcendentals=3_000_000),
-        name="attend_back",
-    )(pos, rows, other_rows, gain_one, page_col, page_row, mask_col, queries, keys, values, attended, attended_grad, lse, weight_qkv)
+            pltpu.SemaphoreType.DMA,
+        ],
+        compiler_params=params(40),
+        cost_estimate=LITTLE,
+        name="project_back",
+    )(pos, rows, other_rows, gain_one, weight_qkv, *grads_one, *grads_two)
 
     back_part = swap(away_part)
+    sums_a = halving(kept_a, sent_a)
+    sums_a.hold(*sums_c.last, *sums_b.last)
+    sums_b.hold(*sums_c.last)
+    sums_c.hold(*sums_b.last)
+    sums_a.send()
+    sums_b.send()
+    sums_c.send()
+    own_rows = lax.dynamic_slice_in_dim(stream_out, stream * half_rows, half_rows, 0)
+    partner_rows = partner_rows.astype(FULL)
+    text_rows = jnp.where(is_text, own_rows, partner_rows)
+    image_rows = jnp.where(is_text, partner_rows, own_rows)
+    joined_rows = mix * text_rows + (1.0 - mix) * image_rows
+    gate_grad = jnp.sum(cot_joined * (text_rows - image_rows), axis=0, keepdims=True) * mix * (1.0 - mix)
+
+    slot_index = lax.iota(jnp.int32, 5)[:, None]
+    small = (
+        jnp.where(slot_index == stream, dgain_one[0:1], 0.0)
+        + jnp.where(slot_index == 1 - stream, dgain_one[1:2], 0.0)
+        + jnp.where(slot_index == 2 + stream, dgain_two[0:1], 0.0)
+        + jnp.where(slot_index == 4, gate_grad, 0.0)
+    )
+    for step in core + along_x + along_y + along_z + [across]:
+        small = after(small, *sums_a.last)
+        small = small + flip(small, *step)
+        for sums_of in (sums_a, sums_b, sums_c):
+            if sums_of.left():
+                sums_of.send()
+    gains_grad = small
     grad_rows = pl.pallas_call(
         functools.partial(tail_kernel, length),
         out_shape=full_rows,
@@ -656,18 +825,9 @@
         out_specs=VMEM,
         compiler_params=params(32),
         name="norm_tail",
-    )(rows, gain_own, own_part, back_part, middle_grad)
-
-    own_rows = lax.dynamic_slice_in_dim(stream_out, stream * half_rows, half_rows, 0)
-    partner_rows = partner_rows.astype(FULL)
-    text_rows = jnp.where(is_text, own_rows, partner_rows)
-    image_rows = jnp.where(is_text, partner_rows, own_rows)
-    joined_rows = mix * text_rows + (1.0 - mix) * image_rows
-    gate_grad = jnp.sum(cot_joined * (text_rows - image_rows), axis=0, keepdims=True) * mix * (1.0 - mix)
-
-    total_b = reduce_pieces(keep_b, send_b, order_b)
-    total_c = reduce_pieces(keep_c, send_c, order_c)
-    total_a = reduce_pieces(keep_a, send_a, order_a)
+    )(rows, gain_own, own_part, back_part, after(middle_grad, *sums_a.last))
+
+    total_a, total_b, total_c = sums_a.total(), sums_b.total(), sums_c.total()
 
     def both(total):
         mine = total[0]
@@ -694,15 +854,6 @@
         jnp.where(query_here, mine_a, theirs_a), jnp.where(query_here, theirs_a, mine_a)
     )
 
-    slot_index = lax.iota(jnp.int32, 5)[:, None]
-    small_terms = (
-        jnp.where(slot_index == stream, dgain_one[0:1], 0.0)
-        + jnp.where(slot_index == 1 - stream, dgain_one[1:2], 0.0)
-        + jnp.where(slot_index == 2 + stream, dgain_two[0:1], 0.0)
-        + jnp.where(slot_index == 4, gate_grad, 0.0)
-    )
-    gains_grad = small_sum(small_terms, core + along_x + along_y + along_z + [across])
-
     qkv_new = adam_update(w_qkv, m_qkv, v_qkv, grad_qkv, 0.12, 0.01)
     out_new = adam_update(w_out, m_out, v_out, grad_out, 0.5, 0.01)
     up_new = adam_update(w_up, m_up, v_up, grad_up, 0.12, 0.01)

time: 463 us -> 371 us (0.80); the launches traced: 463 us -> 366 us
  waiting for transfers between devices: 272 us -> 115 us
  starting transfers between devices: 43.9 us -> 67.4 us
  local copies, waits for them, and re-layouts: 7.46 us -> 25.3 us
  Pallas kernels: 104 us -> 120 us
    ppermute x39 -> x65, waiting for transfers between devices: 272 us -> 115 us  [flip(): return lax.ppermute(value, axis, [(i, i ^ mask) for i in range(count)])]
    ppermute x39 -> x65, starting transfers between devices: 43.9 us -> 67.4 us  [flip(): return lax.ppermute(value, axis, [(i, i ^ mask) for i in range(count)])]
    unnamed x100 -> x194, local copies, waits for them, and re-layouts: 4.55 us -> 21.5 us
    pallas_call x1 -> x4, Pallas kernels: 27 us -> 38.4 us  [the longest x2 16.7 us: attend_back(): pl.pallas_call(functools.partial(scores_back_kernel, (length, width, fact...]
  transfers between devices with their start and end apart: 39 -> 65, of which waited for: 21 -> 29; matrix products, arithmetic and copies ran while one was open for 7% -> 11% of each run, Pallas kernels for 6% -> 16%
where the time goes in v2:
time: 371 us; the launch traced here: 366 us
  Pallas kernels  120 us (32%)
  waiting for transfers between devices  115 us (31%)
  starting transfers between devices  67.4 us (18%)
  other arithmetic  36.3 us (10%)
  local copies, waits for them, and re-layouts  25.3 us (7%)
    ppermute x65, waiting for transfers between devices, flip(): return lax.ppermute(value, axis, [(i, i ^ mask) for i in range(count)])  115 us
    ppermute x65, starting transfers between devices, flip(): return lax.ppermute(value, axis, [(i, i ^ mask) for i in range(count)])  67.4 us
    pallas_call x1, Pallas kernels, shards(): pl.pallas_call(functools.partial(feed_kernel, shape), out_shape=(full_row...  49 us
    pallas_call x1, Pallas kernels, shards(): pl.pallas_call(functools.partial(project_kernel, shape), out_shape=(low_r...  30.1 us
    unnamed x194, local copies, waits for them, and re-layouts  21.5 us
    pallas_call x2, Pallas kernels, attend_back(): pl.pallas_call(functools.partial(scores_back_kernel, (length, width, fact...  16.7 us
    convert_element_type x9, other arithmetic, split_sums(): outgoing = sum((part[half:].astype(FULL) for part in parts)).astype(LOW)  12.1 us
    pallas_call x1, Pallas kernels, shards(): pl.pallas_call(functools.partial(branch_kernel, shape), out_shape=(full_r...  11.2 us
  transfers between devices with their start and end apart: 65, of which 29 were waited for; matrix products, arithmetic and copies ran while one was open for 11% of the time, Pallas kernels for 16%

profile of v2, /device:TPU:0, one launch (start us, length us, event | category | flops | bytes accessed | tf_op | source)
XLA Modules:
  0.0 365.8 jit_solution(12952376921440986738)
XLA Ops:
  0.7 1.6 slice.441
  2.3 4.0 %collective-permute-start = (bf16[64,768]{1,0:T(8,128)(2,1)}, bf16[64,768]{1,0:T(8,128)(2,1)}, u32[]{:S(2)}, u32[]{:S(2)}) collective-permute-start(bf16[64,768]{1,0:T(8,128)(2,1)} %slice.441), channel_id=1, source_target_pairs={{0,4},{1,5},{2,6},{3,7},{4,0},{5,1},{6,2},{7,3},{8,12},{9,13},{10,... | collective-permute-start | bytes 294920 | tf_op jit(solution)/shard_map/ppermute | solution.py:22
  8.5 1.6 collective-permute-start.3
  11.1 2.0 collective-permute-start.15
  13.2 2.7 collective-permute-start.20
  15.8 2.8 collective-permute-start.31
  19.9 5.8 %collective-permute-done.26.refs_13_ = bf16[1,192,384]{2,1,0:T(8,128)(2,1)S(1)} collective-permute-done((bf16[1,192,384]{2,1,0:T(8,128)(2,1)S(1)}, bf16[1,192,384]{2,1,0:T(8,128)(2,1)S(1)}, u32[]{:S(2)}, u32[]{:S(2)}) %collective-permute-start.26) | collective-permute-done | bytes 147488 | tf_op jit(solution)/shard_map/ppermute | solution.py:22
  26.3 11.3 %collective-permute-done.31 = bf16[192,384]{1,0:T(8,128)(2,1)S(1)} collective-permute-done((bf16[192,384]{1,0:T(8,128)(2,1)S(1)}, bf16[192,384]{1,0:T(8,128)(2,1)S(1)}, u32[]{:S(2)}, u32[]{:S(2)}) %collective-permute-start.31) | collective-permute-done | bytes 147488 | tf_op jit(solution)/shard_map/ppermute | solution.py:22
  37.5 1.6 collective-permute-start.4
  44.6 1.6 collective-permute-start.10
  46.4 2.6 collective-permute-start.2
  50.4 1.8 collective-permute-start.22
  54.9 4.5 %collective-permute-done.33.refs_20_ = bf16[2,192,384]{2,1,0:T(8,128)(2,1)} collective-permute-done((bf16[2,192,384]{2,1,0:T(8,128)(2,1)S(1)}, bf16[2,192,384]{2,1,0:T(8,128)(2,1)}, u32[]{:S(2)}, u32[]{:S(2)}) %collective-permute-start.33) | collective-permute-done | bytes 294944 | tf_op jit(solution)/shard_map/ppermute | solution.py:22
  62.5 1.7 collective-permute-start.17
  64.2 4.6 %collective-permute-done.2 = bf16[320,768]{1,0:T(8,128)(2,1)S(1)} collective-permute-done((bf16[320,768]{1,0:T(8,128)(2,1)S(1)}, bf16[320,768]{1,0:T(8,128)(2,1)S(1)}, u32[]{:S(2)}, u32[]{:S(2)}) %collective-permute-start.2) | collective-permute-done | bytes 491552 | tf_op jit(solution)/shard_map/ppermute | solution.py:22
  69.8 3.3 collective-permute-done.5.refs_3_
  76.4 2.0 pad_maximum_fusion.3
  78.4 11.2 %collective-permute-done.28.refs_15_ = bf16[4,192,384]{2,1,0:T(8,128)(2,1)} collective-permute-done((bf16[4,192,384]{2,1,0:T(8,128)(2,1)}, bf16[4,192,384]{2,1,0:T(8,128)(2,1)}, u32[]{:S(2)}, u32[]{:S(2)}) %collective-permute-start.28) | collective-permute-done | bytes 589856 | tf_op jit(solution)/shard_map/ppermute | solution.py:22
  90.1 1.7 collective-permute-start.34
  93.3 1.9 convert_element_type.385
  96.0 6.6 %collective-permute-done.23.refs_9_ = bf16[4,96,1024]{2,1,0:T(8,128)(2,1)} collective-permute-done((bf16[4,96,1024]{2,1,0:T(8,128)(2,1)}, bf16[4,96,1024]{2,1,0:T(8,128)(2,1)}, u32[]{:S(2)}, u32[]{:S(2)}) %collective-permute-start.23) | collective-permute-done | bytes 786464 | tf_op jit(solution)/shard_map/ppermute | solution.py:22
  102.7 2.8 collective-permute-start.14
  115.7 30.1 %project_attend.1 = (bf16[512,768]{1,0:T(8,128)(2,1)S(1)}, bf16[512,768]{1,0:T(8,128)(2,1)S(1)}, bf16[512,768]{1,0:T(8,128)(2,1)}, bf16[512,768]{1,0:T(8,128)(2,...) custom-call(s32[3]{0:T(128)S(1)} %pad_add_fusion.pos, bf16[512,768]{1,0:T(8,128)(2,1)} %own.7, ...), custom_call_target="tpu_custom_call" | custom-call | flops 1000 | bytes 1000 | tf_op jit(solution)/shard_map/project_attend/pallas_call | solution.py:664
  149.0 3.1 collective-permute-done.30.refs_17_
  154.3 49.0 %feed_forward_back.1 = (f32[512,768]{1,0:T(8,128)}, f32[512,768]{1,0:T(8,128)}, f32[512,128]{1,0:T(8,128)}, f32[512,768]{1,0:T(8,128)}, f32[512,768]{1,0:T(8,128...) custom-call(s32[3]{0:T(128)} %copy-done.45, ...), custom_call_target="tpu_custom_call" | custom-call | flops 1000 | bytes 1000 | tf_op jit(solution)/shard_map/feed_forward_back/pallas_call | solution.py:693
  205.6 11.2 %branch_back.1 = (f32[512,768]{1,0:T(8,128)}, bf16[256,768]{1,0:T(8,128)(2,1)S(1)}, f32[512,768]{1,0:T(8,128)S(1)}, bf16[512,768]{1,0:T(8,128)(2,1)S(1)}, f32[8,...) custom-call(s32[3]{0:T(128)S(1)} %copy-done.46, bf16[512,768]{1,0:T(8,128)(2,1)S(1)} %copy-done.2, ...), custom_call_target="tpu_custom_call" | custom-call | flops 1000 | bytes 1000 | tf_op jit(solution)/shard_map/branch_back/pallas_call | solution.py:718
  220.2 8.5 %collective-permute-done.37 = bf16[16,192,384]{2,1,0:T(8,128)(2,1)S(1)} collective-permute-done((bf16[16,192,384]{2,1,0:T(8,128)(2,1)S(1)}, bf16[16,192,384]{2,1,0:T(8,128)(2,1)S(1)}, u32[]{:S(2)}, u32[]{:S(2)}) %collective-permute-start.37) | collective-permute-done | bytes 2359328 | tf_op jit(solution)/shard_map/ppermute | solution.py:22
  236.9 8.4 %attend_back.2 = (bf16[512,384]{1,0:T(8,128)(2,1)S(1)}, bf16[512,384]{1,0:T(8,128)(2,1)S(1)}, bf16[512,384]{1,0:T(8,128)(2,1)S(1)}) custom-call(s32[512,1]{1,0:T(8,128)S(1)} %copy-done.4, s32[1,512]{1,0:T(1,128)S(1)} %bitcast.50, s32[512,1]{1,0:T(8,128)S(1)} %copy-done.12, bf16[512,768]{1,0:T(8,128)(2,1)S(1)} %get-tuple-element.108.q_ref, ...), custom_call_target="tpu_custom_call" | custom-call | flops 1000 | bytes 1000 | tf_op jit(solution)/shard_map/attend_back/pallas_call | solution.py:737
  245.4 3.6 add_convert_fusion
  250.7 1.8 add_convert_fusion.8
  253.3 1.7 collective-permute-start.44
  256.8 8.4 %attend_back.3 = (bf16[512,384]{1,0:T(8,128)(2,1)S(1)}, bf16[512,384]{1,0:T(8,128)(2,1)S(1)}, bf16[512,384]{1,0:T(8,128)(2,1)S(1)}) custom-call(s32[512,1]{1,0:T(8,128)S(1)} %copy-done.4, s32[1,512]{1,0:T(1,128)S(1)} %bitcast.51, s32[512,1]{1,0:T(8,128)S(1)} %copy-done.13, bf16[512,768]{1,0:T(8,128)(2,1)S(1)} %get-tuple-element.108.q_ref, ...), custom_call_target="tpu_custom_call" | custom-call | flops 1000 | bytes 1000 | tf_op jit(solution)/shard_map/attend_back/pallas_call | solution.py:737
  265.2 10.4 %project_back.1 = (f32[512,768]{1,0:T(8,128)S(1)}, bf16[512,768]{1,0:T(8,128)(2,1)S(1)}, f32[8,768]{1,0:T(8,128)S(1)}, bf16[16,96,640]{2,1,0:T(8,128)(2,1)S(1)}, bf16[16,96,640]{2,1,0:T(8,128)(2,1)S(1)}) custom-call(s32[3]{0:T(128)S(1)} %copy-done.46, bf16[512,768]{1,0:T(8,128)(2,1)S(1)} %copy-done.1, bf16[512,768]{1,0:T(8,128)(2,1)S(1)} %copy-done.6, ...), custom_call_target="tpu_custom_call" | custom-call | flops 1000 | bytes 1000 | tf_op jit(solution)/shard_map/project_back/pallas_call | solution.py:776
  275.7 2.2 multiply_add_fusion
  281.6 1.8 add_convert_fusion.7
  285.8 17.3 %collective-permute-done.58 = bf16[2,192,384]{2,1,0:T(8,128)(2,1)S(1)} collective-permute-done((bf16[2,192,384]{2,1,0:T(8,128)(2,1)S(1)}, bf16[2,192,384]{2,1,0:T(8,128)(2,1)S(1)}, u32[]{:S(2)}, u32[]{:S(2)}) %collective-permute-start.58) | collective-permute-done | bytes 294944 | tf_op jit(solution)/shard_map/ppermute | solution.py:22
  304.6 2.3 collective-permute-start.59
  308.8 13.0 %collective-permute-done.59 = bf16[192,384]{1,0:T(8,128)(2,1)S(1)} collective-permute-done((bf16[192,384]{1,0:T(8,128)(2,1)S(1)}, bf16[192,384]{1,0:T(8,128)(2,1)S(1)}, u32[]{:S(2)}, u32[]{:S(2)}) %collective-permute-start.59) | collective-permute-done | bytes 147488 | tf_op jit(solution)/shard_map/ppermute | solution.py:22
  325.1 2.5 collective-permute-done.56
  330.5 4.8 %collective-permute-done.48 = bf16[4,96,640]{2,1,0:T(8,128)(2,1)S(1)} collective-permute-done((bf16[4,96,640]{2,1,0:T(8,128)(2,1)S(1)}, bf16[4,96,640]{2,1,0:T(8,128)(2,1)S(1)}, u32[]{:S(2)}, u32[]{:S(2)}) %collective-permute-start.48) | collective-permute-done | bytes 491552 | tf_op jit(solution)/shard_map/ppermute | solution.py:22
  337.5 2.3 collective-permute-done.57
  340.3 3.4 collective-permute-done.61
  344.1 2.6 collective-permute-start.62
  348.6 1.7 collective-permute-done.52
  352.4 1.7 collective-permute-done.63
  354.1 2.3 collective-permute-start.64
  357.3 2.3 norm_tail.1
  360.5 3.2 collective-permute-done.53
  (356 shorter events, 84.3 us)
Async XLA Ops:
  2.3 10.9 %collective-permute-start = (bf16[64,768]{1,0:T(8,128)(2,1)}, bf16[64,768]{1,0:T(8,128)(2,1)}, u32[]{:S(2)}, u32[]{:S(2)}) collective-permute-start(bf16[64,768]{1,0:T(8,128)(2,1)} %slice.441), channel_id=1, source_target_pairs={{0,4},{1,5},{2,6},{3,7},{4,0},{5,1},{6,2},{7,3},{8,12},{9,13},{10,... | collective-permute-start | bytes 294920 | tf_op jit(solution)/shard_map/ppermute | solution.py:22
  10.1 8.5 %collective-permute-start.8 = (bf16[96,640]{1,0:T(8,128)(2,1)S(1)}, bf16[96,640]{1,0:T(8,128)(2,1)S(1)}, u32[]{:S(2)}, u32[]{:S(2)}) collective-permute-start(bf16[96,640]{1,0:T(8,128)(2,1)S(1)} %get-tuple-element.186), channel_id=1, source_target_pairs={{0,4},{1,5},{2,6},{3,7},{4,0},{5,1},{6,2},{7,3},{8,12},{9,13},{10,... | collective-permute-start | bytes 368648 | tf_op jit(solution)/shard_map/ppermute | solution.py:22
  10.6 15.1 %collective-permute-start.26 = (bf16[1,192,384]{2,1,0:T(8,128)(2,1)S(1)}, bf16[1,192,384]{2,1,0:T(8,128)(2,1)S(1)}, u32[]{:S(2)}, u32[]{:S(2)}) collective-permute-start(bf16[1,192,384]{2,1,0:T(8,128)(2,1)S(1)} %get-tuple-element.185.refs_12_), channel_id=1, source_target_pairs={{0,2},{1,3},{2,0},{3,1},{4,6},{5,7},{6,4},{7,5},{8,10},{9,11},{10,... | collective-permute-start | bytes 442376 | tf_op jit(solution)/shard_map/ppermute | solution.py:22
  11.1 28.0 %collective-permute-start.15 = (bf16[1,96,1024]{2,1,0:T(8,128)(2,1)S(1)}, bf16[1,96,1024]{2,1,0:T(8,128)(2,1)S(1)}, u32[]{:S(2)}, u32[]{:S(2)}) collective-permute-start(bf16[1,96,1024]{2,1,0:T(8,128)(2,1)S(1)} %get-tuple-element.183.refs_0_), channel_id=1, source_target_pairs={{0,2},{1,3},{2,0},{3,1},{4,6},{5,7},{6,4},{7,5},{8,10},{9,11},{10,... | collective-permute-start | bytes 589832 | tf_op jit(solution)/shard_map/ppermute | solution.py:22
  13.2 26.9 %collective-permute-start.20 = (bf16[96,1024]{1,0:T(8,128)(2,1)S(1)}, bf16[96,1024]{1,0:T(8,128)(2,1)S(1)}, u32[]{:S(2)}, u32[]{:S(2)}) collective-permute-start(bf16[96,1024]{1,0:T(8,128)(2,1)S(1)} %get-tuple-element.182), channel_id=1, source_target_pairs={{0,4},{1,5},{2,6},{3,7},{4,0},{5,1},{6,2},{7,3},{8,12},{9,13},{10,... | collective-permute-start | bytes 589832 | tf_op jit(solution)/shard_map/ppermute | solution.py:22
  15.8 21.7 %collective-permute-start.31 = (bf16[192,384]{1,0:T(8,128)(2,1)S(1)}, bf16[192,384]{1,0:T(8,128)(2,1)S(1)}, u32[]{:S(2)}, u32[]{:S(2)}) collective-permute-start(bf16[192,384]{1,0:T(8,128)(2,1)S(1)} %get-tuple-element.184), channel_id=1, source_target_pairs={{0,4},{1,5},{2,6},{3,7},{4,0},{5,1},{6,2},{7,3},{8,12},{9,13},{10,... | collective-permute-start | bytes 442376 | tf_op jit(solution)/shard_map/ppermute | solution.py:22
  18.7 23.6 %collective-permute-start.1 = (bf16[128,768]{1,0:T(8,128)(2,1)S(1)}, bf16[128,768]{1,0:T(8,128)(2,1)S(1)}, u32[]{:S(2)}, u32[]{:S(2)}) collective-permute-start(bf16[128,768]{1,0:T(8,128)(2,1)S(1)} %slice.442), channel_id=1, source_target_pairs={{0,4},{1,5},{2,6},{3,7},{4,0},{5,1},{6,2},{7,3},{8,12},{9,13},{10,... | collective-permute-start | bytes 589832 | tf_op jit(solution)/shard_map/ppermute | solution.py:22
  25.7 16.0 %collective-permute-start.9 = (bf16[1,96,640]{2,1,0:T(8,128)(2,1)S(1)}, bf16[1,96,640]{2,1,0:T(8,128)(2,1)S(1)}, u32[]{:S(2)}, u32[]{:S(2)}) collective-permute-start(bf16[1,96,640]{2,1,0:T(8,128)(2,1)S(1)} %bitcast.44), channel_id=1, source_target_pairs={{0,2},{1,3},{2,0},{3,1},{4,6},{5,7},{6,4},{7,5},{8,10},{9,11},{10,... | collective-permute-start | bytes 368648 | tf_op jit(solution)/shard_map/ppermute | solution.py:22
  37.5 8.9 %collective-permute-start.4 = (bf16[2,96,640]{2,1,0:T(8,128)(2,1)S(1)}, bf16[2,96,640]{2,1,0:T(8,128)(2,1)S(1)}, u32[]{:S(2)}, u32[]{:S(2)}) collective-permute-start(bf16[2,96,640]{2,1,0:T(8,128)(2,1)S(1)} %pad_maximum_fusion.12), channel_id=1, source_target_pairs={{0,8},{8,0},{16,24},{24,16},{1,9},{9,1},{17,25},{25,17},{2,10},{10... | collective-permute-start | bytes 737288 | tf_op jit(solution)/shard_map/ppermute | solution.py:22
  40.1 10.2 %collective-permute-start.27 = (bf16[2,192,384]{2,1,0:T(8,128)(2,1)S(1)}, bf16[2,192,384]{2,1,0:T(8,128)(2,1)S(1)}, u32[]{:S(2)}, u32[]{:S(2)}) collective-permute-start(bf16[2,192,384]{2,1,0:T(8,128)(2,1)S(1)} %pad_maximum_fusion.9), channel_id=1, source_target_pairs={{0,16},{8,24},{16,0},{24,8},{1,17},{9,25},{17,1},{25,9},{2,18},{10... | collective-permute-start | bytes 884744 | tf_op jit(solution)/shard_map/ppermute | solution.py:22
  41.7 13.1 %collective-permute-start.16 = (bf16[2,96,1024]{2,1,0:T(8,128)(2,1)S(1)}, bf16[2,96,1024]{2,1,0:T(8,128)(2,1)S(1)}, u32[]{:S(2)}, u32[]{:S(2)}) collective-permute-start(bf16[2,96,1024]{2,1,0:T(8,128)(2,1)S(1)} %pad_maximum_fusion.6), channel_id=1, source_target_pairs={{0,8},{8,0},{16,24},{24,16},{1,9},{9,1},{17,25},{25,17},{2,10},{10... | collective-permute-start | bytes 1179656 | tf_op jit(solution)/shard_map/ppermute | solution.py:22
  44.6 8.5 %collective-permute-start.10 = (bf16[2,96,640]{2,1,0:T(8,128)(2,1)S(1)}, bf16[2,96,640]{2,1,0:T(8,128)(2,1)S(1)}, u32[]{:S(2)}, u32[]{:S(2)}) collective-permute-start(bf16[2,96,640]{2,1,0:T(8,128)(2,1)S(1)} %pad_maximum_fusion.13), channel_id=1, source_target_pairs={{0,16},{8,24},{16,0},{24,8},{1,17},{9,25},{17,1},{25,9},{2,18},{10... | collective-permute-start | bytes 737288 | tf_op jit(solution)/shard_map/ppermute | solution.py:22
  46.4 22.3 %collective-permute-start.2 = (bf16[320,768]{1,0:T(8,128)(2,1)S(1)}, bf16[320,768]{1,0:T(8,128)(2,1)S(1)}, u32[]{:S(2)}, u32[]{:S(2)}) collective-permute-start(bf16[320,768]{1,0:T(8,128)(2,1)S(1)} %slice.443), channel_id=1, source_target_pairs={{0,4},{1,5},{2,6},{3,7},{4,0},{5,1},{6,2},{7,3},{8,12},{9,13},{10,... | collective-permute-start | bytes 1474568 | tf_op jit(solution)/shard_map/ppermute | solution.py:22
  49.3 10.1 %collective-permute-start.33 = (bf16[2,192,384]{2,1,0:T(8,128)(2,1)S(1)}, bf16[2,192,384]{2,1,0:T(8,128)(2,1)}, u32[]{:S(2)}, u32[]{:S(2)}) collective-permute-start(bf16[2,192,384]{2,1,0:T(8,128)(2,1)S(1)} %pad_maximum_fusion.10), channel_id=1, source_target_pairs={{0,8},{8,0},{16,24},{24,16},{1,9},{9,1},{17,25},{25,17},{2,10},{10... | collective-permute-start | bytes 884744 | tf_op jit(solution)/shard_map/ppermute | solution.py:22
  50.4 12.1 %collective-permute-start.22 = (bf16[2,96,1024]{2,1,0:T(8,128)(2,1)S(1)}, bf16[2,96,1024]{2,1,0:T(8,128)(2,1)S(1)}, u32[]{:S(2)}, u32[]{:S(2)}) collective-permute-start(bf16[2,96,1024]{2,1,0:T(8,128)(2,1)S(1)} %pad_maximum_fusion.7), channel_id=1, source_target_pairs={{0,16},{8,24},{16,0},{24,8},{1,17},{9,25},{17,1},{25,9},{2,18},{10... | collective-permute-start | bytes 1179656 | tf_op jit(solution)/shard_map/ppermute | solution.py:22
  53.1 19.9 %collective-permute-start.5 = (bf16[4,96,640]{2,1,0:T(8,128)(2,1)S(1)}, bf16[4,96,640]{2,1,0:T(8,128)(2,1)S(1)}, u32[]{:S(2)}, u32[]{:S(2)}) collective-permute-start(bf16[4,96,640]{2,1,0:T(8,128)(2,1)S(1)} %pad_maximum_fusion.4), channel_id=1, source_target_pairs={{0,16},{8,24},{16,0},{24,8},{1,17},{9,25},{17,1},{25,9},{2,18},{10... | collective-permute-start | bytes 1474568 | tf_op jit(solution)/shard_map/ppermute | solution.py:22
  54.9 19.2 %collective-permute-start.6 = (bf16[4,96,640]{2,1,0:T(8,128)(2,1)S(1)}, bf16[4,96,640]{2,1,0:T(8,128)(2,1)S(1)}, u32[]{:S(2)}, u32[]{:S(2)}) collective-permute-start(bf16[4,96,640]{2,1,0:T(8,128)(2,1)S(1)} %pad_maximum_fusion.4), channel_id=1, source_target_pairs={{0,1},{1,0},{2,3},{3,2},{4,5},{5,4},{6,7},{7,6},{8,9},{9,8},{10,11... | collective-permute-start | bytes 1474568 | tf_op jit(solution)/shard_map/ppermute | solution.py:22
  59.4 15.7 %collective-permute-start.11 = (bf16[4,96,640]{2,1,0:T(8,128)(2,1)S(1)}, bf16[4,96,640]{2,1,0:T(8,128)(2,1)S(1)}, u32[]{:S(2)}, u32[]{:S(2)}) collective-permute-start(bf16[4,96,640]{2,1,0:T(8,128)(2,1)S(1)} %pad_maximum_fusion.5), channel_id=1, source_target_pairs={{0,8},{8,0},{16,24},{24,16},{1,9},{9,1},{17,25},{25,17},{2,10},{10... | collective-permute-start | bytes 1474568 | tf_op jit(solution)/shard_map/ppermute | solution.py:22
  62.5 27.6 %collective-permute-start.17 = (bf16[4,96,1024]{2,1,0:T(8,128)(2,1)}, bf16[4,96,1024]{2,1,0:T(8,128)(2,1)}, u32[]{:S(2)}, u32[]{:S(2)}) collective-permute-start(bf16[4,96,1024]{2,1,0:T(8,128)(2,1)} %pad_maximum_fusion), channel_id=1, source_target_pairs={{0,16},{8,24},{16,0},{24,8},{1,17},{9,25},{17,1},{25,9},{2,18},{10... | collective-permute-start | bytes 2359304 | tf_op jit(solution)/shard_map/ppermute | solution.py:22
  73.0 16.6 %collective-permute-start.28 = (bf16[4,192,384]{2,1,0:T(8,128)(2,1)}, bf16[4,192,384]{2,1,0:T(8,128)(2,1)}, u32[]{:S(2)}, u32[]{:S(2)}) collective-permute-start(bf16[4,192,384]{2,1,0:T(8,128)(2,1)} %pad_maximum_fusion.2), channel_id=1, source_target_pairs={{0,8},{8,0},{16,24},{24,16},{1,9},{9,1},{17,25},{25,17},{2,10},{10... | collective-permute-start | bytes 1769480 | tf_op jit(solution)/shard_map/ppermute | solution.py:22
  74.1 15.5 %collective-permute-start.7 = (bf16[4,96,640]{2,1,0:T(8,128)(2,1)S(1)}, bf16[4,96,640]{2,1,0:T(8,128)(2,1)}, u32[]{:S(2)}, u32[]{:S(2)}) collective-permute-start(bf16[4,96,640]{2,1,0:T(8,128)(2,1)S(1)} %collective-permute-done.5.refs_3_), channel_id=1, source_target_pairs={{0,1},{1,0},{2,3},{3,2},{4,5},{5,4},{6,7},{7,6},{8,9},{9,8},{10,11... | collective-permute-start | bytes 1474568 | tf_op jit(solution)/shard_map/ppermute | solution.py:22
  75.1 27.5 %collective-permute-start.23 = (bf16[4,96,1024]{2,1,0:T(8,128)(2,1)}, bf16[4,96,1024]{2,1,0:T(8,128)(2,1)}, u32[]{:S(2)}, u32[]{:S(2)}) collective-permute-start(bf16[4,96,1024]{2,1,0:T(8,128)(2,1)} %pad_maximum_fusion.1), channel_id=1, source_target_pairs={{0,8},{8,0},{16,24},{24,16},{1,9},{9,1},{17,25},{25,17},{2,10},{10... | collective-permute-start | bytes 2359304 | tf_op jit(solution)/shard_map/ppermute | solution.py:22
  76.2 19.0 %collective-permute-start.13 = (bf16[4,96,640]{2,1,0:T(8,128)(2,1)S(1)}, bf16[4,96,640]{2,1,0:T(8,128)(2,1)S(1)}, u32[]{:S(2)}, u32[]{:S(2)}) collective-permute-start(bf16[4,96,640]{2,1,0:T(8,128)(2,1)S(1)} %collective-permute-done.11.refs_9_), channel_id=1, source_target_pairs={{0,1},{1,0},{2,3},{3,2},{4,5},{5,4},{6,7},{7,6},{8,9},{9,8},{10,11... | collective-permute-start | bytes 1474568 | tf_op jit(solution)/shard_map/ppermute | solution.py:22
  89.6 56.9 %collective-permute-start.29 = (bf16[4,192,384]{2,1,0:T(8,128)(2,1)}, bf16[4,192,384]{2,1,0:T(8,128)(2,1)}, u32[]{:S(2)}, u32[]{:S(2)}) collective-permute-start(bf16[4,192,384]{2,1,0:T(8,128)(2,1)} %pad_maximum_fusion.2), channel_id=1, source_target_pairs={{0,1},{1,0},{2,3},{3,2},{4,5},{5,4},{6,7},{7,6},{8,9},{9,8},{10,11... | collective-permute-start | bytes 1769480 | tf_op jit(solution)/shard_map/ppermute | solution.py:22
  89.6 58.0 %collective-permute-start.18 = (bf16[4,96,1024]{2,1,0:T(8,128)(2,1)}, bf16[4,96,1024]{2,1,0:T(8,128)(2,1)}, u32[]{:S(2)}, u32[]{:S(2)}) collective-permute-start(bf16[4,96,1024]{2,1,0:T(8,128)(2,1)} %pad_maximum_fusion), channel_id=1, source_target_pairs={{0,1},{1,0},{2,3},{3,2},{4,5},{5,4},{6,7},{7,6},{8,9},{9,8},{10,11... | collective-permute-start | bytes 2359304 | tf_op jit(solution)/shard_map/ppermute | solution.py:22
  90.1 56.9 %collective-permute-start.34 = (bf16[4,192,384]{2,1,0:T(8,128)(2,1)}, bf16[4,192,384]{2,1,0:T(8,128)(2,1)}, u32[]{:S(2)}, u32[]{:S(2)}) collective-permute-start(bf16[4,192,384]{2,1,0:T(8,128)(2,1)} %pad_maximum_fusion.3), channel_id=1, source_target_pairs={{0,16},{8,24},{16,0},{24,8},{1,17},{9,25},{17,1},{25,9},{2,18},{10... | collective-permute-start | bytes 1769480 | tf_op jit(solution)/shard_map/ppermute | solution.py:22
  96.0 51.1 %collective-permute-start.35 = (bf16[4,192,384]{2,1,0:T(8,128)(2,1)}, bf16[4,192,384]{2,1,0:T(8,128)(2,1)}, u32[]{:S(2)}, u32[]{:S(2)}) collective-permute-start(bf16[4,192,384]{2,1,0:T(8,128)(2,1)} %pad_maximum_fusion.3), channel_id=1, source_target_pairs={{0,1},{1,0},{2,3},{3,2},{4,5},{5,4},{6,7},{7,6},{8,9},{9,8},{10,11... | collective-permute-start | bytes 1769480 | tf_op jit(solution)/shard_map/ppermute | solution.py:22
  102.7 43.9 %collective-permute-start.14 = (bf16[256,768]{1,0:T(8,128)(2,1)}, bf16[256,768]{1,0:T(8,128)(2,1)}, u32[]{:S(2)}, u32[]{:S(2)}) collective-permute-start(bf16[256,768]{1,0:T(8,128)(2,1)} %convert_element_type.385), channel_id=1, source_target_pairs={{0,4},{1,5},{2,6},{3,7},{4,0},{5,1},{6,2},{7,3},{8,12},{9,13},{10,... | collective-permute-start | bytes 1179656 | tf_op jit(solution)/shard_map/ppermute | solution.py:22
  219.6 25.7 %collective-permute-start.41 = (bf16[16,96,1024]{2,1,0:T(8,128)(2,1)}, bf16[16,96,1024]{2,1,0:T(8,128)(2,1)}, u32[]{:S(2)}, u32[]{:S(2)}) collective-permute-start(bf16[16,96,1024]{2,1,0:T(8,128)(2,1)} %get-tuple-element.107), channel_id=1, source_target_pairs={{0,1},{1,0},{2,3},{3,2},{4,5},{5,4},{6,7},{7,6},{8,9},{9,8},{10,11... | collective-permute-start | bytes 9437192 | tf_op jit(solution)/shard_map/ppermute | solution.py:22
  219.8 8.9 %collective-permute-start.37 = (bf16[16,192,384]{2,1,0:T(8,128)(2,1)S(1)}, bf16[16,192,384]{2,1,0:T(8,128)(2,1)S(1)}, u32[]{:S(2)}, u32[]{:S(2)}) collective-permute-start(bf16[16,192,384]{2,1,0:T(8,128)(2,1)S(1)} %copy-done.95), channel_id=1, source_target_pairs={{0,1},{1,0},{2,3},{3,2},{4,5},{5,4},{6,7},{7,6},{8,9},{9,8},{10,11... | collective-permute-start | bytes 7077896 | tf_op jit(solution)/shard_map/ppermute | solution.py:22
  230.4 18.6 %collective-permute-start.39 = (bf16[4,192,384]{2,1,0:T(8,128)(2,1)}, bf16[4,192,384]{2,1,0:T(8,128)(2,1)}, u32[]{:S(2)}, u32[]{:S(2)}) collective-permute-start(bf16[4,192,384]{2,1,0:T(8,128)(2,1)} %get-tuple-element.171), channel_id=1, source_target_pairs={{0,8},{8,0},{16,24},{24,16},{1,9},{9,1},{17,25},{25,17},{2,10},{10... | collective-permute-start | bytes 1769480 | tf_op jit(solution)/shard_map/ppermute | solution.py:22
  231.0 18.0 %collective-permute-start.40 = (bf16[4,192,384]{2,1,0:T(8,128)(2,1)}, bf16[4,192,384]{2,1,0:T(8,128)(2,1)}, u32[]{:S(2)}, u32[]{:S(2)}) collective-permute-start(bf16[4,192,384]{2,1,0:T(8,128)(2,1)} %get-tuple-element.170), channel_id=1, source_target_pairs={{0,16},{8,24},{16,0},{24,8},{1,17},{9,25},{17,1},{25,9},{2,18},{10... | collective-permute-start | bytes 1769480 | tf_op jit(solution)/shard_map/ppermute | solution.py:22
  232.3 22.7 %collective-permute-start.38 = (bf16[256,768]{1,0:T(8,128)(2,1)}, bf16[256,768]{1,0:T(8,128)(2,1)}, u32[]{:S(2)}, u32[]{:S(2)}) collective-permute-start(bf16[256,768]{1,0:T(8,128)(2,1)} %copy-done.48), channel_id=1, source_target_pairs={{0,4},{1,5},{2,6},{3,7},{4,0},{5,1},{6,2},{7,3},{8,12},{9,13},{10,... | collective-permute-start | bytes 1179656 | tf_op jit(solution)/shard_map/ppermute | solution.py:22
  249.0 26.6 %collective-permute-start.45 = (bf16[4,96,1024]{2,1,0:T(8,128)(2,1)}, bf16[4,96,1024]{2,1,0:T(8,128)(2,1)}, u32[]{:S(2)}, u32[]{:S(2)}) collective-permute-start(bf16[4,96,1024]{2,1,0:T(8,128)(2,1)} %get-tuple-element.120), channel_id=1, source_target_pairs={{0,8},{8,0},{16,24},{24,16},{1,9},{9,1},{17,25},{25,17},{2,10},{10... | collective-permute-start | bytes 2359304 | tf_op jit(solution)/shard_map/ppermute | solution.py:22
  249.4 26.3 %collective-permute-start.46 = (bf16[4,96,1024]{2,1,0:T(8,128)(2,1)}, bf16[4,96,1024]{2,1,0:T(8,128)(2,1)}, u32[]{:S(2)}, u32[]{:S(2)}) collective-permute-start(bf16[4,96,1024]{2,1,0:T(8,128)(2,1)} %get-tuple-element.121), channel_id=1, source_target_pairs={{0,16},{8,24},{16,0},{24,8},{1,17},{9,25},{17,1},{25,9},{2,18},{10... | collective-permute-start | bytes 2359304 | tf_op jit(solution)/shard_map/ppermute | solution.py:22
  252.5 23.1 %collective-permute-start.43 = (bf16[2,192,384]{2,1,0:T(8,128)(2,1)S(1)}, bf16[2,192,384]{2,1,0:T(8,128)(2,1)S(1)}, u32[]{:S(2)}, u32[]{:S(2)}) collective-permute-start(bf16[2,192,384]{2,1,0:T(8,128)(2,1)S(1)} %get-tuple-element.117), channel_id=1, source_target_pairs={{0,16},{8,24},{16,0},{24,8},{1,17},{9,25},{17,1},{25,9},{2,18},{10... | collective-permute-start | bytes 884744 | tf_op jit(solution)/shard_map/ppermute | solution.py:22
  253.3 22.3 %collective-permute-start.44 = (bf16[2,192,384]{2,1,0:T(8,128)(2,1)S(1)}, bf16[2,192,384]{2,1,0:T(8,128)(2,1)S(1)}, u32[]{:S(2)}, u32[]{:S(2)}) collective-permute-start(bf16[2,192,384]{2,1,0:T(8,128)(2,1)S(1)} %get-tuple-element.118), channel_id=1, source_target_pairs={{0,8},{8,0},{16,24},{24,16},{1,9},{9,1},{17,25},{25,17},{2,10},{10... | collective-permute-start | bytes 884744 | tf_op jit(solution)/shard_map/ppermute | solution.py:22
  275.6 46.1 %collective-permute-start.47 = (bf16[16,96,640]{2,1,0:T(8,128)(2,1)S(1)}, bf16[16,96,640]{2,1,0:T(8,128)(2,1)S(1)}, u32[]{:S(2)}, u32[]{:S(2)}) collective-permute-start(bf16[16,96,640]{2,1,0:T(8,128)(2,1)S(1)} %get-tuple-element.122), channel_id=1, source_target_pairs={{0,1},{1,0},{2,3},{3,2},{4,5},{5,4},{6,7},{7,6},{8,9},{9,8},{10,11... | collective-permute-start | bytes 5898248 | tf_op jit(solution)/shard_map/ppermute | solution.py:22
  277.9 79.3 %collective-permute-start.42 = (bf16[512,768]{1,0:T(8,128)(2,1)S(1)}, bf16[512,768]{1,0:T(8,128)(2,1)S(1)}, u32[]{:S(2)}, u32[]{:S(2)}) collective-permute-start(bf16[512,768]{1,0:T(8,128)(2,1)S(1)} %get-tuple-element.113), channel_id=1, source_target_pairs={{0,4},{1,5},{2,6},{3,7},{4,0},{5,1},{6,2},{7,3},{8,12},{9,13},{10,... | collective-permute-start | bytes 2359304 | tf_op jit(solution)/shard_map/ppermute | solution.py:22
  280.8 22.3 %collective-permute-start.58 = (bf16[2,192,384]{2,1,0:T(8,128)(2,1)S(1)}, bf16[2,192,384]{2,1,0:T(8,128)(2,1)S(1)}, u32[]{:S(2)}, u32[]{:S(2)}) collective-permute-start(bf16[2,192,384]{2,1,0:T(8,128)(2,1)S(1)} %pad_maximum_fusion.11), channel_id=1, source_target_pairs={{0,2},{1,3},{2,0},{3,1},{4,6},{5,7},{6,4},{7,5},{8,10},{9,11},{10,... | collective-permute-start | bytes 884744 | tf_op jit(solution)/shard_map/ppermute | solution.py:22
  283.4 23.5 %collective-permute-start.54 = (bf16[2,96,1024]{2,1,0:T(8,128)(2,1)S(1)}, bf16[2,96,1024]{2,1,0:T(8,128)(2,1)S(1)}, u32[]{:S(2)}, u32[]{:S(2)}) collective-permute-start(bf16[2,96,1024]{2,1,0:T(8,128)(2,1)S(1)} %get-tuple-element.124), channel_id=1, source_target_pairs={{0,16},{8,24},{16,0},{24,8},{1,17},{9,25},{17,1},{25,9},{2,18},{10... | collective-permute-start | bytes 1179656 | tf_op jit(solution)/shard_map/ppermute | solution.py:22
  284.3 22.6 %collective-permute-start.55 = (bf16[2,96,1024]{2,1,0:T(8,128)(2,1)S(1)}, bf16[2,96,1024]{2,1,0:T(8,128)(2,1)S(1)}, u32[]{:S(2)}, u32[]{:S(2)}) collective-permute-start(bf16[2,96,1024]{2,1,0:T(8,128)(2,1)S(1)} %get-tuple-element.125), channel_id=1, source_target_pairs={{0,8},{8,0},{16,24},{24,16},{1,9},{9,1},{17,25},{25,17},{2,10},{10... | collective-permute-start | bytes 1179656 | tf_op jit(solution)/shard_map/ppermute | solution.py:22
  304.6 17.2 %collective-permute-start.59 = (bf16[192,384]{1,0:T(8,128)(2,1)S(1)}, bf16[192,384]{1,0:T(8,128)(2,1)S(1)}, u32[]{:S(2)}, u32[]{:S(2)}) collective-permute-start(bf16[192,384]{1,0:T(8,128)(2,1)S(1)} %get-tuple-element.164), channel_id=1, source_target_pairs={{0,4},{1,5},{2,6},{3,7},{4,0},{5,1},{6,2},{7,3},{8,12},{9,13},{10,... | collective-permute-start | bytes 442376 | tf_op jit(solution)/shard_map/ppermute | solution.py:22
  308.5 19.2 %collective-permute-start.56 = (bf16[2,96,1024]{2,1,0:T(8,128)(2,1)S(1)}, bf16[2,96,1024]{2,1,0:T(8,128)(2,1)S(1)}, u32[]{:S(2)}, u32[]{:S(2)}) collective-permute-start(bf16[2,96,1024]{2,1,0:T(8,128)(2,1)S(1)} %pad_maximum_fusion.8), channel_id=1, source_target_pairs={{0,2},{1,3},{2,0},{3,1},{4,6},{5,7},{6,4},{7,5},{8,10},{9,11},{10,... | collective-permute-start | bytes 1179656 | tf_op jit(solution)/shard_map/ppermute | solution.py:22
  322.0 13.2 %collective-permute-start.48 = (bf16[4,96,640]{2,1,0:T(8,128)(2,1)S(1)}, bf16[4,96,640]{2,1,0:T(8,128)(2,1)S(1)}, u32[]{:S(2)}, u32[]{:S(2)}) collective-permute-start(bf16[4,96,640]{2,1,0:T(8,128)(2,1)S(1)} %get-tuple-element.178), channel_id=1, source_target_pairs={{0,8},{8,0},{16,24},{24,16},{1,9},{9,1},{17,25},{25,17},{2,10},{10... | collective-permute-start | bytes 1474568 | tf_op jit(solution)/shard_map/ppermute | solution.py:22
  322.9 12.6 %collective-permute-start.50 = (bf16[4,96,640]{2,1,0:T(8,128)(2,1)S(1)}, bf16[4,96,640]{2,1,0:T(8,128)(2,1)S(1)}, u32[]{:S(2)}, u32[]{:S(2)}) collective-permute-start(bf16[4,96,640]{2,1,0:T(8,128)(2,1)S(1)} %get-tuple-element.179), channel_id=1, source_target_pairs={{0,16},{8,24},{16,0},{24,8},{1,17},{9,25},{17,1},{25,9},{2,18},{10... | collective-permute-start | bytes 1474568 | tf_op jit(solution)/shard_map/ppermute | solution.py:22
  329.2 10.6 %collective-permute-start.57 = (bf16[96,1024]{1,0:T(8,128)(2,1)S(1)}, bf16[96,1024]{1,0:T(8,128)(2,1)S(1)}, u32[]{:S(2)}, u32[]{:S(2)}) collective-permute-start(bf16[96,1024]{1,0:T(8,128)(2,1)S(1)} %get-tuple-element.157), channel_id=1, source_target_pairs={{0,4},{1,5},{2,6},{3,7},{4,0},{5,1},{6,2},{7,3},{8,12},{9,13},{10,... | collective-permute-start | bytes 589832 | tf_op jit(solution)/shard_map/ppermute | solution.py:22
  330.5 9.4 %collective-permute-start.60 = (f32[5,768]{1,0:T(8,128)S(1)}, f32[5,768]{1,0:T(8,128)S(1)}, u32[]{:S(2)}, u32[]{:S(2)}) collective-permute-start(f32[5,768]{1,0:T(8,128)S(1)} %select_add_fusion), channel_id=1, source_target_pairs={{0,1},{1,0},{2,3},{3,2},{4,5},{5,4},{6,7},{7,6},{8,9},{9,8},{10,11... | collective-permute-start | bytes 46088 | tf_op jit(solution)/shard_map/ppermute | solution.py:22
  (113 other events, 1377.0 us)

commit v3 on v2

v3 whole, which is shorter than its diff:
```python
import functools

import jax
import jax.numpy as jnp
from jax import lax
from jax.experimental import pallas as pl
from jax.experimental.pallas import tpu as pltpu
from jax.sharding import PartitionSpec as P

HEADS = 12
STEP = 10
LANES = 128
CHUNK = 128
ROW_PARTS = (5, 6, 5)
BACK_PARTS = (4, 5, 4, 3)
FIRST_A = False
NEG = -1000000000.0
LOW = jnp.bfloat16
FULL = jnp.float32


def flip(value, axis, mask):
    count = lax.axis_size(axis)
    return lax.ppermute(value, axis, [(i, i ^ mask) for i in range(count)])


def flipped(codes, axis, mask):
    d_mask = mask if axis == "docs" else 0
    w_mask = mask if axis == "wide" else 0
    return [(d ^ d_mask, w ^ w_mask) for d, w in codes]


def after(value, *others):
    return lax.optimization_barrier((value, *others))[0]


class Doubling:
    def __init__(self, unit, slot, order):
        self.slot, self.order, self.step = slot, order, 0
        self.arrays, self.codes = [unit[None]], [[(0, 0)]]
        self.last = ()

    def held(self):
        held = self.arrays[0] if len(self.arrays) == 1 else jnp.concatenate(self.arrays, axis=0)
        return held, [code for group in self.codes for code in group]

    def send(self, *others):
        held, known = self.held()
        if others:
            held = after(held, *others)
        axis, mask = self.order[self.step]
        self.arrays.append(flip(held, axis, mask))
        self.codes.append(flipped(known, axis, mask))
        self.step, self.last = self.step + 1, (self.arrays[-1],)

    def send_all(self):
        while self.step < len(self.order):
            self.send()

    def split_newest(self):
        newest, newest_known = self.arrays.pop(), self.codes.pop()
        held, known = self.held()
        self.arrays.append(newest)
        self.codes.append(newest_known)
        return (held, known), (newest, newest_known)

    def add(self, value, known, axis, mask):
        self.arrays.append(flip(value, axis, mask))
        self.codes.append(flipped(known, axis, mask))
        return self.arrays[-1]

    def slotted(self):
        return [(self.slot, group) for group in self.codes]


def sum_codes(order):
    codes = [(0, 0)]
    for axis, mask in reversed(order):
        codes = codes + flipped(codes, axis, mask)
    return codes


class Halving:
    def __init__(self, kept, sent, steps):
        self.slots, self.sent, self.steps = split(kept), sent, steps
        self.step, self.last = 0, ()
        self.slots = [[half] for half in self.slots]
        self.outgoing = [None, None]

    def left(self):
        return self.step < len(self.steps)

    def hold(self, *others):
        if self.step == 0:
            self.sent = after(self.sent, *others)
        elif self.left():
            self.outgoing = [after(value, *others) for value in self.outgoing]

    def send(self):
        one, two = self.steps[self.step]
        if one == two:
            whole = self.sent if self.step == 0 else jnp.concatenate(self.outgoing, axis=0)
            arrived = flip(whole, *one)
            self.last = (arrived,)
            arrived = split(arrived)
        else:
            arrived = [flip(self.outgoing[0], *one), flip(self.outgoing[1], *two)]
            self.last = tuple(arrived)
        self.slots = [parts + [new] for parts, new in zip(self.slots, arrived)]
        self.step += 1
        if self.left():
            for slot, parts in enumerate(self.slots):
                half = parts[0].shape[0] // 2
                self.outgoing[slot] = sum(part[half:].astype(FULL) for part in parts).astype(LOW)
                self.slots[slot] = [part[:half] for part in parts]

    def total(self):
        while self.left():
            self.send()
        return tuple(sum(part[0].astype(FULL) for part in parts) for parts in self.slots)


def split(value):
    middle = value.shape[0] // 2
    return [value[:middle], value[middle:]]


class Blocks:
    def __init__(self, count, size):
        self.count, self.size = count, size
        shifts = [(i * size) % LANES for i in range(count)]
        self.shifts = sorted(set(shifts))
        self.wide = -(-(size + max(shifts)) // LANES) * LANES
        self.aligned = max(shifts) == 0 and size % LANES == 0
        self.total = count * size
        self.room = max(self.start(i) + self.wide for i in range(count))

    def start(self, index):
        return index * self.size // LANES * LANES

    def start_dynamic(self, index):
        return pl.multiple_of(index * self.size // LANES * LANES, LANES)

    def pad(self, value, index):
        result = None
        for shift in self.shifts:
            low = [(0, 0)] * (value.ndim - 1) + [(shift, self.wide - self.size - shift)]
            placed = jnp.pad(value, low)
            here = (index * self.size) % LANES == shift
            result = placed if result is None else jnp.where(here, placed, result)
        return result

    def cut(self, value, index):
        result = None
        for shift in self.shifts:
            piece = value[..., shift : shift + self.size]
            here = (index * self.size) % LANES == shift
            result = piece if result is None else jnp.where(here, piece, result)
        return result

    def tile_owners(self, tile):
        low, high = tile * LANES, (tile + 1) * LANES
        return [
            (i, low - self.start(i))
            for i in range(self.count)
            if i * self.size < high and (i + 1) * self.size > low
        ]


def matmul(left, right):
    return lax.dot_general(left, right, (((1,), (0,)), ((), ())), preferred_element_type=FULL)


def matmul_nt(left, right):
    return lax.dot_general(left, right, (((1,), (1,)), ((), ())), preferred_element_type=FULL)


def matmul_tn(left, right):
    return lax.dot_general(left, right, (((0,), (0,)), ((), ())), preferred_element_type=FULL)


def normed(values):
    centred = values - jnp.mean(values, axis=-1, keepdims=True)
    spread = jnp.mean(centred * centred, axis=-1, keepdims=True)
    scale = lax.rsqrt(spread + 1e-05)
    return centred * scale, scale


def norm_back(grad, unit, scale, gain):
    inner = grad * gain
    mean_inner = jnp.mean(inner, axis=-1, keepdims=True)
    mean_both = jnp.mean(inner * unit, axis=-1, keepdims=True)
    return scale * (inner - mean_inner - unit * mean_both)


def rows_at(index, size=CHUNK):
    return pl.ds(pl.multiple_of(index * size, size), size)


def places(pos, slot, codes, half):
    owner = pos[2] if slot == 0 else 1 - pos[2]
    for index, (d_mask, w_mask) in enumerate(codes):
        yield index, pos[0] ^ d_mask, owner * half + (pos[1] ^ w_mask)


def load_pieces(pos, refs, codes, half, lanes, target, sem):
    for ref, (slot, group) in zip(refs, codes):
        for index, doc, inner in places(pos, slot, group, half):
            pltpu.make_async_copy(
                ref.at[index, :, pl.ds(lanes[0], lanes[1])], target(doc, inner), sem
            ).start()


def load_folded(pos, refs, codes, half, rows, blocks, begin, folds, held, sem):
    for fold in range(folds):
        def target(doc, inner):
            first = pl.ds(pl.multiple_of((doc * folds + fold) * rows, rows), rows)
            if blocks.aligned:
                return held.at[first, pl.ds(blocks.start_dynamic(inner), blocks.wide)]
            return held.at[inner, first, :]

        load_pieces(pos, refs, codes, half, (begin + fold * blocks.wide, blocks.wide), target, sem)


def begin(source, target, sem):
    pltpu.make_async_copy(source, target, sem).start()


def finish(source, target, sem):
    pltpu.make_async_copy(source, target, sem).wait()


def store_pieces(pos, source, sums, half, targets, lanes, sem):
    for slot, codes in enumerate(sums):
        count = len(codes) // 2
        for index, doc, inner in places(pos, slot, codes, half):
            pltpu.make_async_copy(
                source(doc, inner),
                targets[index // count].at[slot * count + index % count, :, pl.ds(lanes[0], lanes[1])],
                sem,
            ).start()


def wait_whole(ref, sem):
    pltpu.make_async_copy(ref, ref, sem).wait()


def row_target(ref, blocks, rows):
    if blocks.aligned:
        return lambda doc, inner: ref.at[
            pl.ds(pl.multiple_of(inner * rows, rows), rows),
            pl.ds(blocks.start_dynamic(doc), blocks.wide),
        ]
    return lambda doc, inner: ref.at[doc, pl.ds(pl.multiple_of(inner * rows, rows), rows), :]


def held_shape(blocks, height):
    return (height, blocks.total) if blocks.aligned else (blocks.count, height, blocks.wide)


def merge_tiles(held, whole, blocks):
    for tile in range(blocks.total // LANES):
        value = None
        for index, offset in blocks.tile_owners(tile):
            piece = held[index, :, offset : offset + LANES]
            value = piece if value is None else value + piece
        whole[:, tile * LANES : (tile + 1) * LANES] = value


def project_kernel(shape, pos, gains, page_col, page_row, mask_row, own_hbm, *refs):
    codes, half, rows, blocks, length, width, factor, chunks = shape
    arrived, refs = refs[: len(chunks)], refs[len(chunks) :]
    pieces, refs = refs[: len(codes)], refs[len(codes) :]
    outs, refs = refs[:7], refs[7:]
    (q_out, k_out, v_out, att_out, lse_out, weight, other) = kept = refs[:7]
    (own, held, h_own, h_oth, allowed, sem, sem_out, sem_in) = refs[7:]
    begin(own_hbm, own, sem_in.at[0])
    load_pieces(pos, pieces, codes, half, (0, blocks.wide), row_target(held, blocks, rows), sem)
    starts = [sum(chunks[:i]) for i in range(len(chunks))]
    places_in = [other.at[pl.ds(start, size), :] for start, size in zip(starts, chunks)]
    for i, (ref, place) in enumerate(zip(arrived, places_in)):
        begin(ref, place, sem_in.at[i + 1])
    finish(own_hbm, own, sem_in.at[0])
    for i, (ref, place) in enumerate(zip(arrived, places_in)):
        finish(ref, place, sem_in.at[i + 1])
    begin(other, outs[6], sem_out.at[6])
    for i in range(length // CHUNK):
        part = pl.ds(i * CHUNK, CHUNK)
        unit, _ = normed(own[part, :].astype(FULL))
        h_own[part, :] = (unit * gains[0:1, :]).astype(LOW)
        unit, _ = normed(other[part, :].astype(FULL))
        h_oth[part, :] = (unit * gains[1:2, :]).astype(LOW)
        row = lax.broadcasted_iota(jnp.int32, (CHUNK, length), 0) + i * CHUNK
        col = lax.broadcasted_iota(jnp.int32, (CHUNK, length), 1)
        ok = (page_col[part, :] == page_row[...]) & ((mask_row[...] == 1) | (row == col))
        allowed[part, :] = jnp.where(ok, 1.0, 0.0)
    wait_whole(held, sem)
    merge_tiles(held, weight, blocks)
    begin(weight, outs[5], sem_out.at[5])
    lse_out[...] = jnp.zeros_like(lse_out)

    q_out[...] = (matmul(h_own[...], weight[:, :width]).astype(LOW) * factor).astype(LOW)
    k_out[...] = matmul(h_oth[...], weight[:, width : 2 * width]).astype(LOW)
    v_out[...] = matmul(h_oth[...], weight[:, 2 * width :]).astype(LOW)
    for i in range(3):
        begin(kept[i], outs[i], sem_out.at[i])
    size = width // HEADS
    per = LANES // size

    @pl.loop(0, width // LANES)
    def _(pair):
        cols = pl.ds(pl.multiple_of(pair * LANES, LANES), LANES)
        keys, values, queries = k_out[:, cols], v_out[:, cols], q_out[:, cols]
        lane = lax.broadcasted_iota(jnp.int32, queries.shape, 1)
        result, sums = None, lse_out[...]
        for sub in range(per):
            inside = lane // size == sub
            scores = matmul_nt(jnp.where(inside, queries, jnp.zeros_like(queries)), keys)
            scores = jnp.where(allowed[...] > 0.5, scores, NEG)
            top = jnp.max(scores, axis=-1, keepdims=True)
            exps = jnp.exp(scores - top)
            total = jnp.sum(exps, axis=-1, keepdims=True)
            out = matmul(exps.astype(LOW), values) * (1.0 / total)
            result = out if result is None else jnp.where(inside, out, result)
            sums = jnp.where(lane == pair * per + sub, top + jnp.log(total), sums)
        lse_out[...] = sums
        att_out[:, cols] = result.astype(LOW)

    for i in (3, 4):
        begin(kept[i], outs[i], sem_out.at[i])
    for i, ref in enumerate(kept):
        finish(ref, outs[i], sem_out.at[i])


def feed_kernel(shape, pos, coef, gain, page_col, att_hbm, own_hbm, cot_hbm, cotj_hbm, arrived_hbm, *refs):
    (codes, counts, sums_b, sums_c, half, rows, down_rows, ups, outs, downs, length, width, hidden, block) = shape
    pieces, refs = refs[: len(codes)], refs[len(codes) :]
    out_ref, dmid_ref, datt_ref, away_ref, dgain_ref = refs[:5]
    up_targets, down_targets = refs[5:7], refs[7:9]
    (w_up, o_held, w_out, d_held, w_down, g_up, g_out, g_down, att, own, cot, cotj_own, cotj_oth, mid, h2, h2_t, dffn, dffn_t,
     att_t, acts, dpre, acc, dacc, dbranch, sem_up, sem_out, sem_down, sem_gup, sem_gdown, sems) = refs[9:]
    begin(att_hbm, att, sems.at[0])
    last = counts
    load_pieces(pos, pieces[:last], codes[:last], half, (ups.wide, outs.wide), row_target(o_held, outs, rows), sem_out)
    begin(own_hbm, own, sems.at[1])
    begin(cot_hbm, cot, sems.at[2])
    begin(cotj_hbm, cotj_own, sems.at[3])
    begin(arrived_hbm, cotj_oth, sems.at[4])
    load_pieces(pos, pieces[:last], codes[:last], half, (0, ups.wide), row_target(w_up, ups, rows), sem_up)
    folds = down_rows // rows
    load_folded(pos, pieces[last:], codes[last:], half, rows, downs, 0, folds, d_held, sem_down)
    half_rows = length // 2
    parts = length // CHUNK

    def valid_at(part):
        return jnp.where(page_col[part, :] >= 0, 1.0, 0.0)

    finish(att_hbm, att, sems.at[0])
    wait_whole(o_held, sem_out)
    merge_tiles(o_held, w_out, outs)
    mid[...] = matmul(att[...], w_out[...])
    att_t[...] = att[...].T
    finish(own_hbm, own, sems.at[1])
    for i in range(parts):
        part = pl.ds(i * CHUNK, CHUNK)
        middle = own[part, :].astype(FULL) + valid_at(part) * mid[part, :]
        mid[part, :] = middle
        unit, _ = normed(middle)
        h2[part, :] = (unit * gain[...]).astype(LOW)
    finish(cot_hbm, cot, sems.at[2])
    finish(cotj_hbm, cotj_own, sems.at[3])
    finish(arrived_hbm, cotj_oth, sems.at[4])
    for which, ref in ((pos[2], cotj_own), (1 - pos[2], cotj_oth)):
        for i in range(half_rows // CHUNK):
            part = pl.ds(pl.multiple_of(which * half_rows + i * CHUNK, CHUNK), CHUNK)
            grad = cot[part, :] + coef[...] * ref[pl.ds(i * CHUNK, CHUNK), :].astype(FULL)
            cot[part, :] = grad
            dffn[part, :] = (grad * valid_at(part)).astype(LOW)
    dffn_t[...] = dffn[...].T
    h2_t[...] = h2[...].T
    acc[...] = jnp.zeros_like(acc)
    dacc[...] = jnp.zeros_like(dacc)
    wait_whole(w_up, sem_up)
    wait_whole(d_held, sem_down)
    if not downs.aligned:
        merge_tiles(d_held, w_down, downs)
    down = d_held if downs.aligned else w_down
    c0, c1 = 0.7978845608028654, 0.044715

    @pl.loop(0, hidden // block)
    def _(f):
        cols = pl.ds(pl.multiple_of(f * block, LANES), block)
        pre = matmul(h2[...], w_up[:, cols])
        dact = matmul(dffn[...], down[:, cols])
        square = pre * pre
        flat = jnp.tanh(c0 * (pre + c1 * square * pre))
        cdf = 0.5 * (1.0 + flat)
        slope = cdf + pre * (0.5 * (1.0 - flat * flat)) * (c0 * (1.0 + 3.0 * c1 * square))
        acts[...] = (pre * cdf).astype(LOW)
        dpre[...] = (slope * dact).astype(LOW)
        acc[...] += matmul_nt(acts[...], down[:, cols])
        dacc[...] += matmul_nt(dpre[...], w_up[:, cols])
        g_down[:, cols] = matmul(dffn_t[...], acts[...]).astype(LOW)
        g_up[:, cols] = matmul(h2_t[...], dpre[...]).astype(LOW)

    if downs.room > downs.total:
        g_down[:, downs.total :] = jnp.zeros((width, downs.room - downs.total), LOW)
    store_pieces(
        pos,
        lambda doc, inner: g_down.at[
            pl.ds(pl.multiple_of(doc * down_rows, down_rows), down_rows),
            pl.ds(downs.start_dynamic(inner), downs.wide),
        ],
        sums_c, half, down_targets, (0, downs.wide), sem_gdown,
    )
    store_pieces(
        pos,
        lambda doc, inner: g_up.at[
            pl.ds(pl.multiple_of(inner * rows, rows), rows),
            pl.ds(ups.start_dynamic(doc), ups.wide),
        ],
        sums_b, half, up_targets, (0, ups.wide), sem_gup,
    )
    dgain_ref[...] = jnp.zeros_like(dgain_ref)
    for i in range(parts):
        part = pl.ds(i * CHUNK, CHUNK)
        valid = valid_at(part)
        middle = mid[part, :]
        acc[part, :] = middle + valid * acc[part, :]
        unit, scale = normed(middle)
        grad = dacc[part, :]
        dgain_ref[0:1, :] += jnp.sum(grad * unit, axis=0, keepdims=True)
        dmid = cot[part, :] + norm_back(grad, unit, scale, gain[...])
        dacc[part, :] = dmid
        dbranch[part, :] = (dmid * valid).astype(LOW)
    begin(acc, out_ref, sems.at[0])
    begin(dacc, dmid_ref, sems.at[1])
    h2[...] = matmul_nt(dbranch[...], w_out[...]).astype(LOW)
    begin(h2, datt_ref, sems.at[2])
    g_out[:, : outs.total] = matmul(att_t[...], dbranch[...]).astype(LOW)
    if outs.room > outs.total:
        g_out[:, outs.total :] = jnp.zeros((width, outs.room - outs.total), LOW)
    store_pieces(
        pos,
        lambda doc, inner: g_out.at[
            pl.ds(pl.multiple_of(inner * rows, rows), rows),
            pl.ds(outs.start_dynamic(doc), outs.wide),
        ],
        sums_b, half, up_targets, (ups.wide, outs.wide), sem_gup,
    )
    for i in range(half_rows // CHUNK):
        part = pl.ds(pl.multiple_of((1 - pos[2]) * half_rows + i * CHUNK, CHUNK), CHUNK)
        away_ref[pl.ds(i * CHUNK, CHUNK), :] = acc[part, :].astype(LOW)
    for target in down_targets:
        wait_whole(target, sem_gdown)
    for target in up_targets:
        wait_whole(target, sem_gup)
    finish(acc, out_ref, sems.at[0])
    finish(dacc, dmid_ref, sems.at[1])
    finish(h2, datt_ref, sems.at[2])


def scores_back_kernel(shape, pairs, page_col, page_row, mask_row, q_hbm, k_hbm, v_hbm, att_hbm, datt_hbm, lse_hbm, *refs):
    length, width, factor = shape
    outs, refs = refs[:3], refs[3:]
    (q_ref, k_ref, v_ref, att, datt, lse, dq, dk, dv, allowed, lse_t, dots_t, sems) = refs
    size = width // HEADS
    per = LANES // size
    cols_here = pl.ds(pairs[0] * LANES, (pairs[1] - pairs[0]) * LANES)
    loads = [(source.at[:, cols_here], target) for source, target in
             ((datt_hbm, datt), (att_hbm, att), (q_hbm, q_ref), (k_hbm, k_ref), (v_hbm, v_ref))]
    loads.append((lse_hbm, lse))
    for i, (source, target) in enumerate(loads):
        begin(source, target, sems.at[i])
    mask = jnp.broadcast_to(mask_row[...].astype(FULL), (LANES, length)).T[:, 0:1]
    row = lax.broadcasted_iota(jnp.int32, (length, length), 0)
    col = lax.broadcasted_iota(jnp.int32, (length, length), 1)
    ok = (page_col[...] == page_row[...]) & ((mask == 1.0) | (row == col))
    allowed[...] = jnp.where(ok, 1.0, 0.0)
    here_width = cols_here.size
    head = lax.broadcasted_iota(jnp.int32, (LANES, here_width), 0)
    lane = lax.broadcasted_iota(jnp.int32, (LANES, here_width), 1)
    chosen = jnp.where(lane // size == head, 1.0, 0.0)
    for i, (source, target) in enumerate(loads):
        finish(source, target, sems.at[i])
    dots_t[...] = lax.dot_general(
        chosen, att[...].astype(FULL) * datt[...].astype(FULL), (((1,), (1,)), ((), ())),
        preferred_element_type=FULL, precision=lax.Precision.HIGHEST,
    )
    lse_t[...] = lse[...].T

    @pl.loop(0, pairs[1] - pairs[0])
    def _(pair):
        cols = pl.ds(pl.multiple_of(pair * LANES, LANES), LANES)
        queries, grads = q_ref[:, cols], datt[:, cols]
        keys, values = k_ref[:, cols], v_ref[:, cols]
        lane = lax.broadcasted_iota(jnp.int32, (length, LANES), 1)
        zero = jnp.zeros_like(queries)
        trio = None
        for sub in range(per):
            inside = lane // size == sub
            lse_row = lse_t[pl.ds((pair + pairs[0]) * per + sub, 1), :]
            dot_row = dots_t[pl.ds(pair * per + sub, 1), :]
            scores = matmul_nt(keys, jnp.where(inside, queries, zero))
            scores = jnp.where(allowed[...] > 0.5, scores, NEG)
            probs = jnp.exp(scores - lse_row)
            dprob = matmul_nt(values, jnp.where(inside, grads, zero))
            low = (probs * (dprob - dot_row)).astype(LOW)
            three = (matmul_tn(low, keys), matmul(low, queries), matmul(probs.astype(LOW), grads))
            trio = three if trio is None else [jnp.where(inside, new, old) for new, old in zip(three, trio)]
        dq[:, cols] = (trio[0] * factor).astype(LOW)
        dk[:, cols] = trio[1].astype(LOW)
        dv[:, cols] = trio[2].astype(LOW)

    for i, (source, target) in enumerate(zip((dq, dk, dv), outs)):
        begin(source, target, sems.at[i])
    for i, (source, target) in enumerate(zip((dq, dk, dv), outs)):
        finish(source, target, sems.at[i])


def project_back_kernel(shape, pos, gains, own_hbm, other_hbm, weight_hbm, *refs):
    (sums, half, rows, blocks, length, width, runs) = shape
    given, refs = refs[: 3 * len(runs)], refs[3 * len(runs) :]
    own_out, oth_ref, dgain_ref = refs[:3]
    targets, refs = refs[3:5], refs[5:]
    h_t, flat, own_ref, grad, own, other, weight, sem, sems = refs[:9]
    copies = refs[9:]
    grads = [copies[3 * i : 3 * i + 3] for i in range(len(runs))]
    parts = length // CHUNK
    loads = [(own_hbm, own), (other_hbm, other), *zip(given, copies), (weight_hbm, weight)]
    for i, (source, target) in enumerate(loads):
        begin(source, target, sems.at[i])

    def take(i):
        finish(*loads[i], sems.at[i])

    for which, source in ((0, own), (1, other)):
        take(which)
        for i in range(parts):
            part = pl.ds(i * CHUNK, CHUNK)
            unit, _ = normed(source[part, :].astype(FULL))
            flat[part, :] = unit * gains[which : which + 1, :]
        h_t[which] = flat[...].astype(LOW).T
    for i in range(2, len(loads) - 1):
        take(i)
    for (low, high), trio in zip(runs, grads):
        for block, (which, ref) in enumerate(zip((0, 1, 1), trio)):
            grad[:, block * width + low : block * width + high] = matmul(h_t[which], ref[...]).astype(LOW)
    if blocks.room > blocks.total:
        grad[:, blocks.total :] = jnp.zeros((width, blocks.room - blocks.total), LOW)
    store_pieces(
        pos,
        lambda doc, inner: grad.at[
            pl.ds(pl.multiple_of(inner * rows, rows), rows),
            pl.ds(blocks.start_dynamic(doc), blocks.wide),
        ],
        sums, half, targets, (0, blocks.wide), sem,
    )
    dgain_ref[...] = jnp.zeros_like(dgain_ref)
    take(len(loads) - 1)
    own_ref[...] = sum(
        matmul_nt(trio[0][...], weight[:, low:high]) for (low, high), trio in zip(runs, grads)
    )
    begin(own_ref, own_out, sems.at[0])
    flat[...] = sum(
        matmul_nt(trio[block][...], weight[:, block * width + low : block * width + high])
        for (low, high), trio in zip(runs, grads)
        for block in (1, 2)
    )
    for i in range(parts):
        part = pl.ds(i * CHUNK, CHUNK)
        unit, _ = normed(own[part, :].astype(FULL))
        dgain_ref[0:1, :] += jnp.sum(own_ref[part, :] * unit, axis=0, keepdims=True)
        unit, _ = normed(other[part, :].astype(FULL))
        value = flat[part, :]
        oth_ref[part, :] = value.astype(LOW)
        dgain_ref[1:2, :] += jnp.sum(value * unit, axis=0, keepdims=True)
    finish(own_ref, own_out, sems.at[0])
    for target in targets:
        wait_whole(target, sem)


def tail_kernel(length, own, gain, mine, theirs, dmid, out_ref):
    for i in range(length // CHUNK):
        part = pl.ds(i * CHUNK, CHUNK)
        unit, scale = normed(own[part, :].astype(FULL))
        grad = mine[part, :] + theirs[part, :].astype(FULL)
        out_ref[part, :] = dmid[part, :] + norm_back(grad, unit, scale, gain[...])


VMEM = pl.BlockSpec(memory_space=pltpu.VMEM)
HBM = pl.BlockSpec(memory_space=pltpu.HBM)
SMEM = pl.BlockSpec(memory_space=pltpu.SMEM)


LITTLE = pl.CostEstimate(flops=1_000, bytes_accessed=1_000, transcendentals=0)


def params(mebibytes):
    return pltpu.CompilerParams(vmem_limit_bytes=mebibytes * 1024 * 1024)


def adam_update(weight, first, second, grad, rate, decay):
    first_new = 0.9 * first + 0.1 * grad
    second_new = 0.999 * second + 0.001 * grad * grad
    first_hat = first_new / (1.0 - 0.9**STEP)
    second_hat = second_new / (1.0 - 0.999**STEP)
    weight_new = weight - rate * (first_hat / (jnp.sqrt(second_hat) + 1e-08) + decay * weight)
    return (weight_new, first_new, second_new)


def shards(
    rows, cot_stream, cot_joined, page, key_mask,
    w_qkv, m_qkv, v_qkv, w_out, m_out, v_out, w_up, m_up, v_up, w_down, m_down, v_down,
    gains, m_gains, v_gains,
):
    docs, wide = lax.axis_size("docs"), lax.axis_size("wide")
    half = wide // 2
    doc, place = lax.axis_index("docs"), lax.axis_index("wide")
    stream = place // half
    is_text = stream == 0
    pos = jnp.stack((doc, place % half, stream)).astype(jnp.int32)
    length, width = rows.shape
    half_rows = length // 2
    factor = float(width // HEADS) ** (-0.5)
    piece_rows = w_qkv.shape[1]
    hidden = w_up.shape[2] * docs
    qkvs, outs, ups = Blocks(docs, w_qkv.shape[2]), Blocks(docs, w_out.shape[2]), Blocks(docs, w_up.shape[2])
    downs = Blocks(wide, w_down.shape[1])
    down_rows = w_down.shape[2]

    core = [("wide", 1)]
    along_x = [("docs", 1)]
    along_y = [("docs", 1 << b) for b in range(1, docs.bit_length() - 1)]
    along_z = [("wide", 1 << b) for b in range(1, half.bit_length() - 1)]
    across = ("wide", half)

    def swap(value):
        return flip(value, *across)

    column = doc * w_qkv.shape[2] + lax.iota(jnp.int32, w_qkv.shape[2])
    is_query = (column < width)[None, None, :]
    pair_qkv = jnp.where(is_query, w_qkv, w_qkv[::-1]).astype(LOW)

    def own_first(pair):
        return jnp.where(is_text, pair, pair[::-1])

    unit_a = qkvs.pad(own_first(pair_qkv), doc)
    unit_b = jnp.concatenate(
        (ups.pad(own_first(w_up.astype(LOW)), doc), outs.pad(own_first(w_out.astype(LOW)), doc)), axis=-1
    )
    unit_c = downs.pad(jnp.swapaxes(own_first(w_down.astype(LOW)), 1, 2), place)
    folds = down_rows // piece_rows

    def folded(unit):
        return jnp.concatenate([unit[i * piece_rows : (i + 1) * piece_rows] for i in range(folds)], axis=-1)

    unit_a_oth = swap(unit_a[1])
    unit_b_oth = swap(after(unit_b[1], unit_a_oth)) if FIRST_A else swap(unit_b[1])
    if downs.aligned:
        unit_c_oth = swap(after(unit_c[1], unit_a_oth))
    else:
        raw = jnp.swapaxes(own_first(w_down.astype(LOW)), 1, 2)
        unit_c_oth = downs.pad(swap(raw[1]), (place + half) % wide)
    zxy, zyx = along_z + along_x + along_y, along_z + along_y + along_x
    a_own, a_oth = Doubling(unit_a[0], 0, zxy), Doubling(unit_a_oth, 1, zyx)
    b_own = Doubling(unit_b[0], 0, along_y + along_x + along_z)
    c_own = Doubling(folded(unit_c[0]), 0, along_x + along_z + along_y)
    b_oth, c_oth = Doubling(unit_b_oth, 1, zxy), Doubling(folded(unit_c_oth), 1, zyx)
    steps_y, steps_x = len(along_y), len(along_x)
    chunks, begin = [], 0
    for size in [length * part // sum(ROW_PARTS) for part in ROW_PARTS]:
        some = rows[begin : begin + size]
        chunks.append(swap(after(some, chunks[-1] if chunks else unit_a_oth)))
        begin += size
    for _ in range(steps_y):
        b_own.send()
    for _ in range(steps_x):
        c_own.send()
    for _ in range(steps_x):
        b_own.send(unit_a_oth)
    for _ in along_z:
        c_own.send(unit_a_oth)
    a_own.send_all()
    a_oth.send_all()
    first = (a_oth.arrays[len(along_z) + steps_y], a_own.arrays[len(along_z) + steps_x])
    rest = (a_oth.arrays[-1], a_own.arrays[-1])
    for one in (b_oth, c_oth):
        for _ in along_z:
            one.send(*first)
    met = b_oth.last + c_oth.last
    for one in (b_own, c_own):
        while one.step < len(one.order):
            one.send(*met)
    for one, steps in ((b_oth, steps_x), (c_oth, steps_y)):
        for _ in range(steps):
            one.send(*rest, chunks[1])
    for one in (b_oth, c_oth):
        while one.step < len(one.order):
            one.send(chunks[-1])
    pieces_a, codes_a = [], []
    for one in (a_own, a_oth):
        for value, known in one.split_newest():
            one.add(value, known, *core[0])
        pieces_a += one.arrays
        codes_a += one.slotted()
    waiting, passed = [], []
    for one in (b_own, b_oth, c_own, c_oth):
        early, late = one.split_newest()
        passed.append(one.add(after(early[0], chunks[-1]), early[1], *core[0]))
        waiting.append((one, *late))
    other_joined = swap(after(cot_joined.astype(LOW), chunks[-1], *passed))

    page_col, page_row = page[:, None], page[None, :]
    mask_row = key_mask[None, :]
    gain_own = lax.dynamic_index_in_dim(gains, stream, 0, keepdims=True)
    gain_oth = lax.dynamic_index_in_dim(gains, 1 - stream, 0, keepdims=True)
    gain_one = jnp.concatenate((gain_own, gain_oth), axis=0)
    gain_two = lax.dynamic_index_in_dim(gains, 2 + stream, 0, keepdims=True)
    mix = jax.nn.sigmoid(gains[4])[None, :]
    coef = jnp.where(is_text, mix, 1.0 - mix)

    low_rows = jax.ShapeDtypeStruct((length, width), LOW)
    full_rows = jax.ShapeDtypeStruct((length, width), FULL)

    sizes = tuple(chunk.shape[0] for chunk in chunks)
    shape = (codes_a, half, piece_rows, qkvs, length, width, factor, sizes)
    made = (low_rows, low_rows, low_rows, low_rows, jax.ShapeDtypeStruct((length, LANES), FULL),
            jax.ShapeDtypeStruct((width, 3 * width), LOW), low_rows)
    queries, keys, values, attended, lse, weight_qkv, other_rows = pl.pallas_call(
        functools.partial(project_kernel, shape),
        out_shape=made,
        in_specs=[SMEM] + [VMEM] * 4 + [HBM] * (1 + len(chunks) + len(pieces_a)),
        out_specs=(HBM,) * 7,
        scratch_shapes=[pltpu.VMEM(one.shape, one.dtype) for one in made] + [
            pltpu.VMEM((length, width), LOW),
            pltpu.VMEM((docs, width, qkvs.wide), LOW),
            pltpu.VMEM((length, width), LOW),
            pltpu.VMEM((length, width), LOW),
            pltpu.VMEM((length, length), FULL),
            pltpu.SemaphoreType.DMA,
            pltpu.SemaphoreType.DMA((7,)),
            pltpu.SemaphoreType.DMA((1 + len(chunks),)),
        ],
        compiler_params=params(60),
        cost_estimate=LITTLE,
        name="project_attend",
    )(pos, gain_one, page_col, page_row, mask_row, rows, *chunks, *pieces_a)

    here = [value for _, value, _ in waiting]
    for one, value, known in waiting:
        one.add(after(value, lse, other_joined, *here), known, *core[0])
    streams = (b_own, b_oth, c_own, c_oth)
    pieces_b = sum((one.arrays for one in streams), [])
    codes_b = sum((one.slotted() for one in streams), [])
    counts = len(b_own.arrays) + len(b_oth.arrays)
    xy, yx = along_x + along_y, along_y + along_x
    steps_b = [core * 2, *zip(xy, yx), *((step, step) for step in along_z)]
    steps_c = [core * 2, *((step, step) for step in along_z + xy)]
    sums_of = [tuple(sum_codes([pair[slot] for pair in steps]) for slot in (0, 1)) for steps in (steps_b, steps_c)]
    sent_count = len(sums_of[0][0])
    block = 6 * LANES
    shape = (codes_b, counts, *sums_of, half, piece_rows, down_rows, ups, outs, downs, length, width, hidden, block)
    shape_b = jax.ShapeDtypeStruct((sent_count, piece_rows, ups.wide + outs.wide), LOW)
    shape_c = jax.ShapeDtypeStruct((sent_count, down_rows, downs.wide), LOW)
    (stream_out, middle_grad, attended_grad, away, dgain_two, kept_b, sent_b, kept_c, sent_c) = pl.pallas_call(
        functools.partial(feed_kernel, shape),
        out_shape=(full_rows, full_rows, low_rows, jax.ShapeDtypeStruct((half_rows, width), LOW),
                   jax.ShapeDtypeStruct((8, width), FULL), shape_b, shape_b, shape_c, shape_c),
        in_specs=[SMEM] + [VMEM] * 3 + [HBM] * (5 + len(pieces_b)),
        out_specs=(HBM,) * 3 + (VMEM,) * 2 + (HBM,) * 4,
        scratch_shapes=[
            pltpu.VMEM((width, hidden), LOW),
            pltpu.VMEM(held_shape(outs, width), LOW),
            pltpu.VMEM((width, width), LOW),
            pltpu.VMEM(held_shape(downs, width), LOW),
            pltpu.VMEM((8, LANES) if downs.aligned else (width, hidden), LOW),
            pltpu.VMEM((width, hidden), LOW),
            pltpu.VMEM((width, outs.room), LOW),
            pltpu.VMEM((width, downs.room), LOW),
            pltpu.VMEM((length, width), LOW),
            pltpu.VMEM((length, width), LOW),
            pltpu.VMEM((length, width), FULL),
            pltpu.VMEM((half_rows, width), FULL),
            pltpu.VMEM((half_rows, width), LOW),
            pltpu.VMEM((length, width), FULL),
            pltpu.VMEM((length, width), LOW),
            pltpu.VMEM((width, length), LOW),
            pltpu.VMEM((length, width), LOW),
            pltpu.VMEM((width, length), LOW),
            pltpu.VMEM((width, length), LOW),
            pltpu.VMEM((length, block), LOW),
            pltpu.VMEM((length, block), LOW),
            pltpu.VMEM((length, width), FULL),
            pltpu.VMEM((length, width), FULL),
            pltpu.VMEM((length, width), LOW),
        ] + [pltpu.SemaphoreType.DMA] * 5 + [pltpu.SemaphoreType.DMA((5,))],
        compiler_params=params(60),
        cost_estimate=LITTLE,
        name="feed_forward_back",
    )(pos, coef, gain_two, page_col, attended, rows, cot_stream, cot_joined, other_joined, *pieces_b)

    def attend_back(pairs, *operands):
        low_cols = jax.ShapeDtypeStruct((length, (pairs[1] - pairs[0]) * LANES), LOW)
        piece = pltpu.VMEM(low_cols.shape, LOW)
        return pl.pallas_call(
            functools.partial(scores_back_kernel, (length, width, factor), pairs),
            out_shape=(low_cols,) * 3,
            in_specs=[VMEM] * 3 + [HBM] * 6,
            out_specs=(HBM,) * 3,
            scratch_shapes=[piece] * 5 + [pltpu.VMEM((length, LANES), FULL)] + [piece] * 3 + [
                pltpu.VMEM((length, length), FULL),
                pltpu.VMEM((LANES, length), FULL),
                pltpu.VMEM((LANES, length), FULL),
                pltpu.SemaphoreType.DMA((6,)),
            ],
            compiler_params=params(60),
            cost_estimate=LITTLE,
            name="attend_back",
        )(page_col, page_row, mask_row, *operands)

    sums_b, sums_c = Halving(kept_b, sent_b, steps_b), Halving(kept_c, sent_c, steps_c)
    sums_b.send()
    sums_c.send()
    quarter = half_rows // 2
    partner_one = swap(away[:quarter])
    pair_count = width // LANES
    cuts = (0, pair_count * 2 // 3, pair_count)
    grads_one = attend_back(cuts[:2], queries, keys, values, attended, attended_grad, lse)
    met = (*sums_b.last, *sums_c.last, partner_one)
    second = after(queries, grads_one[0], *met)
    sums_b.hold(grads_one[0], *met)
    sums_c.hold(grads_one[0], *met)
    sums_b.send()
    sums_c.send()
    partner_two = swap(after(away[quarter:], grads_one[0], *met))
    partner_rows = jnp.concatenate((partner_one, partner_two), axis=0)
    grads_two = attend_back(cuts[1:], second, keys, values, attended, attended_grad, lse)

    runs = tuple((low * LANES, high * LANES) for low, high in zip(cuts[:-1], cuts[1:]))
    shape = (sums_of[0], half, piece_rows, qkvs, length, width, runs)
    shape_a = jax.ShapeDtypeStruct((sent_count, piece_rows, qkvs.wide), LOW)
    own_part, away_part, dgain_one, kept_a, sent_a = pl.pallas_call(
        functools.partial(project_back_kernel, shape),
        out_shape=(full_rows, low_rows, jax.ShapeDtypeStruct((8, width), FULL)) + (shape_a,) * 2,
        in_specs=[SMEM, VMEM] + [HBM] * (3 + 3 * len(runs)),
        out_specs=(HBM,) + (VMEM,) * 2 + (HBM,) * 2,
        scratch_shapes=[
            pltpu.VMEM((2, width, length), LOW),
            pltpu.VMEM((length, width), FULL),
            pltpu.VMEM((length, width), FULL),
            pltpu.VMEM((width, qkvs.room), LOW),
            pltpu.VMEM((length, width), LOW),
            pltpu.VMEM((length, width), LOW),
            pltpu.VMEM((width, 3 * width), LOW),
            pltpu.SemaphoreType.DMA,
            pltpu.SemaphoreType.DMA((3 + 3 * len(runs),)),
        ] + [pltpu.VMEM((length, high - low), LOW) for low, high in runs for _ in range(3)],
        compiler_params=params(60),
        cost_estimate=LITTLE,
        name="project_back",
    )(pos, gain_one, rows, other_rows, weight_qkv, *grads_one, *grads_two)

    sums_a = Halving(kept_a, sent_a, steps_b)
    sums_a.hold(*sums_b.last, *sums_c.last)
    backs, start = [], 0
    for index, part in enumerate(BACK_PARTS):
        size = length * part // sum(BACK_PARTS)
        backs.append(swap(after(away_part[start : start + size], *sums_a.last)))
        start += size
        before = sums_a.last
        if index == 1:
            sums_a.hold(partner_two)
        sums_a.send()
        for one, steps in ((sums_b, (2, 3)), (sums_c, (1, 3))):
            if index in steps and one.left():
                one.hold(*before)
                one.send()
    back_part = jnp.concatenate(backs, axis=0)

    own_rows = lax.dynamic_slice_in_dim(stream_out, stream * half_rows, half_rows, 0)
    partner_rows = partner_rows.astype(FULL)
    text_rows = jnp.where(is_text, own_rows, partner_rows)
    image_rows = jnp.where(is_text, partner_rows, own_rows)
    joined_rows = mix * text_rows + (1.0 - mix) * image_rows
    gate_grad = jnp.sum(cot_joined * (text_rows - image_rows), axis=0, keepdims=True) * mix * (1.0 - mix)

    slot_index = lax.iota(jnp.int32, 5)[:, None]
    small = (
        jnp.where(slot_index == stream, dgain_one[0:1], 0.0)
        + jnp.where(slot_index == 1 - stream, dgain_one[1:2], 0.0)
        + jnp.where(slot_index == 2 + stream, dgain_two[0:1], 0.0)
        + jnp.where(slot_index == 4, gate_grad, 0.0)
    )
    for step in core + along_x + along_y + along_z + [across]:
        small = small + flip(small, *step)
    gains_grad = small
    grad_rows = pl.pallas_call(
        functools.partial(tail_kernel, length),
        out_shape=full_rows,
        in_specs=[VMEM] * 5,
        out_specs=VMEM,
        compiler_params=params(10),
        name="norm_tail",
    )(rows, gain_own, own_part, back_part, after(middle_grad, *sums_a.last))

    def late(pair):
        return tuple(after(value, *sums_a.last) for value in pair)

    total_a, total_b, total_c = sums_a.total(), sums_b.total(), sums_c.total()

    def both(total):
        return total[0], swap(total[1].astype(LOW))

    def placed(mine, theirs):
        theirs = theirs.astype(FULL)
        return jnp.where(is_text, jnp.stack((mine, theirs)), jnp.stack((theirs, mine)))

    mine_b, theirs_b = late(both(total_b))
    grad_b = placed(mine_b, theirs_b)
    grad_up = ups.cut(grad_b[..., : ups.wide], doc)
    grad_out = outs.cut(grad_b[..., ups.wide :], doc)
    if downs.aligned:
        mine_c, theirs_c = late(both(total_c))
    else:
        mine_c = downs.cut(total_c[0], place)
        theirs_c = swap(downs.cut(total_c[1], (place + half) % wide).astype(LOW))
    grad_down = jnp.swapaxes(placed(mine_c, theirs_c), 1, 2)
    mine_a, theirs_a = both(total_a)
    mine_a, theirs_a = qkvs.cut(mine_a, doc), qkvs.cut(theirs_a.astype(FULL), doc)
    query_here = is_query[0]
    grad_qkv = placed(
        jnp.where(query_here, mine_a, theirs_a), jnp.where(query_here, theirs_a, mine_a)
    )

    qkv_new = adam_update(w_qkv, m_qkv, v_qkv, grad_qkv, 0.12, 0.01)
    out_new = adam_update(w_out, m_out, v_out, grad_out, 0.5, 0.01)
    up_new = adam_update(w_up, m_up, v_up, grad_up, 0.12, 0.01)
    down_new = adam_update(w_down, m_down, v_down, grad_down, 0.06, 0.01)
    gains_new = adam_update(gains, m_gains, v_gains, gains_grad, 0.8, 0.0)
    return (stream_out, joined_rows, grad_rows, *qkv_new, *out_new, *up_new, *down_new, *gains_new)


def solution(mesh):
    by_rows = P(("docs", "wide"), None)
    by_row = P(("docs", "wide"))
    weight = P(None, "wide", "docs")
    return jax.shard_map(
        shards,
        mesh=mesh,
        in_specs=(by_rows,) * 3 + (by_row,) * 2 + (weight,) * 12 + (P(),) * 3,
        out_specs=(by_rows,) * 3 + (weight,) * 12 + (P(),) * 3,
        check_vma=False,
    )
```

time: 371 us -> 318 us (0.86); the launches traced: 366 us -> 318 us
  Pallas kernels: 120 us -> 92.7 us
  local copies, waits for them, and re-layouts: 25.3 us -> 5.94 us
  starting transfers between devices: 67.4 us -> 73.9 us
  other arithmetic: 36.3 us -> 30.1 us
    pallas_call x2 -> x1, Pallas kernels: 41.3 us -> 15.5 us  [shards(): pl.pallas_call(functools.partial(project_kernel, shape), out_shape=made,...]
    unnamed x194 -> x132, local copies, waits for them, and re-layouts: 21.5 us -> 2.26 us
    pallas_call x1, Pallas kernels: 49 us -> 32.2 us  [shards(): pl.pallas_call(functools.partial(feed_kernel, shape), out_shape=(full_row...]
    pallas_call x2, Pallas kernels: 16.7 us -> 33 us  [attend_back(): pl.pallas_call(functools.partial(scores_back_kernel, (length, width, fact...]
    ppermute x65 -> x67, starting transfers between devices: 67.4 us -> 73.9 us  [flip(): return lax.ppermute(value, axis, [(i, i ^ mask) for i in range(count)])]
    convert_element_type x13, other arithmetic: 15.6 us -> 11.6 us  [the longest x9 10 us: send(): sum((part[half:].astype(FULL) for part in parts)).astype(LOW)]
    ppermute x65 -> x67, waiting for transfers between devices: 115 us -> 113 us  [flip(): return lax.ppermute(value, axis, [(i, i ^ mask) for i in range(count)])]
  transfers between devices with their start and end apart: 65 -> 67, of which waited for: 29 -> 23; matrix products, arithmetic and copies ran while one was open for 11% -> 9% of each run, Pallas kernels for 16% -> 19%
where the time goes in v3:
time: 318 us
  waiting for transfers between devices  113 us (36%)
  Pallas kernels  92.7 us (29%)
  starting transfers between devices  73.9 us (23%)
  other arithmetic  30.1 us (9%)
  local copies, waits for them, and re-layouts  5.94 us (2%)
    ppermute x67, waiting for transfers between devices, flip(): return lax.ppermute(value, axis, [(i, i ^ mask) for i in range(count)])  113 us
    ppermute x67, starting transfers between devices, flip(): return lax.ppermute(value, axis, [(i, i ^ mask) for i in range(count)])  73.9 us
    pallas_call x2, Pallas kernels, attend_back(): pl.pallas_call(functools.partial(scores_back_kernel, (length, width, fact...  33 us
    pallas_call x1, Pallas kernels, shards(): pl.pallas_call(functools.partial(feed_kernel, shape), out_shape=(full_row...  32.2 us
    pallas_call x1, Pallas kernels, shards(): pl.pallas_call(functools.partial(project_kernel, shape), out_shape=made,...  15.5 us
    convert_element_type x9, other arithmetic, send(): sum((part[half:].astype(FULL) for part in parts)).astype(LOW)  10 us
    pallas_call x1, Pallas kernels, shards(): pl.pallas_call(functools.partial(project_back_kernel, shape), out_shape=(...  9.79 us
  transfers between devices with their start and end apart: 67, of which 23 were waited for; matrix products, arithmetic and copies ran while one was open for 9% of the time, Pallas kernels for 19%

profile of v3, /device:TPU:0, one launch (start us, length us, event | category | flops | bytes accessed | tf_op | source)
XLA Modules:
  0.0 317.8 jit_solution(2943909935019701241)
XLA Ops:
  2.3 4.1 %collective-permute-start = (bf16[96,640]{1,0:T(8,128)(2,1)S(1)}, bf16[96,640]{1,0:T(8,128)(2,1)S(1)}, u32[]{:S(2)}, u32[]{:S(2)}) collective-permute-start(bf16[96,640]{1,0:T(8,128)(2,1)S(1)} %get-tuple-element.223), channel_id=1, source_target_pairs={{0,4},{1,5},{2,6},{3,7},{4,0},{5,1},{6,2},{7,3},{8,12},{9,13},{10,... | collective-permute-start | bytes 368648 | tf_op jit(solution)/shard_map/ppermute | solution.py:24
  6.4 1.6 collective-permute-start.4
  8.9 1.6 collective-permute-start.21
  12.0 1.9 collective-permute-done
  14.1 1.6 collective-permute-start.5
  15.7 6.1 %collective-permute-done.9.refs_10_ = bf16[1,96,640]{2,1,0:T(8,128)(2,1)S(1)} collective-permute-done((bf16[1,96,640]{2,1,0:T(8,128)(2,1)S(1)}, bf16[1,96,640]{2,1,0:T(8,128)(2,1)S(1)}, u32[]{:S(2)}, u32[]{:S(2)}) %collective-permute-start.9) | collective-permute-done | bytes 122912 | tf_op jit(solution)/shard_map/ppermute | solution.py:24
  21.9 2.3 collective-permute-start.1
  24.3 1.6 collective-permute-start.10
  26.9 12.5 %collective-permute-done.1.refs_0_ = bf16[160,768]{1,0:T(8,128)(2,1)} collective-permute-done((bf16[160,768]{1,0:T(8,128)(2,1)S(1)}, bf16[160,768]{1,0:T(8,128)(2,1)}, u32[]{:S(2)}, u32[]{:S(2)}) %collective-permute-start.1) | collective-permute-done | bytes 245792 | tf_op jit(solution)/shard_map/ppermute | solution.py:24
  43.4 6.8 %collective-permute-start.18 = (bf16[1,96,1024]{2,1,0:T(8,128)(2,1)S(1)}, bf16[1,96,1024]{2,1,0:T(8,128)(2,1)S(1)}, u32[]{:S(2)}, u32[]{:S(2)}) collective-permute-start(bf16[1,96,1024]{2,1,0:T(8,128)(2,1)S(1)} %bitcast.56), channel_id=1, source_target_pairs={{0,2},{1,3},{2,0},{3,1},{4,6},{5,7},{6,4},{7,5},{8,10},{9,11},{10,... | collective-permute-start | bytes 589832 | tf_op jit(solution)/shard_map/ppermute | solution.py:24
  50.2 4.8 %collective-permute-done.2.refs_1_ = bf16[192,768]{1,0:T(8,128)(2,1)S(1)} collective-permute-done((bf16[192,768]{1,0:T(8,128)(2,1)S(1)}, bf16[192,768]{1,0:T(8,128)(2,1)S(1)}, u32[]{:S(2)}, u32[]{:S(2)}) %collective-permute-start.2) | collective-permute-done | bytes 294944 | tf_op jit(solution)/shard_map/ppermute | solution.py:24
  55.0 2.6 collective-permute-done.18.refs_7_
  57.6 4.3 %collective-permute-start.3 = (bf16[160,768]{1,0:T(8,128)(2,1)S(1)}, bf16[160,768]{1,0:T(8,128)(2,1)S(1)}, u32[]{:S(2)}, u32[]{:S(2)}) collective-permute-start(bf16[160,768]{1,0:T(8,128)(2,1)S(1)} %get-tuple-element.93), channel_id=1, source_target_pairs={{0,4},{1,5},{2,6},{3,7},{4,0},{5,1},{6,2},{7,3},{8,12},{9,13},{10,... | collective-permute-start | bytes 737288 | tf_op jit(solution)/shard_map/ppermute | solution.py:24
  62.0 1.6 collective-permute-start.19
  64.2 5.0 %collective-permute-done.3.refs_2_ = bf16[160,768]{1,0:T(8,128)(2,1)S(1)} collective-permute-done((bf16[160,768]{1,0:T(8,128)(2,1)S(1)}, bf16[160,768]{1,0:T(8,128)(2,1)S(1)}, u32[]{:S(2)}, u32[]{:S(2)}) %collective-permute-start.3) | collective-permute-done | bytes 245792 | tf_op jit(solution)/shard_map/ppermute | solution.py:24
  74.3 2.3 collective-permute-done.26.refs_20_
  78.1 6.3 %collective-permute-start.29 = (bf16[4,96,1024]{2,1,0:T(8,128)(2,1)}, bf16[4,96,1024]{2,1,0:T(8,128)(2,1)}, u32[]{:S(2)}, u32[]{:S(2)}) collective-permute-start(bf16[4,96,1024]{2,1,0:T(8,128)(2,1)} %pad_maximum_fusion.1), channel_id=1, source_target_pairs={{0,2},{1,3},{2,0},{3,1},{4,6},{5,7},{6,4},{7,5},{8,10},{9,11},{10,... | collective-permute-start | bytes 2359304 | tf_op jit(solution)/shard_map/ppermute | solution.py:24
  86.4 1.6 collective-permute-start.32
  92.3 15.5 %project_attend.1 = (bf16[512,768]{1,0:T(8,128)(2,1)}, bf16[512,768]{1,0:T(8,128)(2,1)}, bf16[512,768]{1,0:T(8,128)(2,1)}, bf16[512,768]{1,0:T(8,128)(2,1)}, f32...) custom-call(s32[3]{0:T(128)} %pad_add_fusion.pos, f32[2,768]{1,0:T(2,128)} %pad_maximum_fusion.20.gains, ...), custom_call_target="tpu_custom_call" | custom-call | flops 1000 | bytes 1000 | tf_op jit(solution)/shard_map/project_attend/pallas_call | solution.py:730
  107.9 9.1 %collective-permute-done.31.refs_15_ = bf16[4,96,768]{2,1,0:T(8,128)(2,1)} collective-permute-done((bf16[4,96,768]{2,1,0:T(8,128)(2,1)}, bf16[4,96,768]{2,1,0:T(8,128)(2,1)}, u32[]{:S(2)}, u32[]{:S(2)}) %collective-permute-start.31) | collective-permute-done | bytes 589856 | tf_op jit(solution)/shard_map/ppermute | solution.py:24
  118.2 3.3 %collective-permute-done.36.refs_23_ = bf16[4,96,768]{2,1,0:T(8,128)(2,1)S(1)} collective-permute-done((bf16[4,96,768]{2,1,0:T(8,128)(2,1)}, bf16[4,96,768]{2,1,0:T(8,128)(2,1)S(1)}, u32[]{:S(2)}, u32[]{:S(2)}) %collective-permute-start.36) | collective-permute-done | bytes 589856 | tf_op jit(solution)/shard_map/ppermute | solution.py:24
  123.7 32.2 %feed_forward_back.1 = (f32[512,768]{1,0:T(8,128)}, f32[512,768]{1,0:T(8,128)}, bf16[512,768]{1,0:T(8,128)(2,1)}, bf16[256,768]{1,0:T(8,128)(2,1)}, f32[8,768]{1...) custom-call(s32[3]{0:T(128)} %pad_add_fusion.pos, ...), custom_call_target="tpu_custom_call" | custom-call | flops 1000 | bytes 1000 | tf_op jit(solution)/shard_map/feed_forward_back/pallas_call | solution.py:766
  159.0 25.2 %attend_back.2 = (bf16[512,512]{1,0:T(8,128)(2,1)}, bf16[512,512]{1,0:T(8,128)(2,1)}, bf16[512,512]{1,0:T(8,128)(2,1)}) custom-call(s32[512,1]{1,0:T(8,128)} %copy.39.page_col, s32[1,512]{1,0:T(1,128)} %bitcast.67, s32[1,512]{1,0:T(1,128)} %bitcast.71, bf16[512,768]{1,0:T(8,128)(2,1)} %get-tuple-element.128.q_hbm, ...), custom_call_target="tpu_custom_call" | custom-call | flops 1000 | bytes 1000 | tf_op jit(solution)/shard_map/attend_back/pallas_call | solution.py:806
  184.3 2.0 add_convert_fusion.3
  188.0 1.9 add_convert_fusion
  192.9 7.8 %attend_back.3 = (bf16[512,256]{1,0:T(8,128)(2,1)}, bf16[512,256]{1,0:T(8,128)(2,1)}, bf16[512,256]{1,0:T(8,128)(2,1)}) custom-call(s32[512,1]{1,0:T(8,128)} %copy.39.page_col, s32[1,512]{1,0:T(1,128)} %bitcast.68, s32[1,512]{1,0:T(1,128)} %bitcast.72, bf16[512,768]{1,0:T(8,128)(2,1)} %get-tuple-element.128.q_hbm, ...), custom_call_target="tpu_custom_call" | custom-call | flops 1000 | bytes 1000 | tf_op jit(solution)/shard_map/attend_back/pallas_call | solution.py:806
  200.7 1.5 collective-permute-start.40
  202.2 9.8 %project_back.1 = (f32[512,768]{1,0:T(8,128)}, bf16[512,768]{1,0:T(8,128)(2,1)}, f32[8,768]{1,0:T(8,128)}, bf16[16,96,640]{2,1,0:T(8,128)(2,1)}, bf16[16,96,640]{2,1,0:T(8,128)(2,1)}) custom-call(s32[3]{0:T(128)} %pad_add_fusion.pos, f32[2,768]{1,0:T(2,128)} %pad_maximum_fusion.20.gains, bf16[512,768]{1,0:T(8,128)(2,1)} %own.1, ...), custom_call_target="tpu_custom_call" | custom-call | flops 1000 | bytes 1000 | tf_op jit(solution)/shard_map/project_back/pallas_call | solution.py:843
  212.0 7.8 %collective-permute-done.44 = bf16[8,192,384]{2,1,0:T(8,128)(2,1)} collective-permute-done((bf16[8,192,384]{2,1,0:T(8,128)(2,1)}, bf16[8,192,384]{2,1,0:T(8,128)(2,1)}, u32[]{:S(2)}, u32[]{:S(2)}) %collective-permute-start.44) | collective-permute-done | bytes 1179680 | tf_op jit(solution)/shard_map/ppermute | solution.py:24
  223.9 1.6 collective-permute-start.63
  225.5 2.3 collective-permute-done.63
  227.9 1.6 collective-permute-start.64
  229.7 2.1 collective-permute-done.64
  232.9 4.4 %collective-permute-done.65 = f32[5,768]{1,0:T(8,128)S(1)} collective-permute-done((f32[5,768]{1,0:T(8,128)S(1)}, f32[5,768]{1,0:T(8,128)S(1)}, u32[]{:S(2)}, u32[]{:S(2)}) %collective-permute-start.65) | collective-permute-done | bytes 15392 | tf_op jit(solution)/shard_map/ppermute | solution.py:24
  237.3 1.6 add_convert_fusion.9
  239.0 1.6 collective-permute-start.59
  244.2 3.0 collective-permute-start.46
  247.2 15.6 %collective-permute-done.47 = bf16[4,96,640]{2,1,0:T(8,128)(2,1)S(1)} collective-permute-done((bf16[4,96,640]{2,1,0:T(8,128)(2,1)S(1)}, bf16[4,96,640]{2,1,0:T(8,128)(2,1)S(1)}, u32[]{:S(2)}, u32[]{:S(2)}) %collective-permute-start.47) | collective-permute-done | bytes 491552 | tf_op jit(solution)/shard_map/ppermute | solution.py:24
  263.0 1.6 collective-permute-start.51
  266.4 5.5 %collective-permute-done.50 = bf16[2,96,640]{2,1,0:T(8,128)(2,1)S(1)} collective-permute-done((bf16[2,96,640]{2,1,0:T(8,128)(2,1)S(1)}, bf16[2,96,640]{2,1,0:T(8,128)(2,1)S(1)}, u32[]{:S(2)}, u32[]{:S(2)}) %collective-permute-start.50) | collective-permute-done | bytes 245792 | tf_op jit(solution)/shard_map/ppermute | solution.py:24
  271.9 2.2 collective-permute-start.49
  275.4 6.7 %collective-permute-done.55 = bf16[2,96,1024]{2,1,0:T(8,128)(2,1)S(1)} collective-permute-done((bf16[2,96,1024]{2,1,0:T(8,128)(2,1)S(1)}, bf16[2,96,1024]{2,1,0:T(8,128)(2,1)S(1)}, u32[]{:S(2)}, u32[]{:S(2)}) %collective-permute-start.55) | collective-permute-done | bytes 393248 | tf_op jit(solution)/shard_map/ppermute | solution.py:24
  283.4 2.3 collective-permute-start.60
  285.7 7.1 %collective-permute-done.52 = bf16[96,768]{1,0:T(8,128)(2,1)S(1)} collective-permute-done((bf16[96,768]{1,0:T(8,128)(2,1)S(1)}, bf16[96,768]{1,0:T(8,128)(2,1)S(1)}, u32[]{:S(2)}, u32[]{:S(2)}) %collective-permute-start.52) | collective-permute-done | bytes 147488 | tf_op jit(solution)/shard_map/ppermute | solution.py:24
  293.2 2.2 norm_tail.1
  296.8 3.0 collective-permute-start.61
  301.6 4.9 %collective-permute-done.61 = bf16[192,384]{1,0:T(8,128)(2,1)S(1)} collective-permute-done((bf16[192,384]{1,0:T(8,128)(2,1)S(1)}, bf16[192,384]{1,0:T(8,128)(2,1)S(1)}, u32[]{:S(2)}, u32[]{:S(2)}) %collective-permute-start.61) | collective-permute-done | bytes 147488 | tf_op jit(solution)/shard_map/ppermute | solution.py:24
  309.5 5.4 %collective-permute-done.58 = bf16[96,1024]{1,0:T(8,128)(2,1)S(1)} collective-permute-done((bf16[96,1024]{1,0:T(8,128)(2,1)S(1)}, bf16[96,1024]{1,0:T(8,128)(2,1)S(1)}, u32[]{:S(2)}, u32[]{:S(2)}) %collective-permute-start.58) | collective-permute-done | bytes 196640 | tf_op jit(solution)/shard_map/ppermute | solution.py:24
  (305 shorter events, 56.6 us)
Async XLA Ops:
  2.3 11.6 %collective-permute-start = (bf16[96,640]{1,0:T(8,128)(2,1)S(1)}, bf16[96,640]{1,0:T(8,128)(2,1)S(1)}, u32[]{:S(2)}, u32[]{:S(2)}) collective-permute-start(bf16[96,640]{1,0:T(8,128)(2,1)S(1)} %get-tuple-element.223), channel_id=1, source_target_pairs={{0,4},{1,5},{2,6},{3,7},{4,0},{5,1},{6,2},{7,3},{8,12},{9,13},{10,... | collective-permute-start | bytes 368648 | tf_op jit(solution)/shard_map/ppermute | solution.py:24
  8.3 34.4 %collective-permute-start.17 = (bf16[96,1024]{1,0:T(8,128)(2,1)S(1)}, bf16[96,1024]{1,0:T(8,128)(2,1)S(1)}, u32[]{:S(2)}, u32[]{:S(2)}) collective-permute-start(bf16[96,1024]{1,0:T(8,128)(2,1)S(1)} %get-tuple-element.218), channel_id=1, source_target_pairs={{0,4},{1,5},{2,6},{3,7},{4,0},{5,1},{6,2},{7,3},{8,12},{9,13},{10,... | collective-permute-start | bytes 589832 | tf_op jit(solution)/shard_map/ppermute | solution.py:24
  8.9 34.5 %collective-permute-start.21 = (bf16[1,96,768]{2,1,0:T(8,128)(2,1)S(1)}, bf16[1,96,768]{2,1,0:T(8,128)(2,1)S(1)}, u32[]{:S(2)}, u32[]{:S(2)}) collective-permute-start(bf16[1,96,768]{2,1,0:T(8,128)(2,1)S(1)} %maximum_bitcast_fusion.refs_12_), channel_id=1, source_target_pairs={{0,8},{8,0},{16,24},{24,16},{1,9},{9,1},{17,25},{25,17},{2,10},{10... | collective-permute-start | bytes 442376 | tf_op jit(solution)/shard_map/ppermute | solution.py:24
  10.4 13.8 %collective-permute-start.14 = (bf16[1,96,1024]{2,1,0:T(8,128)(2,1)S(1)}, bf16[1,96,1024]{2,1,0:T(8,128)(2,1)S(1)}, u32[]{:S(2)}, u32[]{:S(2)}) collective-permute-start(bf16[1,96,1024]{2,1,0:T(8,128)(2,1)S(1)} %get-tuple-element.219.refs_0_), channel_id=1, source_target_pairs={{0,16},{8,24},{16,0},{24,8},{1,17},{9,25},{17,1},{25,9},{2,18},{10... | collective-permute-start | bytes 589832 | tf_op jit(solution)/shard_map/ppermute | solution.py:24
  14.1 11.8 %collective-permute-start.5 = (bf16[2,96,640]{2,1,0:T(8,128)(2,1)S(1)}, bf16[2,96,640]{2,1,0:T(8,128)(2,1)S(1)}, u32[]{:S(2)}, u32[]{:S(2)}) collective-permute-start(bf16[2,96,640]{2,1,0:T(8,128)(2,1)S(1)} %pad_maximum_fusion.16), channel_id=1, source_target_pairs={{0,8},{8,0},{16,24},{24,16},{1,9},{9,1},{17,25},{25,17},{2,10},{10... | collective-permute-start | bytes 737288 | tf_op jit(solution)/shard_map/ppermute | solution.py:24
  21.9 17.5 %collective-permute-start.1 = (bf16[160,768]{1,0:T(8,128)(2,1)S(1)}, bf16[160,768]{1,0:T(8,128)(2,1)}, u32[]{:S(2)}, u32[]{:S(2)}) collective-permute-start(bf16[160,768]{1,0:T(8,128)(2,1)S(1)} %get-tuple-element.91), channel_id=1, source_target_pairs={{0,4},{1,5},{2,6},{3,7},{4,0},{5,1},{6,2},{7,3},{8,12},{9,13},{10,... | collective-permute-start | bytes 737288 | tf_op jit(solution)/shard_map/ppermute | solution.py:24
  24.3 16.7 %collective-permute-start.10 = (bf16[2,96,640]{2,1,0:T(8,128)(2,1)S(1)}, bf16[2,96,640]{2,1,0:T(8,128)(2,1)S(1)}, u32[]{:S(2)}, u32[]{:S(2)}) collective-permute-start(bf16[2,96,640]{2,1,0:T(8,128)(2,1)S(1)} %pad_maximum_fusion.17), channel_id=1, source_target_pairs={{0,16},{8,24},{16,0},{24,8},{1,17},{9,25},{17,1},{25,9},{2,18},{10... | collective-permute-start | bytes 737288 | tf_op jit(solution)/shard_map/ppermute | solution.py:24
  25.9 15.3 %collective-permute-start.24 = (bf16[192,384]{1,0:T(8,128)(2,1)S(1)}, bf16[192,384]{1,0:T(8,128)(2,1)S(1)}, u32[]{:S(2)}, u32[]{:S(2)}) collective-permute-start(bf16[192,384]{1,0:T(8,128)(2,1)S(1)} %slice_bitcast_fusion), channel_id=1, source_target_pairs={{0,4},{1,5},{2,6},{3,7},{4,0},{5,1},{6,2},{7,3},{8,12},{9,13},{10,... | collective-permute-start | bytes 442376 | tf_op jit(solution)/shard_map/ppermute | solution.py:24
  39.4 18.2 %collective-permute-start.6 = (bf16[4,96,640]{2,1,0:T(8,128)(2,1)S(1)}, bf16[4,96,640]{2,1,0:T(8,128)(2,1)S(1)}, u32[]{:S(2)}, u32[]{:S(2)}) collective-permute-start(bf16[4,96,640]{2,1,0:T(8,128)(2,1)S(1)} %pad_maximum_fusion.7), channel_id=1, source_target_pairs={{0,16},{8,24},{16,0},{24,8},{1,17},{9,25},{17,1},{25,9},{2,18},{10... | collective-permute-start | bytes 1474568 | tf_op jit(solution)/shard_map/ppermute | solution.py:24
  40.9 14.0 %collective-permute-start.2 = (bf16[192,768]{1,0:T(8,128)(2,1)S(1)}, bf16[192,768]{1,0:T(8,128)(2,1)S(1)}, u32[]{:S(2)}, u32[]{:S(2)}) collective-permute-start(bf16[192,768]{1,0:T(8,128)(2,1)S(1)} %slice.492), channel_id=1, source_target_pairs={{0,4},{1,5},{2,6},{3,7},{4,0},{5,1},{6,2},{7,3},{8,12},{9,13},{10,... | collective-permute-start | bytes 884744 | tf_op jit(solution)/shard_map/ppermute | solution.py:24
  41.2 20.8 %collective-permute-start.11 = (bf16[4,96,640]{2,1,0:T(8,128)(2,1)S(1)}, bf16[4,96,640]{2,1,0:T(8,128)(2,1)}, u32[]{:S(2)}, u32[]{:S(2)}) collective-permute-start(bf16[4,96,640]{2,1,0:T(8,128)(2,1)S(1)} %pad_maximum_fusion.8), channel_id=1, source_target_pairs={{0,8},{8,0},{16,24},{24,16},{1,9},{9,1},{17,25},{25,17},{2,10},{10... | collective-permute-start | bytes 1474568 | tf_op jit(solution)/shard_map/ppermute | solution.py:24
  42.8 20.8 %collective-permute-start.15 = (bf16[2,96,1024]{2,1,0:T(8,128)(2,1)S(1)}, bf16[2,96,1024]{2,1,0:T(8,128)(2,1)S(1)}, u32[]{:S(2)}, u32[]{:S(2)}) collective-permute-start(bf16[2,96,1024]{2,1,0:T(8,128)(2,1)S(1)} %pad_maximum_fusion.9), channel_id=1, source_target_pairs={{0,8},{8,0},{16,24},{24,16},{1,9},{9,1},{17,25},{25,17},{2,10},{10... | collective-permute-start | bytes 1179656 | tf_op jit(solution)/shard_map/ppermute | solution.py:24
  43.4 14.2 %collective-permute-start.18 = (bf16[1,96,1024]{2,1,0:T(8,128)(2,1)S(1)}, bf16[1,96,1024]{2,1,0:T(8,128)(2,1)S(1)}, u32[]{:S(2)}, u32[]{:S(2)}) collective-permute-start(bf16[1,96,1024]{2,1,0:T(8,128)(2,1)S(1)} %bitcast.56), channel_id=1, source_target_pairs={{0,2},{1,3},{2,0},{3,1},{4,6},{5,7},{6,4},{7,5},{8,10},{9,11},{10,... | collective-permute-start | bytes 589832 | tf_op jit(solution)/shard_map/ppermute | solution.py:24
  57.6 14.2 %collective-permute-start.22 = (bf16[2,96,768]{2,1,0:T(8,128)(2,1)S(1)}, bf16[2,96,768]{2,1,0:T(8,128)(2,1)S(1)}, u32[]{:S(2)}, u32[]{:S(2)}) collective-permute-start(bf16[2,96,768]{2,1,0:T(8,128)(2,1)S(1)} %pad_maximum_fusion.13), channel_id=1, source_target_pairs={{0,2},{1,3},{2,0},{3,1},{4,6},{5,7},{6,4},{7,5},{8,10},{9,11},{10,... | collective-permute-start | bytes 884744 | tf_op jit(solution)/shard_map/ppermute | solution.py:24
  57.6 11.6 %collective-permute-start.3 = (bf16[160,768]{1,0:T(8,128)(2,1)S(1)}, bf16[160,768]{1,0:T(8,128)(2,1)S(1)}, u32[]{:S(2)}, u32[]{:S(2)}) collective-permute-start(bf16[160,768]{1,0:T(8,128)(2,1)S(1)} %get-tuple-element.93), channel_id=1, source_target_pairs={{0,4},{1,5},{2,6},{3,7},{4,0},{5,1},{6,2},{7,3},{8,12},{9,13},{10,... | collective-permute-start | bytes 737288 | tf_op jit(solution)/shard_map/ppermute | solution.py:24
  62.0 10.6 %collective-permute-start.19 = (bf16[2,96,1024]{2,1,0:T(8,128)(2,1)S(1)}, bf16[2,96,1024]{2,1,0:T(8,128)(2,1)S(1)}, u32[]{:S(2)}, u32[]{:S(2)}) collective-permute-start(bf16[2,96,1024]{2,1,0:T(8,128)(2,1)S(1)} %pad_maximum_fusion.10), channel_id=1, source_target_pairs={{0,8},{8,0},{16,24},{24,16},{1,9},{9,1},{17,25},{25,17},{2,10},{10... | collective-permute-start | bytes 1179656 | tf_op jit(solution)/shard_map/ppermute | solution.py:24
  63.5 10.6 %collective-permute-start.7 = (bf16[4,96,640]{2,1,0:T(8,128)(2,1)S(1)}, bf16[4,96,640]{2,1,0:T(8,128)(2,1)S(1)}, u32[]{:S(2)}, u32[]{:S(2)}) collective-permute-start(bf16[4,96,640]{2,1,0:T(8,128)(2,1)S(1)} %pad_maximum_fusion.7), channel_id=1, source_target_pairs={{0,1},{1,0},{2,3},{3,2},{4,5},{5,4},{6,7},{7,6},{8,9},{9,8},{10,11... | collective-permute-start | bytes 1474568 | tf_op jit(solution)/shard_map/ppermute | solution.py:24
  63.6 13.8 %collective-permute-start.12 = (bf16[4,96,640]{2,1,0:T(8,128)(2,1)S(1)}, bf16[4,96,640]{2,1,0:T(8,128)(2,1)S(1)}, u32[]{:S(2)}, u32[]{:S(2)}) collective-permute-start(bf16[4,96,640]{2,1,0:T(8,128)(2,1)S(1)} %pad_maximum_fusion.8), channel_id=1, source_target_pairs={{0,1},{1,0},{2,3},{3,2},{4,5},{5,4},{6,7},{7,6},{8,9},{9,8},{10,11... | collective-permute-start | bytes 1474568 | tf_op jit(solution)/shard_map/ppermute | solution.py:24
  71.7 12.7 %collective-permute-start.16 = (bf16[4,96,1024]{2,1,0:T(8,128)(2,1)}, bf16[4,96,1024]{2,1,0:T(8,128)(2,1)}, u32[]{:S(2)}, u32[]{:S(2)}) collective-permute-start(bf16[4,96,1024]{2,1,0:T(8,128)(2,1)} %pad_maximum_fusion.1), channel_id=1, source_target_pairs={{0,1},{1,0},{2,3},{3,2},{4,5},{5,4},{6,7},{7,6},{8,9},{9,8},{10,11... | collective-permute-start | bytes 2359304 | tf_op jit(solution)/shard_map/ppermute | solution.py:24
  76.5 9.9 %collective-permute-start.20 = (bf16[4,96,1024]{2,1,0:T(8,128)(2,1)}, bf16[4,96,1024]{2,1,0:T(8,128)(2,1)S(1)}, u32[]{:S(2)}, u32[]{:S(2)}) collective-permute-start(bf16[4,96,1024]{2,1,0:T(8,128)(2,1)} %pad_maximum_fusion.2), channel_id=1, source_target_pairs={{0,1},{1,0},{2,3},{3,2},{4,5},{5,4},{6,7},{7,6},{8,9},{9,8},{10,11... | collective-permute-start | bytes 2359304 | tf_op jit(solution)/shard_map/ppermute | solution.py:24
  78.0 10.1 %collective-permute-start.13 = (bf16[4,96,640]{2,1,0:T(8,128)(2,1)}, bf16[4,96,640]{2,1,0:T(8,128)(2,1)}, u32[]{:S(2)}, u32[]{:S(2)}) collective-permute-start(bf16[4,96,640]{2,1,0:T(8,128)(2,1)} %collective-permute-done.11.refs_12_), channel_id=1, source_target_pairs={{0,1},{1,0},{2,3},{3,2},{4,5},{5,4},{6,7},{7,6},{8,9},{9,8},{10,11... | collective-permute-start | bytes 1474568 | tf_op jit(solution)/shard_map/ppermute | solution.py:24
  78.1 38.8 %collective-permute-start.29 = (bf16[4,96,1024]{2,1,0:T(8,128)(2,1)}, bf16[4,96,1024]{2,1,0:T(8,128)(2,1)}, u32[]{:S(2)}, u32[]{:S(2)}) collective-permute-start(bf16[4,96,1024]{2,1,0:T(8,128)(2,1)} %pad_maximum_fusion.1), channel_id=1, source_target_pairs={{0,2},{1,3},{2,0},{3,1},{4,6},{5,7},{6,4},{7,5},{8,10},{9,11},{10,... | collective-permute-start | bytes 2359304 | tf_op jit(solution)/shard_map/ppermute | solution.py:24
  84.4 32.6 %collective-permute-start.30 = (bf16[4,96,1024]{2,1,0:T(8,128)(2,1)}, bf16[4,96,1024]{2,1,0:T(8,128)(2,1)}, u32[]{:S(2)}, u32[]{:S(2)}) collective-permute-start(bf16[4,96,1024]{2,1,0:T(8,128)(2,1)} %pad_maximum_fusion.2), channel_id=1, source_target_pairs={{0,16},{8,24},{16,0},{24,8},{1,17},{9,25},{17,1},{25,9},{2,18},{10... | collective-permute-start | bytes 2359304 | tf_op jit(solution)/shard_map/ppermute | solution.py:24
  85.9 31.0 %collective-permute-start.31 = (bf16[4,96,768]{2,1,0:T(8,128)(2,1)}, bf16[4,96,768]{2,1,0:T(8,128)(2,1)}, u32[]{:S(2)}, u32[]{:S(2)}) collective-permute-start(bf16[4,96,768]{2,1,0:T(8,128)(2,1)} %pad_maximum_fusion.4), channel_id=1, source_target_pairs={{0,16},{8,24},{16,0},{24,8},{1,17},{9,25},{17,1},{25,9},{2,18},{10... | collective-permute-start | bytes 1769480 | tf_op jit(solution)/shard_map/ppermute | solution.py:24
  86.4 30.5 %collective-permute-start.32 = (bf16[4,96,768]{2,1,0:T(8,128)(2,1)}, bf16[4,96,768]{2,1,0:T(8,128)(2,1)}, u32[]{:S(2)}, u32[]{:S(2)}) collective-permute-start(bf16[4,96,768]{2,1,0:T(8,128)(2,1)} %pad_maximum_fusion.5), channel_id=1, source_target_pairs={{0,8},{8,0},{16,24},{24,16},{1,9},{9,1},{17,25},{25,17},{2,10},{10... | collective-permute-start | bytes 1769480 | tf_op jit(solution)/shard_map/ppermute | solution.py:24
  88.1 28.9 %collective-permute-start.28 = (bf16[256,768]{1,0:T(8,128)(2,1)S(1)}, bf16[256,768]{1,0:T(8,128)(2,1)S(1)}, u32[]{:S(2)}, u32[]{:S(2)}) collective-permute-start(bf16[256,768]{1,0:T(8,128)(2,1)S(1)} %convert_element_type.389), channel_id=1, source_target_pairs={{0,4},{1,5},{2,6},{3,7},{4,0},{5,1},{6,2},{7,3},{8,12},{9,13},{10,... | collective-permute-start | bytes 1179656 | tf_op jit(solution)/shard_map/ppermute | solution.py:24
  155.8 30.5 %collective-permute-start.38 = (bf16[16,96,1024]{2,1,0:T(8,128)(2,1)}, bf16[16,96,1024]{2,1,0:T(8,128)(2,1)S(1)}, u32[]{:S(2)}, u32[]{:S(2)}) collective-permute-start(bf16[16,96,1024]{2,1,0:T(8,128)(2,1)} %get-tuple-element.121), channel_id=1, source_target_pairs={{0,1},{1,0},{2,3},{3,2},{4,5},{5,4},{6,7},{7,6},{8,9},{9,8},{10,11... | collective-permute-start | bytes 9437192 | tf_op jit(solution)/shard_map/ppermute | solution.py:24
  156.0 28.2 %collective-permute-start.39 = (bf16[16,192,384]{2,1,0:T(8,128)(2,1)}, bf16[16,192,384]{2,1,0:T(8,128)(2,1)}, u32[]{:S(2)}, u32[]{:S(2)}) collective-permute-start(bf16[16,192,384]{2,1,0:T(8,128)(2,1)} %get-tuple-element.122), channel_id=1, source_target_pairs={{0,1},{1,0},{2,3},{3,2},{4,5},{5,4},{6,7},{7,6},{8,9},{9,8},{10,11... | collective-permute-start | bytes 7077896 | tf_op jit(solution)/shard_map/ppermute | solution.py:24
  157.5 28.8 %collective-permute-start.37 = (bf16[128,768]{1,0:T(8,128)(2,1)S(1)}, bf16[128,768]{1,0:T(8,128)(2,1)S(1)}, u32[]{:S(2)}, u32[]{:S(2)}) collective-permute-start(bf16[128,768]{1,0:T(8,128)(2,1)S(1)} %get-tuple-element.216), channel_id=1, source_target_pairs={{0,4},{1,5},{2,6},{3,7},{4,0},{5,1},{6,2},{7,3},{8,12},{9,13},{10,... | collective-permute-start | bytes 589832 | tf_op jit(solution)/shard_map/ppermute | solution.py:24
  187.6 32.2 %collective-permute-start.44 = (bf16[8,192,384]{2,1,0:T(8,128)(2,1)}, bf16[8,192,384]{2,1,0:T(8,128)(2,1)}, u32[]{:S(2)}, u32[]{:S(2)}) collective-permute-start(bf16[8,192,384]{2,1,0:T(8,128)(2,1)} %pad_maximum_fusion), channel_id=1, source_target_pairs={{0,2},{1,3},{2,0},{3,1},{4,6},{5,7},{6,4},{7,5},{8,10},{9,11},{10,... | collective-permute-start | bytes 3538952 | tf_op jit(solution)/shard_map/ppermute | solution.py:24
  189.8 22.2 %collective-permute-start.43 = (bf16[4,96,1024]{2,1,0:T(8,128)(2,1)}, bf16[4,96,1024]{2,1,0:T(8,128)(2,1)}, u32[]{:S(2)}, u32[]{:S(2)}) collective-permute-start(bf16[4,96,1024]{2,1,0:T(8,128)(2,1)} %get-tuple-element.137), channel_id=1, source_target_pairs={{0,16},{8,24},{16,0},{24,8},{1,17},{9,25},{17,1},{25,9},{2,18},{10... | collective-permute-start | bytes 2359304 | tf_op jit(solution)/shard_map/ppermute | solution.py:24
  191.3 20.7 %collective-permute-start.42 = (bf16[4,96,1024]{2,1,0:T(8,128)(2,1)}, bf16[4,96,1024]{2,1,0:T(8,128)(2,1)}, u32[]{:S(2)}, u32[]{:S(2)}) collective-permute-start(bf16[4,96,1024]{2,1,0:T(8,128)(2,1)} %get-tuple-element.136), channel_id=1, source_target_pairs={{0,8},{8,0},{16,24},{24,16},{1,9},{9,1},{17,25},{25,17},{2,10},{10... | collective-permute-start | bytes 2359304 | tf_op jit(solution)/shard_map/ppermute | solution.py:24
  200.7 20.8 %collective-permute-start.40 = (bf16[128,768]{1,0:T(8,128)(2,1)S(1)}, bf16[128,768]{1,0:T(8,128)(2,1)S(1)}, u32[]{:S(2)}, u32[]{:S(2)}) collective-permute-start(bf16[128,768]{1,0:T(8,128)(2,1)S(1)} %get-tuple-element.123), channel_id=1, source_target_pairs={{0,4},{1,5},{2,6},{3,7},{4,0},{5,1},{6,2},{7,3},{8,12},{9,13},{10,... | collective-permute-start | bytes 589832 | tf_op jit(solution)/shard_map/ppermute | solution.py:24
  219.8 19.1 %collective-permute-start.45 = (bf16[16,96,640]{2,1,0:T(8,128)(2,1)}, bf16[16,96,640]{2,1,0:T(8,128)(2,1)S(1)}, u32[]{:S(2)}, u32[]{:S(2)}) collective-permute-start(bf16[16,96,640]{2,1,0:T(8,128)(2,1)} %get-tuple-element.141), channel_id=1, source_target_pairs={{0,1},{1,0},{2,3},{3,2},{4,5},{5,4},{6,7},{7,6},{8,9},{9,8},{10,11... | collective-permute-start | bytes 5898248 | tf_op jit(solution)/shard_map/ppermute | solution.py:24
  229.6 53.9 %collective-permute-start.41 = (bf16[128,768]{1,0:T(8,128)(2,1)S(1)}, bf16[128,768]{1,0:T(8,128)(2,1)S(1)}, u32[]{:S(2)}, u32[]{:S(2)}) collective-permute-start(bf16[128,768]{1,0:T(8,128)(2,1)S(1)} %get-tuple-element.210), channel_id=1, source_target_pairs={{0,4},{1,5},{2,6},{3,7},{4,0},{5,1},{6,2},{7,3},{8,12},{9,13},{10,... | collective-permute-start | bytes 589832 | tf_op jit(solution)/shard_map/ppermute | solution.py:24
  239.0 25.6 %collective-permute-start.59 = (bf16[4,192,384]{2,1,0:T(8,128)(2,1)S(1)}, bf16[4,192,384]{2,1,0:T(8,128)(2,1)S(1)}, u32[]{:S(2)}, u32[]{:S(2)}) collective-permute-start(bf16[4,192,384]{2,1,0:T(8,128)(2,1)S(1)} %pad_maximum_fusion.6), channel_id=1, source_target_pairs={{0,8},{8,0},{16,24},{24,16},{1,9},{9,1},{17,25},{25,17},{2,10},{10... | collective-permute-start | bytes 1769480 | tf_op jit(solution)/shard_map/ppermute | solution.py:24
  240.8 21.9 %collective-permute-start.47 = (bf16[4,96,640]{2,1,0:T(8,128)(2,1)S(1)}, bf16[4,96,640]{2,1,0:T(8,128)(2,1)S(1)}, u32[]{:S(2)}, u32[]{:S(2)}) collective-permute-start(bf16[4,96,640]{2,1,0:T(8,128)(2,1)S(1)} %get-tuple-element.144), channel_id=1, source_target_pairs={{0,8},{8,0},{16,24},{24,16},{1,9},{9,1},{17,25},{25,17},{2,10},{10... | collective-permute-start | bytes 1474568 | tf_op jit(solution)/shard_map/ppermute | solution.py:24
  241.4 21.4 %collective-permute-start.48 = (bf16[4,96,640]{2,1,0:T(8,128)(2,1)S(1)}, bf16[4,96,640]{2,1,0:T(8,128)(2,1)S(1)}, u32[]{:S(2)}, u32[]{:S(2)}) collective-permute-start(bf16[4,96,640]{2,1,0:T(8,128)(2,1)S(1)} %get-tuple-element.145), channel_id=1, source_target_pairs={{0,16},{8,24},{16,0},{24,8},{1,17},{9,25},{17,1},{25,9},{2,18},{10... | collective-permute-start | bytes 1474568 | tf_op jit(solution)/shard_map/ppermute | solution.py:24
  244.2 41.5 %collective-permute-start.46 = (bf16[160,768]{1,0:T(8,128)(2,1)S(1)}, bf16[160,768]{1,0:T(8,128)(2,1)S(1)}, u32[]{:S(2)}, u32[]{:S(2)}) collective-permute-start(bf16[160,768]{1,0:T(8,128)(2,1)S(1)} %slice.507), channel_id=1, source_target_pairs={{0,4},{1,5},{2,6},{3,7},{4,0},{5,1},{6,2},{7,3},{8,12},{9,13},{10,... | collective-permute-start | bytes 737288 | tf_op jit(solution)/shard_map/ppermute | solution.py:24
  263.0 8.9 %collective-permute-start.50 = (bf16[2,96,640]{2,1,0:T(8,128)(2,1)S(1)}, bf16[2,96,640]{2,1,0:T(8,128)(2,1)S(1)}, u32[]{:S(2)}, u32[]{:S(2)}) collective-permute-start(bf16[2,96,640]{2,1,0:T(8,128)(2,1)S(1)} %get-tuple-element.207), channel_id=1, source_target_pairs={{0,16},{8,24},{16,0},{24,8},{1,17},{9,25},{17,1},{25,9},{2,18},{10... | collective-permute-start | bytes 737288 | tf_op jit(solution)/shard_map/ppermute | solution.py:24
  264.6 10.7 %collective-permute-start.56 = (bf16[2,96,1024]{2,1,0:T(8,128)(2,1)S(1)}, bf16[2,96,1024]{2,1,0:T(8,128)(2,1)S(1)}, u32[]{:S(2)}, u32[]{:S(2)}) collective-permute-start(bf16[2,96,1024]{2,1,0:T(8,128)(2,1)S(1)} %get-tuple-element.152), channel_id=1, source_target_pairs={{0,8},{8,0},{16,24},{24,16},{1,9},{9,1},{17,25},{25,17},{2,10},{10... | collective-permute-start | bytes 1179656 | tf_op jit(solution)/shard_map/ppermute | solution.py:24
  271.9 10.2 %collective-permute-start.55 = (bf16[2,96,1024]{2,1,0:T(8,128)(2,1)S(1)}, bf16[2,96,1024]{2,1,0:T(8,128)(2,1)S(1)}, u32[]{:S(2)}, u32[]{:S(2)}) collective-permute-start(bf16[2,96,1024]{2,1,0:T(8,128)(2,1)S(1)} %get-tuple-element.150), channel_id=1, source_target_pairs={{0,16},{8,24},{16,0},{24,8},{1,17},{9,25},{17,1},{25,9},{2,18},{10... | collective-permute-start | bytes 1179656 | tf_op jit(solution)/shard_map/ppermute | solution.py:24
  271.9 13.9 %collective-permute-start.49 = (bf16[128,768]{1,0:T(8,128)(2,1)S(1)}, bf16[128,768]{1,0:T(8,128)(2,1)S(1)}, u32[]{:S(2)}, u32[]{:S(2)}) collective-permute-start(bf16[128,768]{1,0:T(8,128)(2,1)S(1)} %get-tuple-element.146), channel_id=1, source_target_pairs={{0,4},{1,5},{2,6},{3,7},{4,0},{5,1},{6,2},{7,3},{8,12},{9,13},{10,... | collective-permute-start | bytes 589832 | tf_op jit(solution)/shard_map/ppermute | solution.py:24
  275.3 17.6 %collective-permute-start.53 = (bf16[2,96,640]{2,1,0:T(8,128)(2,1)S(1)}, bf16[2,96,640]{2,1,0:T(8,128)(2,1)S(1)}, u32[]{:S(2)}, u32[]{:S(2)}) collective-permute-start(bf16[2,96,640]{2,1,0:T(8,128)(2,1)S(1)} %pad_maximum_fusion.18), channel_id=1, source_target_pairs={{0,2},{1,3},{2,0},{3,1},{4,6},{5,7},{6,4},{7,5},{8,10},{9,11},{10,... | collective-permute-start | bytes 737288 | tf_op jit(solution)/shard_map/ppermute | solution.py:24
  282.1 10.7 %collective-permute-start.52 = (bf16[96,768]{1,0:T(8,128)(2,1)S(1)}, bf16[96,768]{1,0:T(8,128)(2,1)S(1)}, u32[]{:S(2)}, u32[]{:S(2)}) collective-permute-start(bf16[96,768]{1,0:T(8,128)(2,1)S(1)} %slice.521), channel_id=1, source_target_pairs={{0,4},{1,5},{2,6},{3,7},{4,0},{5,1},{6,2},{7,3},{8,12},{9,13},{10,... | collective-permute-start | bytes 442376 | tf_op jit(solution)/shard_map/ppermute | solution.py:24
  283.4 12.0 %collective-permute-start.60 = (bf16[2,192,384]{2,1,0:T(8,128)(2,1)S(1)}, bf16[2,192,384]{2,1,0:T(8,128)(2,1)S(1)}, u32[]{:S(2)}, u32[]{:S(2)}) collective-permute-start(bf16[2,192,384]{2,1,0:T(8,128)(2,1)S(1)} %pad_maximum_fusion.15), channel_id=1, source_target_pairs={{0,16},{8,24},{16,0},{24,8},{1,17},{9,25},{17,1},{25,9},{2,18},{10... | collective-permute-start | bytes 884744 | tf_op jit(solution)/shard_map/ppermute | solution.py:24
  285.7 20.9 %collective-permute-start.57 = (bf16[2,96,1024]{2,1,0:T(8,128)(2,1)S(1)}, bf16[2,96,1024]{2,1,0:T(8,128)(2,1)S(1)}, u32[]{:S(2)}, u32[]{:S(2)}) collective-permute-start(bf16[2,96,1024]{2,1,0:T(8,128)(2,1)S(1)} %pad_maximum_fusion.12), channel_id=1, source_target_pairs={{0,2},{1,3},{2,0},{3,1},{4,6},{5,7},{6,4},{7,5},{8,10},{9,11},{10,... | collective-permute-start | bytes 1179656 | tf_op jit(solution)/shard_map/ppermute | solution.py:24
  296.8 9.7 %collective-permute-start.61 = (bf16[192,384]{1,0:T(8,128)(2,1)S(1)}, bf16[192,384]{1,0:T(8,128)(2,1)S(1)}, u32[]{:S(2)}, u32[]{:S(2)}) collective-permute-start(bf16[192,384]{1,0:T(8,128)(2,1)S(1)} %get-tuple-element.186), channel_id=1, source_target_pairs={{0,4},{1,5},{2,6},{3,7},{4,0},{5,1},{6,2},{7,3},{8,12},{9,13},{10,... | collective-permute-start | bytes 442376 | tf_op jit(solution)/shard_map/ppermute | solution.py:24
  (85 other events, 1045.0 us)

commit v4 on v3

--- a/solution.py
+++ b/solution.py
@@ -12,7 +12,6 @@
 LANES = 128
 CHUNK = 128
 ROW_PARTS = (5, 6, 5)
-BACK_PARTS = (4, 5, 4, 3)
 FIRST_A = False
 NEG = -1000000000.0
 LOW = jnp.bfloat16
@@ -80,12 +79,51 @@
     return codes
 
 
+def halves_of(value):
+    high = lax.reduce_precision(value, 8, 7)
+    return high, lax.reduce_precision(value - high, 8, 7)
+
+
+def with_rider(value, rider):
+    lanes = value.shape[-1]
+    rows = -(-rider.size // lanes)
+    flat = [jnp.pad(part.reshape(-1), (0, rows * lanes - rider.size)) for part in halves_of(rider)]
+    tail = jnp.concatenate(flat).astype(LOW).reshape(2 * rows, lanes)
+    tail = jnp.pad(tail, ((0, -(2 * rows) % 16), (0, 0)))
+    return jnp.concatenate((value.reshape(-1, lanes), tail), axis=0)
+
+
+def rider_of(message, shape, value_shape):
+    count = value_shape[0] * value_shape[1]
+    lanes = message.shape[-1]
+    rows = -(-(shape[0] * shape[1]) // lanes)
+    parts = [
+        message[count + i * rows : count + (i + 1) * rows].reshape(-1)[: shape[0] * shape[1]].reshape(shape)
+        for i in (0, 1)
+    ]
+    return message[:count].reshape(value_shape), parts[0].astype(FULL) + parts[1].astype(FULL)
+
+
+def kept_rider(rider):
+    high, low = halves_of(rider)
+    return high + low
+
+
 class Halving:
     def __init__(self, kept, sent, steps):
         self.slots, self.sent, self.steps = split(kept), sent, steps
         self.step, self.last = 0, ()
         self.slots = [[half] for half in self.slots]
         self.outgoing = [None, None]
+        self.rider = None
+
+    def carry(self, value, axis, mask):
+        if self.rider is None or self.step == 0:
+            return flip(value, axis, mask)
+        message = flip(with_rider(value, self.rider), axis, mask)
+        value, rider = rider_of(message, self.rider.shape, value.shape)
+        self.rider = kept_rider(self.rider) + rider
+        return value
 
     def left(self):
         return self.step < len(self.steps)
@@ -100,11 +138,11 @@
         one, two = self.steps[self.step]
         if one == two:
             whole = self.sent if self.step == 0 else jnp.concatenate(self.outgoing, axis=0)
-            arrived = flip(whole, *one)
+            arrived = self.carry(whole, *one)
             self.last = (arrived,)
             arrived = split(arrived)
         else:
-            arrived = [flip(self.outgoing[0], *one), flip(self.outgoing[1], *two)]
+            arrived = [self.carry(self.outgoing[0], *one), flip(self.outgoing[1], *two)]
             self.last = tuple(arrived)
         self.slots = [parts + [new] for parts, new in zip(self.slots, arrived)]
         self.step += 1
@@ -822,19 +860,16 @@
     sums_b, sums_c = Halving(kept_b, sent_b, steps_b), Halving(kept_c, sent_c, steps_c)
     sums_b.send()
     sums_c.send()
-    quarter = half_rows // 2
-    partner_one = swap(away[:quarter])
+    partner_rows = swap(away)
     pair_count = width // LANES
     cuts = (0, pair_count * 2 // 3, pair_count)
     grads_one = attend_back(cuts[:2], queries, keys, values, attended, attended_grad, lse)
-    met = (*sums_b.last, *sums_c.last, partner_one)
+    met = (*sums_b.last, *sums_c.last, partner_rows)
     second = after(queries, grads_one[0], *met)
     sums_b.hold(grads_one[0], *met)
     sums_c.hold(grads_one[0], *met)
     sums_b.send()
     sums_c.send()
-    partner_two = swap(after(away[quarter:], grads_one[0], *met))
-    partner_rows = jnp.concatenate((partner_one, partner_two), axis=0)
     grads_two = attend_back(cuts[1:], second, keys, values, attended, attended_grad, lse)
 
     runs = tuple((low * LANES, high * LANES) for low, high in zip(cuts[:-1], cuts[1:]))
@@ -861,23 +896,6 @@
         name="project_back",
     )(pos, gain_one, rows, other_rows, weight_qkv, *grads_one, *grads_two)
 
-    sums_a = Halving(kept_a, sent_a, steps_b)
-    sums_a.hold(*sums_b.last, *sums_c.last)
-    backs, start = [], 0
-    for index, part in enumerate(BACK_PARTS):
-        size = length * part // sum(BACK_PARTS)
-        backs.append(swap(after(away_part[start : start + size], *sums_a.last)))
-        start += size
-        before = sums_a.last
-        if index == 1:
-            sums_a.hold(partner_two)
-        sums_a.send()
-        for one, steps in ((sums_b, (2, 3)), (sums_c, (1, 3))):
-            if index in steps and one.left():
-                one.hold(*before)
-                one.send()
-    back_part = jnp.concatenate(backs, axis=0)
-
     own_rows = lax.dynamic_slice_in_dim(stream_out, stream * half_rows, half_rows, 0)
     partner_rows = partner_rows.astype(FULL)
     text_rows = jnp.where(is_text, own_rows, partner_rows)
@@ -892,9 +910,17 @@
         + jnp.where(slot_index == 2 + stream, dgain_two[0:1], 0.0)
         + jnp.where(slot_index == 4, gate_grad, 0.0)
     )
-    for step in core + along_x + along_y + along_z + [across]:
-        small = small + flip(small, *step)
-    gains_grad = small
+    sums_a = Halving(kept_a, sent_a, steps_b)
+    sums_a.hold(*sums_b.last, *sums_c.last)
+    sums_a.send()
+    sums_a.rider = small + flip(small, *core[0])
+    back_part = swap(away_part)
+    for one in (sums_b, sums_c):
+        one.hold(*[value for value in sums_a.outgoing if value is not None])
+    for one in (sums_a, sums_b, sums_c):
+        while one.left():
+            one.send()
+
     grad_rows = pl.pallas_call(
         functools.partial(tail_kernel, length),
         out_shape=full_rows,
@@ -926,7 +952,10 @@
         mine_c = downs.cut(total_c[0], place)
         theirs_c = swap(downs.cut(total_c[1], (place + half) % wide).astype(LOW))
     grad_down = jnp.swapaxes(placed(mine_c, theirs_c), 1, 2)
-    mine_a, theirs_a = both(total_a)
+    last = total_a[1].astype(LOW)[None]
+    last, rider = rider_of(swap(with_rider(last, sums_a.rider)), sums_a.rider.shape, last.shape)
+    gains_grad = kept_rider(sums_a.rider) + rider
+    mine_a, theirs_a = total_a[0], last[0]
     mine_a, theirs_a = qkvs.cut(mine_a, doc), qkvs.cut(theirs_a.astype(FULL), doc)
     query_here = is_query[0]
     grad_qkv = placed(

time: 318 us -> 306 us (0.962)
  waiting for transfers between devices: 113 us -> 84 us
  other arithmetic: 30.1 us -> 44.5 us
  local copies, waits for them, and re-layouts: 5.94 us -> 10.7 us
  starting transfers between devices: 73.9 us -> 69.3 us
    ppermute x67 -> x59, waiting for transfers between devices: 113 us -> 84 us  [flip(): return lax.ppermute(value, axis, [(i, i ^ mask) for i in range(count)])]
    convert_element_type x9, other arithmetic: 10 us -> 16 us  [send(): sum((part[half:].astype(FULL) for part in parts)).astype(LOW)]
    unnamed x132 -> x170, local copies, waits for them, and re-layouts: 2.26 us -> 7.02 us
    ppermute x67 -> x59, starting transfers between devices: 73.9 us -> 69.3 us  [flip(): return lax.ppermute(value, axis, [(i, i ^ mask) for i in range(count)])]
  transfers between devices with their start and end apart: 67 -> 59, of which waited for: 23 -> 17; matrix products, arithmetic and copies ran while one was open for 9% -> 14% of each run, Pallas kernels for 19% -> 20%
where the time goes in v4:
time: 306 us; the launch traced here: 303 us
  Pallas kernels  92.6 us (30%)
  waiting for transfers between devices  84 us (27%)
  starting transfers between devices  69.3 us (23%)
  other arithmetic  44.5 us (15%)
  local copies, waits for them, and re-layouts  10.7 us (3%)
    ppermute x59, waiting for transfers between devices, flip(): return lax.ppermute(value, axis, [(i, i ^ mask) for i in range(count)])  84 us
    ppermute x59, starting transfers between devices, flip(): return lax.ppermute(value, axis, [(i, i ^ mask) for i in range(count)])  69.3 us
    pallas_call x2, Pallas kernels, attend_back(): pl.pallas_call(functools.partial(scores_back_kernel, (length, width, fact...  32.9 us
    pallas_call x1, Pallas kernels, shards(): pl.pallas_call(functools.partial(feed_kernel, shape), out_shape=(full_row...  32.1 us
    convert_element_type x9, other arithmetic, send(): sum((part[half:].astype(FULL) for part in parts)).astype(LOW)  16 us
    pallas_call x1, Pallas kernels, shards(): pl.pallas_call(functools.partial(project_kernel, shape), out_shape=made,...  15.5 us
    pallas_call x1, Pallas kernels, shards(): pl.pallas_call(functools.partial(project_back_kernel, shape), out_shape=(...  9.83 us
    unnamed x170, local copies, waits for them, and re-layouts  7.02 us
  transfers between devices with their start and end apart: 59, of which 17 were waited for; matrix products, arithmetic and copies ran while one was open for 14% of the time, Pallas kernels for 20%

profile of v4, /device:TPU:0, one launch (start us, length us, event | category | flops | bytes accessed | tf_op | source)
XLA Modules:
  0.0 303.4 jit_solution(16617694451021786549)
XLA Ops:
  2.3 4.1 %collective-permute-start = (bf16[96,640]{1,0:T(8,128)(2,1)S(1)}, bf16[96,640]{1,0:T(8,128)(2,1)S(1)}, u32[]{:S(2)}, u32[]{:S(2)}) collective-permute-start(bf16[96,640]{1,0:T(8,128)(2,1)S(1)} %get-tuple-element.203), channel_id=1, source_target_pairs={{0,4},{1,5},{2,6},{3,7},{4,0},{5,1},{6,2},{7,3},{8,12},{9,13},{10,... | collective-permute-start | bytes 368648 | tf_op jit(solution)/shard_map/ppermute | solution.py:23
  6.4 1.6 collective-permute-start.4
  8.9 1.6 collective-permute-start.21
  10.5 1.5 collective-permute-start.14
  12.0 1.9 collective-permute-done
  14.2 1.6 collective-permute-start.5
  15.8 6.1 %collective-permute-done.9.refs_10_ = bf16[1,96,640]{2,1,0:T(8,128)(2,1)S(1)} collective-permute-done((bf16[1,96,640]{2,1,0:T(8,128)(2,1)S(1)}, bf16[1,96,640]{2,1,0:T(8,128)(2,1)S(1)}, u32[]{:S(2)}, u32[]{:S(2)}) %collective-permute-start.9) | collective-permute-done | bytes 122912 | tf_op jit(solution)/shard_map/ppermute | solution.py:23
  21.9 2.3 collective-permute-start.1
  24.3 1.6 collective-permute-start.10
  26.9 12.4 %collective-permute-done.1.refs_0_ = bf16[160,768]{1,0:T(8,128)(2,1)S(1)} collective-permute-done((bf16[160,768]{1,0:T(8,128)(2,1)S(1)}, bf16[160,768]{1,0:T(8,128)(2,1)S(1)}, u32[]{:S(2)}, u32[]{:S(2)}) %collective-permute-start.1) | collective-permute-done | bytes 245792 | tf_op jit(solution)/shard_map/ppermute | solution.py:23
  39.3 1.5 collective-permute-start.6
  43.5 6.7 %collective-permute-start.18 = (bf16[1,96,1024]{2,1,0:T(8,128)(2,1)S(1)}, bf16[1,96,1024]{2,1,0:T(8,128)(2,1)S(1)}, u32[]{:S(2)}, u32[]{:S(2)}) collective-permute-start(bf16[1,96,1024]{2,1,0:T(8,128)(2,1)S(1)} %bitcast.79), channel_id=1, source_target_pairs={{0,2},{1,3},{2,0},{3,1},{4,6},{5,7},{6,4},{7,5},{8,10},{9,11},{10,... | collective-permute-start | bytes 589832 | tf_op jit(solution)/shard_map/ppermute | solution.py:23
  50.2 4.8 %collective-permute-done.2.refs_1_ = bf16[192,768]{1,0:T(8,128)(2,1)} collective-permute-done((bf16[192,768]{1,0:T(8,128)(2,1)S(1)}, bf16[192,768]{1,0:T(8,128)(2,1)}, u32[]{:S(2)}, u32[]{:S(2)}) %collective-permute-start.2) | collective-permute-done | bytes 294944 | tf_op jit(solution)/shard_map/ppermute | solution.py:23
  55.0 2.6 collective-permute-done.18.refs_7_
  57.6 4.3 %collective-permute-start.3 = (bf16[160,768]{1,0:T(8,128)(2,1)S(1)}, bf16[160,768]{1,0:T(8,128)(2,1)S(1)}, u32[]{:S(2)}, u32[]{:S(2)}) collective-permute-start(bf16[160,768]{1,0:T(8,128)(2,1)S(1)} %get-tuple-element.83), channel_id=1, source_target_pairs={{0,4},{1,5},{2,6},{3,7},{4,0},{5,1},{6,2},{7,3},{8,12},{9,13},{10,... | collective-permute-start | bytes 737288 | tf_op jit(solution)/shard_map/ppermute | solution.py:23
  62.0 1.6 collective-permute-start.19
  64.2 5.0 %collective-permute-done.3.refs_2_ = bf16[160,768]{1,0:T(8,128)(2,1)S(1)} collective-permute-done((bf16[160,768]{1,0:T(8,128)(2,1)S(1)}, bf16[160,768]{1,0:T(8,128)(2,1)S(1)}, u32[]{:S(2)}, u32[]{:S(2)}) %collective-permute-start.3) | collective-permute-done | bytes 245792 | tf_op jit(solution)/shard_map/ppermute | solution.py:23
  69.2 1.5 collective-permute-start.26
  74.3 2.3 collective-permute-done.26.refs_20_
  78.1 6.3 %collective-permute-start.29 = (bf16[4,96,1024]{2,1,0:T(8,128)(2,1)}, bf16[4,96,1024]{2,1,0:T(8,128)(2,1)}, u32[]{:S(2)}, u32[]{:S(2)}) collective-permute-start(bf16[4,96,1024]{2,1,0:T(8,128)(2,1)} %pad_maximum_fusion.1), channel_id=1, source_target_pairs={{0,2},{1,3},{2,0},{3,1},{4,6},{5,7},{6,4},{7,5},{8,10},{9,11},{10,... | collective-permute-start | bytes 2359304 | tf_op jit(solution)/shard_map/ppermute | solution.py:23
  84.4 1.5 collective-permute-start.30
  86.5 1.6 collective-permute-start.32
  93.0 15.5 %project_attend.1 = (bf16[512,768]{1,0:T(8,128)(2,1)}, bf16[512,768]{1,0:T(8,128)(2,1)}, bf16[512,768]{1,0:T(8,128)(2,1)}, bf16[512,768]{1,0:T(8,128)(2,1)}, f32...) custom-call(s32[3]{0:T(128)} %pad_add_fusion.pos, f32[2,768]{1,0:T(2,128)} %pad_maximum_fusion.22.gains, ...), custom_call_target="tpu_custom_call" | custom-call | flops 1000 | bytes 1000 | tf_op jit(solution)/shard_map/project_attend/pallas_call | solution.py:768
  108.5 8.4 %collective-permute-done.31.refs_15_ = bf16[4,96,768]{2,1,0:T(8,128)(2,1)} collective-permute-done((bf16[4,96,768]{2,1,0:T(8,128)(2,1)}, bf16[4,96,768]{2,1,0:T(8,128)(2,1)}, u32[]{:S(2)}, u32[]{:S(2)}) %collective-permute-start.31) | collective-permute-done | bytes 589856 | tf_op jit(solution)/shard_map/ppermute | solution.py:23
  118.7 3.4 %collective-permute-done.36.refs_23_ = bf16[4,96,768]{2,1,0:T(8,128)(2,1)S(1)} collective-permute-done((bf16[4,96,768]{2,1,0:T(8,128)(2,1)}, bf16[4,96,768]{2,1,0:T(8,128)(2,1)S(1)}, u32[]{:S(2)}, u32[]{:S(2)}) %collective-permute-start.36) | collective-permute-done | bytes 589856 | tf_op jit(solution)/shard_map/ppermute | solution.py:23
  124.4 32.1 %feed_forward_back.1 = (f32[512,768]{1,0:T(8,128)}, f32[512,768]{1,0:T(8,128)}, bf16[512,768]{1,0:T(8,128)(2,1)}, bf16[256,768]{1,0:T(8,128)(2,1)}, f32[8,768]{1...) custom-call(s32[3]{0:T(128)} %pad_add_fusion.pos, ...), custom_call_target="tpu_custom_call" | custom-call | flops 1000 | bytes 1000 | tf_op jit(solution)/shard_map/feed_forward_back/pallas_call | solution.py:804
  158.5 25.2 %attend_back.2 = (bf16[512,512]{1,0:T(8,128)(2,1)}, bf16[512,512]{1,0:T(8,128)(2,1)}, bf16[512,512]{1,0:T(8,128)(2,1)}) custom-call(s32[512,1]{1,0:T(8,128)} %copy.39.page_col, s32[1,512]{1,0:T(1,128)} %bitcast.93, s32[1,512]{1,0:T(1,128)} %bitcast.97, bf16[512,768]{1,0:T(8,128)(2,1)} %get-tuple-element.117.q_hbm, ...), custom_call_target="tpu_custom_call" | custom-call | flops 1000 | bytes 1000 | tf_op jit(solution)/shard_map/attend_back/pallas_call | solution.py:844
  183.7 2.0 add_convert_fusion.3
  187.4 1.8 add_convert_fusion
  192.2 7.7 %attend_back.3 = (bf16[512,256]{1,0:T(8,128)(2,1)}, bf16[512,256]{1,0:T(8,128)(2,1)}, bf16[512,256]{1,0:T(8,128)(2,1)}) custom-call(s32[512,1]{1,0:T(8,128)} %copy.39.page_col, s32[1,512]{1,0:T(1,128)} %bitcast.94, s32[1,512]{1,0:T(1,128)} %bitcast.98, bf16[512,768]{1,0:T(8,128)(2,1)} %get-tuple-element.117.q_hbm, ...), custom_call_target="tpu_custom_call" | custom-call | flops 1000 | bytes 1000 | tf_op jit(solution)/shard_map/attend_back/pallas_call | solution.py:844
  200.0 9.8 %project_back.1 = (f32[512,768]{1,0:T(8,128)}, bf16[512,768]{1,0:T(8,128)(2,1)}, f32[8,768]{1,0:T(8,128)}, bf16[16,96,640]{2,1,0:T(8,128)(2,1)}, bf16[16,96,640]{2,1,0:T(8,128)(2,1)}) custom-call(s32[3]{0:T(128)} %pad_add_fusion.pos, f32[2,768]{1,0:T(2,128)} %pad_maximum_fusion.22.gains, bf16[512,768]{1,0:T(8,128)(2,1)} %own.1, ...), custom_call_target="tpu_custom_call" | custom-call | flops 1000 | bytes 1000 | tf_op jit(solution)/shard_map/project_back/pallas_call | solution.py:878
  209.9 5.2 %collective-permute-done.43 = bf16[8,192,384]{2,1,0:T(8,128)(2,1)} collective-permute-done((bf16[8,192,384]{2,1,0:T(8,128)(2,1)}, bf16[8,192,384]{2,1,0:T(8,128)(2,1)}, u32[]{:S(2)}, u32[]{:S(2)}) %collective-permute-start.43) | collective-permute-done | bytes 1179680 | tf_op jit(solution)/shard_map/ppermute | solution.py:23
  220.9 1.9 add_convert_fusion.7
  222.8 2.6 add_convert_fusion.4
  227.0 1.5 collective-permute-start.52
  232.1 5.4 %collective-permute-done.53 = bf16[2,96,1024]{2,1,0:T(8,128)(2,1)S(1)} collective-permute-done((bf16[2,96,1024]{2,1,0:T(8,128)(2,1)S(1)}, bf16[2,96,1024]{2,1,0:T(8,128)(2,1)S(1)}, u32[]{:S(2)}, u32[]{:S(2)}) %collective-permute-start.53) | collective-permute-done | bytes 393248 | tf_op jit(solution)/shard_map/ppermute | solution.py:23
  239.0 1.7 add_convert_fusion.13
  241.9 6.6 %collective-permute-done.46 = bf16[400,640]{1,0:T(8,128)(2,1)S(1)} collective-permute-done((bf16[400,640]{1,0:T(8,128)(2,1)S(1)}, bf16[400,640]{1,0:T(8,128)(2,1)S(1)}, u32[]{:S(2)}, u32[]{:S(2)}) %collective-permute-start.46) | collective-permute-done | bytes 512032 | tf_op jit(solution)/shard_map/ppermute | solution.py:23
  250.5 1.6 add_convert_fusion.10
  252.1 1.6 collective-permute-start.47
  255.2 6.0 %collective-permute-done.56 = bf16[4,192,384]{2,1,0:T(8,128)(2,1)} collective-permute-done((bf16[4,192,384]{2,1,0:T(8,128)(2,1)}, bf16[4,192,384]{2,1,0:T(8,128)(2,1)}, u32[]{:S(2)}, u32[]{:S(2)}) %collective-permute-start.56) | collective-permute-done | bytes 589856 | tf_op jit(solution)/shard_map/ppermute | solution.py:23
  263.4 1.5 collective-permute-start.57
  267.6 2.6 add_bitcast_fusion
  271.7 2.3 fusion.15
  278.5 1.6 fusion.8
  280.5 11.0 %collective-permute-done.58 = bf16[192,384]{1,0:T(8,128)(2,1)S(1)} collective-permute-done((bf16[192,384]{1,0:T(8,128)(2,1)}, bf16[192,384]{1,0:T(8,128)(2,1)S(1)}, u32[]{:S(2)}, u32[]{:S(2)}) %collective-permute-start.58) | collective-permute-done | bytes 147488 | tf_op jit(solution)/shard_map/ppermute | solution.py:23
  292.6 1.5 multiply_subtract_fusion
  297.4 2.3 norm_tail.1
  (349 shorter events, 63.9 us)
Async XLA Ops:
  2.3 11.6 %collective-permute-start = (bf16[96,640]{1,0:T(8,128)(2,1)S(1)}, bf16[96,640]{1,0:T(8,128)(2,1)S(1)}, u32[]{:S(2)}, u32[]{:S(2)}) collective-permute-start(bf16[96,640]{1,0:T(8,128)(2,1)S(1)} %get-tuple-element.203), channel_id=1, source_target_pairs={{0,4},{1,5},{2,6},{3,7},{4,0},{5,1},{6,2},{7,3},{8,12},{9,13},{10,... | collective-permute-start | bytes 368648 | tf_op jit(solution)/shard_map/ppermute | solution.py:23
  8.3 34.5 %collective-permute-start.17 = (bf16[96,1024]{1,0:T(8,128)(2,1)S(1)}, bf16[96,1024]{1,0:T(8,128)(2,1)S(1)}, u32[]{:S(2)}, u32[]{:S(2)}) collective-permute-start(bf16[96,1024]{1,0:T(8,128)(2,1)S(1)} %get-tuple-element.198), channel_id=1, source_target_pairs={{0,4},{1,5},{2,6},{3,7},{4,0},{5,1},{6,2},{7,3},{8,12},{9,13},{10,... | collective-permute-start | bytes 589832 | tf_op jit(solution)/shard_map/ppermute | solution.py:23
  8.9 34.6 %collective-permute-start.21 = (bf16[1,96,768]{2,1,0:T(8,128)(2,1)S(1)}, bf16[1,96,768]{2,1,0:T(8,128)(2,1)S(1)}, u32[]{:S(2)}, u32[]{:S(2)}) collective-permute-start(bf16[1,96,768]{2,1,0:T(8,128)(2,1)S(1)} %maximum_bitcast_fusion.refs_12_), channel_id=1, source_target_pairs={{0,8},{8,0},{16,24},{24,16},{1,9},{9,1},{17,25},{25,17},{2,10},{10... | collective-permute-start | bytes 442376 | tf_op jit(solution)/shard_map/ppermute | solution.py:23
  10.5 13.8 %collective-permute-start.14 = (bf16[1,96,1024]{2,1,0:T(8,128)(2,1)S(1)}, bf16[1,96,1024]{2,1,0:T(8,128)(2,1)S(1)}, u32[]{:S(2)}, u32[]{:S(2)}) collective-permute-start(bf16[1,96,1024]{2,1,0:T(8,128)(2,1)S(1)} %get-tuple-element.199.refs_0_), channel_id=1, source_target_pairs={{0,16},{8,24},{16,0},{24,8},{1,17},{9,25},{17,1},{25,9},{2,18},{10... | collective-permute-start | bytes 589832 | tf_op jit(solution)/shard_map/ppermute | solution.py:23
  14.2 11.8 %collective-permute-start.5 = (bf16[2,96,640]{2,1,0:T(8,128)(2,1)S(1)}, bf16[2,96,640]{2,1,0:T(8,128)(2,1)S(1)}, u32[]{:S(2)}, u32[]{:S(2)}) collective-permute-start(bf16[2,96,640]{2,1,0:T(8,128)(2,1)S(1)} %pad_maximum_fusion.17), channel_id=1, source_target_pairs={{0,8},{8,0},{16,24},{24,16},{1,9},{9,1},{17,25},{25,17},{2,10},{10... | collective-permute-start | bytes 737288 | tf_op jit(solution)/shard_map/ppermute | solution.py:23
  21.9 17.4 %collective-permute-start.1 = (bf16[160,768]{1,0:T(8,128)(2,1)S(1)}, bf16[160,768]{1,0:T(8,128)(2,1)S(1)}, u32[]{:S(2)}, u32[]{:S(2)}) collective-permute-start(bf16[160,768]{1,0:T(8,128)(2,1)S(1)} %get-tuple-element.81), channel_id=1, source_target_pairs={{0,4},{1,5},{2,6},{3,7},{4,0},{5,1},{6,2},{7,3},{8,12},{9,13},{10,... | collective-permute-start | bytes 737288 | tf_op jit(solution)/shard_map/ppermute | solution.py:23
  24.3 16.6 %collective-permute-start.10 = (bf16[2,96,640]{2,1,0:T(8,128)(2,1)S(1)}, bf16[2,96,640]{2,1,0:T(8,128)(2,1)S(1)}, u32[]{:S(2)}, u32[]{:S(2)}) collective-permute-start(bf16[2,96,640]{2,1,0:T(8,128)(2,1)S(1)} %pad_maximum_fusion.18), channel_id=1, source_target_pairs={{0,16},{8,24},{16,0},{24,8},{1,17},{9,25},{17,1},{25,9},{2,18},{10... | collective-permute-start | bytes 737288 | tf_op jit(solution)/shard_map/ppermute | solution.py:23
  25.9 15.4 %collective-permute-start.24 = (bf16[192,384]{1,0:T(8,128)(2,1)S(1)}, bf16[192,384]{1,0:T(8,128)(2,1)S(1)}, u32[]{:S(2)}, u32[]{:S(2)}) collective-permute-start(bf16[192,384]{1,0:T(8,128)(2,1)S(1)} %slice_bitcast_fusion), channel_id=1, source_target_pairs={{0,4},{1,5},{2,6},{3,7},{4,0},{5,1},{6,2},{7,3},{8,12},{9,13},{10,... | collective-permute-start | bytes 442376 | tf_op jit(solution)/shard_map/ppermute | solution.py:23
  39.3 18.3 %collective-permute-start.6 = (bf16[4,96,640]{2,1,0:T(8,128)(2,1)S(1)}, bf16[4,96,640]{2,1,0:T(8,128)(2,1)S(1)}, u32[]{:S(2)}, u32[]{:S(2)}) collective-permute-start(bf16[4,96,640]{2,1,0:T(8,128)(2,1)S(1)} %pad_maximum_fusion.7), channel_id=1, source_target_pairs={{0,16},{8,24},{16,0},{24,8},{1,17},{9,25},{17,1},{25,9},{2,18},{10... | collective-permute-start | bytes 1474568 | tf_op jit(solution)/shard_map/ppermute | solution.py:23
  40.8 14.2 %collective-permute-start.2 = (bf16[192,768]{1,0:T(8,128)(2,1)S(1)}, bf16[192,768]{1,0:T(8,128)(2,1)}, u32[]{:S(2)}, u32[]{:S(2)}) collective-permute-start(bf16[192,768]{1,0:T(8,128)(2,1)S(1)} %slice.520), channel_id=1, source_target_pairs={{0,4},{1,5},{2,6},{3,7},{4,0},{5,1},{6,2},{7,3},{8,12},{9,13},{10,... | collective-permute-start | bytes 884744 | tf_op jit(solution)/shard_map/ppermute | solution.py:23
  41.3 20.7 %collective-permute-start.11 = (bf16[4,96,640]{2,1,0:T(8,128)(2,1)S(1)}, bf16[4,96,640]{2,1,0:T(8,128)(2,1)}, u32[]{:S(2)}, u32[]{:S(2)}) collective-permute-start(bf16[4,96,640]{2,1,0:T(8,128)(2,1)S(1)} %pad_maximum_fusion.8), channel_id=1, source_target_pairs={{0,8},{8,0},{16,24},{24,16},{1,9},{9,1},{17,25},{25,17},{2,10},{10... | collective-permute-start | bytes 1474568 | tf_op jit(solution)/shard_map/ppermute | solution.py:23
  42.9 20.7 %collective-permute-start.15 = (bf16[2,96,1024]{2,1,0:T(8,128)(2,1)S(1)}, bf16[2,96,1024]{2,1,0:T(8,128)(2,1)S(1)}, u32[]{:S(2)}, u32[]{:S(2)}) collective-permute-start(bf16[2,96,1024]{2,1,0:T(8,128)(2,1)S(1)} %pad_maximum_fusion.9), channel_id=1, source_target_pairs={{0,8},{8,0},{16,24},{24,16},{1,9},{9,1},{17,25},{25,17},{2,10},{10... | collective-permute-start | bytes 1179656 | tf_op jit(solution)/shard_map/ppermute | solution.py:23
  43.5 14.1 %collective-permute-start.18 = (bf16[1,96,1024]{2,1,0:T(8,128)(2,1)S(1)}, bf16[1,96,1024]{2,1,0:T(8,128)(2,1)S(1)}, u32[]{:S(2)}, u32[]{:S(2)}) collective-permute-start(bf16[1,96,1024]{2,1,0:T(8,128)(2,1)S(1)} %bitcast.79), channel_id=1, source_target_pairs={{0,2},{1,3},{2,0},{3,1},{4,6},{5,7},{6,4},{7,5},{8,10},{9,11},{10,... | collective-permute-start | bytes 589832 | tf_op jit(solution)/shard_map/ppermute | solution.py:23
  55.0 8.6 %collective-permute-start.25 = (bf16[1,96,768]{2,1,0:T(8,128)(2,1)S(1)}, bf16[1,96,768]{2,1,0:T(8,128)(2,1)S(1)}, u32[]{:S(2)}, u32[]{:S(2)}) collective-permute-start(bf16[1,96,768]{2,1,0:T(8,128)(2,1)S(1)} %maximum_bitcast_fusion.1.refs_18_), channel_id=1, source_target_pairs={{0,2},{1,3},{2,0},{3,1},{4,6},{5,7},{6,4},{7,5},{8,10},{9,11},{10,... | collective-permute-start | bytes 442376 | tf_op jit(solution)/shard_map/ppermute | solution.py:23
  57.6 14.1 %collective-permute-start.22 = (bf16[2,96,768]{2,1,0:T(8,128)(2,1)S(1)}, bf16[2,96,768]{2,1,0:T(8,128)(2,1)S(1)}, u32[]{:S(2)}, u32[]{:S(2)}) collective-permute-start(bf16[2,96,768]{2,1,0:T(8,128)(2,1)S(1)} %pad_maximum_fusion.12), channel_id=1, source_target_pairs={{0,2},{1,3},{2,0},{3,1},{4,6},{5,7},{6,4},{7,5},{8,10},{9,11},{10,... | collective-permute-start | bytes 884744 | tf_op jit(solution)/shard_map/ppermute | solution.py:23
  57.6 11.6 %collective-permute-start.3 = (bf16[160,768]{1,0:T(8,128)(2,1)S(1)}, bf16[160,768]{1,0:T(8,128)(2,1)S(1)}, u32[]{:S(2)}, u32[]{:S(2)}) collective-permute-start(bf16[160,768]{1,0:T(8,128)(2,1)S(1)} %get-tuple-element.83), channel_id=1, source_target_pairs={{0,4},{1,5},{2,6},{3,7},{4,0},{5,1},{6,2},{7,3},{8,12},{9,13},{10,... | collective-permute-start | bytes 737288 | tf_op jit(solution)/shard_map/ppermute | solution.py:23
  62.0 10.6 %collective-permute-start.19 = (bf16[2,96,1024]{2,1,0:T(8,128)(2,1)S(1)}, bf16[2,96,1024]{2,1,0:T(8,128)(2,1)S(1)}, u32[]{:S(2)}, u32[]{:S(2)}) collective-permute-start(bf16[2,96,1024]{2,1,0:T(8,128)(2,1)S(1)} %pad_maximum_fusion.10), channel_id=1, source_target_pairs={{0,8},{8,0},{16,24},{24,16},{1,9},{9,1},{17,25},{25,17},{2,10},{10... | collective-permute-start | bytes 1179656 | tf_op jit(solution)/shard_map/ppermute | solution.py:23
  63.6 10.6 %collective-permute-start.7 = (bf16[4,96,640]{2,1,0:T(8,128)(2,1)S(1)}, bf16[4,96,640]{2,1,0:T(8,128)(2,1)S(1)}, u32[]{:S(2)}, u32[]{:S(2)}) collective-permute-start(bf16[4,96,640]{2,1,0:T(8,128)(2,1)S(1)} %pad_maximum_fusion.7), channel_id=1, source_target_pairs={{0,1},{1,0},{2,3},{3,2},{4,5},{5,4},{6,7},{7,6},{8,9},{9,8},{10,11... | collective-permute-start | bytes 1474568 | tf_op jit(solution)/shard_map/ppermute | solution.py:23
  63.6 13.8 %collective-permute-start.12 = (bf16[4,96,640]{2,1,0:T(8,128)(2,1)S(1)}, bf16[4,96,640]{2,1,0:T(8,128)(2,1)S(1)}, u32[]{:S(2)}, u32[]{:S(2)}) collective-permute-start(bf16[4,96,640]{2,1,0:T(8,128)(2,1)S(1)} %pad_maximum_fusion.8), channel_id=1, source_target_pairs={{0,1},{1,0},{2,3},{3,2},{4,5},{5,4},{6,7},{7,6},{8,9},{9,8},{10,11... | collective-permute-start | bytes 1474568 | tf_op jit(solution)/shard_map/ppermute | solution.py:23
  71.7 12.7 %collective-permute-start.16 = (bf16[4,96,1024]{2,1,0:T(8,128)(2,1)}, bf16[4,96,1024]{2,1,0:T(8,128)(2,1)}, u32[]{:S(2)}, u32[]{:S(2)}) collective-permute-start(bf16[4,96,1024]{2,1,0:T(8,128)(2,1)} %pad_maximum_fusion.1), channel_id=1, source_target_pairs={{0,1},{1,0},{2,3},{3,2},{4,5},{5,4},{6,7},{7,6},{8,9},{9,8},{10,11... | collective-permute-start | bytes 2359304 | tf_op jit(solution)/shard_map/ppermute | solution.py:23
  76.6 9.9 %collective-permute-start.20 = (bf16[4,96,1024]{2,1,0:T(8,128)(2,1)}, bf16[4,96,1024]{2,1,0:T(8,128)(2,1)S(1)}, u32[]{:S(2)}, u32[]{:S(2)}) collective-permute-start(bf16[4,96,1024]{2,1,0:T(8,128)(2,1)} %pad_maximum_fusion.2), channel_id=1, source_target_pairs={{0,1},{1,0},{2,3},{3,2},{4,5},{5,4},{6,7},{7,6},{8,9},{9,8},{10,11... | collective-permute-start | bytes 2359304 | tf_op jit(solution)/shard_map/ppermute | solution.py:23
  77.5 8.5 %collective-permute-start.27 = (bf16[4,96,768]{2,1,0:T(8,128)(2,1)}, bf16[4,96,768]{2,1,0:T(8,128)(2,1)S(1)}, u32[]{:S(2)}, u32[]{:S(2)}) collective-permute-start(bf16[4,96,768]{2,1,0:T(8,128)(2,1)} %pad_maximum_fusion.4), channel_id=1, source_target_pairs={{0,1},{1,0},{2,3},{3,2},{4,5},{5,4},{6,7},{7,6},{8,9},{9,8},{10,11... | collective-permute-start | bytes 1769480 | tf_op jit(solution)/shard_map/ppermute | solution.py:23
  78.0 10.8 %collective-permute-start.13 = (bf16[4,96,640]{2,1,0:T(8,128)(2,1)}, bf16[4,96,640]{2,1,0:T(8,128)(2,1)}, u32[]{:S(2)}, u32[]{:S(2)}) collective-permute-start(bf16[4,96,640]{2,1,0:T(8,128)(2,1)} %collective-permute-done.11.refs_12_), channel_id=1, source_target_pairs={{0,1},{1,0},{2,3},{3,2},{4,5},{5,4},{6,7},{7,6},{8,9},{9,8},{10,11... | collective-permute-start | bytes 1474568 | tf_op jit(solution)/shard_map/ppermute | solution.py:23
  78.1 38.8 %collective-permute-start.29 = (bf16[4,96,1024]{2,1,0:T(8,128)(2,1)}, bf16[4,96,1024]{2,1,0:T(8,128)(2,1)}, u32[]{:S(2)}, u32[]{:S(2)}) collective-permute-start(bf16[4,96,1024]{2,1,0:T(8,128)(2,1)} %pad_maximum_fusion.1), channel_id=1, source_target_pairs={{0,2},{1,3},{2,0},{3,1},{4,6},{5,7},{6,4},{7,5},{8,10},{9,11},{10,... | collective-permute-start | bytes 2359304 | tf_op jit(solution)/shard_map/ppermute | solution.py:23
  84.4 32.6 %collective-permute-start.30 = (bf16[4,96,1024]{2,1,0:T(8,128)(2,1)}, bf16[4,96,1024]{2,1,0:T(8,128)(2,1)}, u32[]{:S(2)}, u32[]{:S(2)}) collective-permute-start(bf16[4,96,1024]{2,1,0:T(8,128)(2,1)} %pad_maximum_fusion.2), channel_id=1, source_target_pairs={{0,16},{8,24},{16,0},{24,8},{1,17},{9,25},{17,1},{25,9},{2,18},{10... | collective-permute-start | bytes 2359304 | tf_op jit(solution)/shard_map/ppermute | solution.py:23
  85.9 31.0 %collective-permute-start.31 = (bf16[4,96,768]{2,1,0:T(8,128)(2,1)}, bf16[4,96,768]{2,1,0:T(8,128)(2,1)}, u32[]{:S(2)}, u32[]{:S(2)}) collective-permute-start(bf16[4,96,768]{2,1,0:T(8,128)(2,1)} %pad_maximum_fusion.3), channel_id=1, source_target_pairs={{0,16},{8,24},{16,0},{24,8},{1,17},{9,25},{17,1},{25,9},{2,18},{10... | collective-permute-start | bytes 1769480 | tf_op jit(solution)/shard_map/ppermute | solution.py:23
  86.5 30.5 %collective-permute-start.32 = (bf16[4,96,768]{2,1,0:T(8,128)(2,1)}, bf16[4,96,768]{2,1,0:T(8,128)(2,1)}, u32[]{:S(2)}, u32[]{:S(2)}) collective-permute-start(bf16[4,96,768]{2,1,0:T(8,128)(2,1)} %pad_maximum_fusion.4), channel_id=1, source_target_pairs={{0,8},{8,0},{16,24},{24,16},{1,9},{9,1},{17,25},{25,17},{2,10},{10... | collective-permute-start | bytes 1769480 | tf_op jit(solution)/shard_map/ppermute | solution.py:23
  88.8 28.1 %collective-permute-start.28 = (bf16[256,768]{1,0:T(8,128)(2,1)}, bf16[256,768]{1,0:T(8,128)(2,1)S(1)}, u32[]{:S(2)}, u32[]{:S(2)}) collective-permute-start(bf16[256,768]{1,0:T(8,128)(2,1)} %convert_element_type.435), channel_id=1, source_target_pairs={{0,4},{1,5},{2,6},{3,7},{4,0},{5,1},{6,2},{7,3},{8,12},{9,13},{10,... | collective-permute-start | bytes 1179656 | tf_op jit(solution)/shard_map/ppermute | solution.py:23
  156.5 29.3 %collective-permute-start.38 = (bf16[16,96,1024]{2,1,0:T(8,128)(2,1)}, bf16[16,96,1024]{2,1,0:T(8,128)(2,1)S(1)}, u32[]{:S(2)}, u32[]{:S(2)}) collective-permute-start(bf16[16,96,1024]{2,1,0:T(8,128)(2,1)} %get-tuple-element.115), channel_id=1, source_target_pairs={{0,1},{1,0},{2,3},{3,2},{4,5},{5,4},{6,7},{7,6},{8,9},{9,8},{10,11... | collective-permute-start | bytes 9437192 | tf_op jit(solution)/shard_map/ppermute | solution.py:23
  156.7 27.0 %collective-permute-start.39 = (bf16[16,192,384]{2,1,0:T(8,128)(2,1)}, bf16[16,192,384]{2,1,0:T(8,128)(2,1)}, u32[]{:S(2)}, u32[]{:S(2)}) collective-permute-start(bf16[16,192,384]{2,1,0:T(8,128)(2,1)} %get-tuple-element.116), channel_id=1, source_target_pairs={{0,1},{1,0},{2,3},{3,2},{4,5},{5,4},{6,7},{7,6},{8,9},{9,8},{10,11... | collective-permute-start | bytes 7077896 | tf_op jit(solution)/shard_map/ppermute | solution.py:23
  157.0 28.7 %collective-permute-start.37 = (bf16[256,768]{1,0:T(8,128)(2,1)}, bf16[256,768]{1,0:T(8,128)(2,1)S(1)}, u32[]{:S(2)}, u32[]{:S(2)}) collective-permute-start(bf16[256,768]{1,0:T(8,128)(2,1)} %get-tuple-element.105), channel_id=1, source_target_pairs={{0,4},{1,5},{2,6},{3,7},{4,0},{5,1},{6,2},{7,3},{8,12},{9,13},{10,... | collective-permute-start | bytes 1179656 | tf_op jit(solution)/shard_map/ppermute | solution.py:23
  187.0 28.1 %collective-permute-start.43 = (bf16[8,192,384]{2,1,0:T(8,128)(2,1)}, bf16[8,192,384]{2,1,0:T(8,128)(2,1)}, u32[]{:S(2)}, u32[]{:S(2)}) collective-permute-start(bf16[8,192,384]{2,1,0:T(8,128)(2,1)} %pad_maximum_fusion), channel_id=1, source_target_pairs={{0,2},{1,3},{2,0},{3,1},{4,6},{5,7},{6,4},{7,5},{8,10},{9,11},{10,... | collective-permute-start | bytes 3538952 | tf_op jit(solution)/shard_map/ppermute | solution.py:23
  189.2 20.6 %collective-permute-start.42 = (bf16[4,96,1024]{2,1,0:T(8,128)(2,1)}, bf16[4,96,1024]{2,1,0:T(8,128)(2,1)S(1)}, u32[]{:S(2)}, u32[]{:S(2)}) collective-permute-start(bf16[4,96,1024]{2,1,0:T(8,128)(2,1)} %get-tuple-element.128), channel_id=1, source_target_pairs={{0,16},{8,24},{16,0},{24,8},{1,17},{9,25},{17,1},{25,9},{2,18},{10... | collective-permute-start | bytes 2359304 | tf_op jit(solution)/shard_map/ppermute | solution.py:23
  190.7 19.1 %collective-permute-start.41 = (bf16[4,96,1024]{2,1,0:T(8,128)(2,1)}, bf16[4,96,1024]{2,1,0:T(8,128)(2,1)}, u32[]{:S(2)}, u32[]{:S(2)}) collective-permute-start(bf16[4,96,1024]{2,1,0:T(8,128)(2,1)} %get-tuple-element.127), channel_id=1, source_target_pairs={{0,8},{8,0},{16,24},{24,16},{1,9},{9,1},{17,25},{25,17},{2,10},{10... | collective-permute-start | bytes 2359304 | tf_op jit(solution)/shard_map/ppermute | solution.py:23
  218.6 77.7 %collective-permute-start.40 = (bf16[512,768]{1,0:T(8,128)(2,1)}, bf16[512,768]{1,0:T(8,128)(2,1)S(1)}, u32[]{:S(2)}, u32[]{:S(2)}) collective-permute-start(bf16[512,768]{1,0:T(8,128)(2,1)} %get-tuple-element.122), channel_id=1, source_target_pairs={{0,4},{1,5},{2,6},{3,7},{4,0},{5,1},{6,2},{7,3},{8,12},{9,13},{10,... | collective-permute-start | bytes 2359304 | tf_op jit(solution)/shard_map/ppermute | solution.py:23
  225.5 12.0 %collective-permute-start.53 = (bf16[2,96,1024]{2,1,0:T(8,128)(2,1)S(1)}, bf16[2,96,1024]{2,1,0:T(8,128)(2,1)S(1)}, u32[]{:S(2)}, u32[]{:S(2)}) collective-permute-start(bf16[2,96,1024]{2,1,0:T(8,128)(2,1)S(1)} %get-tuple-element.137), channel_id=1, source_target_pairs={{0,8},{8,0},{16,24},{24,16},{1,9},{9,1},{17,25},{25,17},{2,10},{10... | collective-permute-start | bytes 1179656 | tf_op jit(solution)/shard_map/ppermute | solution.py:23
  227.0 12.1 %collective-permute-start.52 = (bf16[2,96,1024]{2,1,0:T(8,128)(2,1)S(1)}, bf16[2,96,1024]{2,1,0:T(8,128)(2,1)S(1)}, u32[]{:S(2)}, u32[]{:S(2)}) collective-permute-start(bf16[2,96,1024]{2,1,0:T(8,128)(2,1)S(1)} %get-tuple-element.136), channel_id=1, source_target_pairs={{0,16},{8,24},{16,0},{24,8},{1,17},{9,25},{17,1},{25,9},{2,18},{10... | collective-permute-start | bytes 1179656 | tf_op jit(solution)/shard_map/ppermute | solution.py:23
  230.0 20.5 %collective-permute-start.48 = (bf16[4,96,640]{2,1,0:T(8,128)(2,1)}, bf16[4,96,640]{2,1,0:T(8,128)(2,1)}, u32[]{:S(2)}, u32[]{:S(2)}) collective-permute-start(bf16[4,96,640]{2,1,0:T(8,128)(2,1)} %get-tuple-element.192), channel_id=1, source_target_pairs={{0,16},{8,24},{16,0},{24,8},{1,17},{9,25},{17,1},{25,9},{2,18},{10... | collective-permute-start | bytes 1474568 | tf_op jit(solution)/shard_map/ppermute | solution.py:23
  230.6 17.9 %collective-permute-start.46 = (bf16[400,640]{1,0:T(8,128)(2,1)S(1)}, bf16[400,640]{1,0:T(8,128)(2,1)S(1)}, u32[]{:S(2)}, u32[]{:S(2)}) collective-permute-start(bf16[400,640]{1,0:T(8,128)(2,1)S(1)} %pad_maximum_fusion.6), channel_id=1, source_target_pairs={{0,8},{8,0},{16,24},{24,16},{1,9},{9,1},{17,25},{25,17},{2,10},{10... | collective-permute-start | bytes 1536008 | tf_op jit(solution)/shard_map/ppermute | solution.py:23
  237.5 23.7 %collective-permute-start.56 = (bf16[4,192,384]{2,1,0:T(8,128)(2,1)}, bf16[4,192,384]{2,1,0:T(8,128)(2,1)}, u32[]{:S(2)}, u32[]{:S(2)}) collective-permute-start(bf16[4,192,384]{2,1,0:T(8,128)(2,1)} %pad_maximum_fusion.5), channel_id=1, source_target_pairs={{0,8},{8,0},{16,24},{24,16},{1,9},{9,1},{17,25},{25,17},{2,10},{10... | collective-permute-start | bytes 1769480 | tf_op jit(solution)/shard_map/ppermute | solution.py:23
  241.5 26.1 %collective-permute-start.54 = (bf16[2,96,1024]{2,1,0:T(8,128)(2,1)}, bf16[2,96,1024]{2,1,0:T(8,128)(2,1)}, u32[]{:S(2)}, u32[]{:S(2)}) collective-permute-start(bf16[2,96,1024]{2,1,0:T(8,128)(2,1)} %pad_maximum_fusion.11), channel_id=1, source_target_pairs={{0,2},{1,3},{2,0},{3,1},{4,6},{5,7},{6,4},{7,5},{8,10},{9,11},{10,... | collective-permute-start | bytes 1179656 | tf_op jit(solution)/shard_map/ppermute | solution.py:23
  252.1 12.8 %collective-permute-start.47 = (bf16[208,640]{1,0:T(8,128)(2,1)S(1)}, bf16[208,640]{1,0:T(8,128)(2,1)S(1)}, u32[]{:S(2)}, u32[]{:S(2)}) collective-permute-start(bf16[208,640]{1,0:T(8,128)(2,1)S(1)} %pad_maximum_fusion.15), channel_id=1, source_target_pairs={{0,16},{8,24},{16,0},{24,8},{1,17},{9,25},{17,1},{25,9},{2,18},{10... | collective-permute-start | bytes 798728 | tf_op jit(solution)/shard_map/ppermute | solution.py:23
  253.7 11.9 %collective-permute-start.49 = (bf16[2,96,640]{2,1,0:T(8,128)(2,1)S(1)}, bf16[2,96,640]{2,1,0:T(8,128)(2,1)}, u32[]{:S(2)}, u32[]{:S(2)}) collective-permute-start(bf16[2,96,640]{2,1,0:T(8,128)(2,1)S(1)} %get-tuple-element.190), channel_id=1, source_target_pairs={{0,8},{8,0},{16,24},{24,16},{1,9},{9,1},{17,25},{25,17},{2,10},{10... | collective-permute-start | bytes 737288 | tf_op jit(solution)/shard_map/ppermute | solution.py:23
  263.4 8.3 %collective-permute-start.57 = (bf16[2,192,384]{2,1,0:T(8,128)(2,1)}, bf16[2,192,384]{2,1,0:T(8,128)(2,1)}, u32[]{:S(2)}, u32[]{:S(2)}) collective-permute-start(bf16[2,192,384]{2,1,0:T(8,128)(2,1)} %pad_maximum_fusion.14), channel_id=1, source_target_pairs={{0,16},{8,24},{16,0},{24,8},{1,17},{9,25},{17,1},{25,9},{2,18},{10... | collective-permute-start | bytes 884744 | tf_op jit(solution)/shard_map/ppermute | solution.py:23
  267.2 9.7 %collective-permute-start.50 = (bf16[208,640]{1,0:T(8,128)(2,1)S(1)}, bf16[208,640]{1,0:T(8,128)(2,1)S(1)}, u32[]{:S(2)}, u32[]{:S(2)}) collective-permute-start(bf16[208,640]{1,0:T(8,128)(2,1)S(1)} %pad_maximum_fusion.16), channel_id=1, source_target_pairs={{0,2},{1,3},{2,0},{3,1},{4,6},{5,7},{6,4},{7,5},{8,10},{9,11},{10,... | collective-permute-start | bytes 798728 | tf_op jit(solution)/shard_map/ppermute | solution.py:23
  270.2 21.3 %collective-permute-start.55 = (bf16[96,1024]{1,0:T(8,128)(2,1)}, bf16[96,1024]{1,0:T(8,128)(2,1)}, u32[]{:S(2)}, u32[]{:S(2)}) collective-permute-start(bf16[96,1024]{1,0:T(8,128)(2,1)} %get-tuple-element.173), channel_id=1, source_target_pairs={{0,4},{1,5},{2,6},{3,7},{4,0},{5,1},{6,2},{7,3},{8,12},{9,13},{10,... | collective-permute-start | bytes 589832 | tf_op jit(solution)/shard_map/ppermute | solution.py:23
  273.9 17.5 %collective-permute-start.58 = (bf16[192,384]{1,0:T(8,128)(2,1)}, bf16[192,384]{1,0:T(8,128)(2,1)S(1)}, u32[]{:S(2)}, u32[]{:S(2)}) collective-permute-start(bf16[192,384]{1,0:T(8,128)(2,1)} %get-tuple-element.170), channel_id=1, source_target_pairs={{0,4},{1,5},{2,6},{3,7},{4,0},{5,1},{6,2},{7,3},{8,12},{9,13},{10,... | collective-permute-start | bytes 442376 | tf_op jit(solution)/shard_map/ppermute | solution.py:23
  280.2 20.7 %collective-permute-start.51 = (bf16[112,640]{1,0:T(8,128)(2,1)S(1)}, bf16[112,640]{1,0:T(8,128)(2,1)S(1)}, u32[]{:S(2)}, u32[]{:S(2)}) collective-permute-start(bf16[112,640]{1,0:T(8,128)(2,1)S(1)} %pad_maximum_fusion.21), channel_id=1, source_target_pairs={{0,4},{1,5},{2,6},{3,7},{4,0},{5,1},{6,2},{7,3},{8,12},{9,13},{10,... | collective-permute-start | bytes 430088 | tf_op jit(solution)/shard_map/ppermute | solution.py:23
  (96 other events, 1071.6 us)

commit v5 on v4

--- a/solution.py
+++ b/solution.py
@@ -1,4 +1,5 @@
 import functools
+import math
 
 import jax
 import jax.numpy as jnp
@@ -84,23 +85,29 @@
     return high, lax.reduce_precision(value - high, 8, 7)
 
 
+def rider_rows(value, lanes):
+    rows, width = value.shape
+    runs = [value[:, i : i + lanes] for i in range(0, width, lanes)]
+    runs = [jnp.pad(run, ((0, -rows % 8), (0, lanes - run.shape[1]))) for run in runs]
+    return jnp.concatenate(runs, axis=0)
+
+
+def rider_value(laid, shape):
+    rows, width = shape
+    high = rows + -rows % 8
+    runs = [laid[i * high : i * high + rows] for i in range(laid.shape[0] // high)]
+    return jnp.concatenate(runs, axis=1)[:, :width]
+
+
 def with_rider(value, rider):
     lanes = value.shape[-1]
-    rows = -(-rider.size // lanes)
-    flat = [jnp.pad(part.reshape(-1), (0, rows * lanes - rider.size)) for part in halves_of(rider)]
-    tail = jnp.concatenate(flat).astype(LOW).reshape(2 * rows, lanes)
-    tail = jnp.pad(tail, ((0, -(2 * rows) % 16), (0, 0)))
-    return jnp.concatenate((value.reshape(-1, lanes), tail), axis=0)
+    tail = [part.astype(LOW) for part in halves_of(rider)]
+    return jnp.concatenate((value.reshape(-1, lanes), *tail), axis=0)
 
 
 def rider_of(message, shape, value_shape):
-    count = value_shape[0] * value_shape[1]
-    lanes = message.shape[-1]
-    rows = -(-(shape[0] * shape[1]) // lanes)
-    parts = [
-        message[count + i * rows : count + (i + 1) * rows].reshape(-1)[: shape[0] * shape[1]].reshape(shape)
-        for i in (0, 1)
-    ]
+    count, rows = math.prod(value_shape[:-1]), shape[0]
+    parts = message[count : count + rows], message[count + rows :]
     return message[:count].reshape(value_shape), parts[0].astype(FULL) + parts[1].astype(FULL)
 
 
@@ -111,51 +118,63 @@
 
 class Halving:
     def __init__(self, kept, sent, steps):
-        self.slots, self.sent, self.steps = split(kept), sent, steps
-        self.step, self.last = 0, ()
-        self.slots = [[half] for half in self.slots]
-        self.outgoing = [None, None]
+        self.slots, self.sent, self.steps = [[half] for half in split(kept)], sent, steps
+        self.step, self.last, self.messages, self.waits = 0, (), (), ()
         self.rider = None
+
+    def left(self):
+        return self.step < len(self.steps)
+
+    def hold(self, *others):
+        self.waits = self.waits + others
 
     def carry(self, value, axis, mask):
         if self.rider is None or self.step == 0:
+            self.messages += (value,)
             return flip(value, axis, mask)
-        message = flip(with_rider(value, self.rider), axis, mask)
+        message = with_rider(value, self.rider)
+        self.messages += (message,)
+        message = flip(message, axis, mask)
         value, rider = rider_of(message, self.rider.shape, value.shape)
         self.rider = kept_rider(self.rider) + rider
         return value
 
-    def left(self):
-        return self.step < len(self.steps)
-
-    def hold(self, *others):
+    def part_sums(self):
+        outgoing = []
+        for slot, parts in enumerate(self.slots):
+            if self.waits:
+                parts = parts[:-1] + [after(parts[-1], *self.waits)]
+            half = parts[0].shape[0] // 2
+            outgoing.append(sum(part[half:].astype(FULL) for part in parts).astype(LOW))
+            self.slots[slot] = [part[:half] for part in parts]
+        return outgoing
+
+    def send(self, *others):
+        one, two = self.steps[self.step]
+        self.messages = ()
         if self.step == 0:
-            self.sent = after(self.sent, *others)
-        elif self.left():
-            self.outgoing = [after(value, *others) for value in self.outgoing]
-
-    def send(self):
-        one, two = self.steps[self.step]
+            whole = after(self.sent, *self.waits) if self.waits else self.sent
+        else:
+            outgoing = self.part_sums()
+            if others:
+                outgoing = [after(value, *others) for value in outgoing]
+            whole = jnp.concatenate(outgoing, axis=0) if one == two else None
         if one == two:
-            whole = self.sent if self.step == 0 else jnp.concatenate(self.outgoing, axis=0)
             arrived = self.carry(whole, *one)
             self.last = (arrived,)
             arrived = split(arrived)
         else:
-            arrived = [self.carry(self.outgoing[0], *one), flip(self.outgoing[1], *two)]
+            arrived = [self.carry(outgoing[0], *one), flip(outgoing[1], *two)]
+            self.messages += (outgoing[1],)
             self.last = tuple(arrived)
         self.slots = [parts + [new] for parts, new in zip(self.slots, arrived)]
-        self.step += 1
-        if self.left():
-            for slot, parts in enumerate(self.slots):
-                half = parts[0].shape[0] // 2
-                self.outgoing[slot] = sum(part[half:].astype(FULL) for part in parts).astype(LOW)
-                self.slots[slot] = [part[:half] for part in parts]
+        self.step, self.waits = self.step + 1, ()
 
     def total(self):
         while self.left():
             self.send()
-        return tuple(sum(part[0].astype(FULL) for part in parts) for parts in self.slots)
+        slots = [parts[:-1] + [after(parts[-1], *self.waits)] if self.waits else parts for parts in self.slots]
+        return tuple(sum(part[0].astype(FULL) for part in parts) for parts in slots)
 
 
 def split(value):
@@ -467,7 +486,7 @@
         acc[part, :] = middle + valid * acc[part, :]
         unit, scale = normed(middle)
         grad = dacc[part, :]
-        dgain_ref[0:1, :] += jnp.sum(grad * unit, axis=0, keepdims=True)
+        dgain_ref[pl.ds(2 + pos[2], 1), :] += jnp.sum(grad * unit, axis=0, keepdims=True)
         dmid = cot[part, :] + norm_back(grad, unit, scale, gain[...])
         dacc[part, :] = dmid
         dbranch[part, :] = (dmid * valid).astype(LOW)
@@ -608,11 +627,11 @@
     for i in range(parts):
         part = pl.ds(i * CHUNK, CHUNK)
         unit, _ = normed(own[part, :].astype(FULL))
-        dgain_ref[0:1, :] += jnp.sum(own_ref[part, :] * unit, axis=0, keepdims=True)
+        dgain_ref[pl.ds(pos[2], 1), :] += jnp.sum(own_ref[part, :] * unit, axis=0, keepdims=True)
         unit, _ = normed(other[part, :].astype(FULL))
         value = flat[part, :]
         oth_ref[part, :] = value.astype(LOW)
-        dgain_ref[1:2, :] += jnp.sum(value * unit, axis=0, keepdims=True)
+        dgain_ref[pl.ds(1 - pos[2], 1), :] += jnp.sum(value * unit, axis=0, keepdims=True)
     finish(own_ref, own_out, sems.at[0])
     for target in targets:
         wait_whole(target, sem)
@@ -693,6 +712,16 @@
     def folded(unit):
         return jnp.concatenate([unit[i * piece_rows : (i + 1) * piece_rows] for i in range(folds)], axis=-1)
 
+    page_col, page_row = page[:, None], page[None, :]
+    mask_row = key_mask[None, :]
+    gain_own = lax.dynamic_index_in_dim(gains, stream, 0, keepdims=True)
+    gain_oth = lax.dynamic_index_in_dim(gains, 1 - stream, 0, keepdims=True)
+    gain_one = jnp.concatenate((gain_own, gain_oth), axis=0)
+    gain_two = lax.dynamic_index_in_dim(gains, 2 + stream, 0, keepdims=True)
+    mix = jax.nn.sigmoid(gains[4])[None, :]
+    coef = jnp.where(is_text, mix, 1.0 - mix)
+
+    cot_low = cot_joined.astype(LOW)
     unit_a_oth = swap(unit_a[1])
     unit_b_oth = swap(after(unit_b[1], unit_a_oth)) if FIRST_A else swap(unit_b[1])
     if downs.aligned:
@@ -703,7 +732,7 @@
     zxy, zyx = along_z + along_x + along_y, along_z + along_y + along_x
     a_own, a_oth = Doubling(unit_a[0], 0, zxy), Doubling(unit_a_oth, 1, zyx)
     b_own = Doubling(unit_b[0], 0, along_y + along_x + along_z)
-    c_own = Doubling(folded(unit_c[0]), 0, along_x + along_z + along_y)
+    c_own = Doubling(folded(unit_c[0]), 0, along_y + along_z + along_x)
     b_oth, c_oth = Doubling(unit_b_oth, 1, zxy), Doubling(folded(unit_c_oth), 1, zyx)
     steps_y, steps_x = len(along_y), len(along_x)
     chunks, begin = [], 0
@@ -713,7 +742,7 @@
         begin += size
     for _ in range(steps_y):
         b_own.send()
-    for _ in range(steps_x):
+    for _ in range(steps_y):
         c_own.send()
     for _ in range(steps_x):
         b_own.send(unit_a_oth)
@@ -725,7 +754,7 @@
     rest = (a_oth.arrays[-1], a_own.arrays[-1])
     for one in (b_oth, c_oth):
         for _ in along_z:
-            one.send(*first)
+            one.send(*first, page_col, gain_one, gain_two, coef, cot_low)
     met = b_oth.last + c_oth.last
     for one in (b_own, c_own):
         while one.step < len(one.order):
@@ -747,16 +776,7 @@
         early, late = one.split_newest()
         passed.append(one.add(after(early[0], chunks[-1]), early[1], *core[0]))
         waiting.append((one, *late))
-    other_joined = swap(after(cot_joined.astype(LOW), chunks[-1], *passed))
-
-    page_col, page_row = page[:, None], page[None, :]
-    mask_row = key_mask[None, :]
-    gain_own = lax.dynamic_index_in_dim(gains, stream, 0, keepdims=True)
-    gain_oth = lax.dynamic_index_in_dim(gains, 1 - stream, 0, keepdims=True)
-    gain_one = jnp.concatenate((gain_own, gain_oth), axis=0)
-    gain_two = lax.dynamic_index_in_dim(gains, 2 + stream, 0, keepdims=True)
-    mix = jax.nn.sigmoid(gains[4])[None, :]
-    coef = jnp.where(is_text, mix, 1.0 - mix)
+    other_joined = swap(after(cot_low, chunks[-1], *passed))
 
     low_rows = jax.ShapeDtypeStruct((length, width), LOW)
     full_rows = jax.ShapeDtypeStruct((length, width), FULL)
@@ -794,7 +814,7 @@
     counts = len(b_own.arrays) + len(b_oth.arrays)
     xy, yx = along_x + along_y, along_y + along_x
     steps_b = [core * 2, *zip(xy, yx), *((step, step) for step in along_z)]
-    steps_c = [core * 2, *((step, step) for step in along_z + xy)]
+    steps_c = [core * 2, *((step, step) for step in along_z), *zip(xy, yx)]
     sums_of = [tuple(sum_codes([pair[slot] for pair in steps]) for slot in (0, 1)) for steps in (steps_b, steps_c)]
     sent_count = len(sums_of[0][0])
     block = 6 * LANES
@@ -866,10 +886,10 @@
     grads_one = attend_back(cuts[:2], queries, keys, values, attended, attended_grad, lse)
     met = (*sums_b.last, *sums_c.last, partner_rows)
     second = after(queries, grads_one[0], *met)
-    sums_b.hold(grads_one[0], *met)
-    sums_c.hold(grads_one[0], *met)
-    sums_b.send()
-    sums_c.send()
+    sums_b.hold(grads_one[0])
+    sums_c.hold(grads_one[0])
+    sums_b.send(*met)
+    sums_c.send(*met)
     grads_two = attend_back(cuts[1:], second, keys, values, attended, attended_grad, lse)
 
     runs = tuple((low * LANES, high * LANES) for low, high in zip(cuts[:-1], cuts[1:]))
@@ -904,23 +924,27 @@
     gate_grad = jnp.sum(cot_joined * (text_rows - image_rows), axis=0, keepdims=True) * mix * (1.0 - mix)
 
     slot_index = lax.iota(jnp.int32, 5)[:, None]
-    small = (
-        jnp.where(slot_index == stream, dgain_one[0:1], 0.0)
-        + jnp.where(slot_index == 1 - stream, dgain_one[1:2], 0.0)
-        + jnp.where(slot_index == 2 + stream, dgain_two[0:1], 0.0)
-        + jnp.where(slot_index == 4, gate_grad, 0.0)
-    )
+    small = dgain_one[:5] + dgain_two[:5] + jnp.where(slot_index == 4, gate_grad, 0.0)
     sums_a = Halving(kept_a, sent_a, steps_b)
     sums_a.hold(*sums_b.last, *sums_c.last)
     sums_a.send()
-    sums_a.rider = small + flip(small, *core[0])
+    sums_a.rider = rider_rows(small + flip(small, *core[0]), qkvs.wide)
     back_part = swap(away_part)
-    for one in (sums_b, sums_c):
-        one.hold(*[value for value in sums_a.outgoing if value is not None])
-    for one in (sums_a, sums_b, sums_c):
-        while one.left():
-            one.send()
-
+    sums_a.send()
+    sums_b.hold(*sums_a.messages)
+    sums_b.send()
+    sums_a.hold(*sums_b.messages)
+    sums_a.send()
+    sums_c.hold(*sums_a.messages)
+    sums_c.send()
+    sums_b.hold(*sums_a.messages)
+
+    total_a, total_b, total_c = sums_a.total(), sums_b.total(), sums_c.total()
+
+    last = total_a[1].astype(LOW)[None]
+    packed = with_rider(last, sums_a.rider)
+    arrived = swap(packed)
+    packed_c = total_c[1].astype(LOW)
     grad_rows = pl.pallas_call(
         functools.partial(tail_kernel, length),
         out_shape=full_rows,
@@ -928,12 +952,7 @@
         out_specs=VMEM,
         compiler_params=params(10),
         name="norm_tail",
-    )(rows, gain_own, own_part, back_part, after(middle_grad, *sums_a.last))
-
-    def late(pair):
-        return tuple(after(value, *sums_a.last) for value in pair)
-
-    total_a, total_b, total_c = sums_a.total(), sums_b.total(), sums_c.total()
+    )(rows, gain_own, own_part, back_part, after(middle_grad, packed, packed_c))
 
     def both(total):
         return total[0], swap(total[1].astype(LOW))
@@ -942,19 +961,24 @@
         theirs = theirs.astype(FULL)
         return jnp.where(is_text, jnp.stack((mine, theirs)), jnp.stack((theirs, mine)))
 
-    mine_b, theirs_b = late(both(total_b))
+    mine_b, theirs_b = both(total_b)
+    theirs_b = after(theirs_b, packed, packed_c)
     grad_b = placed(mine_b, theirs_b)
     grad_up = ups.cut(grad_b[..., : ups.wide], doc)
     grad_out = outs.cut(grad_b[..., ups.wide :], doc)
+    out_new = adam_update(w_out, m_out, v_out, grad_out, 0.5, 0.01)
+    up_new = adam_update(w_up, m_up, v_up, grad_up, 0.12, 0.01)
     if downs.aligned:
-        mine_c, theirs_c = late(both(total_c))
+        mine_c, theirs_c = total_c[0], swap(packed_c)
     else:
         mine_c = downs.cut(total_c[0], place)
         theirs_c = swap(downs.cut(total_c[1], (place + half) % wide).astype(LOW))
+    theirs_c = after(theirs_c, packed, grad_rows, up_new[0], out_new[0])
     grad_down = jnp.swapaxes(placed(mine_c, theirs_c), 1, 2)
-    last = total_a[1].astype(LOW)[None]
-    last, rider = rider_of(swap(with_rider(last, sums_a.rider)), sums_a.rider.shape, last.shape)
-    gains_grad = kept_rider(sums_a.rider) + rider
+    down_new = adam_update(w_down, m_down, v_down, grad_down, 0.06, 0.01)
+    arrived = after(arrived, grad_rows, up_new[0], out_new[0], down_new[0])
+    last, rider = rider_of(arrived, sums_a.rider.shape, last.shape)
+    gains_grad = rider_value(kept_rider(sums_a.rider) + rider, gains.shape)
     mine_a, theirs_a = total_a[0], last[0]
     mine_a, theirs_a = qkvs.cut(mine_a, doc), qkvs.cut(theirs_a.astype(FULL), doc)
     query_here = is_query[0]
@@ -963,9 +987,6 @@
     )
 
     qkv_new = adam_update(w_qkv, m_qkv, v_qkv, grad_qkv, 0.12, 0.01)
-    out_new = adam_update(w_out, m_out, v_out, grad_out, 0.5, 0.01)
-    up_new = adam_update(w_up, m_up, v_up, grad_up, 0.12, 0.01)
-    down_new = adam_update(w_down, m_down, v_down, grad_down, 0.06, 0.01)
     gains_new = adam_update(gains, m_gains, v_gains, gains_grad, 0.8, 0.0)
     return (stream_out, joined_rows, grad_rows, *qkv_new, *out_new, *up_new, *down_new, *gains_new)
 

time: 306 us -> 296 us (0.967)
  other arithmetic: 44.5 us -> 32.7 us
    convert_element_type x12 -> x16, other arithmetic: 20.7 us -> 10.4 us  [the longest x9 9.37 us: part_sums(): sum((part[half:].astype(FULL) for part in parts)).astype(LOW)]
    slice x3 -> x7, local copies, waits for them, and re-layouts: 2.56 us -> 5.92 us  [the longest x3 5.86 us: split(): return [value[:middle], value[middle:]]]
    unnamed x170 -> x152, local copies, waits for them, and re-layouts: 7.02 us -> 4.3 us
    ppermute x59 -> x61, waiting for transfers between devices: 84 us -> 85.4 us  [flip(): return lax.ppermute(value, axis, [(i, i ^ mask) for i in range(count)])]
    ppermute x59 -> x61, starting transfers between devices: 69.3 us -> 68.2 us  [flip(): return lax.ppermute(value, axis, [(i, i ^ mask) for i in range(count)])]
  transfers between devices with their start and end apart: 59 -> 61, of which waited for: 17 -> 21; matrix products, arithmetic and copies ran while one was open for 14% -> 12% of each run, Pallas kernels for 20% -> 21%
where the time goes in v5:
time: 296 us; the launch traced here: 295 us
  Pallas kernels  94.5 us (32%)
  waiting for transfers between devices  85.4 us (29%)
  starting transfers between devices  68.2 us (23%)
  other arithmetic  32.7 us (11%)
  local copies, waits for them, and re-layouts  12 us (4%)
    ppermute x61, waiting for transfers between devices, flip(): return lax.ppermute(value, axis, [(i, i ^ mask) for i in range(count)])  85.4 us
    ppermute x61, starting transfers between devices, flip(): return lax.ppermute(value, axis, [(i, i ^ mask) for i in range(count)])  68.2 us
    pallas_call x2, Pallas kernels, attend_back(): pl.pallas_call(functools.partial(scores_back_kernel, (length, width, fact...  34.8 us
    pallas_call x1, Pallas kernels, shards(): pl.pallas_call(functools.partial(feed_kernel, shape), out_shape=(full_row...  32.1 us
    pallas_call x1, Pallas kernels, shards(): pl.pallas_call(functools.partial(project_kernel, shape), out_shape=made,...  15.6 us
    pallas_call x1, Pallas kernels, shards(): pl.pallas_call(functools.partial(project_back_kernel, shape), out_shape=(...  9.9 us
    convert_element_type x9, other arithmetic, part_sums(): sum((part[half:].astype(FULL) for part in parts)).astype(LOW)  9.37 us
    sub x5, other arithmetic, adam_update(): weight - rate * (first_hat / (jnp.sqrt(second_hat) + 1e-08) + decay * wei...  6.03 us
  transfers between devices with their start and end apart: 61, of which 21 were waited for; matrix products, arithmetic and copies ran while one was open for 12% of the time, Pallas kernels for 21%

profile of v5, /device:TPU:0, one launch (start us, length us, event | category | flops | bytes accessed | tf_op | source)
XLA Modules:
  0.0 295.0 jit_solution(14455862292866416073)
XLA Ops:
  2.3 4.1 %collective-permute-start = (bf16[96,640]{1,0:T(8,128)(2,1)S(1)}, bf16[96,640]{1,0:T(8,128)(2,1)S(1)}, u32[]{:S(2)}, u32[]{:S(2)}) collective-permute-start(bf16[96,640]{1,0:T(8,128)(2,1)S(1)} %get-tuple-element.221), channel_id=1, source_target_pairs={{0,4},{1,5},{2,6},{3,7},{4,0},{5,1},{6,2},{7,3},{8,12},{9,13},{10,... | collective-permute-start | bytes 368648 | tf_op jit(solution)/shard_map/ppermute | solution.py:24
  6.4 1.6 collective-permute-start.4
  8.2 1.6 collective-permute-start.21
  14.1 1.6 collective-permute-start.5
  17.1 4.8 %collective-permute-done.9.refs_10_ = bf16[1,96,640]{2,1,0:T(8,128)(2,1)S(1)} collective-permute-done((bf16[1,96,640]{2,1,0:T(8,128)(2,1)S(1)}, bf16[1,96,640]{2,1,0:T(8,128)(2,1)S(1)}, u32[]{:S(2)}, u32[]{:S(2)}) %collective-permute-start.9) | collective-permute-done | bytes 122912 | tf_op jit(solution)/shard_map/ppermute | solution.py:24
  22.0 2.2 collective-permute-start.1
  24.3 1.6 collective-permute-start.10
  26.1 13.2 %collective-permute-done.1.refs_0_ = bf16[160,768]{1,0:T(8,128)(2,1)S(1)} collective-permute-done((bf16[160,768]{1,0:T(8,128)(2,1)S(1)}, bf16[160,768]{1,0:T(8,128)(2,1)S(1)}, u32[]{:S(2)}, u32[]{:S(2)}) %collective-permute-start.1) | collective-permute-done | bytes 245792 | tf_op jit(solution)/shard_map/ppermute | solution.py:24
  39.3 1.5 collective-permute-start.6
  41.0 1.6 collective-permute-start.11
  43.2 6.9 %collective-permute-start.18 = (bf16[1,96,1024]{2,1,0:T(8,128)(2,1)S(1)}, bf16[1,96,1024]{2,1,0:T(8,128)(2,1)S(1)}, u32[]{:S(2)}, u32[]{:S(2)}) collective-permute-start(bf16[1,96,1024]{2,1,0:T(8,128)(2,1)S(1)} %bitcast.67), channel_id=1, source_target_pairs={{0,2},{1,3},{2,0},{3,1},{4,6},{5,7},{6,4},{7,5},{8,10},{9,11},{10,... | collective-permute-start | bytes 589832 | tf_op jit(solution)/shard_map/ppermute | solution.py:24
  50.2 3.4 %collective-permute-done.2.refs_1_ = bf16[192,768]{1,0:T(8,128)(2,1)S(1)} collective-permute-done((bf16[192,768]{1,0:T(8,128)(2,1)S(1)}, bf16[192,768]{1,0:T(8,128)(2,1)S(1)}, u32[]{:S(2)}, u32[]{:S(2)}) %collective-permute-start.2) | collective-permute-done | bytes 294944 | tf_op jit(solution)/shard_map/ppermute | solution.py:24
  54.3 3.5 %collective-permute-done.18.refs_7_ = bf16[1,96,1024]{2,1,0:T(8,128)(2,1)S(1)} collective-permute-done((bf16[1,96,1024]{2,1,0:T(8,128)(2,1)S(1)}, bf16[1,96,1024]{2,1,0:T(8,128)(2,1)S(1)}, u32[]{:S(2)}, u32[]{:S(2)}) %collective-permute-start.18) | collective-permute-done | bytes 196640 | tf_op jit(solution)/shard_map/ppermute | solution.py:24
  57.8 4.1 %collective-permute-start.3 = (bf16[160,768]{1,0:T(8,128)(2,1)S(1)}, bf16[160,768]{1,0:T(8,128)(2,1)}, u32[]{:S(2)}, u32[]{:S(2)}) collective-permute-start(bf16[160,768]{1,0:T(8,128)(2,1)S(1)} %copy-done.66), channel_id=1, source_target_pairs={{0,4},{1,5},{2,6},{3,7},{4,0},{5,1},{6,2},{7,3},{8,12},{9,13},{10,... | collective-permute-start | bytes 737288 | tf_op jit(solution)/shard_map/ppermute | solution.py:24
  62.1 1.6 collective-permute-start.19
  64.3 5.5 %collective-permute-done.3.refs_2_ = bf16[160,768]{1,0:T(8,128)(2,1)} collective-permute-done((bf16[160,768]{1,0:T(8,128)(2,1)S(1)}, bf16[160,768]{1,0:T(8,128)(2,1)}, u32[]{:S(2)}, u32[]{:S(2)}) %collective-permute-start.3) | collective-permute-done | bytes 245792 | tf_op jit(solution)/shard_map/ppermute | solution.py:24
  69.8 1.5 collective-permute-start.26
  75.0 3.1 %collective-permute-done.26.refs_20_ = bf16[2,96,768]{2,1,0:T(8,128)(2,1)S(1)} collective-permute-done((bf16[2,96,768]{2,1,0:T(8,128)(2,1)S(1)}, bf16[2,96,768]{2,1,0:T(8,128)(2,1)S(1)}, u32[]{:S(2)}, u32[]{:S(2)}) %collective-permute-start.26) | collective-permute-done | bytes 294944 | tf_op jit(solution)/shard_map/ppermute | solution.py:24
  79.6 4.7 %collective-permute-start.29 = (bf16[4,96,1024]{2,1,0:T(8,128)(2,1)}, bf16[4,96,1024]{2,1,0:T(8,128)(2,1)}, u32[]{:S(2)}, u32[]{:S(2)}) collective-permute-start(bf16[4,96,1024]{2,1,0:T(8,128)(2,1)} %pad_maximum_fusion.1), channel_id=1, source_target_pairs={{0,2},{1,3},{2,0},{3,1},{4,6},{5,7},{6,4},{7,5},{8,10},{9,11},{10,... | collective-permute-start | bytes 2359304 | tf_op jit(solution)/shard_map/ppermute | solution.py:24
  84.3 1.5 collective-permute-start.30
  91.7 15.6 %project_attend.1 = (bf16[512,768]{1,0:T(8,128)(2,1)}, bf16[512,768]{1,0:T(8,128)(2,1)}, bf16[512,768]{1,0:T(8,128)(2,1)}, bf16[512,768]{1,0:T(8,128)(2,1)}, f32...) custom-call(s32[3]{0:T(128)} %pad_add_fusion.pos, f32[2,768]{1,0:T(2,128)} %pad_maximum_fusion.21.gains, ...), custom_call_target="tpu_custom_call" | custom-call | flops 1000 | bytes 1000 | tf_op jit(solution)/shard_map/project_attend/pallas_call | solution.py:788
  107.3 3.9 %collective-permute-done.29.refs_3_ = bf16[4,96,1024]{2,1,0:T(8,128)(2,1)} collective-permute-done((bf16[4,96,1024]{2,1,0:T(8,128)(2,1)}, bf16[4,96,1024]{2,1,0:T(8,128)(2,1)}, u32[]{:S(2)}, u32[]{:S(2)}) %collective-permute-start.29) | collective-permute-done | bytes 786464 | tf_op jit(solution)/shard_map/ppermute | solution.py:24
  111.2 2.7 collective-permute-done.32.refs_21_
  115.7 3.4 %collective-permute-done.36.refs_23_ = bf16[4,96,768]{2,1,0:T(8,128)(2,1)S(1)} collective-permute-done((bf16[4,96,768]{2,1,0:T(8,128)(2,1)}, bf16[4,96,768]{2,1,0:T(8,128)(2,1)S(1)}, u32[]{:S(2)}, u32[]{:S(2)}) %collective-permute-start.36) | collective-permute-done | bytes 589856 | tf_op jit(solution)/shard_map/ppermute | solution.py:24
  121.3 32.1 %feed_forward_back.1 = (f32[512,768]{1,0:T(8,128)}, f32[512,768]{1,0:T(8,128)}, bf16[512,768]{1,0:T(8,128)(2,1)}, bf16[256,768]{1,0:T(8,128)(2,1)}, f32[8,768]{1...) custom-call(s32[3]{0:T(128)} %pad_add_fusion.pos, ...), custom_call_target="tpu_custom_call" | custom-call | flops 1000 | bytes 1000 | tf_op jit(solution)/shard_map/feed_forward_back/pallas_call | solution.py:824
  155.4 27.1 %attend_back.2 = (bf16[512,512]{1,0:T(8,128)(2,1)}, bf16[512,512]{1,0:T(8,128)(2,1)}, bf16[512,512]{1,0:T(8,128)(2,1)}) custom-call(s32[512,1]{1,0:T(8,128)} %copy.39.page_col, s32[1,512]{1,0:T(1,128)} %bitcast.78, s32[1,512]{1,0:T(1,128)} %bitcast.82, bf16[512,768]{1,0:T(8,128)(2,1)} %get-tuple-element.124.q_hbm, ...), custom_call_target="tpu_custom_call" | custom-call | flops 1000 | bytes 1000 | tf_op jit(solution)/shard_map/attend_back/pallas_call | solution.py:864
  182.5 2.0 fusion.34
  187.3 2.5 fusion.33
  189.9 1.9 add_convert_fusion
  194.4 7.7 %attend_back.3 = (bf16[512,256]{1,0:T(8,128)(2,1)}, bf16[512,256]{1,0:T(8,128)(2,1)}, bf16[512,256]{1,0:T(8,128)(2,1)}) custom-call(s32[512,1]{1,0:T(8,128)} %copy.39.page_col, s32[1,512]{1,0:T(1,128)} %bitcast.79, s32[1,512]{1,0:T(1,128)} %bitcast.83, bf16[512,768]{1,0:T(8,128)(2,1)} %get-tuple-element.124.q_hbm, ...), custom_call_target="tpu_custom_call" | custom-call | flops 1000 | bytes 1000 | tf_op jit(solution)/shard_map/attend_back/pallas_call | solution.py:864
  202.2 9.9 %project_back.1 = (f32[512,768]{1,0:T(8,128)}, bf16[512,768]{1,0:T(8,128)(2,1)}, f32[8,768]{1,0:T(8,128)}, bf16[16,96,640]{2,1,0:T(8,128)(2,1)}, bf16[16,96,640]{2,1,0:T(8,128)(2,1)}) custom-call(s32[3]{0:T(128)} %pad_add_fusion.pos, f32[2,768]{1,0:T(2,128)} %pad_maximum_fusion.21.gains, bf16[512,768]{1,0:T(8,128)(2,1)} %own.1, ...), custom_call_target="tpu_custom_call" | custom-call | flops 1000 | bytes 1000 | tf_op jit(solution)/shard_map/project_back/pallas_call | solution.py:898
  212.1 2.6 collective-permute-done.43
  214.8 1.6 multiply_reduce_fusion
  220.4 1.6 add_convert_fusion.5
  222.1 1.6 collective-permute-start.48
  225.5 1.5 add_convert_fusion.6
  227.7 1.5 collective-permute-start.54
  229.2 8.6 %collective-permute-done.45 = bf16[4,96,640]{2,1,0:T(8,128)(2,1)S(1)} collective-permute-done((bf16[4,96,640]{2,1,0:T(8,128)(2,1)S(1)}, bf16[4,96,640]{2,1,0:T(8,128)(2,1)S(1)}, u32[]{:S(2)}, u32[]{:S(2)}) %collective-permute-start.45) | collective-permute-done | bytes 491552 | tf_op jit(solution)/shard_map/ppermute | solution.py:24
  240.7 4.8 %collective-permute-done.55 = bf16[2,96,1024]{2,1,0:T(8,128)(2,1)S(1)} collective-permute-done((bf16[2,96,1024]{2,1,0:T(8,128)(2,1)S(1)}, bf16[2,96,1024]{2,1,0:T(8,128)(2,1)S(1)}, u32[]{:S(2)}, u32[]{:S(2)}) %collective-permute-start.55) | collective-permute-done | bytes 393248 | tf_op jit(solution)/shard_map/ppermute | solution.py:24
  252.5 1.7 collective-permute-start.50
  254.3 1.6 collective-permute-done.58
  257.0 7.9 %collective-permute-done.56 = bf16[2,96,1024]{2,1,0:T(8,128)(2,1)S(1)} collective-permute-done((bf16[2,96,1024]{2,1,0:T(8,128)(2,1)S(1)}, bf16[2,96,1024]{2,1,0:T(8,128)(2,1)S(1)}, u32[]{:S(2)}, u32[]{:S(2)}) %collective-permute-start.56) | collective-permute-done | bytes 393248 | tf_op jit(solution)/shard_map/ppermute | solution.py:24
  266.5 1.6 collective-permute-start.52
  268.1 2.9 collective-permute-done.50
  272.4 3.0 %collective-permute-start.60 = (bf16[192,384]{1,0:T(8,128)(2,1)S(1)}, bf16[192,384]{1,0:T(8,128)(2,1)S(1)}, u32[]{:S(2)}, u32[]{:S(2)}) collective-permute-start(bf16[192,384]{1,0:T(8,128)(2,1)S(1)} %fusion.13), channel_id=1, source_target_pairs={{0,4},{1,5},{2,6},{3,7},{4,0},{5,1},{6,2},{7,3},{8,12},{9,13},{10,... | collective-permute-start | bytes 442376 | tf_op jit(solution)/shard_map/ppermute | solution.py:24
  275.4 2.2 norm_tail.1
  277.6 6.3 %collective-permute-done.57 = bf16[96,1024]{1,0:T(8,128)(2,1)S(1)} collective-permute-done((bf16[96,1024]{1,0:T(8,128)(2,1)S(1)}, bf16[96,1024]{1,0:T(8,128)(2,1)S(1)}, u32[]{:S(2)}, u32[]{:S(2)}) %collective-permute-start.57) | collective-permute-done | bytes 196640 | tf_op jit(solution)/shard_map/ppermute | solution.py:24
  286.6 3.8 %collective-permute-done.60 = bf16[192,384]{1,0:T(8,128)(2,1)S(1)} collective-permute-done((bf16[192,384]{1,0:T(8,128)(2,1)S(1)}, bf16[192,384]{1,0:T(8,128)(2,1)S(1)}, u32[]{:S(2)}, u32[]{:S(2)}) %collective-permute-start.60) | collective-permute-done | bytes 147488 | tf_op jit(solution)/shard_map/ppermute | solution.py:24
  (318 shorter events, 59.6 us)
Async XLA Ops:
  2.3 10.7 %collective-permute-start = (bf16[96,640]{1,0:T(8,128)(2,1)S(1)}, bf16[96,640]{1,0:T(8,128)(2,1)S(1)}, u32[]{:S(2)}, u32[]{:S(2)}) collective-permute-start(bf16[96,640]{1,0:T(8,128)(2,1)S(1)} %get-tuple-element.221), channel_id=1, source_target_pairs={{0,4},{1,5},{2,6},{3,7},{4,0},{5,1},{6,2},{7,3},{8,12},{9,13},{10,... | collective-permute-start | bytes 368648 | tf_op jit(solution)/shard_map/ppermute | solution.py:24
  8.2 35.1 %collective-permute-start.21 = (bf16[1,96,768]{2,1,0:T(8,128)(2,1)S(1)}, bf16[1,96,768]{2,1,0:T(8,128)(2,1)S(1)}, u32[]{:S(2)}, u32[]{:S(2)}) collective-permute-start(bf16[1,96,768]{2,1,0:T(8,128)(2,1)S(1)} %maximum_bitcast_fusion.refs_12_), channel_id=1, source_target_pairs={{0,16},{8,24},{16,0},{24,8},{1,17},{9,25},{17,1},{25,9},{2,18},{10... | collective-permute-start | bytes 442376 | tf_op jit(solution)/shard_map/ppermute | solution.py:24
  10.7 31.8 %collective-permute-start.17 = (bf16[96,1024]{1,0:T(8,128)(2,1)}, bf16[96,1024]{1,0:T(8,128)(2,1)S(1)}, u32[]{:S(2)}, u32[]{:S(2)}) collective-permute-start(bf16[96,1024]{1,0:T(8,128)(2,1)} %get-tuple-element.214), channel_id=1, source_target_pairs={{0,4},{1,5},{2,6},{3,7},{4,0},{5,1},{6,2},{7,3},{8,12},{9,13},{10,... | collective-permute-start | bytes 589832 | tf_op jit(solution)/shard_map/ppermute | solution.py:24
  11.1 13.2 %collective-permute-start.14 = (bf16[1,96,1024]{2,1,0:T(8,128)(2,1)S(1)}, bf16[1,96,1024]{2,1,0:T(8,128)(2,1)S(1)}, u32[]{:S(2)}, u32[]{:S(2)}) collective-permute-start(bf16[1,96,1024]{2,1,0:T(8,128)(2,1)S(1)} %get-tuple-element.215.refs_0_), channel_id=1, source_target_pairs={{0,16},{8,24},{16,0},{24,8},{1,17},{9,25},{17,1},{25,9},{2,18},{10... | collective-permute-start | bytes 589832 | tf_op jit(solution)/shard_map/ppermute | solution.py:24
  13.1 8.9 %collective-permute-start.9 = (bf16[1,96,640]{2,1,0:T(8,128)(2,1)S(1)}, bf16[1,96,640]{2,1,0:T(8,128)(2,1)S(1)}, u32[]{:S(2)}, u32[]{:S(2)}) collective-permute-start(bf16[1,96,640]{2,1,0:T(8,128)(2,1)S(1)} %bitcast.71), channel_id=1, source_target_pairs={{0,2},{1,3},{2,0},{3,1},{4,6},{5,7},{6,4},{7,5},{8,10},{9,11},{10,... | collective-permute-start | bytes 368648 | tf_op jit(solution)/shard_map/ppermute | solution.py:24
  14.1 11.8 %collective-permute-start.5 = (bf16[2,96,640]{2,1,0:T(8,128)(2,1)S(1)}, bf16[2,96,640]{2,1,0:T(8,128)(2,1)S(1)}, u32[]{:S(2)}, u32[]{:S(2)}) collective-permute-start(bf16[2,96,640]{2,1,0:T(8,128)(2,1)S(1)} %pad_maximum_fusion.15), channel_id=1, source_target_pairs={{0,8},{8,0},{16,24},{24,16},{1,9},{9,1},{17,25},{25,17},{2,10},{10... | collective-permute-start | bytes 737288 | tf_op jit(solution)/shard_map/ppermute | solution.py:24
  22.0 17.3 %collective-permute-start.1 = (bf16[160,768]{1,0:T(8,128)(2,1)S(1)}, bf16[160,768]{1,0:T(8,128)(2,1)S(1)}, u32[]{:S(2)}, u32[]{:S(2)}) collective-permute-start(bf16[160,768]{1,0:T(8,128)(2,1)S(1)} %copy-done.67), channel_id=1, source_target_pairs={{0,4},{1,5},{2,6},{3,7},{4,0},{5,1},{6,2},{7,3},{8,12},{9,13},{10,... | collective-permute-start | bytes 737288 | tf_op jit(solution)/shard_map/ppermute | solution.py:24
  24.3 16.6 %collective-permute-start.10 = (bf16[2,96,640]{2,1,0:T(8,128)(2,1)S(1)}, bf16[2,96,640]{2,1,0:T(8,128)(2,1)S(1)}, u32[]{:S(2)}, u32[]{:S(2)}) collective-permute-start(bf16[2,96,640]{2,1,0:T(8,128)(2,1)S(1)} %pad_maximum_fusion.16), channel_id=1, source_target_pairs={{0,16},{8,24},{16,0},{24,8},{1,17},{9,25},{17,1},{25,9},{2,18},{10... | collective-permute-start | bytes 737288 | tf_op jit(solution)/shard_map/ppermute | solution.py:24
  25.9 15.1 %collective-permute-start.24 = (bf16[192,384]{1,0:T(8,128)(2,1)S(1)}, bf16[192,384]{1,0:T(8,128)(2,1)S(1)}, u32[]{:S(2)}, u32[]{:S(2)}) collective-permute-start(bf16[192,384]{1,0:T(8,128)(2,1)S(1)} %slice_bitcast_fusion), channel_id=1, source_target_pairs={{0,4},{1,5},{2,6},{3,7},{4,0},{5,1},{6,2},{7,3},{8,12},{9,13},{10,... | collective-permute-start | bytes 442376 | tf_op jit(solution)/shard_map/ppermute | solution.py:24
  39.3 18.5 %collective-permute-start.6 = (bf16[4,96,640]{2,1,0:T(8,128)(2,1)S(1)}, bf16[4,96,640]{2,1,0:T(8,128)(2,1)S(1)}, u32[]{:S(2)}, u32[]{:S(2)}) collective-permute-start(bf16[4,96,640]{2,1,0:T(8,128)(2,1)S(1)} %pad_maximum_fusion.6), channel_id=1, source_target_pairs={{0,16},{8,24},{16,0},{24,8},{1,17},{9,25},{17,1},{25,9},{2,18},{10... | collective-permute-start | bytes 1474568 | tf_op jit(solution)/shard_map/ppermute | solution.py:24
  40.8 12.8 %collective-permute-start.2 = (bf16[192,768]{1,0:T(8,128)(2,1)S(1)}, bf16[192,768]{1,0:T(8,128)(2,1)S(1)}, u32[]{:S(2)}, u32[]{:S(2)}) collective-permute-start(bf16[192,768]{1,0:T(8,128)(2,1)S(1)} %slice.514), channel_id=1, source_target_pairs={{0,4},{1,5},{2,6},{3,7},{4,0},{5,1},{6,2},{7,3},{8,12},{9,13},{10,... | collective-permute-start | bytes 884744 | tf_op jit(solution)/shard_map/ppermute | solution.py:24
  41.0 21.0 %collective-permute-start.11 = (bf16[4,96,640]{2,1,0:T(8,128)(2,1)S(1)}, bf16[4,96,640]{2,1,0:T(8,128)(2,1)S(1)}, u32[]{:S(2)}, u32[]{:S(2)}) collective-permute-start(bf16[4,96,640]{2,1,0:T(8,128)(2,1)S(1)} %pad_maximum_fusion.7), channel_id=1, source_target_pairs={{0,8},{8,0},{16,24},{24,16},{1,9},{9,1},{17,25},{25,17},{2,10},{10... | collective-permute-start | bytes 1474568 | tf_op jit(solution)/shard_map/ppermute | solution.py:24
  42.6 21.1 %collective-permute-start.15 = (bf16[2,96,1024]{2,1,0:T(8,128)(2,1)S(1)}, bf16[2,96,1024]{2,1,0:T(8,128)(2,1)S(1)}, u32[]{:S(2)}, u32[]{:S(2)}) collective-permute-start(bf16[2,96,1024]{2,1,0:T(8,128)(2,1)S(1)} %pad_maximum_fusion.8), channel_id=1, source_target_pairs={{0,8},{8,0},{16,24},{24,16},{1,9},{9,1},{17,25},{25,17},{2,10},{10... | collective-permute-start | bytes 1179656 | tf_op jit(solution)/shard_map/ppermute | solution.py:24
  43.2 14.6 %collective-permute-start.18 = (bf16[1,96,1024]{2,1,0:T(8,128)(2,1)S(1)}, bf16[1,96,1024]{2,1,0:T(8,128)(2,1)S(1)}, u32[]{:S(2)}, u32[]{:S(2)}) collective-permute-start(bf16[1,96,1024]{2,1,0:T(8,128)(2,1)S(1)} %bitcast.67), channel_id=1, source_target_pairs={{0,2},{1,3},{2,0},{3,1},{4,6},{5,7},{6,4},{7,5},{8,10},{9,11},{10,... | collective-permute-start | bytes 589832 | tf_op jit(solution)/shard_map/ppermute | solution.py:24
  53.6 10.0 %collective-permute-start.25 = (bf16[1,96,768]{2,1,0:T(8,128)(2,1)S(1)}, bf16[1,96,768]{2,1,0:T(8,128)(2,1)S(1)}, u32[]{:S(2)}, u32[]{:S(2)}) collective-permute-start(bf16[1,96,768]{2,1,0:T(8,128)(2,1)S(1)} %maximum_bitcast_fusion.1.refs_18_), channel_id=1, source_target_pairs={{0,2},{1,3},{2,0},{3,1},{4,6},{5,7},{6,4},{7,5},{8,10},{9,11},{10,... | collective-permute-start | bytes 442376 | tf_op jit(solution)/shard_map/ppermute | solution.py:24
  57.8 14.7 %collective-permute-start.22 = (bf16[2,96,768]{2,1,0:T(8,128)(2,1)S(1)}, bf16[2,96,768]{2,1,0:T(8,128)(2,1)S(1)}, u32[]{:S(2)}, u32[]{:S(2)}) collective-permute-start(bf16[2,96,768]{2,1,0:T(8,128)(2,1)S(1)} %pad_maximum_fusion.11), channel_id=1, source_target_pairs={{0,2},{1,3},{2,0},{3,1},{4,6},{5,7},{6,4},{7,5},{8,10},{9,11},{10,... | collective-permute-start | bytes 884744 | tf_op jit(solution)/shard_map/ppermute | solution.py:24
  57.8 11.9 %collective-permute-start.3 = (bf16[160,768]{1,0:T(8,128)(2,1)S(1)}, bf16[160,768]{1,0:T(8,128)(2,1)}, u32[]{:S(2)}, u32[]{:S(2)}) collective-permute-start(bf16[160,768]{1,0:T(8,128)(2,1)S(1)} %copy-done.66), channel_id=1, source_target_pairs={{0,4},{1,5},{2,6},{3,7},{4,0},{5,1},{6,2},{7,3},{8,12},{9,13},{10,... | collective-permute-start | bytes 737288 | tf_op jit(solution)/shard_map/ppermute | solution.py:24
  62.1 11.3 %collective-permute-start.19 = (bf16[2,96,1024]{2,1,0:T(8,128)(2,1)S(1)}, bf16[2,96,1024]{2,1,0:T(8,128)(2,1)S(1)}, u32[]{:S(2)}, u32[]{:S(2)}) collective-permute-start(bf16[2,96,1024]{2,1,0:T(8,128)(2,1)S(1)} %pad_maximum_fusion.9), channel_id=1, source_target_pairs={{0,8},{8,0},{16,24},{24,16},{1,9},{9,1},{17,25},{25,17},{2,10},{10... | collective-permute-start | bytes 1179656 | tf_op jit(solution)/shard_map/ppermute | solution.py:24
  63.6 11.3 %collective-permute-start.7 = (bf16[4,96,640]{2,1,0:T(8,128)(2,1)S(1)}, bf16[4,96,640]{2,1,0:T(8,128)(2,1)S(1)}, u32[]{:S(2)}, u32[]{:S(2)}) collective-permute-start(bf16[4,96,640]{2,1,0:T(8,128)(2,1)S(1)} %pad_maximum_fusion.6), channel_id=1, source_target_pairs={{0,1},{1,0},{2,3},{3,2},{4,5},{5,4},{6,7},{7,6},{8,9},{9,8},{10,11... | collective-permute-start | bytes 1474568 | tf_op jit(solution)/shard_map/ppermute | solution.py:24
  63.7 15.3 %collective-permute-start.12 = (bf16[4,96,640]{2,1,0:T(8,128)(2,1)S(1)}, bf16[4,96,640]{2,1,0:T(8,128)(2,1)S(1)}, u32[]{:S(2)}, u32[]{:S(2)}) collective-permute-start(bf16[4,96,640]{2,1,0:T(8,128)(2,1)S(1)} %pad_maximum_fusion.7), channel_id=1, source_target_pairs={{0,1},{1,0},{2,3},{3,2},{4,5},{5,4},{6,7},{7,6},{8,9},{9,8},{10,11... | collective-permute-start | bytes 1474568 | tf_op jit(solution)/shard_map/ppermute | solution.py:24
  72.5 11.8 %collective-permute-start.16 = (bf16[4,96,1024]{2,1,0:T(8,128)(2,1)}, bf16[4,96,1024]{2,1,0:T(8,128)(2,1)S(1)}, u32[]{:S(2)}, u32[]{:S(2)}) collective-permute-start(bf16[4,96,1024]{2,1,0:T(8,128)(2,1)} %pad_maximum_fusion.1), channel_id=1, source_target_pairs={{0,1},{1,0},{2,3},{3,2},{4,5},{5,4},{6,7},{7,6},{8,9},{9,8},{10,11... | collective-permute-start | bytes 2359304 | tf_op jit(solution)/shard_map/ppermute | solution.py:24
  78.1 9.3 %collective-permute-start.20 = (bf16[4,96,1024]{2,1,0:T(8,128)(2,1)}, bf16[4,96,1024]{2,1,0:T(8,128)(2,1)S(1)}, u32[]{:S(2)}, u32[]{:S(2)}) collective-permute-start(bf16[4,96,1024]{2,1,0:T(8,128)(2,1)} %pad_maximum_fusion.2), channel_id=1, source_target_pairs={{0,1},{1,0},{2,3},{3,2},{4,5},{5,4},{6,7},{7,6},{8,9},{9,8},{10,11... | collective-permute-start | bytes 2359304 | tf_op jit(solution)/shard_map/ppermute | solution.py:24
  79.5 8.4 %collective-permute-start.13 = (bf16[4,96,640]{2,1,0:T(8,128)(2,1)S(1)}, bf16[4,96,640]{2,1,0:T(8,128)(2,1)S(1)}, u32[]{:S(2)}, u32[]{:S(2)}) collective-permute-start(bf16[4,96,640]{2,1,0:T(8,128)(2,1)S(1)} %collective-permute-done.11.refs_12_), channel_id=1, source_target_pairs={{0,1},{1,0},{2,3},{3,2},{4,5},{5,4},{6,7},{7,6},{8,9},{9,8},{10,11... | collective-permute-start | bytes 1474568 | tf_op jit(solution)/shard_map/ppermute | solution.py:24
  79.6 31.5 %collective-permute-start.29 = (bf16[4,96,1024]{2,1,0:T(8,128)(2,1)}, bf16[4,96,1024]{2,1,0:T(8,128)(2,1)}, u32[]{:S(2)}, u32[]{:S(2)}) collective-permute-start(bf16[4,96,1024]{2,1,0:T(8,128)(2,1)} %pad_maximum_fusion.1), channel_id=1, source_target_pairs={{0,2},{1,3},{2,0},{3,1},{4,6},{5,7},{6,4},{7,5},{8,10},{9,11},{10,... | collective-permute-start | bytes 2359304 | tf_op jit(solution)/shard_map/ppermute | solution.py:24
  84.3 29.6 %collective-permute-start.30 = (bf16[4,96,1024]{2,1,0:T(8,128)(2,1)}, bf16[4,96,1024]{2,1,0:T(8,128)(2,1)}, u32[]{:S(2)}, u32[]{:S(2)}) collective-permute-start(bf16[4,96,1024]{2,1,0:T(8,128)(2,1)} %pad_maximum_fusion.2), channel_id=1, source_target_pairs={{0,16},{8,24},{16,0},{24,8},{1,17},{9,25},{17,1},{25,9},{2,18},{10... | collective-permute-start | bytes 2359304 | tf_op jit(solution)/shard_map/ppermute | solution.py:24
  85.8 21.4 %collective-permute-start.31 = (bf16[4,96,768]{2,1,0:T(8,128)(2,1)}, bf16[4,96,768]{2,1,0:T(8,128)(2,1)}, u32[]{:S(2)}, u32[]{:S(2)}) collective-permute-start(bf16[4,96,768]{2,1,0:T(8,128)(2,1)} %pad_maximum_fusion.3), channel_id=1, source_target_pairs={{0,8},{8,0},{16,24},{24,16},{1,9},{9,1},{17,25},{25,17},{2,10},{10... | collective-permute-start | bytes 1769480 | tf_op jit(solution)/shard_map/ppermute | solution.py:24
  87.3 26.6 %collective-permute-start.32 = (bf16[4,96,768]{2,1,0:T(8,128)(2,1)}, bf16[4,96,768]{2,1,0:T(8,128)(2,1)}, u32[]{:S(2)}, u32[]{:S(2)}) collective-permute-start(bf16[4,96,768]{2,1,0:T(8,128)(2,1)} %pad_maximum_fusion.4), channel_id=1, source_target_pairs={{0,8},{8,0},{16,24},{24,16},{1,9},{9,1},{17,25},{25,17},{2,10},{10... | collective-permute-start | bytes 1769480 | tf_op jit(solution)/shard_map/ppermute | solution.py:24
  88.8 25.2 %collective-permute-start.28 = (bf16[256,768]{1,0:T(8,128)(2,1)}, bf16[256,768]{1,0:T(8,128)(2,1)S(1)}, u32[]{:S(2)}, u32[]{:S(2)}) collective-permute-start(bf16[256,768]{1,0:T(8,128)(2,1)} %convert_element_type.433), channel_id=1, source_target_pairs={{0,4},{1,5},{2,6},{3,7},{4,0},{5,1},{6,2},{7,3},{8,12},{9,13},{10,... | collective-permute-start | bytes 1179656 | tf_op jit(solution)/shard_map/ppermute | solution.py:24
  153.4 32.2 %collective-permute-start.38 = (bf16[16,96,1024]{2,1,0:T(8,128)(2,1)}, bf16[16,96,1024]{2,1,0:T(8,128)(2,1)}, u32[]{:S(2)}, u32[]{:S(2)}) collective-permute-start(bf16[16,96,1024]{2,1,0:T(8,128)(2,1)} %get-tuple-element.122), channel_id=1, source_target_pairs={{0,1},{1,0},{2,3},{3,2},{4,5},{5,4},{6,7},{7,6},{8,9},{9,8},{10,11... | collective-permute-start | bytes 9437192 | tf_op jit(solution)/shard_map/ppermute | solution.py:24
  153.6 28.9 %collective-permute-start.39 = (bf16[16,192,384]{2,1,0:T(8,128)(2,1)}, bf16[16,192,384]{2,1,0:T(8,128)(2,1)}, u32[]{:S(2)}, u32[]{:S(2)}) collective-permute-start(bf16[16,192,384]{2,1,0:T(8,128)(2,1)} %get-tuple-element.123), channel_id=1, source_target_pairs={{0,1},{1,0},{2,3},{3,2},{4,5},{5,4},{6,7},{7,6},{8,9},{9,8},{10,11... | collective-permute-start | bytes 7077896 | tf_op jit(solution)/shard_map/ppermute | solution.py:24
  154.0 31.6 %collective-permute-start.37 = (bf16[256,768]{1,0:T(8,128)(2,1)}, bf16[256,768]{1,0:T(8,128)(2,1)S(1)}, u32[]{:S(2)}, u32[]{:S(2)}) collective-permute-start(bf16[256,768]{1,0:T(8,128)(2,1)} %get-tuple-element.112), channel_id=1, source_target_pairs={{0,4},{1,5},{2,6},{3,7},{4,0},{5,1},{6,2},{7,3},{8,12},{9,13},{10,... | collective-permute-start | bytes 1179656 | tf_op jit(solution)/shard_map/ppermute | solution.py:24
  186.7 28.1 %collective-permute-start.43 = (bf16[8,192,384]{2,1,0:T(8,128)(2,1)}, bf16[8,192,384]{2,1,0:T(8,128)(2,1)}, u32[]{:S(2)}, u32[]{:S(2)}) collective-permute-start(bf16[8,192,384]{2,1,0:T(8,128)(2,1)} %pad_maximum_fusion), channel_id=1, source_target_pairs={{0,2},{1,3},{2,0},{3,1},{4,6},{5,7},{6,4},{7,5},{8,10},{9,11},{10,... | collective-permute-start | bytes 3538952 | tf_op jit(solution)/shard_map/ppermute | solution.py:24
  191.7 20.4 %collective-permute-start.42 = (bf16[4,96,1024]{2,1,0:T(8,128)(2,1)}, bf16[4,96,1024]{2,1,0:T(8,128)(2,1)}, u32[]{:S(2)}, u32[]{:S(2)}) collective-permute-start(bf16[4,96,1024]{2,1,0:T(8,128)(2,1)} %get-tuple-element.137), channel_id=1, source_target_pairs={{0,16},{8,24},{16,0},{24,8},{1,17},{9,25},{17,1},{25,9},{2,18},{10... | collective-permute-start | bytes 2359304 | tf_op jit(solution)/shard_map/ppermute | solution.py:24
  192.9 19.2 %collective-permute-start.41 = (bf16[4,96,1024]{2,1,0:T(8,128)(2,1)}, bf16[4,96,1024]{2,1,0:T(8,128)(2,1)}, u32[]{:S(2)}, u32[]{:S(2)}) collective-permute-start(bf16[4,96,1024]{2,1,0:T(8,128)(2,1)} %get-tuple-element.135), channel_id=1, source_target_pairs={{0,8},{8,0},{16,24},{24,16},{1,9},{9,1},{17,25},{25,17},{2,10},{10... | collective-permute-start | bytes 2359304 | tf_op jit(solution)/shard_map/ppermute | solution.py:24
  218.9 56.5 %collective-permute-start.40 = (bf16[512,768]{1,0:T(8,128)(2,1)}, bf16[512,768]{1,0:T(8,128)(2,1)S(1)}, u32[]{:S(2)}, u32[]{:S(2)}) collective-permute-start(bf16[512,768]{1,0:T(8,128)(2,1)} %get-tuple-element.129), channel_id=1, source_target_pairs={{0,4},{1,5},{2,6},{3,7},{4,0},{5,1},{6,2},{7,3},{8,12},{9,13},{10,... | collective-permute-start | bytes 2359304 | tf_op jit(solution)/shard_map/ppermute | solution.py:24
  222.1 15.7 %collective-permute-start.48 = (bf16[416,640]{1,0:T(8,128)(2,1)S(1)}, bf16[416,640]{1,0:T(8,128)(2,1)S(1)}, u32[]{:S(2)}, u32[]{:S(2)}) collective-permute-start(bf16[416,640]{1,0:T(8,128)(2,1)S(1)} %pad_maximum_fusion.5), channel_id=1, source_target_pairs={{0,8},{8,0},{16,24},{24,16},{1,9},{9,1},{17,25},{25,17},{2,10},{10... | collective-permute-start | bytes 1597448 | tf_op jit(solution)/shard_map/ppermute | solution.py:24
  223.7 14.2 %collective-permute-start.45 = (bf16[4,96,640]{2,1,0:T(8,128)(2,1)S(1)}, bf16[4,96,640]{2,1,0:T(8,128)(2,1)S(1)}, u32[]{:S(2)}, u32[]{:S(2)}) collective-permute-start(bf16[4,96,640]{2,1,0:T(8,128)(2,1)S(1)} %get-tuple-element.186), channel_id=1, source_target_pairs={{0,16},{8,24},{16,0},{24,8},{1,17},{9,25},{17,1},{25,9},{2,18},{10... | collective-permute-start | bytes 1474568 | tf_op jit(solution)/shard_map/ppermute | solution.py:24
  227.1 18.5 %collective-permute-start.55 = (bf16[2,96,1024]{2,1,0:T(8,128)(2,1)S(1)}, bf16[2,96,1024]{2,1,0:T(8,128)(2,1)S(1)}, u32[]{:S(2)}, u32[]{:S(2)}) collective-permute-start(bf16[2,96,1024]{2,1,0:T(8,128)(2,1)S(1)} %get-tuple-element.192), channel_id=1, source_target_pairs={{0,8},{8,0},{16,24},{24,16},{1,9},{9,1},{17,25},{25,17},{2,10},{10... | collective-permute-start | bytes 1179656 | tf_op jit(solution)/shard_map/ppermute | solution.py:24
  227.7 18.6 %collective-permute-start.54 = (bf16[2,96,1024]{2,1,0:T(8,128)(2,1)S(1)}, bf16[2,96,1024]{2,1,0:T(8,128)(2,1)S(1)}, u32[]{:S(2)}, u32[]{:S(2)}) collective-permute-start(bf16[2,96,1024]{2,1,0:T(8,128)(2,1)S(1)} %get-tuple-element.193), channel_id=1, source_target_pairs={{0,16},{8,24},{16,0},{24,8},{1,17},{9,25},{17,1},{25,9},{2,18},{10... | collective-permute-start | bytes 1179656 | tf_op jit(solution)/shard_map/ppermute | solution.py:24
  239.4 11.5 %collective-permute-start.49 = (bf16[224,640]{1,0:T(8,128)(2,1)S(1)}, bf16[224,640]{1,0:T(8,128)(2,1)S(1)}, u32[]{:S(2)}, u32[]{:S(2)}) collective-permute-start(bf16[224,640]{1,0:T(8,128)(2,1)S(1)} %pad_maximum_fusion.13), channel_id=1, source_target_pairs={{0,16},{8,24},{16,0},{24,8},{1,17},{9,25},{17,1},{25,9},{2,18},{10... | collective-permute-start | bytes 860168 | tf_op jit(solution)/shard_map/ppermute | solution.py:24
  239.9 11.4 %collective-permute-start.47 = (bf16[2,96,640]{2,1,0:T(8,128)(2,1)S(1)}, bf16[2,96,640]{2,1,0:T(8,128)(2,1)S(1)}, u32[]{:S(2)}, u32[]{:S(2)}) collective-permute-start(bf16[2,96,640]{2,1,0:T(8,128)(2,1)S(1)} %get-tuple-element.184), channel_id=1, source_target_pairs={{0,8},{8,0},{16,24},{24,16},{1,9},{9,1},{17,25},{25,17},{2,10},{10... | collective-permute-start | bytes 737288 | tf_op jit(solution)/shard_map/ppermute | solution.py:24
  247.6 17.3 %collective-permute-start.56 = (bf16[2,96,1024]{2,1,0:T(8,128)(2,1)S(1)}, bf16[2,96,1024]{2,1,0:T(8,128)(2,1)S(1)}, u32[]{:S(2)}, u32[]{:S(2)}) collective-permute-start(bf16[2,96,1024]{2,1,0:T(8,128)(2,1)S(1)} %pad_maximum_fusion.10), channel_id=1, source_target_pairs={{0,2},{1,3},{2,0},{3,1},{4,6},{5,7},{6,4},{7,5},{8,10},{9,11},{10,... | collective-permute-start | bytes 1179656 | tf_op jit(solution)/shard_map/ppermute | solution.py:24
  250.8 15.5 %collective-permute-start.51 = (bf16[2,192,384]{2,1,0:T(8,128)(2,1)S(1)}, bf16[2,192,384]{2,1,0:T(8,128)(2,1)S(1)}, u32[]{:S(2)}, u32[]{:S(2)}) collective-permute-start(bf16[2,192,384]{2,1,0:T(8,128)(2,1)S(1)} %get-tuple-element.201), channel_id=1, source_target_pairs={{0,16},{8,24},{16,0},{24,8},{1,17},{9,25},{17,1},{25,9},{2,18},{10... | collective-permute-start | bytes 884744 | tf_op jit(solution)/shard_map/ppermute | solution.py:24
  252.5 18.5 %collective-permute-start.50 = (bf16[224,640]{1,0:T(8,128)(2,1)S(1)}, bf16[224,640]{1,0:T(8,128)(2,1)S(1)}, u32[]{:S(2)}, u32[]{:S(2)}) collective-permute-start(bf16[224,640]{1,0:T(8,128)(2,1)S(1)} %pad_maximum_fusion.14), channel_id=1, source_target_pairs={{0,2},{1,3},{2,0},{3,1},{4,6},{5,7},{6,4},{7,5},{8,10},{9,11},{10,... | collective-permute-start | bytes 860168 | tf_op jit(solution)/shard_map/ppermute | solution.py:24
  256.0 10.3 %collective-permute-start.59 = (bf16[1,192,384]{2,1,0:T(8,128)(2,1)S(1)}, bf16[1,192,384]{2,1,0:T(8,128)(2,1)S(1)}, u32[]{:S(2)}, u32[]{:S(2)}) collective-permute-start(bf16[1,192,384]{2,1,0:T(8,128)(2,1)S(1)} %add_convert_fusion.16), channel_id=1, source_target_pairs={{0,16},{8,24},{16,0},{24,8},{1,17},{9,25},{17,1},{25,9},{2,18},{10... | collective-permute-start | bytes 442376 | tf_op jit(solution)/shard_map/ppermute | solution.py:24
  266.2 17.7 %collective-permute-start.57 = (bf16[96,1024]{1,0:T(8,128)(2,1)S(1)}, bf16[96,1024]{1,0:T(8,128)(2,1)S(1)}, u32[]{:S(2)}, u32[]{:S(2)}) collective-permute-start(bf16[96,1024]{1,0:T(8,128)(2,1)S(1)} %get-tuple-element.189), channel_id=1, source_target_pairs={{0,4},{1,5},{2,6},{3,7},{4,0},{5,1},{6,2},{7,3},{8,12},{9,13},{10,... | collective-permute-start | bytes 589832 | tf_op jit(solution)/shard_map/ppermute | solution.py:24
  272.2 19.8 %collective-permute-start.53 = (bf16[128,640]{1,0:T(8,128)(2,1)S(1)}, bf16[128,640]{1,0:T(8,128)(2,1)S(1)}, u32[]{:S(2)}, u32[]{:S(2)}) collective-permute-start(bf16[128,640]{1,0:T(8,128)(2,1)S(1)} %pad_maximum_fusion.19), channel_id=1, source_target_pairs={{0,4},{1,5},{2,6},{3,7},{4,0},{5,1},{6,2},{7,3},{8,12},{9,13},{10,... | collective-permute-start | bytes 491528 | tf_op jit(solution)/shard_map/ppermute | solution.py:24
  272.4 18.1 %collective-permute-start.60 = (bf16[192,384]{1,0:T(8,128)(2,1)S(1)}, bf16[192,384]{1,0:T(8,128)(2,1)S(1)}, u32[]{:S(2)}, u32[]{:S(2)}) collective-permute-start(bf16[192,384]{1,0:T(8,128)(2,1)S(1)} %fusion.13), channel_id=1, source_target_pairs={{0,4},{1,5},{2,6},{3,7},{4,0},{5,1},{6,2},{7,3},{8,12},{9,13},{10,... | collective-permute-start | bytes 442376 | tf_op jit(solution)/shard_map/ppermute | solution.py:24
  (89 other events, 919.7 us)
